TPU v7x, 32 devices: a whole 2x2x4 slice. The times are simulated.
32 devices in a mesh: rep: 2 (over y), head: 4 (over x, core), row: 4 (over z).
Axes of the slice: x: 2, y: 2, z: 4, core: 2. Of those that a mesh axis runs over, the one named last changes fastest.
Arguments:
- hidden: bfloat16 [256, 2, 8192], P(('rep', 'row'), None, 'head'), parts along dimension 0, may hold values from -6 to 6
- input_norm_scale: float32 [8192], P('head'), may hold values from 0.5 to 1.5
- projection_signal: bfloat16 [8192, 4096], P('row', 'head'), may hold values from -0.0625 to 0.0625
- projection_gate: bfloat16 [8192, 4096], P('row', 'head'), may hold values from -0.0625 to 0.0625
- projection_step: bfloat16 [8192, 64], P('row', 'head'), may hold values from -0.0625 to 0.0625
- projection_input_output: bfloat16 [8192, 256], P('row'), may hold values from -0.0625 to 0.0625
- step_bias: float32 [64], P('head'), may hold values from -4 to 0
- head_decay_rate: float32 [64], P('head'), may hold values from 0.5 to 16
- head_skip_weight: float32 [64], P('head'), may hold values from 0.5 to 1.5
- gated_norm_scale: float32 [4096], P('head'), may hold values from 0.5 to 1.5
- adapter_down_weight: bfloat16 [512, 8192, 16], P('row', 'head'), may hold values from -0.0625 to 0.0625
- adapter_up_weight: bfloat16 [512, 16, 4096], P('row', None, 'head'), may hold values from -1.5 to 1.5
- output_weight: bfloat16 [4096, 8192], P('head'), may hold values from -0.125 to 0.125
- scan_state: bfloat16 [256, 64, 64, 128], P(('rep', 'row'), 'head'), parts along dimension 0, may hold values from -6 to 6
- stream_tenant_index: int32 [256], P(('rep', 'row')), parts along dimension 0, may hold values from 0 to 511, as said below
- live_block_rows: int32 [8], P(('rep', 'row')), parts along dimension 0, may hold values from 1 to 32
Outputs:
- mixed: bfloat16 [256, 2, 8192], P(('rep', 'row'), None, 'head'), parts along dimension 0
- new_state: bfloat16 [256, 64, 64, 128], P(('rep', 'row'), 'head'), parts along dimension 0
There are 2 independent parts, one for each index of `rep`. A program takes and returns all parts, laid end to end along the dimension named above; an argument that names none is the same for every part. Nothing has to cross between parts.
Inputs may be any that keep to these rules, and one draw needn't show every extreme that they name: `stream_tenant_index`: a stream of block b has a tenant of b * 128 up to (b + 1) * 128 - 1.
All inputs are finite; a program needn't handle non-finite values.
Results may differ from a plain program's by a relative error of at most 0.02.
Values may be sent and summed in bfloat16 or wider, within the bound.
No kernel may reach another device: no remote copies, remote signals or barrier semaphores. Data moves between devices by JAX's collectives and lax.ppermute only.
A program may use at most 128 MiB of HBM per device.

v0:
```python
import jax
import jax.numpy as jnp
from jax import lax
from jax.sharding import PartitionSpec as P

MODEL_WIDTH = 8192
INNER_WIDTH = 4096


def on_device(
    hidden,
    input_norm_scale,
    projection_signal,
    projection_gate,
    projection_step,
    projection_input_output,
    step_bias,
    head_decay_rate,
    head_skip_weight,
    gated_norm_scale,
    adapter_down_weight,
    adapter_up_weight,
    output_weight,
    scan_state,
    stream_tenant_index,
    live_block_rows,
):
    epsilon = 1e-05
    streams = hidden.shape[0]
    positions = hidden.shape[1]
    inner = projection_signal.shape[1]
    heads_here = projection_step.shape[1]
    state_width = projection_input_output.shape[1] // 2
    feature_width = hidden.shape[2]
    wide = hidden.astype(jnp.float32)
    tenant_local = stream_tenant_index - lax.axis_index("row") * adapter_down_weight.shape[0]
    scaled = (wide * input_norm_scale).astype(jnp.bfloat16)
    down_weight_rows = jnp.take(adapter_down_weight, tenant_local, axis=0)
    square_part = jnp.sum(wide * wide, -1)
    lowrank_part = jnp.einsum(
        "spd,sdr->spr", scaled, down_weight_rows, preferred_element_type=jnp.float32
    )
    squares, lowrank_sum = lax.psum((square_part, lowrank_part), "head")
    inverse = lax.rsqrt(squares / MODEL_WIDTH + epsilon)
    lowrank = (lowrank_sum * inverse[..., None]).astype(jnp.bfloat16)
    normed = (wide * input_norm_scale * inverse[..., None]).astype(jnp.bfloat16)
    features = lax.all_gather(normed, "head", axis=2, tiled=True)
    weight_cat = jnp.concatenate(
        [projection_signal, projection_gate, projection_step, projection_input_output], axis=1
    )
    moved = lax.all_to_all(features, "row", split_axis=2, concat_axis=0, tiled=True)
    moved_flat = moved.reshape(-1, moved.shape[2])
    projected = lax.psum_scatter(
        jnp.dot(moved_flat, weight_cat, preferred_element_type=jnp.float32).astype(jnp.bfloat16),
        "row",
        scatter_dimension=0,
        tiled=True,
    ).astype(jnp.float32)
    projected = projected.reshape(streams, positions, -1)
    xin = projected[..., :inner]
    zin = projected[..., inner : 2 * inner]
    dtin = projected[..., 2 * inner : 2 * inner + heads_here]
    bcin = projected[..., 2 * inner + heads_here :]
    up_weight_rows = jnp.take(adapter_up_weight, tenant_local, axis=0)
    signal = jax.nn.silu(
        xin
        + jnp.einsum("spr,srk->spk", lowrank, up_weight_rows, preferred_element_type=jnp.float32)
    )
    bgate = jax.nn.silu(bcin[..., :state_width])
    cgate = jax.nn.silu(bcin[..., state_width:])
    steps_dt = jax.nn.softplus(dtin + step_bias)
    decay = jnp.exp(-steps_dt * head_decay_rate)
    live = jnp.arange(streams) < live_block_rows[0]
    signal_heads = signal.reshape(streams, positions, heads_here, -1)
    carried = scan_state.astype(jnp.float32)
    outputs = []
    for position in range(positions):
        updated = (
            carried * decay[:, position, :, None, None]
            + (steps_dt[:, position, :, None] * signal_heads[:, position])[..., None]
            * bgate[:, position, None, None, :]
        )
        carried = jnp.where(live[:, None, None, None], updated, carried)
        outputs.append(
            jnp.sum(carried * cgate[:, position, None, None, :], -1)
            + head_skip_weight[None, :, None] * signal_heads[:, position]
        )
    new_state = carried.astype(jnp.bfloat16)
    result = jnp.stack(outputs, 1).reshape(streams, positions, inner)
    gated = result * jax.nn.silu(zin)
    gate_squares = lax.psum(jnp.sum(gated * gated, -1), "head")
    outnorm = (
        gated * lax.rsqrt(gate_squares / INNER_WIDTH + epsilon)[..., None] * gated_norm_scale
    ).astype(jnp.bfloat16)
    out_flat = outnorm.reshape(streams * positions, inner)
    partial_out = jnp.dot(out_flat, output_weight, preferred_element_type=jnp.float32)
    mixer = lax.psum_scatter(
        partial_out.astype(jnp.bfloat16), "head", scatter_dimension=1, tiled=True
    ).astype(jnp.float32)
    mixer = mixer.reshape(streams, positions, feature_width)
    mixed = (wide + jnp.where(live[:, None, None], mixer, 0.0)).astype(jnp.bfloat16)
    return (mixed, new_state)


def solution(mesh):
    in_specs = (
        P(("rep", "row"), None, "head"),
        P("head"),
        P("row", "head"),
        P("row", "head"),
        P("row", "head"),
        P("row", None),
        P("head"),
        P("head"),
        P("head"),
        P("head"),
        P("row", "head", None),
        P("row", None, "head"),
        P("head", None),
        P(("rep", "row"), "head", None, None),
        P(("rep", "row")),
        P(("rep", "row")),
    )
    out_specs = (P(("rep", "row"), None, "head"), P(("rep", "row"), "head", None, None))
    return jax.shard_map(
        on_device, mesh=mesh, in_specs=in_specs, out_specs=out_specs, check_vma=False
    )
```

profile of v0, /device:TPU:0, one launch (start us, length us, event | category | flops | bytes accessed | tf_op | source)
XLA Modules:
  0.0 219.5 jit_solution(15513517323388367327)
XLA Ops:
  7.2 0.7 compare_and_fusion
  7.9 4.1 %gather_fusion = bf16[32,2048,16]{1,2,0:T(8,128)(2,1)S(1)} fusion(bf16[128,2048,16]{1,2,0:T(8,128)(2,1)} %param.26, s32[1024]{0:T(1024)S(1)} %pad_clamp_fusion), kind=kCustom, calls=%fused_computation | custom fusion | bytes 4194432 | tf_op jit(solution)/shard_map/jit(_take)/gather | solution.py:38
  12.2 1.0 fusion.2
  13.3 13.7 %all-reduce = (f32[32,2]{0,1:T(2,128)S(1)}, f32[32,2,16]{2,1,0:T(2,128)}) all-reduce(f32[32,2]{0,1:T(2,128)S(1)} %get-tuple-element.32, f32[32,2,16]{2,1,0:T(2,128)S(1)} %fusion.2), channel_id=1, replica_groups=mesh['rep'=2,'head'=4,'row'=4] {'head'}, use_global_device_ids=true, to_apply=%region_1.2 | all-reduce | flops 1088 | bytes 8704 | tf_op jit(solution)/shard_map/psum | solution.py:43
  27.0 0.8 fusion.10
  27.8 17.2 %all-gather.2.cloned.1.call-done = bf16[32,2,8192]{2,0,1:T(8,128)(2,1)} async-done(((bf16[32,2,2048]{2,0,1:T(8,128)(2,1)}), bf16[32,2,8192]{2,0,1:T(8,128)(2,1)}) %all-gather.2.cloned.1.call-update) | async-done | bytes 1048592 | tf_op jit(solution)/shard_map/all_gather | solution.py:47
  45.0 9.2 %copy.76 = bf16[32,2,8192]{0,1,2:T(2,128)(2,1)} copy(bf16[32,2,8192]{2,0,1:T(8,128)(2,1)} %all-gather.2.cloned.1.call-done) | data formatting | bytes 2097152 | tf_op jit(solution)/shard_map/all_gather | solution.py:47
  54.2 6.4 %reshape.98 = bf16[4,2,65536]{2,1,0:T(2,128)(2,1)} reshape(bf16[8192,2,32]{2,1,0:T(2,128)(2,1)} %bitcast.34) | data formatting | bytes 2097152
  60.6 4.6 %all-to-all-start = ((bf16[4,2,65536]{2,1,0:T(2,128)(2,1)}), bf16[4,2,65536]{2,1,0:T(2,128)(2,1)S(1)}, u32[]{:S(2)}, u32[]{:S(2)}) async-start(bf16[4,2,65536]{2,1,0:T(2,128)(2,1)} %reshape.98), calls=%async_computation | async-start | bytes 2097152 | tf_op jit(solution)/shard_map/all_to_all | solution.py:51
  65.5 15.0 %concatenate.4 = bf16[2048,2320]{1,0:T(8,128)(2,1)} concatenate(bf16[2048,1024]{1,0:T(8,128)(2,1)} %param.18, bf16[2048,1024]{1,0:T(8,128)(2,1)} %param.19, bf16[2048,16]{1,0:T(8,128)(2,1)S(1)} %copy.78, bf16[2048,256]{1,0:T(8,128)(2,1)S(1)} %copy-done.1), dimensions={1} | concatenate | bytes 19005440 | tf_op jit(solution)/shard_map/concatenate | solution.py:48
  80.5 10.8 %all-to-all-done = bf16[4,2,65536]{2,1,0:T(2,128)(2,1)S(1)} async-done(((bf16[4,2,65536]{2,1,0:T(2,128)(2,1)}), bf16[4,2,65536]{2,1,0:T(2,128)(2,1)S(1)}, u32[]{:S(2)}, u32[]{:S(2)}) %all-to-all-start) | async-done | bytes 1048608 | tf_op jit(solution)/shard_map/all_to_all | solution.py:51
  91.3 3.5 %reshape.99 = bf16[8192,2,32]{2,1,0:T(2,128)(2,1)} reshape(bf16[4,2,65536]{2,1,0:T(2,128)(2,1)S(1)} %all-to-all-done) | data formatting | bytes 2097152
  94.8 9.7 %copy.77 = bf16[32,2,4,2048]{3,1,0,2:T(2,128)(2,1)S(1)} copy(bf16[32,2,4,2048]{0,1,3,2:T(2,128)(2,1)} %bitcast.35) | data formatting | bytes 2097152 | tf_op jit(solution)/shard_map/all_to_all | solution.py:51
  104.9 7.7 %convolution_convert_fusion.1 = bf16[256,2320]{1,0:T(8,128)(2,1)} fusion(bf16[256,2048]{1,0:T(8,128)(2,1)S(1)} %reshape.69, bf16[2048,2320]{1,0:T(8,128)(2,1)} %concatenate.4), kind=kOutput, calls=%fused_computation.10 | convolution fusion | flops 2433290240 | bytes 11739136 | tf_op jit(solution)/shard_map/dot_general | solution.py:54
  112.8 2.8 %gather_fusion.1 = bf16[32,16,1024]{2,1,0:T(8,128)(2,1)S(1)} fusion(bf16[128,16,1024]{2,1,0:T(8,128)(2,1)} %param.27, s32[1024]{0:T(1024)S(1)} %pad_clamp_fusion), kind=kCustom, calls=%fused_computation.1 | custom fusion | bytes 2097280 | tf_op jit(solution)/shard_map/jit(_take)/gather | solution.py:64
  116.3 24.9 %reduce-scatter.3.cloned.1.call-done = bf16[64,2320]{1,0:T(8,128)(2,1)} async-done(((bf16[256,2320]{1,0:T(8,128)(2,1)}), bf16[64,2320]{1,0:T(8,128)(2,1)}) %reduce-scatter.3.cloned.1.call-update) | async-done | bytes 296976 | tf_op jit(solution)/shard_map/reduce_scatter | solution.py:53
  141.2 1.3 reshape.77
  144.3 24.9 %multiply_reduce_fusion.1 = (f32[32,16,64]{2,1,0:T(8,128)S(1)}, f32[32,16,64]{2,1,0:T(8,128)S(1)}, bf16[32,16,64,128]{3,2,1,0:T(8,128)(2,1)}) fusion(bf16[32,16,64,128]{3,2,1,0:T(8,128)(2,1)} %param.29, f32[32,128]{1,0:T(8,128)S(1)} %bitcast.39, f32[32,128]{1,0:T(8,128)S(1)} %bitcast.38, f32[32,16,64]{2,1,0:T(8,128)S(1)} %get-tuple-element.30, ...), kind=kLoop, calls=%fused_computation.7 | loop fusion | flops 58654720 | bytes 17371168 | tf_op jit(solution)/shard_map/reduce_sum | solution.py:85
  169.6 0.6 multiply_reduce_fusion.2
  170.3 6.6 %psum.23 = f32[32,2]{0,1:T(2,128)S(1)} all-reduce(f32[32,2]{0,1:T(2,128)S(1)} %copy.86), channel_id=1, replica_groups=mesh['rep'=2,'head'=4,'row'=4] {'head'}, use_global_device_ids=true, to_apply=%region_7.8 | all-reduce | flops 64 | bytes 512 | tf_op jit(solution)/shard_map/psum | solution.py:91
  177.2 9.8 %convolution_convert_fusion = bf16[64,8192]{1,0:T(8,128)(2,1)} fusion(bf16[64,1024]{1,0:T(8,128)(2,1)S(1)} %reshape.73, bf16[1024,8192]{1,0:T(8,128)(2,1)} %param.28), kind=kOutput, calls=%fused_computation.9 | convolution fusion | flops 1074266112 | bytes 17956864 | tf_op jit(solution)/shard_map/dot_general | solution.py:96
  187.0 23.3 %reduce-scatter.5.cloned.1.call-done = bf16[64,2048]{1,0:T(8,128)(2,1)} async-done(((bf16[64,8192]{1,0:T(8,128)(2,1)}), bf16[64,2048]{1,0:T(8,128)(2,1)}) %reduce-scatter.5.cloned.1.call-update) | async-done | bytes 262160 | tf_op jit(solution)/shard_map/reduce_scatter | solution.py:97
  210.3 1.3 reshape.79
  212.0 1.0 copy.89
  (53 shorter events, 4.2 us)
Async XLA Ops:
  7.2 37.9 %all-gather.2.cloned.1.call-start = ((), (), s32[]{:S(2)}) async-start(), calls=%async_computation.3 | async-start | bytes 1310720 | tf_op jit(solution)/shard_map/all_gather | solution.py:47
  7.9 4.1 %copy-start = (bf16[32,2,2048]{2,1,0:T(2,128)(2,1)S(1)}, bf16[32,2,2048]{2,1,0:T(2,128)(2,1)}, u32[]{:S(2)}) copy-start(bf16[32,2,2048]{2,1,0:T(2,128)(2,1)} %param.16) | copy-start | bytes 786436
  7.9 4.1 %copy-start.3 = (f32[2048]{0:T(1024)S(1)}, f32[2048]{0:T(1024)}, u32[]{:S(2)}) copy-start(f32[2048]{0:T(1024)} %param.17) | copy-start | bytes 24580
  12.0 53.1 %copy-start.2 = (bf16[2048,16]{0,1:T(8,128)(2,1)S(1)}, bf16[2048,16]{0,1:T(8,128)(2,1)}, u32[]{:S(2)}) copy-start(bf16[2048,16]{0,1:T(8,128)(2,1)} %param.20) | copy-start | bytes 196612
  12.1 53.4 %copy-start.1 = (bf16[2048,256]{1,0:T(8,128)(2,1)S(1)}, bf16[2048,256]{1,0:T(8,128)(2,1)}, u32[]{:S(2)}) copy-start(bf16[2048,256]{1,0:T(8,128)(2,1)} %param.21) | copy-start | bytes 3145732
  60.6 30.7 %all-to-all-start = ((bf16[4,2,65536]{2,1,0:T(2,128)(2,1)}), bf16[4,2,65536]{2,1,0:T(2,128)(2,1)S(1)}, u32[]{:S(2)}, u32[]{:S(2)}) async-start(bf16[4,2,65536]{2,1,0:T(2,128)(2,1)} %reshape.98), calls=%async_computation | async-start | bytes 2097152 | tf_op jit(solution)/shard_map/all_to_all | solution.py:51
  65.2 76.0 %reduce-scatter.3.cloned.1.call-start = ((), (), s32[]{:S(2)}) async-start(), calls=%async_computation.4 | async-start | bytes 1556480 | tf_op jit(solution)/shard_map/reduce_scatter | solution.py:53
  104.9 37.7 %copy-start.8 = (f32[32,2,16]{2,1,0:T(2,128)S(1)}, f32[32,2,16]{2,1,0:T(2,128)}, u32[]{:S(2)}) copy-start(f32[32,2,16]{2,1,0:T(2,128)} %get-tuple-element.17) | copy-start | bytes 12292
  112.7 30.9 %copy-start.5 = (f32[16]{0:T(128)S(1)}, f32[16]{0:T(128)}, u32[]{:S(2)}) copy-start(f32[16]{0:T(128)} %param.23) | copy-start | bytes 196
  112.7 30.9 %copy-start.6 = (f32[16]{0:T(128)S(1)}, f32[16]{0:T(128)}, u32[]{:S(2)}) copy-start(f32[16]{0:T(128)} %param.22) | copy-start | bytes 196
  112.7 97.6 %reduce-scatter.5.cloned.1.call-start = ((), (), s32[]{:S(2)}) async-start(), calls=%async_computation.5 | async-start | bytes 1310720 | tf_op jit(solution)/shard_map/reduce_scatter | solution.py:97
  143.1 26.0 %copy-start.7 = (f32[16]{0:T(128)S(1)}, f32[16]{0:T(128)}, u32[]{:S(2)}) copy-start(f32[16]{0:T(128)} %param.24) | copy-start | bytes 196
  144.2 32.7 %copy-start.4 = (f32[1024]{0:T(1024)S(1)}, f32[1024]{0:T(1024)}, u32[]{:S(2)}) copy-start(f32[1024]{0:T(1024)} %param.25) | copy-start | bytes 12292
Sparse Core Ops, SparseCore 0:
  28.0 17.0 all-gather.1
  112.8 28.3 reduce-scatter.2
  187.1 23.1 reduce-scatter.4
where the time goes:
time: 221 us; the launch traced here: 220 us
  waiting for transfers between devices  76.3 us (35%)
  local copies, waits for them, and re-layouts  56.3 us (25%)
  other arithmetic  28.3 us (13%)
  blocking collectives  20.3 us (9%)
  matrix products  19 us (9%)
  between operations  14.6 us (7%)
  starting transfers between devices  4.68 us (2%)
    reduce_scatter x1, waiting for transfers between devices, on_device(): lax.psum_scatter(jnp.dot(moved_flat, weight_cat, preferred_element_type=j...  24.9 us
    reduce_sum x1, other arithmetic, on_device(): jnp.sum(carried * cgate[:, position, None, None, :], -1)  24.9 us
    reduce_scatter x1, waiting for transfers between devices, on_device(): lax.psum_scatter(partial_out.astype(jnp.bfloat16), 'head', scatter_dimens...  23.3 us
    all_gather x1, waiting for transfers between devices, on_device(): features = lax.all_gather(normed, 'head', axis=2, tiled=True)  17.2 us
    concatenate x1, local copies, waits for them, and re-layouts, on_device(): jnp.concatenate([projection_signal, projection_gate, projection_step, pro...  15 us
    psum x1, blocking collectives, on_device(): squares, lowrank_sum = lax.psum((square_part, lowrank_part), 'head')  13.7 us
    unnamed x23, local copies, waits for them, and re-layouts  11.2 us
    all_to_all x1, waiting for transfers between devices, on_device(): lax.all_to_all(features, 'row', split_axis=2, concat_axis=0, tiled=True)  10.8 us
  transfers between devices with their start and end apart: 4, of which 4 were waited for; matrix products, arithmetic and copies ran while one was open for 8% of the time, Pallas kernels for 0%

commit v1 on v0

v1 whole, which is shorter than its diff:
```python
import functools

import jax
import jax.numpy as jnp
from jax import lax
from jax.experimental import pallas as pl
from jax.experimental.pallas import tpu as pltpu
from jax.sharding import PartitionSpec as P

BF16 = jnp.bfloat16
F32 = jnp.float32
VMEM_GRANT = 24 * 1024 * 1024


def swap(values, axis, distance):
    size = lax.axis_size(axis)
    return lax.ppermute(values, axis, [(i, i ^ distance) for i in range(size)])


def bits_of(size):
    return [1 << i for i in range(size.bit_length() - 1)]


def sum_over(values, axis):
    for distance in bits_of(lax.axis_size(axis)):
        values = values + swap(values, axis, distance)
    return values


def gather_relative(block, axis):
    blocks = block[None]
    order = [0]
    for distance in reversed(bits_of(lax.axis_size(axis))):
        other = swap(blocks, axis, distance)
        blocks = jnp.concatenate([blocks, other], 0)
        order = order + [i ^ distance for i in order]
    return blocks, order


def params(**more):
    return pltpu.CompilerParams(vmem_limit_bytes=VMEM_GRANT, **more)


def cost(flops, size):
    return pl.CostEstimate(flops=int(flops), bytes_accessed=int(size), transcendentals=0)


def ordered_rows(index_ref, blocks_ref):
    count = blocks_ref.shape[0]
    return jnp.concatenate([blocks_ref[index_ref[k]] for k in range(count)], 0)


def put_parts(acc, send_ref, keep_ref, columns):
    rows = send_ref.shape[1]
    count = acc.shape[0] // rows
    for k in range(count):
        target = send_ref if k % 2 else keep_ref
        target[k // 2, :, columns] = acc[k * rows : (k + 1) * rows].astype(target.dtype)


def project_body(index_ref, blocks_ref, weight_ref, send_ref, keep_ref):
    lhs = ordered_rows(index_ref, blocks_ref)
    acc = jnp.dot(lhs, weight_ref[...], preferred_element_type=F32)
    put_parts(acc, send_ref, keep_ref, slice(None))


def project(index, blocks, weight):
    count, rows, depth = blocks.shape
    columns = weight.shape[1]
    tile = min(columns, 256)
    half = jax.ShapeDtypeStruct((count // 2, rows, columns), BF16)
    part = pl.BlockSpec((count // 2, rows, tile), lambda i, s: (0, 0, i))
    return pl.pallas_call(
        project_body,
        out_shape=(half, half),
        grid_spec=pltpu.PrefetchScalarGridSpec(
            num_scalar_prefetch=1,
            grid=(columns // tile,),
            in_specs=[
                pl.BlockSpec((count, rows, depth), lambda i, s: (0, 0, 0)),
                pl.BlockSpec((depth, tile), lambda i, s: (0, i)),
            ],
            out_specs=(part, part),
        ),
        compiler_params=params(),
        cost_estimate=cost(
            2 * count * rows * depth * columns, 2 * (depth * columns + count * rows * (depth + columns))
        ),
        name="project",
    )(index, blocks, weight)


def project_small_body(index_ref, blocks_ref, weight_ref, step_ref, send_ref, keep_ref):
    lhs = ordered_rows(index_ref, blocks_ref)
    width = weight_ref.shape[1]
    acc = jnp.dot(lhs, weight_ref[...], preferred_element_type=F32)
    put_parts(acc, send_ref, keep_ref, slice(0, width))
    acc = lax.dot_general(lhs, step_ref[...], (((1,), (1,)), ((), ())), preferred_element_type=F32)
    put_parts(acc, send_ref, keep_ref, slice(width, width + step_ref.shape[0]))


def project_small(index, blocks, weight, step_rows):
    count, rows, depth = blocks.shape
    columns = weight.shape[1] + step_rows.shape[0]
    half = jax.ShapeDtypeStruct((count // 2, rows, columns), BF16)
    whole = pl.BlockSpec(memory_space=pltpu.VMEM)
    return pl.pallas_call(
        project_small_body,
        out_shape=(half, half),
        in_specs=[pl.BlockSpec(memory_space=pltpu.SMEM), whole, whole, whole],
        out_specs=(whole, whole),
        compiler_params=params(),
        cost_estimate=cost(
            2 * count * rows * depth * columns, 2 * (depth * columns + count * rows * (depth + columns))
        ),
        name="project_small",
    )(index, blocks, weight, step_rows)


def scatter_rows(send, keep, axis):
    terms = None
    for distance in bits_of(lax.axis_size(axis)):
        other = swap(send, axis, distance)
        if keep.shape[0] == 1:
            return [t[0] for t in ([keep] if terms is None else terms) + [other]]
        if terms is None:
            terms = [keep]
        now = terms + [other]
        send = sum(t[1::2].astype(F32) for t in now).astype(BF16)
        terms = [t[0::2] for t in now]
        keep = terms[0]
    return [t[0] for t in terms]


def state_read_body(pairs_ref, state_ref, out_ref):
    group, heads, head, width = state_ref.shape
    for g in range(group):
        state = state_ref[g].reshape(heads * head, width)
        both = lax.dot_general(
            pairs_ref[g], state, (((1,), (1,)), ((), ())), preferred_element_type=F32
        )
        out_ref[0, g : g + 1, :] = both[0:1] + both[2:3]
        out_ref[1, g : g + 1, :] = both[1:2] + both[3:4]


def state_read(pairs, state):
    streams, heads, head, width = state.shape
    group = 8
    inner = heads * head
    return pl.pallas_call(
        state_read_body,
        out_shape=jax.ShapeDtypeStruct((2, streams, inner), F32),
        grid=(streams // group,),
        in_specs=[
            pl.BlockSpec((group, pairs.shape[1], width), lambda i: (i, 0, 0)),
            pl.BlockSpec((group, heads, head, width), lambda i: (i, 0, 0, 0)),
        ],
        out_specs=pl.BlockSpec((2, group, inner), lambda i: (0, i, 0)),
        compiler_params=params(),
        cost_estimate=cost(32 * state.size, 2 * state.size),
        name="state_read",
    )(pairs, state)


def state_write_body(left_ref, right_ref, decay_ref, state_ref, out_ref):
    group, heads, head, width = state_ref.shape
    for g in range(group):
        outer = lax.dot_general(
            left_ref[g], right_ref[g], (((0,), (0,)), ((), ())), preferred_element_type=F32
        )
        scaled = state_ref[g].astype(F32) * decay_ref[g][:, None, :]
        out_ref[g] = (scaled + outer.reshape(heads, head, width)).astype(out_ref.dtype)


def state_write(left, right, decay, state):
    streams, heads, head, width = state.shape
    group = 4
    rank = left.shape[1]
    block = pl.BlockSpec((group, heads, head, width), lambda i: (i, 0, 0, 0))
    return pl.pallas_call(
        state_write_body,
        out_shape=jax.ShapeDtypeStruct(state.shape, state.dtype),
        grid=(streams // group,),
        in_specs=[
            pl.BlockSpec((group, rank, heads * head), lambda i: (i, 0, 0)),
            pl.BlockSpec((group, rank, width), lambda i: (i, 0, 0)),
            pl.BlockSpec((group, heads, width), lambda i: (i, 0, 0)),
            block,
        ],
        out_specs=block,
        compiler_params=params(),
        cost_estimate=cost(32 * state.size, 4 * state.size),
        name="state_write",
    )(left, right, decay, state)


def output_body(index_ref, lhs_ref, weight_ref, out_ref):
    out_ref[0] = jnp.dot(lhs_ref[...], weight_ref[...], preferred_element_type=F32).astype(out_ref.dtype)


def output_parts(index, lhs, weight, width):
    rows, depth = lhs.shape
    count = index.shape[0]
    tile = min(width, 512)
    tiles = width // tile
    return pl.pallas_call(
        output_body,
        out_shape=jax.ShapeDtypeStruct((count, rows, width), BF16),
        grid_spec=pltpu.PrefetchScalarGridSpec(
            num_scalar_prefetch=1,
            grid=(count, tiles),
            in_specs=[
                pl.BlockSpec((rows, depth), lambda j, t, s: (0, 0)),
                pl.BlockSpec((depth, tile), lambda j, t, s: (0, s[j] * tiles + t)),
            ],
            out_specs=pl.BlockSpec((1, rows, tile), lambda j, t, s: (j, 0, t)),
        ),
        compiler_params=params(),
        cost_estimate=cost(2 * rows * depth * width * count, 2 * depth * width * count),
        name="output_parts",
    )(index, lhs, weight)


def split(values):
    high = values.astype(BF16)
    return high, (values - high.astype(F32)).astype(BF16)


def on_device(
    hidden,
    input_norm_scale,
    projection_signal,
    projection_gate,
    projection_step,
    projection_input_output,
    step_bias,
    head_decay_rate,
    head_skip_weight,
    gated_norm_scale,
    adapter_down_weight,
    adapter_up_weight,
    output_weight,
    scan_state,
    stream_tenant_index,
    live_block_rows,
):
    epsilon = 1e-05
    streams, positions, feature_width = hidden.shape
    rows = streams * positions
    heads_n = lax.axis_size("head")
    rows_n = lax.axis_size("row")
    model_width = feature_width * heads_n
    depth, inner = projection_signal.shape
    inner_width = inner * heads_n
    heads_here = projection_step.shape[1]
    state_width = projection_input_output.shape[1] // 2
    head_at = lax.axis_index("head")
    row_at = lax.axis_index("row")

    wide = jnp.swapaxes(hidden, 0, 1).astype(F32)
    scaled = (wide * input_norm_scale).astype(BF16)
    scaled_flat = scaled.reshape(rows, feature_width)

    steps = jnp.arange(rows_n, dtype=jnp.int32)
    if heads_n == rows_n:
        turned = lax.ppermute(
            scaled_flat,
            ("head", "row"),
            [(h * rows_n + r, r * rows_n + h) for h in range(heads_n) for r in range(rows_n)],
        )
        blocks, order = gather_relative(turned, "head")
        place = jnp.asarray([order.index(i) for i in range(heads_n)], jnp.int32)
        index = place[head_at ^ row_at ^ steps]
    else:
        features = lax.all_gather(scaled_flat, "head", axis=1, tiled=True)
        blocks = lax.all_to_all(features, "row", split_axis=1, concat_axis=0, tiled=True)
        blocks = blocks.reshape(rows_n, rows, depth)
        index = row_at ^ steps

    small = project_small(index, blocks, projection_input_output, projection_step.T)
    small_terms = scatter_rows(*small, "row")
    signal_terms = scatter_rows(*project(index, blocks, projection_signal), "row")
    gate_terms = scatter_rows(*project(index, blocks, projection_gate), "row")

    tenant_local = stream_tenant_index - row_at * adapter_down_weight.shape[0]
    down_weight_rows = jnp.take(adapter_down_weight, tenant_local, axis=0)
    square_part = jnp.sum(wide * wide, -1)
    lowrank_part = jnp.einsum(
        "psd,sdr->psr", scaled, down_weight_rows, preferred_element_type=F32
    )
    sums = sum_over(jnp.concatenate([lowrank_part, square_part[..., None]], -1), "head")
    inverse = lax.rsqrt(sums[..., -1:] / model_width + epsilon)
    lowrank = (sums[..., :-1] * inverse).astype(BF16)
    up_weight_rows = jnp.take(adapter_up_weight, tenant_local, axis=0)
    adapted = jnp.einsum("psr,srk->psk", lowrank, up_weight_rows, preferred_element_type=F32)

    def total(terms):
        whole = sum(t.astype(F32) for t in terms)
        return whole.reshape(positions, streams, -1) * inverse

    small_in = total(small_terms)
    gates = jax.nn.silu(small_in[..., : 2 * state_width])
    bgate = gates[..., :state_width]
    cgate = gates[..., state_width:]
    live = jnp.arange(streams) < live_block_rows[0]
    steps_dt = jax.nn.softplus(small_in[..., 2 * state_width :] + step_bias)
    decay = jnp.where(live[:, None], jnp.exp(-steps_dt * head_decay_rate), 1.0)
    fed = jnp.where(live[:, None], steps_dt, 0.0)

    c_high, c_low = split(jnp.swapaxes(cgate, 0, 1))
    b_high, b_low = split(jnp.swapaxes(bgate, 0, 1))
    zero = jnp.zeros_like(c_high)
    read = state_read(jnp.concatenate([c_high, c_low, zero, zero], 1), scan_state)

    def expand(values):
        spread = jnp.broadcast_to(values[..., None], values.shape + (inner // heads_here,))
        return spread.reshape(values.shape[:-1] + (inner,))

    def inner_product(b, c):
        return jnp.sum(bgate[b] * cgate[c], -1, keepdims=True)

    both = decay[0] * decay[1]
    late = decay[1] * fed[0]
    base0 = expand(decay[0]) * read[0]
    base1 = expand(both) * read[1]
    own0 = expand(fed[0] * inner_product(0, 0) + head_skip_weight)
    own1 = expand(fed[1] * inner_product(1, 1) + head_skip_weight)
    cross = expand(late * inner_product(0, 1))
    feed0 = expand(late)
    feed1 = expand(fed[1])

    signal = jax.nn.silu(total(signal_terms) + adapted)
    result = jnp.stack([base0 + own0 * signal[0], base1 + cross * signal[0] + own1 * signal[1]])
    gated = result * jax.nn.silu(total(gate_terms))
    gate_squares = sum_over(jnp.sum(gated * gated, -1), "head")
    out_lhs = (gated * gated_norm_scale).astype(BF16).reshape(rows, inner)

    distances = jnp.arange(heads_n, dtype=jnp.int32) ^ head_at
    odd = output_parts(distances[1::2], out_lhs, output_weight, feature_width)
    even = output_parts(distances[0::2], out_lhs, output_weight, feature_width)
    mixer = sum(t.astype(F32) for t in scatter_rows(odd, even, "head"))
    mixer = mixer.reshape(positions, streams, feature_width)
    mixer = mixer * lax.rsqrt(gate_squares / inner_width + epsilon)[..., None]
    mixed = (wide + jnp.where(live[:, None], mixer, 0.0)).astype(BF16)

    feeds = jnp.stack([feed0 * signal[0], feed1 * signal[1]], 1)
    f_high, f_low = split(feeds)
    left = jnp.concatenate([f_high, f_low, f_high, jnp.zeros_like(f_high)], 1)
    right = jnp.concatenate([b_high, b_high, b_low, zero], 1)
    spread = jnp.broadcast_to(both[..., None], both.shape + (state_width,))
    new_state = state_write(left, right, spread, scan_state)
    return (jnp.swapaxes(mixed, 0, 1), new_state)


def solution(mesh):
    in_specs = (
        P(("rep", "row"), None, "head"),
        P("head"),
        P("row", "head"),
        P("row", "head"),
        P("row", "head"),
        P("row", None),
        P("head"),
        P("head"),
        P("head"),
        P("head"),
        P("row", "head", None),
        P("row", None, "head"),
        P("head", None),
        P(("rep", "row"), "head", None, None),
        P(("rep", "row")),
        P(("rep", "row")),
    )
    out_specs = (P(("rep", "row"), None, "head"), P(("rep", "row"), "head", None, None))
    return jax.shard_map(
        on_device, mesh=mesh, in_specs=in_specs, out_specs=out_specs, check_vma=False
    )
```

time: 221 us -> 109 us (0.49)
  waiting for transfers between devices: 76.3 us -> 15.2 us
  local copies, waits for them, and re-layouts: 56.3 us -> 30.2 us
  Pallas kernels: 0 us -> 24 us
  blocking collectives: 20.3 us -> 0 us
  starting transfers between devices: 4.68 us -> 24.9 us
  other arithmetic: 28.3 us -> 10.5 us
  matrix products: 19 us -> 1.53 us
  between operations: 14.6 us -> 1.93 us
    reduce_scatter x2 -> x0, waiting for transfers between devices: 48.2 us -> none  [the longest x1 24.9 us: on_device(): lax.psum_scatter(jnp.dot(moved_flat, weight_cat, preferred_element_type=j...]
    ppermute x0 -> x15, starting transfers between devices: none -> 24.9 us  [the longest x14 23.3 us: swap(): return lax.ppermute(values, axis, [(i, i ^ distance) for i in range(size)])]
    pallas_call x0 -> x7, Pallas kernels: none -> 24 us  [the longest x2 7.64 us: output_parts(): pl.pallas_call(output_body, out_shape=jax.ShapeDtypeStruct((count, rows,...]
    reduce_sum x2 -> x3, other arithmetic: 25.4 us -> 1.99 us  [the longest x1 1.4 us: on_device(): square_part = jnp.sum(wide * wide, -1)]
    psum x2 -> x0, blocking collectives: 20.3 us -> none  [the longest x1 13.7 us: on_device(): squares, lowrank_sum = lax.psum((square_part, lowrank_part), 'head')]
    dot_general x4 -> x2, matrix products: 19 us -> 1.53 us  [the longest x1 0.98 us: on_device(): jnp.einsum('psd,sdr->psr', scaled, down_weight_rows, preferred_element_ty...]
    all_gather x1 -> x0, waiting for transfers between devices: 17.2 us -> none  [on_device(): features = lax.all_gather(normed, 'head', axis=2, tiled=True)]
    ppermute x0 -> x15, waiting for transfers between devices: none -> 15.2 us  [the longest x14 15.2 us: swap(): return lax.ppermute(values, axis, [(i, i ^ distance) for i in range(size)])]
  transfers between devices with their start and end apart: 4 -> 15, of which waited for: 4 -> 4; matrix products, arithmetic and copies ran while one was open for 8% -> 18% of each run, Pallas kernels for 0% -> 21%
where the time goes in v1:
time: 109 us; the launch traced here: 108 us
  local copies, waits for them, and re-layouts  30.2 us (28%)
  starting transfers between devices  24.9 us (23%)
  Pallas kernels  24 us (22%)
  waiting for transfers between devices  15.2 us (14%)
  other arithmetic  10.5 us (10%)
  between operations  1.93 us (2%)
  matrix products  1.53 us (1%)
    ppermute x14, starting transfers between devices, swap(): return lax.ppermute(values, axis, [(i, i ^ distance) for i in range(size)])  23.3 us
    unnamed x36, local copies, waits for them, and re-layouts  17.2 us
    ppermute x14, waiting for transfers between devices, swap(): return lax.ppermute(values, axis, [(i, i ^ distance) for i in range(size)])  15.2 us
    pallas_call x2, Pallas kernels, output_parts(): pl.pallas_call(output_body, out_shape=jax.ShapeDtypeStruct((count, rows,...  7.64 us
    pallas_call x1, Pallas kernels, state_write(): pl.pallas_call(state_write_body, out_shape=jax.ShapeDtypeStruct(state.sha...  6.31 us
    pallas_call x2, Pallas kernels, project(): pl.pallas_call(project_body, out_shape=(half, half), grid_spec=pltpu.Pref...  6.11 us
    gather x1, local copies, waits for them, and re-layouts, on_device(): down_weight_rows = jnp.take(adapter_down_weight, tenant_local, axis=0)  4.07 us
    gather x1, local copies, waits for them, and re-layouts, on_device(): up_weight_rows = jnp.take(adapter_up_weight, tenant_local, axis=0)  2.8 us
  transfers between devices with their start and end apart: 15, of which 4 were waited for; matrix products, arithmetic and copies ran while one was open for 18% of the time, Pallas kernels for 21%

profile of v1, /device:TPU:0, one launch (start us, length us, event | category | flops | bytes accessed | tf_op | source)
XLA Modules:
  0.0 108.3 jit_solution(7812100504069786230)
XLA Ops:
  0.6 1.4 %fusion.7 = (f32[2,32]{0,1:T(8,128)S(1)}, bf16[2,32,2048]{2,0,1:T(2,128)(2,1)S(1)}) fusion(bf16[32,2,2048]{2,1,0:T(2,128)(2,1)} %param.17, f32[2048]{0:T(1024)} %param.18), kind=kLoop, calls=%fused_computation.17 | loop fusion | flops 655296 | bytes 532736 | tf_op jit(solution)/shard_map/reduce_sum | solution.py:287
  2.8 1.6 %collective-permute-start = (bf16[64,2048]{1,0:T(8,128)(2,1)}, bf16[64,2048]{1,0:T(8,128)(2,1)S(1)}, u32[]{:S(2)}, u32[]{:S(2)}) collective-permute-start(bf16[64,2048]{1,0:T(8,128)(2,1)} %bitcast.3), channel_id=1, source_target_pairs={{0,0},{1,4},{2,8},{3,12},{4,1},{5,5},{6,9},{7,13},{8,2},{9,6},{10,... | collective-permute-start | bytes 786440 | tf_op jit(solution)/shard_map/ppermute | solution.py:266
  5.2 4.1 %gather_fusion.1 = bf16[32,2048,16]{1,2,0:T(8,128)(2,1)S(1)} fusion(bf16[128,2048,16]{1,2,0:T(8,128)(2,1)} %param.27, s32[1024]{0:T(1024)S(1)} %pad_clamp_fusion), kind=kCustom, calls=%fused_computation.1 | custom fusion | bytes 4194432 | tf_op jit(solution)/shard_map/jit(_take)/gather | solution.py:286
  10.4 3.5 %collective-permute-start.5 = (f32[2,32,17]{1,0,2:T(2,128)S(1)}, f32[2,32,17]{1,0,2:T(2,128)S(1)}, u32[]{:S(2)}, u32[]{:S(2)}) collective-permute-start(f32[2,32,17]{1,0,2:T(2,128)S(1)} %pad_maximum_fusion.4), channel_id=1, source_target_pairs={{0,4},{4,0},{8,12},{12,8},{1,5},{5,1},{9,13},{13,9},{2,6},{6,2},{1... | collective-permute-start | bytes 13064 | tf_op jit(solution)/shard_map/ppermute | solution.py:17
  13.9 10.2 %collective-permute-start.1 = (bf16[1,64,2048]{2,1,0:T(8,128)(2,1)S(1)}, bf16[1,64,2048]{2,1,0:T(8,128)(2,1)S(1)}, u32[]{:S(2)}, u32[]{:S(2)}) collective-permute-start(bf16[1,64,2048]{2,1,0:T(8,128)(2,1)S(1)} %bitcast.91), channel_id=1, source_target_pairs={{0,8},{4,12},{8,0},{12,4},{1,9},{5,13},{9,1},{13,5},{2,10},{6,14},... | collective-permute-start | bytes 786440 | tf_op jit(solution)/shard_map/ppermute | solution.py:17
  24.9 3.6 %collective-permute-done.1 = bf16[1,64,2048]{2,1,0:T(8,128)(2,1)S(1)} collective-permute-done((bf16[1,64,2048]{2,1,0:T(8,128)(2,1)S(1)}, bf16[1,64,2048]{2,1,0:T(8,128)(2,1)S(1)}, u32[]{:S(2)}, u32[]{:S(2)}) %collective-permute-start.1) | collective-permute-done | bytes 262176 | tf_op jit(solution)/shard_map/ppermute | solution.py:17
  28.9 2.8 %gather_fusion.2 = bf16[32,16,1024]{2,1,0:T(8,128)(2,1)S(1)} fusion(bf16[128,16,1024]{2,1,0:T(8,128)(2,1)} %param.28, s32[1024]{0:T(1024)S(1)} %pad_clamp_fusion), kind=kCustom, calls=%fused_computation.2 | custom fusion | bytes 2097280 | tf_op jit(solution)/shard_map/jit(_take)/gather | solution.py:294
  32.7 1.3 %pad_maximum_fusion.blocks_ref = bf16[4,64,2048]{2,1,0:T(8,128)(2,1)S(1)} fusion(bf16[2,64,2048]{2,1,0:T(8,128)(2,1)} %collective-permute-done.2, bf16[1,64,2048]{2,1,0:T(8,128)(2,1)S(1)} %collective-permute-done.1, bf16[1,64,2048]{2,1,0:T(8,128)(2,1)S(1)} %bitcast.93), kind=kLoop, calls=%fused_computation.7 | loop fusion | flops 1048576 | bytes 2097152 | tf_op jit(solution)/shard_map/concatenate | solution.py:35
  36.5 3.1 %project.3 = (bf16[2,64,1024]{2,1,0:T(8,128)(2,1)S(1)}, bf16[2,64,1024]{2,1,0:T(8,128)(2,1)S(1)}) custom-call(s32[4]{0:T(128)S(1)} %gather_fusion, bf16[4,64,2048]{2,1,0:T(8,128)(2,1)S(1)} %pad_maximum_fusion.blocks_ref, bf16[2048,1024]{1,0:T(8,128)(2,1)S(1)} %copy-done.3), custom_call_target="tpu_custom_call" | custom-call | flops 1073741824 | bytes 5767168 | tf_op jit(solution)/shard_map/project/pallas_call | solution.py:73
  40.6 2.7 %collective-permute-start.4 = (bf16[1,64,272]{2,1,0:T(8,128)(2,1)S(1)}, bf16[1,64,272]{2,1,0:T(8,128)(2,1)S(1)}, u32[]{:S(2)}, u32[]{:S(2)}) collective-permute-start(bf16[1,64,272]{2,1,0:T(8,128)(2,1)S(1)} %add_convert_fusion.3), channel_id=1, source_target_pairs={{0,2},{1,3},{2,0},{3,1},{4,6},{5,7},{6,4},{7,5},{8,10},{9,11},{10,... | collective-permute-start | bytes 104456 | tf_op jit(solution)/shard_map/ppermute | solution.py:17
  43.2 2.2 %copy-done.4 = bf16[2048,1024]{1,0:T(8,128)(2,1)S(1)} copy-done((bf16[2048,1024]{1,0:T(8,128)(2,1)S(1)}, bf16[2048,1024]{1,0:T(8,128)(2,1)}, u32[]{:S(2)}) %copy-start.4) | copy-done | bytes 4194328
  45.4 3.1 %project.2 = (bf16[2,64,1024]{2,1,0:T(8,128)(2,1)S(1)}, bf16[2,64,1024]{2,1,0:T(8,128)(2,1)S(1)}) custom-call(s32[4]{0:T(128)S(1)} %gather_fusion, bf16[4,64,2048]{2,1,0:T(8,128)(2,1)S(1)} %pad_maximum_fusion.blocks_ref, bf16[2048,1024]{1,0:T(8,128)(2,1)S(1)} %copy-done.4), custom_call_target="tpu_custom_call" | custom-call | flops 1073741824 | bytes 5767168 | tf_op jit(solution)/shard_map/project/pallas_call | solution.py:73
  49.0 1.6 %collective-permute-start.9 = (bf16[2,64,1024]{2,1,0:T(8,128)(2,1)S(1)}, bf16[2,64,1024]{2,1,0:T(8,128)(2,1)S(1)}, u32[]{:S(2)}, u32[]{:S(2)}) collective-permute-start(bf16[2,64,1024]{2,1,0:T(8,128)(2,1)S(1)} %get-tuple-element.13), channel_id=1, source_target_pairs={{0,1},{1,0},{2,3},{3,2},{4,5},{5,4},{6,7},{7,6},{8,9},{9,8},{10,11... | collective-permute-start | bytes 786440 | tf_op jit(solution)/shard_map/ppermute | solution.py:17
  51.5 2.7 %state_read.1 = f32[2,32,1024]{2,1,0:T(8,128)S(1)} custom-call(bf16[32,8,128]{2,1,0:T(8,128)(2,1)S(1)} %maximum_maximum_fusion.1.pairs_ref, bf16[32,16,64,128]{3,2,1,0:T(8,128)(2,1)S(1)} %bitcast.87), custom_call_target="tpu_custom_call" | custom-call | flops 134217728 | bytes 8388608 | tf_op jit(solution)/shard_map/state_read/pallas_call | solution.py:150
  59.5 2.4 %collective-permute-done.9 = bf16[2,64,1024]{2,1,0:T(8,128)(2,1)S(1)} collective-permute-done((bf16[2,64,1024]{2,1,0:T(8,128)(2,1)S(1)}, bf16[2,64,1024]{2,1,0:T(8,128)(2,1)S(1)}, u32[]{:S(2)}, u32[]{:S(2)}) %collective-permute-start.9) | collective-permute-done | bytes 262176 | tf_op jit(solution)/shard_map/ppermute | solution.py:17
  62.4 8.2 %collective-permute-done.8 = bf16[1,64,1024]{2,1,0:T(8,128)(2,1)S(1)} collective-permute-done((bf16[1,64,1024]{2,1,0:T(8,128)(2,1)S(1)}, bf16[1,64,1024]{2,1,0:T(8,128)(2,1)S(1)}, u32[]{:S(2)}, u32[]{:S(2)}) %collective-permute-start.8) | collective-permute-done | bytes 131104 | tf_op jit(solution)/shard_map/ppermute | solution.py:17
  73.6 5.8 %copy-done = bf16[1024,8192]{1,0:T(8,128)(2,1)S(1)} copy-done((bf16[1024,8192]{1,0:T(8,128)(2,1)S(1)}, bf16[1024,8192]{1,0:T(8,128)(2,1)}, u32[]{:S(2)}) %copy-start) | copy-done | bytes 16777240
  79.4 3.8 %output_parts.3 = bf16[2,64,2048]{2,1,0:T(8,128)(2,1)S(1)} custom-call(s32[2]{0:T(128)S(1)} %slice.168.index_ref, bf16[64,1024]{1,0:T(8,128)(2,1)S(1)} %fusion.14.lhs_ref, bf16[1024,8192]{1,0:T(8,128)(2,1)S(1)} %copy-done), custom_call_target="tpu_custom_call" | custom-call | flops 536870912 | bytes 8388608 | tf_op jit(solution)/shard_map/output_parts/pallas_call | solution.py:206
  83.8 5.8 %copy-done.1 = bf16[1024,8192]{1,0:T(8,128)(2,1)S(1)} copy-done((bf16[1024,8192]{1,0:T(8,128)(2,1)S(1)}, bf16[1024,8192]{1,0:T(8,128)(2,1)}, u32[]{:S(2)}) %copy-start.1) | copy-done | bytes 16777240
  89.5 3.8 %output_parts.2 = bf16[2,64,2048]{2,1,0:T(8,128)(2,1)S(1)} custom-call(s32[2]{0:T(128)S(1)} %slice.137.index_ref, bf16[64,1024]{1,0:T(8,128)(2,1)S(1)} %fusion.14.lhs_ref, bf16[1024,8192]{1,0:T(8,128)(2,1)S(1)} %copy-done.1), custom_call_target="tpu_custom_call" | custom-call | flops 536870912 | bytes 8388608 | tf_op jit(solution)/shard_map/output_parts/pallas_call | solution.py:206
  95.3 1.6 %collective-permute-start.14 = (f32[2,32]{1,0:T(2,128)S(1)}, f32[2,32]{1,0:T(2,128)S(1)}, u32[]{:S(2)}, u32[]{:S(2)}) collective-permute-start(f32[2,32]{1,0:T(2,128)S(1)} %add.214), channel_id=1, source_target_pairs={{0,8},{4,12},{8,0},{12,4},{1,9},{5,13},{9,1},{13,5},{2,10},{6,14},... | collective-permute-start | bytes 776 | tf_op jit(solution)/shard_map/ppermute | solution.py:17
  97.0 3.4 %copy-done.2 = bf16[32,16,64,128]{3,2,1,0:T(8,128)(2,1)S(1)} copy-done((bf16[32,16,64,128]{3,2,1,0:T(8,128)(2,1)S(1)}, bf16[32,16,64,128]{3,2,1,0:T(8,128)(2,1)}, u32[]{:S(2)}) %copy-start.2) | copy-done | bytes 8388632
  100.4 6.3 %state_write.1 = bf16[32,16,64,128]{3,2,1,0:T(8,128)(2,1)} custom-call(bf16[32,8,1024]{2,1,0:T(8,128)(2,1)S(1)} %maximum_maximum_fusion.left_ref, bf16[32,8,128]{2,1,0:T(8,128)(2,1)S(1)} %maximum_maximum_fusion.2.right_ref, f32[32,16,128]{2,1,0:T(8,128)S(1)} %broadcast_in_dim.145.decay_ref, bf16[32,16,64,128]{3,2,1,0:T(8,128)(2,1)S(1)} %copy-done.2), custom_call_target="tpu_custom_call" | custom-call | flops 134217728 | bytes 16777216 | tf_op jit(solution)/shard_map/state_write/pallas_call | solution.py:180
  106.9 1.3 %fusion.16 = bf16[32,2,2048]{2,1,0:T(2,128)(2,1)} fusion(f32[2,32]{0,1:T(8,128)S(1)} %copy.86, f32[2,32,2048]{2,1,0:T(8,128)S(1)} %bitcast.90, pred[32]{0:T(512)(128)(4,1)S(1)} %iota_compare_fusion, bf16[32,2,2048]{2,1,0:T(2,128)(2,1)S(1)} %copy-done.8), kind=kLoop, calls=%fused_computation.41 | loop fusion | flops 655360 | bytes 1048864 | tf_op jit(solution)/shard_map/transpose | solution.py:352
  (129 shorter events, 20.1 us)
Async XLA Ops:
  2.8 11.1 %collective-permute-start = (bf16[64,2048]{1,0:T(8,128)(2,1)}, bf16[64,2048]{1,0:T(8,128)(2,1)S(1)}, u32[]{:S(2)}, u32[]{:S(2)}) collective-permute-start(bf16[64,2048]{1,0:T(8,128)(2,1)} %bitcast.3), channel_id=1, source_target_pairs={{0,0},{1,4},{2,8},{3,12},{4,1},{5,5},{6,9},{7,13},{8,2},{9,6},{10,... | collective-permute-start | bytes 786440 | tf_op jit(solution)/shard_map/ppermute | solution.py:266
  9.2 22.5 %copy-start.7 = (s32[4]{0:T(128)S(1)}, s32[4]{0:T(128)}, u32[]{:S(2)}) copy-start(s32[4]{0:T(128)} %constant.65.clone) | copy-start | bytes 52
  10.2 23.8 %copy-start.5 = (bf16[2048,256]{1,0:T(8,128)(2,1)S(1)}, bf16[2048,256]{1,0:T(8,128)(2,1)}, u32[]{:S(2)}) copy-start(bf16[2048,256]{1,0:T(8,128)(2,1)} %weight_ref.5) | copy-start | bytes 3145732
  10.2 23.8 %copy-start.6 = (bf16[2048,16]{0,1:T(8,128)(2,1)S(1)}, bf16[2048,16]{0,1:T(8,128)(2,1)}, u32[]{:S(2)}) copy-start(bf16[2048,16]{0,1:T(8,128)(2,1)} %param.21) | copy-start | bytes 196612
  10.4 14.4 %collective-permute-start.5 = (f32[2,32,17]{1,0,2:T(2,128)S(1)}, f32[2,32,17]{1,0,2:T(2,128)S(1)}, u32[]{:S(2)}, u32[]{:S(2)}) collective-permute-start(f32[2,32,17]{1,0,2:T(2,128)S(1)} %pad_maximum_fusion.4), channel_id=1, source_target_pairs={{0,4},{4,0},{8,12},{12,8},{1,5},{5,1},{9,13},{13,9},{2,6},{6,2},{1... | collective-permute-start | bytes 13064 | tf_op jit(solution)/shard_map/ppermute | solution.py:17
  13.9 14.5 %collective-permute-start.1 = (bf16[1,64,2048]{2,1,0:T(8,128)(2,1)S(1)}, bf16[1,64,2048]{2,1,0:T(8,128)(2,1)S(1)}, u32[]{:S(2)}, u32[]{:S(2)}) collective-permute-start(bf16[1,64,2048]{2,1,0:T(8,128)(2,1)S(1)} %bitcast.91), channel_id=1, source_target_pairs={{0,8},{4,12},{8,0},{12,4},{1,9},{5,13},{9,1},{13,5},{2,10},{6,14},... | collective-permute-start | bytes 786440 | tf_op jit(solution)/shard_map/ppermute | solution.py:17
  24.8 7.6 %collective-permute-start.6 = (f32[2,32,17]{1,0,2:T(2,128)S(1)}, f32[2,32,17]{1,0,2:T(2,128)S(1)}, u32[]{:S(2)}, u32[]{:S(2)}) collective-permute-start(f32[2,32,17]{1,0,2:T(2,128)S(1)} %fusion.39), channel_id=1, source_target_pairs={{0,8},{4,12},{8,0},{12,4},{1,9},{5,13},{9,1},{13,5},{2,10},{6,14},... | collective-permute-start | bytes 13064 | tf_op jit(solution)/shard_map/ppermute | solution.py:17
  28.5 4.2 %collective-permute-start.2 = (bf16[2,64,2048]{2,1,0:T(8,128)(2,1)S(1)}, bf16[2,64,2048]{2,1,0:T(8,128)(2,1)}, u32[]{:S(2)}, u32[]{:S(2)}) collective-permute-start(bf16[2,64,2048]{2,1,0:T(8,128)(2,1)S(1)} %pad_maximum_fusion.1), channel_id=1, source_target_pairs={{0,4},{4,0},{8,12},{12,8},{1,5},{5,1},{9,13},{13,9},{2,6},{6,2},{1... | collective-permute-start | bytes 1572872 | tf_op jit(solution)/shard_map/ppermute | solution.py:17
  32.7 18.7 %slice-start = ((s8[8388608]{0:T(1024)(128)(4,1)}), s8[4194304]{0:T(1024)(128)(4,1)S(1)}, s32[]{:S(2)}) async-start(s8[8388608]{0:T(1024)(128)(4,1)} %bitcast.86), calls=%async_computation | async-start | bytes 8388608
  35.3 16.2 %slice-start.1 = ((s8[8388608]{0:T(1024)(128)(4,1)}), s8[4194304]{0:T(1024)(128)(4,1)S(1)}, s32[]{:S(2)}) async-start(s8[8388608]{0:T(1024)(128)(4,1)} %bitcast.86), calls=%async_computation.1 | async-start | bytes 8388608
  35.3 5.3 %collective-permute-start.3 = (bf16[2,64,272]{2,1,0:T(8,128)(2,1)S(1)}, bf16[2,64,272]{2,1,0:T(8,128)(2,1)S(1)}, u32[]{:S(2)}, u32[]{:S(2)}) collective-permute-start(bf16[2,64,272]{2,1,0:T(8,128)(2,1)S(1)} %get-tuple-element.9), channel_id=1, source_target_pairs={{0,1},{1,0},{2,3},{3,2},{4,5},{5,4},{6,7},{7,6},{8,9},{9,8},{10,11... | collective-permute-start | bytes 208904 | tf_op jit(solution)/shard_map/ppermute | solution.py:17
  40.6 10.0 %collective-permute-start.4 = (bf16[1,64,272]{2,1,0:T(8,128)(2,1)S(1)}, bf16[1,64,272]{2,1,0:T(8,128)(2,1)S(1)}, u32[]{:S(2)}, u32[]{:S(2)}) collective-permute-start(bf16[1,64,272]{2,1,0:T(8,128)(2,1)S(1)} %add_convert_fusion.3), channel_id=1, source_target_pairs={{0,2},{1,3},{2,0},{3,1},{4,6},{5,7},{6,4},{7,5},{8,10},{9,11},{10,... | collective-permute-start | bytes 104456 | tf_op jit(solution)/shard_map/ppermute | solution.py:17
  48.5 9.6 %collective-permute-start.7 = (bf16[2,64,1024]{2,1,0:T(8,128)(2,1)S(1)}, bf16[2,64,1024]{2,1,0:T(8,128)(2,1)}, u32[]{:S(2)}, u32[]{:S(2)}) collective-permute-start(bf16[2,64,1024]{2,1,0:T(8,128)(2,1)S(1)} %get-tuple-element.11), channel_id=1, source_target_pairs={{0,1},{1,0},{2,3},{3,2},{4,5},{5,4},{6,7},{7,6},{8,9},{9,8},{10,11... | collective-permute-start | bytes 786440 | tf_op jit(solution)/shard_map/ppermute | solution.py:17
  49.0 13.0 %collective-permute-start.9 = (bf16[2,64,1024]{2,1,0:T(8,128)(2,1)S(1)}, bf16[2,64,1024]{2,1,0:T(8,128)(2,1)S(1)}, u32[]{:S(2)}, u32[]{:S(2)}) collective-permute-start(bf16[2,64,1024]{2,1,0:T(8,128)(2,1)S(1)} %get-tuple-element.13), channel_id=1, source_target_pairs={{0,1},{1,0},{2,3},{3,2},{4,5},{5,4},{6,7},{7,6},{8,9},{9,8},{10,11... | collective-permute-start | bytes 786440 | tf_op jit(solution)/shard_map/ppermute | solution.py:17
  59.1 13.0 %copy-start.9 = (f32[1,32,1024]{2,0,1:T(1,128)S(1)}, f32[1,32,1024]{2,0,1:T(1,128)}, u32[]{:S(2)}) copy-start(f32[1,32,1024]{2,0,1:T(1,128)} %reshape.250) | copy-start | bytes 393220
  59.1 13.0 %copy-start.10 = (f32[1,32,1024]{2,1,0:T(8,128)S(1)}, f32[1,32,1024]{2,1,0:T(8,128)}, u32[]{:S(2)}) copy-start(f32[1,32,1024]{2,1,0:T(8,128)} %get-tuple-element.31) | copy-start | bytes 393220
  59.1 13.0 %copy-start.11 = (f32[1,32,1024]{2,1,0:T(8,128)S(1)}, f32[1,32,1024]{2,1,0:T(8,128)}, u32[]{:S(2)}) copy-start(f32[1,32,1024]{2,1,0:T(8,128)} %get-tuple-element.32) | copy-start | bytes 393220
  59.1 11.4 %collective-permute-start.8 = (bf16[1,64,1024]{2,1,0:T(8,128)(2,1)S(1)}, bf16[1,64,1024]{2,1,0:T(8,128)(2,1)S(1)}, u32[]{:S(2)}, u32[]{:S(2)}) collective-permute-start(bf16[1,64,1024]{2,1,0:T(8,128)(2,1)S(1)} %add_convert_fusion.2), channel_id=1, source_target_pairs={{0,2},{1,3},{2,0},{3,1},{4,6},{5,7},{6,4},{7,5},{8,10},{9,11},{10,... | collective-permute-start | bytes 393224 | tf_op jit(solution)/shard_map/ppermute | solution.py:17
  62.0 11.1 %collective-permute-start.10 = (bf16[1,64,1024]{2,1,0:T(8,128)(2,1)S(1)}, bf16[1,64,1024]{2,1,0:T(8,128)(2,1)S(1)}, u32[]{:S(2)}, u32[]{:S(2)}) collective-permute-start(bf16[1,64,1024]{2,1,0:T(8,128)(2,1)S(1)} %add_convert_fusion.1), channel_id=1, source_target_pairs={{0,2},{1,3},{2,0},{3,1},{4,6},{5,7},{6,4},{7,5},{8,10},{9,11},{10,... | collective-permute-start | bytes 393224 | tf_op jit(solution)/shard_map/ppermute | solution.py:17
  73.4 21.9 %collective-permute-start.13 = (f32[2,32]{1,0:T(2,128)S(1)}, f32[2,32]{1,0:T(2,128)S(1)}, u32[]{:S(2)}, u32[]{:S(2)}) collective-permute-start(f32[2,32]{1,0:T(2,128)S(1)} %reduce_sum.52), channel_id=1, source_target_pairs={{0,4},{4,0},{8,12},{12,8},{1,5},{5,1},{9,13},{13,9},{2,6},{6,2},{1... | collective-permute-start | bytes 776 | tf_op jit(solution)/shard_map/ppermute | solution.py:17
  83.2 11.0 %collective-permute-start.11 = (bf16[2,64,2048]{2,1,0:T(8,128)(2,1)S(1)}, bf16[2,64,2048]{2,1,0:T(8,128)(2,1)S(1)}, u32[]{:S(2)}, u32[]{:S(2)}) collective-permute-start(bf16[2,64,2048]{2,1,0:T(8,128)(2,1)S(1)} %output_parts.3), channel_id=1, source_target_pairs={{0,4},{4,0},{8,12},{12,8},{1,5},{5,1},{9,13},{13,9},{2,6},{6,2},{1... | collective-permute-start | bytes 1572872 | tf_op jit(solution)/shard_map/ppermute | solution.py:17
  94.3 12.5 %collective-permute-start.12 = (bf16[1,64,2048]{2,1,0:T(8,128)(2,1)S(1)}, bf16[1,64,2048]{2,1,0:T(8,128)(2,1)S(1)}, u32[]{:S(2)}, u32[]{:S(2)}) collective-permute-start(bf16[1,64,2048]{2,1,0:T(8,128)(2,1)S(1)} %add_convert_fusion), channel_id=1, source_target_pairs={{0,8},{4,12},{8,0},{12,4},{1,9},{5,13},{9,1},{13,5},{2,10},{6,14},... | collective-permute-start | bytes 786440 | tf_op jit(solution)/shard_map/ppermute | solution.py:17
  95.3 11.4 %collective-permute-start.14 = (f32[2,32]{1,0:T(2,128)S(1)}, f32[2,32]{1,0:T(2,128)S(1)}, u32[]{:S(2)}, u32[]{:S(2)}) collective-permute-start(f32[2,32]{1,0:T(2,128)S(1)} %add.214), channel_id=1, source_target_pairs={{0,8},{4,12},{8,0},{12,4},{1,9},{5,13},{9,1},{13,5},{2,10},{6,14},... | collective-permute-start | bytes 776 | tf_op jit(solution)/shard_map/ppermute | solution.py:17
  100.4 6.5 %copy-start.8 = (bf16[32,2,2048]{2,1,0:T(2,128)(2,1)S(1)}, bf16[32,2,2048]{2,1,0:T(2,128)(2,1)}, u32[]{:S(2)}) copy-start(bf16[32,2,2048]{2,1,0:T(2,128)(2,1)} %param.17) | copy-start | bytes 786436
  (9 other events, 35.7 us)

commit v2 on v1

v2 whole, which is shorter than its diff:
```python
import functools

import jax
import jax.numpy as jnp
from jax import lax
from jax.experimental import pallas as pl
from jax.experimental.pallas import tpu as pltpu
from jax.sharding import PartitionSpec as P

BF16 = jnp.bfloat16
F32 = jnp.float32
VMEM_GRANT = 24 * 1024 * 1024


def swap(values, axis, distance):
    size = lax.axis_size(axis)
    return lax.ppermute(values, axis, [(i, i ^ distance) for i in range(size)])


def bits_of(size):
    return [1 << i for i in range(size.bit_length() - 1)]


def sum_over(values, axis):
    for distance in bits_of(lax.axis_size(axis)):
        values = values + swap(values, axis, distance)
    return values


def reverse_bits(value, size):
    result = 0
    for distance in bits_of(size):
        result = result * 2 + (1 if value & distance else 0)
    return result


def gather_relative(block, axis):
    blocks, order = [block], [0]
    for distance in reversed(bits_of(lax.axis_size(axis))):
        blocks = blocks + [swap(b, axis, distance) for b in blocks]
        order = order + [i ^ distance for i in order]
    return blocks, order


def params(**more):
    return pltpu.CompilerParams(vmem_limit_bytes=VMEM_GRANT, **more)


def cost(flops, size):
    return pl.CostEstimate(flops=int(flops), bytes_accessed=int(size), transcendentals=0)


def in_hbm(values):
    return pltpu.with_memory_space_constraint(values, pltpu.HBM)


def project_body(count, tile, small, index_ref, *refs):
    blocks = refs[:count]
    weights = refs[count : count + 1 + 2 * small]
    send_ref, keep_ref, lhs, *scratch = refs[count + 1 + 2 * small :]
    held, semaphores = scratch[:-1], scratch[-1]
    rows = blocks[0].shape[0]
    columns = weights[0].shape[1]
    copies = []
    for i in range(count):
        at = pl.multiple_of(index_ref[i] * rows, rows)
        copies.append(
            pltpu.make_async_copy(blocks[i], lhs.at[pl.ds(at, rows), :], semaphores.at[i])
        )
    tiles = columns // tile
    for t in range(tiles):
        copies.append(
            pltpu.make_async_copy(
                weights[0].at[:, pl.ds(t * tile, tile)], held[0].at[t], semaphores.at[count + t]
            )
        )
    for i in range(2 * small):
        copies.append(
            pltpu.make_async_copy(weights[1 + i], held[1 + i], semaphores.at[count + tiles + i])
        )
    for copy in copies:
        copy.start()

    def put(acc, start):
        for k in range(count):
            target = send_ref if k % 2 else keep_ref
            target[k // 2, :, start : start + acc.shape[1]] = acc[
                k * rows : (k + 1) * rows
            ].astype(target.dtype)

    for copy in copies[:count]:
        copy.wait()
    for t in range(tiles):
        copies[count + t].wait()
        put(jnp.dot(lhs[...], held[0][t], preferred_element_type=F32), t * tile)
    if small:
        for copy in copies[count + tiles :]:
            copy.wait()
        put(jnp.dot(lhs[...], held[1][...], preferred_element_type=F32), columns)
        put(
            lax.dot_general(
                lhs[...], held[2][...], (((1,), (1,)), ((), ())), preferred_element_type=F32
            ),
            columns + held[1].shape[1],
        )


def project(index, blocks, weight, *small):
    count = len(blocks)
    rows, depth = blocks[0].shape
    columns = weight.shape[1]
    tile = min(columns, 256)
    wide = columns
    held = [pltpu.VMEM((columns // tile, depth, tile), BF16)]
    if small:
        wide += small[0].shape[1] + small[1].shape[0]
        held += [pltpu.VMEM(w.shape, BF16) for w in small]
    half = jax.ShapeDtypeStruct((count // 2, rows, wide), BF16)
    anywhere = pl.BlockSpec(memory_space=pl.ANY)
    whole = pl.BlockSpec(memory_space=pltpu.VMEM)
    return pl.pallas_call(
        functools.partial(project_body, count, tile, len(small) // 2),
        out_shape=(half, half),
        in_specs=[pl.BlockSpec(memory_space=pltpu.SMEM)] + [anywhere] * (count + 1 + len(small)),
        out_specs=(whole, whole),
        scratch_shapes=[pltpu.VMEM((count * rows, depth), BF16)]
        + held
        + [pltpu.SemaphoreType.DMA((count + columns // tile + len(small),))],
        compiler_params=params(),
        cost_estimate=cost(
            2 * count * rows * depth * wide, 2 * (depth * wide + count * rows * (depth + wide))
        ),
        name="project_signal" if small else "project_gate",
    )(index, *blocks, in_hbm(weight), *[in_hbm(w) for w in small])


def scatter_rows(send, keep, axis):
    terms = None
    for distance in bits_of(lax.axis_size(axis)):
        other = swap(send, axis, distance)
        if keep.shape[0] == 1:
            return [t[0] for t in ([keep] if terms is None else terms) + [other]]
        if terms is None:
            terms = [keep]
        now = terms + [other]
        send = sum(t[1::2].astype(F32) for t in now).astype(BF16)
        terms = [t[0::2] for t in now]
        keep = terms[0]
    return [t[0] for t in terms]


def softplus(values):
    return jnp.maximum(values, 0.0) + jnp.log1p(jnp.exp(-jnp.abs(values)))


def silu(values):
    return values / (1.0 + jnp.exp(-values))


def recur_body(
    terms,
    group,
    live_ref,
    *refs,
):
    term_refs = refs[:terms]
    inverse_ref, adapted_ref, bias_ref, rate_ref, skip_ref, state_ref = refs[terms : terms + 6]
    result_ref, feeds_ref, b_ref, both_ref, c_ref, read_ref, spread_ref, signal_ref = refs[terms + 6 :]
    _, heads, head, width = state_ref.shape
    streams, inner = feeds_ref.shape[1:]
    step = pl.program_id(0)

    @pl.when(step == 0)
    def _():
        total = sum(t[...].astype(F32) for t in term_refs) * inverse_ref[...]
        signal_ref[...] = silu(total[:, :inner] + adapted_ref[...])
        gates = silu(total[:, inner : inner + 2 * width])
        steps_dt = softplus(total[:, inner + 2 * width :] + bias_ref[...])
        b = [gates[p * streams : (p + 1) * streams, :width] for p in range(2)]
        c = [gates[p * streams : (p + 1) * streams, width:] for p in range(2)]
        for p in range(2):
            b_ref[p] = b[p]
            c_ref[p] = c[p]
        live = lax.broadcasted_iota(jnp.int32, (streams, heads), 0) < live_ref[0]
        dt = [steps_dt[p * streams : (p + 1) * streams] for p in range(2)]
        decay = [jnp.where(live, jnp.exp(-d * rate_ref[...]), 1.0) for d in dt]
        fed = [jnp.where(live, d, 0.0) for d in dt]

        def match(i, j):
            return jnp.sum(b[i] * c[j], -1, keepdims=True)

        both = decay[0] * decay[1]
        both_ref[...] = both
        late = decay[1] * fed[0]
        skip = skip_ref[...]
        factors = jnp.concatenate(
            [
                decay[0],
                both,
                fed[0] * match(0, 0) + skip,
                fed[1] * match(1, 1) + skip,
                late * match(0, 1),
                late,
                fed[1],
            ],
            0,
        )
        high, low = split(factors)
        place = lax.broadcasted_iota(jnp.int32, (heads, inner), 1) // head
        ones = (place == lax.broadcasted_iota(jnp.int32, (heads, inner), 0)).astype(BF16)
        spread_ref[...] = jnp.dot(high, ones, preferred_element_type=F32) + jnp.dot(
            low, ones, preferred_element_type=F32
        )

    at = pl.multiple_of(step * group, group)
    c = jnp.concatenate([c_ref[p, pl.ds(at, group), :] for p in range(2)], 0)
    lhs = jnp.concatenate(split(c), 0)
    for g in range(group):
        state = state_ref[g].reshape(inner, width)
        found = lax.dot_general(lhs, state, (((1,), (1,)), ((), ())), preferred_element_type=F32)
        for p in range(2):
            row = p * group + g
            low = 2 * group + row
            read_ref[p, pl.ds(at + g, 1), :] = found[row : row + 1] + found[low : low + 1]

    @pl.when(step == pl.num_programs(0) - 1)
    def _():
        factor = [spread_ref[i * streams : (i + 1) * streams, :] for i in range(7)]
        first = signal_ref[:streams, :]
        second = signal_ref[streams:, :]
        result_ref[:streams, :] = factor[0] * read_ref[0] + factor[2] * first
        result_ref[streams:, :] = factor[1] * read_ref[1] + factor[4] * first + factor[3] * second
        feeds_ref[0] = factor[5] * first
        feeds_ref[1] = factor[6] * second


def recur(live_rows, terms, inverse, adapted, bias, rate, skip, state):
    streams, heads, head, width = state.shape
    group = 8
    inner = heads * head
    rows = 2 * streams
    whole = pl.BlockSpec(memory_space=pltpu.VMEM)
    return pl.pallas_call(
        functools.partial(recur_body, len(terms), group),
        out_shape=(
            jax.ShapeDtypeStruct((rows, inner), F32),
            jax.ShapeDtypeStruct((2, streams, inner), F32),
            jax.ShapeDtypeStruct((2, streams, width), F32),
            jax.ShapeDtypeStruct((streams, heads), F32),
        ),
        grid=(streams // group,),
        in_specs=[pl.BlockSpec(memory_space=pltpu.SMEM)]
        + [whole] * (len(terms) + 5)
        + [pl.BlockSpec((group, heads, head, width), lambda i: (i, 0, 0, 0))],
        out_specs=(whole, whole, whole, whole),
        scratch_shapes=[
            pltpu.VMEM((2, streams, width), F32),
            pltpu.VMEM((2, streams, inner), F32),
            pltpu.VMEM((7 * streams, inner), F32),
            pltpu.VMEM((rows, inner), F32),
        ],
        compiler_params=params(),
        cost_estimate=cost(64 * state.size, 2 * state.size + 32 * rows * inner),
        name="recur",
    )(
        live_rows,
        *terms,
        inverse,
        adapted,
        bias[None],
        rate[None],
        skip[None],
        in_hbm(state),
    )


def state_write_body(left_ref, right_ref, decay_ref, state_ref, out_ref):
    group, heads, head, width = state_ref.shape
    for g in range(group):
        outer = lax.dot_general(
            left_ref[g], right_ref[g], (((0,), (0,)), ((), ())), preferred_element_type=F32
        )
        scaled = state_ref[g].astype(F32) * decay_ref[g][:, None, :]
        out_ref[g] = (scaled + outer.reshape(heads, head, width)).astype(out_ref.dtype)


def state_write(left, right, decay, state):
    streams, heads, head, width = state.shape
    group = 4
    rank = left.shape[1]
    block = pl.BlockSpec((group, heads, head, width), lambda i: (i, 0, 0, 0))
    return pl.pallas_call(
        state_write_body,
        out_shape=jax.ShapeDtypeStruct(state.shape, state.dtype),
        grid=(streams // group,),
        in_specs=[
            pl.BlockSpec((group, rank, heads * head), lambda i: (i, 0, 0)),
            pl.BlockSpec((group, rank, width), lambda i: (i, 0, 0)),
            pl.BlockSpec((group, heads, width), lambda i: (i, 0, 0)),
            block,
        ],
        out_specs=block,
        compiler_params=params(),
        cost_estimate=cost(32 * state.size, 4 * state.size),
        name="state_write",
    )(left, right, decay, in_hbm(state))


def output_first_body(terms, index_ref, *refs):
    term_refs = refs[:terms]
    inverse_ref, result_ref, scale_ref, weight_ref, out_ref, lhs_ref, squares_ref = refs[terms:]

    @pl.when((pl.program_id(0) == 0) & (pl.program_id(1) == 0))
    def _():
        total = sum(t[...].astype(F32) for t in term_refs) * inverse_ref[...]
        gated = result_ref[...] * silu(total)
        squares_ref[...] = jnp.sum(gated * gated, -1, keepdims=True)
        lhs_ref[...] = (gated * scale_ref[...]).astype(lhs_ref.dtype)

    out_ref[0] = jnp.dot(lhs_ref[...], weight_ref[...], preferred_element_type=F32).astype(out_ref.dtype)


def output_second_body(index_ref, lhs_ref, weight_ref, out_ref):
    out_ref[0] = jnp.dot(lhs_ref[...], weight_ref[...], preferred_element_type=F32).astype(out_ref.dtype)


def output_parts(index, weight, width, operands, first):
    rows, depth = operands[-1].shape if not first else operands[0].shape
    count = index.shape[0]
    tile = min(width, 1024)
    tiles = width // tile
    whole = pl.BlockSpec(memory_space=pltpu.VMEM)
    out_shape = [jax.ShapeDtypeStruct((count, rows, width), BF16)]
    out_specs = [pl.BlockSpec((1, rows, tile), lambda j, t, s: (j, 0, t))]
    if first:
        out_shape += [
            jax.ShapeDtypeStruct((rows, depth), BF16),
            jax.ShapeDtypeStruct((rows, 1), F32),
        ]
        out_specs += [whole, whole]
    return pl.pallas_call(
        functools.partial(output_first_body, len(operands) - 3) if first else output_second_body,
        out_shape=tuple(out_shape),
        grid_spec=pltpu.PrefetchScalarGridSpec(
            num_scalar_prefetch=1,
            grid=(count, tiles),
            in_specs=[whole] * len(operands)
            + [pl.BlockSpec((depth, tile), lambda j, t, s: (0, s[j] * tiles + t))],
            out_specs=tuple(out_specs),
        ),
        compiler_params=params(),
        cost_estimate=cost(2 * rows * depth * width * count, 2 * depth * width * count),
        name="output_first" if first else "output_second",
    )(index, *operands, in_hbm(weight))


def split(values):
    high = values.astype(BF16)
    return high, (values - high.astype(F32)).astype(BF16)


def on_device(
    hidden,
    input_norm_scale,
    projection_signal,
    projection_gate,
    projection_step,
    projection_input_output,
    step_bias,
    head_decay_rate,
    head_skip_weight,
    gated_norm_scale,
    adapter_down_weight,
    adapter_up_weight,
    output_weight,
    scan_state,
    stream_tenant_index,
    live_block_rows,
):
    epsilon = 1e-05
    streams, positions, feature_width = hidden.shape
    rows = streams * positions
    heads_n = lax.axis_size("head")
    rows_n = lax.axis_size("row")
    model_width = feature_width * heads_n
    depth, inner = projection_signal.shape
    inner_width = inner * heads_n
    heads_here = projection_step.shape[1]
    head_at = lax.axis_index("head")
    row_at = lax.axis_index("row")

    wide = jnp.swapaxes(hidden, 0, 1).astype(F32)
    scaled = (wide * input_norm_scale).astype(BF16)
    scaled_flat = scaled.reshape(rows, feature_width)

    if heads_n == rows_n:
        turned = lax.ppermute(
            scaled_flat,
            ("head", "row"),
            [
                (h * rows_n + r, reverse_bits(r, rows_n) * rows_n + h)
                for h in range(heads_n)
                for r in range(rows_n)
            ],
        )
        blocks, order = gather_relative(turned, "head")
        owner = jnp.asarray([reverse_bits(i, rows_n) for i in range(rows_n)], jnp.int32)
        index = owner[head_at ^ jnp.asarray(order, jnp.int32)] ^ row_at
    else:
        features = lax.all_gather(scaled_flat, "head", axis=1, tiled=True)
        blocks = lax.all_to_all(features, "row", split_axis=1, concat_axis=0, tiled=True)
        blocks = blocks.reshape(rows_n, rows, depth)
        blocks = [blocks[i] for i in range(rows_n)]
        index = jnp.arange(rows_n, dtype=jnp.int32) ^ row_at

    signal_parts = project(index, blocks, projection_signal, projection_input_output, projection_step.T)
    signal_terms = scatter_rows(*signal_parts, "row")
    gate_terms = scatter_rows(*project(index, blocks, projection_gate), "row")

    tenant_local = stream_tenant_index - row_at * adapter_down_weight.shape[0]
    down_weight_rows = jnp.take(adapter_down_weight, tenant_local, axis=0)
    square_part = jnp.sum(wide * wide, -1)
    lowrank_part = jnp.einsum(
        "psd,sdr->psr", scaled, down_weight_rows, preferred_element_type=F32
    )
    sums = sum_over(
        jnp.concatenate([lowrank_part, square_part[..., None]], -1).reshape(rows, -1), "head"
    )
    inverse = lax.rsqrt(sums[:, -1:] / model_width + epsilon)
    lowrank = (sums[:, :-1] * inverse).astype(BF16).reshape(positions, streams, -1)
    up_weight_rows = jnp.take(adapter_up_weight, tenant_local, axis=0)
    adapted = jnp.einsum("psr,srk->psk", lowrank, up_weight_rows, preferred_element_type=F32)

    result, feeds, bgate, both = recur(
        live_block_rows,
        signal_terms,
        inverse,
        adapted.reshape(rows, inner),
        step_bias,
        head_decay_rate,
        head_skip_weight,
        scan_state,
    )

    distances = jnp.arange(heads_n, dtype=jnp.int32) ^ head_at
    odd, out_lhs, gate_squares = output_parts(
        distances[1::2],
        output_weight,
        feature_width,
        [*gate_terms, inverse, result, gated_norm_scale[None]],
        True,
    )
    (even,) = output_parts(distances[0::2], output_weight, feature_width, [out_lhs], False)
    gate_squares = sum_over(gate_squares, "head")
    mixer = sum(t.astype(F32) for t in scatter_rows(odd, even, "head"))
    mixer = mixer * lax.rsqrt(gate_squares / inner_width + epsilon)
    mixer = mixer.reshape(positions, streams, feature_width)
    live = jnp.arange(streams) < live_block_rows[0]
    mixed = (wide + jnp.where(live[:, None], mixer, 0.0)).astype(BF16)

    b_high, b_low = split(jnp.swapaxes(bgate, 0, 1))
    f_high, f_low = split(jnp.swapaxes(feeds, 0, 1))
    left = jnp.concatenate([f_high, f_low, f_high, jnp.zeros_like(f_high)], 1)
    right = jnp.concatenate([b_high, b_high, b_low, jnp.zeros_like(b_high)], 1)
    spread = jnp.broadcast_to(both[..., None], both.shape + (bgate.shape[-1],))
    new_state = state_write(left, right, spread, scan_state)
    return (jnp.swapaxes(mixed, 0, 1), new_state)


def solution(mesh):
    in_specs = (
        P(("rep", "row"), None, "head"),
        P("head"),
        P("row", "head"),
        P("row", "head"),
        P("row", "head"),
        P("row", None),
        P("head"),
        P("head"),
        P("head"),
        P("head"),
        P("row", "head", None),
        P("row", None, "head"),
        P("head", None),
        P(("rep", "row"), "head", None, None),
        P(("rep", "row")),
        P(("rep", "row")),
    )
    out_specs = (P(("rep", "row"), None, "head"), P(("rep", "row"), "head", None, None))
    return jax.shard_map(
        on_device, mesh=mesh, in_specs=in_specs, out_specs=out_specs, check_vma=False
    )
```

time: 109 us -> 97.8 us (0.90)
  local copies, waits for them, and re-layouts: 30.2 us -> 8.98 us
  Pallas kernels: 24 us -> 38.4 us
  waiting for transfers between devices: 15.2 us -> 25 us
  starting transfers between devices: 24.9 us -> 17.2 us
  other arithmetic: 10.5 us -> 4.86 us
    unnamed x36 -> x12, local copies, waits for them, and re-layouts: 17.2 us -> 0.03 us
    pallas_call x6 -> x5, Pallas kernels: 17.7 us -> 27.8 us  [the longest x2 11.4 us: output_parts(): pl.pallas_call(functools.partial(output_first_body, len(operands) - 3) if...]
    ppermute x14 -> x13, waiting for transfers between devices: 15.2 us -> 25 us  [swap(): return lax.ppermute(values, axis, [(i, i ^ distance) for i in range(size)])]
    ppermute x14 -> x13, starting transfers between devices: 23.3 us -> 16.5 us  [swap(): return lax.ppermute(values, axis, [(i, i ^ distance) for i in range(size)])]
    pallas_call x1, Pallas kernels: 6.31 us -> 10.7 us  [state_write(): pl.pallas_call(state_write_body, out_shape=jax.ShapeDtypeStruct(state.sha...]
    reshape x7 -> x0, local copies, waits for them, and re-layouts: 1.94 us -> none  [expand(): return spread.reshape(values.shape[:-1] + (inner,))]
    add x3 -> x0, other arithmetic: 1.56 us -> none  [the longest x2 0.98 us: total(): whole = sum((t.astype(F32) for t in terms))]
    concatenate x4 -> x1, other arithmetic: 1.52 us -> 0.08 us  [on_device(): right = jnp.concatenate([b_high, b_high, b_low, jnp.zeros_like(b_high)], 1)]
  transfers between devices with their start and end apart: 15 -> 14, of which waited for: 4 -> 5; matrix products, arithmetic and copies ran while one was open for 18% -> 13% of each run, Pallas kernels for 21% -> 29%
where the time goes in v2:
time: 97.8 us; the launch traced here: 97.4 us
  Pallas kernels  38.4 us (39%)
  waiting for transfers between devices  25 us (26%)
  starting transfers between devices  17.2 us (18%)
  local copies, waits for them, and re-layouts  8.98 us (9%)
  other arithmetic  4.86 us (5%)
  between operations  1.62 us (2%)
  matrix products  1.33 us (1%)
    ppermute x13, waiting for transfers between devices, swap(): return lax.ppermute(values, axis, [(i, i ^ distance) for i in range(size)])  25 us
    ppermute x13, starting transfers between devices, swap(): return lax.ppermute(values, axis, [(i, i ^ distance) for i in range(size)])  16.5 us
    pallas_call x2, Pallas kernels, output_parts(): pl.pallas_call(functools.partial(output_first_body, len(operands) - 3) if...  11.4 us
    pallas_call x1, Pallas kernels, state_write(): pl.pallas_call(state_write_body, out_shape=jax.ShapeDtypeStruct(state.sha...  10.7 us
    pallas_call x2, Pallas kernels, project(): pl.pallas_call(functools.partial(project_body, count, tile, len(small) //...  10.1 us
    pallas_call x1, Pallas kernels, recur(): pl.pallas_call(functools.partial(recur_body, len(terms), group), out_shap...  6.36 us
    gather x1, local copies, waits for them, and re-layouts, on_device(): down_weight_rows = jnp.take(adapter_down_weight, tenant_local, axis=0)  4.07 us
    gather x1, local copies, waits for them, and re-layouts, on_device(): up_weight_rows = jnp.take(adapter_up_weight, tenant_local, axis=0)  2.8 us
  transfers between devices with their start and end apart: 14, of which 5 were waited for; matrix products, arithmetic and copies ran while one was open for 13% of the time, Pallas kernels for 29%

profile of v2, /device:TPU:0, one launch (start us, length us, event | category | flops | bytes accessed | tf_op | source)
XLA Modules:
  0.0 97.4 jit_solution(14176595254980552175)
XLA Ops:
  0.6 1.4 %fusion.10 = (f32[2,32]{0,1:T(8,128)S(1)}, bf16[2,32,2048]{2,0,1:T(2,128)(2,1)S(1)}) fusion(bf16[32,2,2048]{2,1,0:T(2,128)(2,1)} %param.18, f32[2048]{0:T(1024)} %param.19), kind=kLoop, calls=%fused_computation.16 | loop fusion | flops 655296 | bytes 532736 | tf_op jit(solution)/shard_map/reduce_sum | solution.py:422
  2.1 0.7 collective-permute-start
  2.8 0.7 compare_and_fusion
  3.6 4.1 %gather_fusion.1 = bf16[32,2048,16]{1,2,0:T(8,128)(2,1)S(1)} fusion(bf16[128,2048,16]{1,2,0:T(8,128)(2,1)} %param.28, s32[1024]{0:T(1024)S(1)} %pad_clamp_fusion), kind=kCustom, calls=%fused_computation.1 | custom fusion | bytes 4194432 | tf_op jit(solution)/shard_map/jit(_take)/gather | solution.py:421
  7.7 1.0 %fusion.3 = f32[2,32,16]{2,0,1:T(2,128)S(1)} fusion(bf16[2,32,2048]{2,0,1:T(2,128)(2,1)S(1)} %get-tuple-element.27, bf16[32,2048,16]{1,2,0:T(8,128)(2,1)S(1)} %gather_fusion.1, pred[32]{0:T(512)(128)(4,1)S(1)} %get-tuple-element.24), kind=kOutput, calls=%fused_computation.7 | convolution fusion | flops 5242880 | bytes 2363424 | tf_op jit(solution)/shard_map/psd,sdr->psr/dot_general | solution.py:423
  9.0 4.4 %collective-permute-start.6 = (f32[64,17]{1,0:T(8,128)S(1)}, f32[64,17]{1,0:T(8,128)S(1)}, u32[]{:S(2)}, u32[]{:S(2)}) collective-permute-start(f32[64,17]{1,0:T(8,128)S(1)} %copy.52), channel_id=1, source_target_pairs={{0,4},{4,0},{8,12},{12,8},{1,5},{5,1},{9,13},{13,9},{2,6},{6,2},{1... | collective-permute-start | bytes 13064 | tf_op jit(solution)/shard_map/ppermute | solution.py:17
  13.4 0.6 gather_fusion
  14.7 3.6 %collective-permute-start.7 = (f32[64,17]{1,0:T(8,128)S(1)}, f32[64,17]{1,0:T(8,128)S(1)}, u32[]{:S(2)}, u32[]{:S(2)}) collective-permute-start(f32[64,17]{1,0:T(8,128)S(1)} %add.61), channel_id=1, source_target_pairs={{0,8},{4,12},{8,0},{12,4},{1,9},{5,13},{9,1},{13,5},{2,10},{6,14},... | collective-permute-start | bytes 13064 | tf_op jit(solution)/shard_map/ppermute | solution.py:17
  18.6 2.8 %gather_fusion.2 = bf16[32,16,1024]{2,1,0:T(8,128)(2,1)S(1)} fusion(bf16[128,16,1024]{2,1,0:T(8,128)(2,1)} %param.29, s32[1024]{0:T(1024)S(1)} %pad_clamp_fusion), kind=kCustom, calls=%fused_computation.2 | custom fusion | bytes 2097280 | tf_op jit(solution)/shard_map/jit(_take)/gather | solution.py:431
  21.7 1.6 %collective-permute-start.2 = (bf16[64,2048]{1,0:T(8,128)(2,1)S(1)}, bf16[64,2048]{1,0:T(8,128)(2,1)S(1)}, u32[]{:S(2)}, u32[]{:S(2)}) collective-permute-start(bf16[64,2048]{1,0:T(8,128)(2,1)S(1)} %collective-permute-done.refs_0_), channel_id=1, source_target_pairs={{0,4},{4,0},{8,12},{12,8},{1,5},{5,1},{9,13},{13,9},{2,6},{6,2},{1... | collective-permute-start | bytes 786440 | tf_op jit(solution)/shard_map/ppermute | solution.py:17
  23.3 3.5 %collective-permute-done.1.refs_1_ = bf16[64,2048]{1,0:T(8,128)(2,1)S(1)} collective-permute-done((bf16[64,2048]{1,0:T(8,128)(2,1)S(1)}, bf16[64,2048]{1,0:T(8,128)(2,1)S(1)}, u32[]{:S(2)}, u32[]{:S(2)}) %collective-permute-start.1) | collective-permute-done | bytes 262176 | tf_op jit(solution)/shard_map/ppermute | solution.py:17
  28.5 4.7 %project_gate.1 = (bf16[2,64,1024]{2,1,0:T(8,128)(2,1)S(1)}, bf16[2,64,1024]{2,1,0:T(8,128)(2,1)S(1)}) custom-call(s32[4]{0:T(128)S(1)} %broadcast_xor_fusion.index_ref, bf16[64,2048]{1,0:T(8,128)(2,1)S(1)} %collective-permute-done.refs_0_, bf16[64,2048]{1,0:T(8,128)(2,1)S(1)} %collective-permute-done.1.refs_1_, ...), custom_call_target="tpu_custom_call" | custom-call | flops 1073741824 | bytes 5767168 | tf_op jit(solution)/shard_map/project_gate/pallas_call | solution.py:121
  33.2 2.1 %collective-permute-start.4 = (bf16[2,64,1024]{2,1,0:T(8,128)(2,1)S(1)}, bf16[2,64,1024]{2,1,0:T(8,128)(2,1)S(1)}, u32[]{:S(2)}, u32[]{:S(2)}) collective-permute-start(bf16[2,64,1024]{2,1,0:T(8,128)(2,1)S(1)} %get-tuple-element.14), channel_id=1, source_target_pairs={{0,1},{1,0},{2,3},{3,2},{4,5},{5,4},{6,7},{7,6},{8,9},{9,8},{10,11... | collective-permute-start | bytes 786440 | tf_op jit(solution)/shard_map/ppermute | solution.py:17
  35.3 5.4 %project_signal.1 = (bf16[2,64,1296]{2,1,0:T(8,128)(2,1)S(1)}, bf16[2,64,1296]{2,1,0:T(8,128)(2,1)S(1)}) custom-call(s32[4]{0:T(128)S(1)} %broadcast_xor_fusion.index_ref, bf16[64,2048]{1,0:T(8,128)(2,1)S(1)} %collective-permute-done.refs_0_, bf16[64,2048]{1,0:T(8,128)(2,1)S(1)} %collective-permute-done.1.refs_1_, ...), custom_call_target="tpu_custom_call" | custom-call | flops 1358954496 | bytes 7020544 | tf_op jit(solution)/shard_map/project_signal/pallas_call | solution.py:121
  40.9 1.1 %collective-permute-done.4 = bf16[2,64,1024]{2,1,0:T(8,128)(2,1)S(1)} collective-permute-done((bf16[2,64,1024]{2,1,0:T(8,128)(2,1)S(1)}, bf16[2,64,1024]{2,1,0:T(8,128)(2,1)S(1)}, u32[]{:S(2)}, u32[]{:S(2)}) %collective-permute-start.4) | collective-permute-done | bytes 262176 | tf_op jit(solution)/shard_map/ppermute | solution.py:17
  41.9 1.2 %collective-permute-start.5 = (bf16[1,64,1024]{2,1,0:T(8,128)(2,1)S(1)}, bf16[1,64,1024]{2,1,0:T(8,128)(2,1)S(1)}, u32[]{:S(2)}, u32[]{:S(2)}) collective-permute-start(bf16[1,64,1024]{2,1,0:T(8,128)(2,1)S(1)} %add_convert_fusion.2), channel_id=1, source_target_pairs={{0,2},{1,3},{2,0},{3,1},{4,6},{5,7},{6,4},{7,5},{8,10},{9,11},{10,... | collective-permute-start | bytes 393224 | tf_op jit(solution)/shard_map/ppermute | solution.py:17
  43.2 10.6 %collective-permute-done.8 = bf16[2,64,1296]{2,1,0:T(8,128)(2,1)S(1)} collective-permute-done((bf16[2,64,1296]{2,1,0:T(8,128)(2,1)S(1)}, bf16[2,64,1296]{2,1,0:T(8,128)(2,1)S(1)}, u32[]{:S(2)}, u32[]{:S(2)}) %collective-permute-start.8) | collective-permute-done | bytes 331808 | tf_op jit(solution)/shard_map/ppermute | solution.py:17
  53.9 9.1 %collective-permute-done.9 = bf16[1,64,1296]{2,1,0:T(8,128)(2,1)S(1)} collective-permute-done((bf16[1,64,1296]{2,1,0:T(8,128)(2,1)S(1)}, bf16[1,64,1296]{2,1,0:T(8,128)(2,1)S(1)}, u32[]{:S(2)}, u32[]{:S(2)}) %collective-permute-start.9) | collective-permute-done | bytes 165920 | tf_op jit(solution)/shard_map/ppermute | solution.py:17
  63.1 6.4 %recur.1 = (f32[64,1024]{1,0:T(8,128)S(1)}, f32[2,32,1024]{2,1,0:T(8,128)S(1)}, f32[2,32,128]{2,1,0:T(8,128)S(1)}, f32[32,16]{1,0:T(8,128)S(1)}) custom-call(s32[1]{0:T(128)} %copy.78.live_ref, bf16[64,1296]{1,0:T(8,128)(2,1)S(1)} %slice_bitcast_fusion.1.refs_0_, bf16[64,1296]{1,0:T(8,128)(2,1)S(1)} %slice_bitcast_fusion.refs_1_, ...), custom_call_target="tpu_custom_call" | custom-call | flops 268435456 | bytes 10485760 | tf_op jit(solution)/shard_map/recur/pallas_call | solution.py:243
  69.5 5.8 %output_first.1 = (bf16[2,64,2048]{2,1,0:T(8,128)(2,1)S(1)}, bf16[64,1024]{1,0:T(8,128)(2,1)S(1)}, f32[64,1]{1,0:T(8,128)S(1)}) custom-call(s32[2]{0:T(128)S(1)} %slice.61.index_ref, bf16[64,1024]{1,0:T(8,128)(2,1)S(1)} %slice_bitcast_fusion.3.refs_0_, bf16[64,1024]{1,0:T(8,128)(2,1)S(1)} %slice_bitcast_fusion.2.refs_1_, bf16[64,1024]{1,0:T(8,128)(2,1)S(1)} %bitcast.60, ...), custom_call_target="tpu_custom_call" | custom-call | flops 536870912 | bytes 8388608 | tf_op jit(solution)/shard_map/output_first/pallas_call | solution.py:341
  76.2 5.6 %output_second.1 = bf16[2,64,2048]{2,1,0:T(8,128)(2,1)S(1)} custom-call(s32[2]{0:T(128)S(1)} %slice.60.index_ref, bf16[64,1024]{1,0:T(8,128)(2,1)S(1)} %get-tuple-element.18.lhs_ref, bf16[1024,8192]{1,0:T(8,128)(2,1)} %weight_ref.1), custom_call_target="tpu_custom_call" | custom-call | flops 536870912 | bytes 8388608 | tf_op jit(solution)/shard_map/output_second/pallas_call | solution.py:341
  82.5 1.8 %collective-permute-start.11 = (bf16[1,64,2048]{2,1,0:T(8,128)(2,1)S(1)}, bf16[1,64,2048]{2,1,0:T(8,128)(2,1)S(1)}, u32[]{:S(2)}, u32[]{:S(2)}) collective-permute-start(bf16[1,64,2048]{2,1,0:T(8,128)(2,1)S(1)} %add_convert_fusion), channel_id=1, source_target_pairs={{0,8},{4,12},{8,0},{12,4},{1,9},{5,13},{9,1},{13,5},{2,10},{6,14},... | collective-permute-start | bytes 786440 | tf_op jit(solution)/shard_map/ppermute | solution.py:17
  84.9 10.7 %state_write.1 = bf16[32,16,64,128]{3,2,1,0:T(8,128)(2,1)} custom-call(bf16[32,8,1024]{2,1,0:T(8,128)(2,1)S(1)} %maximum_maximum_fusion.left_ref, bf16[32,8,128]{2,1,0:T(8,128)(2,1)S(1)} %maximum_maximum_fusion.1.right_ref, f32[32,16,128]{2,1,0:T(8,128)S(1)} %broadcast_in_dim.78.decay_ref, bf16[32,16,64,128]{3,2,1,0:T(8,128)(2,1)} %state_ref.1), custom_call_target="tpu_custom_call" | custom-call | flops 134217728 | bytes 16777216 | tf_op jit(solution)/shard_map/state_write/pallas_call | solution.py:292
  96.0 1.4 %fusion.15 = bf16[32,2,2048]{2,1,0:T(2,128)(2,1)} fusion(f32[2,32]{0,1:T(8,128)S(1)} %copy.55, f32[2,32,2048]{2,1,0:T(8,128)S(1)} %bitcast.65, pred[32]{0:T(512)(128)(4,1)S(1)} %iota_compare_fusion, bf16[32,2,2048]{2,1,0:T(2,128)(2,1)S(1)} %copy-done.5), kind=kLoop, calls=%fused_computation.28 | loop fusion | flops 655360 | bytes 1048864 | tf_op jit(solution)/shard_map/transpose | solution.py:467
  (71 shorter events, 5.6 us)
Async XLA Ops:
  2.1 16.2 %collective-permute-start = (bf16[64,2048]{1,0:T(8,128)(2,1)S(1)}, bf16[64,2048]{1,0:T(8,128)(2,1)S(1)}, u32[]{:S(2)}, u32[]{:S(2)}) collective-permute-start(bf16[64,2048]{1,0:T(8,128)(2,1)S(1)} %bitcast.67), channel_id=1, source_target_pairs={{0,0},{1,8},{2,4},{3,12},{4,1},{5,9},{6,5},{7,13},{8,2},{9,10},{10... | collective-permute-start | bytes 786440 | tf_op jit(solution)/shard_map/ppermute | solution.py:397
  7.7 5.7 %copy-start.4 = (s32[4]{0:T(128)S(1)}, s32[4]{0:T(128)}, u32[]{:S(2)}) copy-start(s32[4]{0:T(128)} %constant.54.clone) | copy-start | bytes 52
  9.0 5.7 %collective-permute-start.6 = (f32[64,17]{1,0:T(8,128)S(1)}, f32[64,17]{1,0:T(8,128)S(1)}, u32[]{:S(2)}, u32[]{:S(2)}) collective-permute-start(f32[64,17]{1,0:T(8,128)S(1)} %copy.52), channel_id=1, source_target_pairs={{0,4},{4,0},{8,12},{12,8},{1,5},{5,1},{9,13},{13,9},{2,6},{6,2},{1... | collective-permute-start | bytes 13064 | tf_op jit(solution)/shard_map/ppermute | solution.py:17
  14.7 6.7 %collective-permute-start.7 = (f32[64,17]{1,0:T(8,128)S(1)}, f32[64,17]{1,0:T(8,128)S(1)}, u32[]{:S(2)}, u32[]{:S(2)}) collective-permute-start(f32[64,17]{1,0:T(8,128)S(1)} %add.61), channel_id=1, source_target_pairs={{0,8},{4,12},{8,0},{12,4},{1,9},{5,13},{9,1},{13,5},{2,10},{6,14},... | collective-permute-start | bytes 13064 | tf_op jit(solution)/shard_map/ppermute | solution.py:17
  18.3 8.5 %collective-permute-start.1 = (bf16[64,2048]{1,0:T(8,128)(2,1)S(1)}, bf16[64,2048]{1,0:T(8,128)(2,1)S(1)}, u32[]{:S(2)}, u32[]{:S(2)}) collective-permute-start(bf16[64,2048]{1,0:T(8,128)(2,1)S(1)} %collective-permute-done.refs_0_), channel_id=1, source_target_pairs={{0,8},{4,12},{8,0},{12,4},{1,9},{5,13},{9,1},{13,5},{2,10},{6,14},... | collective-permute-start | bytes 786440 | tf_op jit(solution)/shard_map/ppermute | solution.py:17
  21.7 6.2 %collective-permute-start.2 = (bf16[64,2048]{1,0:T(8,128)(2,1)S(1)}, bf16[64,2048]{1,0:T(8,128)(2,1)S(1)}, u32[]{:S(2)}, u32[]{:S(2)}) collective-permute-start(bf16[64,2048]{1,0:T(8,128)(2,1)S(1)} %collective-permute-done.refs_0_), channel_id=1, source_target_pairs={{0,4},{4,0},{8,12},{12,8},{1,5},{5,1},{9,13},{13,9},{2,6},{6,2},{1... | collective-permute-start | bytes 786440 | tf_op jit(solution)/shard_map/ppermute | solution.py:17
  26.8 1.6 %collective-permute-start.3 = (bf16[64,2048]{1,0:T(8,128)(2,1)S(1)}, bf16[64,2048]{1,0:T(8,128)(2,1)S(1)}, u32[]{:S(2)}, u32[]{:S(2)}) collective-permute-start(bf16[64,2048]{1,0:T(8,128)(2,1)S(1)} %collective-permute-done.1.refs_1_), channel_id=1, source_target_pairs={{0,4},{4,0},{8,12},{12,8},{1,5},{5,1},{9,13},{13,9},{2,6},{6,2},{1... | collective-permute-start | bytes 786440 | tf_op jit(solution)/shard_map/ppermute | solution.py:17
  33.2 8.8 %collective-permute-start.4 = (bf16[2,64,1024]{2,1,0:T(8,128)(2,1)S(1)}, bf16[2,64,1024]{2,1,0:T(8,128)(2,1)S(1)}, u32[]{:S(2)}, u32[]{:S(2)}) collective-permute-start(bf16[2,64,1024]{2,1,0:T(8,128)(2,1)S(1)} %get-tuple-element.14), channel_id=1, source_target_pairs={{0,1},{1,0},{2,3},{3,2},{4,5},{5,4},{6,7},{7,6},{8,9},{9,8},{10,11... | collective-permute-start | bytes 786440 | tf_op jit(solution)/shard_map/ppermute | solution.py:17
  35.3 27.8 %copy-start.1 = (f32[16]{0:T(128)S(1)}, f32[16]{0:T(128)}, u32[]{:S(2)}) copy-start(f32[16]{0:T(128)} %param.24) | copy-start | bytes 196
  35.3 27.8 %copy-start.2 = (f32[16]{0:T(128)S(1)}, f32[16]{0:T(128)}, u32[]{:S(2)}) copy-start(f32[16]{0:T(128)} %param.25) | copy-start | bytes 196
  35.3 27.8 %copy-start.3 = (f32[16]{0:T(128)S(1)}, f32[16]{0:T(128)}, u32[]{:S(2)}) copy-start(f32[16]{0:T(128)} %param.26) | copy-start | bytes 196
  40.7 13.0 %collective-permute-start.8 = (bf16[2,64,1296]{2,1,0:T(8,128)(2,1)S(1)}, bf16[2,64,1296]{2,1,0:T(8,128)(2,1)S(1)}, u32[]{:S(2)}, u32[]{:S(2)}) collective-permute-start(bf16[2,64,1296]{2,1,0:T(8,128)(2,1)S(1)} %get-tuple-element.16), channel_id=1, source_target_pairs={{0,1},{1,0},{2,3},{3,2},{4,5},{5,4},{6,7},{7,6},{8,9},{9,8},{10,11... | collective-permute-start | bytes 995336 | tf_op jit(solution)/shard_map/ppermute | solution.py:17
  41.9 27.5 %collective-permute-start.5 = (bf16[1,64,1024]{2,1,0:T(8,128)(2,1)S(1)}, bf16[1,64,1024]{2,1,0:T(8,128)(2,1)S(1)}, u32[]{:S(2)}, u32[]{:S(2)}) collective-permute-start(bf16[1,64,1024]{2,1,0:T(8,128)(2,1)S(1)} %add_convert_fusion.2), channel_id=1, source_target_pairs={{0,2},{1,3},{2,0},{3,1},{4,6},{5,7},{6,4},{7,5},{8,10},{9,11},{10,... | collective-permute-start | bytes 393224 | tf_op jit(solution)/shard_map/ppermute | solution.py:17
  53.8 9.2 %collective-permute-start.9 = (bf16[1,64,1296]{2,1,0:T(8,128)(2,1)S(1)}, bf16[1,64,1296]{2,1,0:T(8,128)(2,1)S(1)}, u32[]{:S(2)}, u32[]{:S(2)}) collective-permute-start(bf16[1,64,1296]{2,1,0:T(8,128)(2,1)S(1)} %add_convert_fusion.1), channel_id=1, source_target_pairs={{0,2},{1,3},{2,0},{3,1},{4,6},{5,7},{6,4},{7,5},{8,10},{9,11},{10,... | collective-permute-start | bytes 497672 | tf_op jit(solution)/shard_map/ppermute | solution.py:17
  63.1 6.4 %copy-start = (f32[1024]{0:T(1024)S(1)}, f32[1024]{0:T(1024)}, u32[]{:S(2)}) copy-start(f32[1024]{0:T(1024)} %param.27) | copy-start | bytes 12292
  75.3 7.1 %collective-permute-start.10 = (bf16[2,64,2048]{2,1,0:T(8,128)(2,1)S(1)}, bf16[2,64,2048]{2,1,0:T(8,128)(2,1)S(1)}, u32[]{:S(2)}, u32[]{:S(2)}) collective-permute-start(bf16[2,64,2048]{2,1,0:T(8,128)(2,1)S(1)} %get-tuple-element.19), channel_id=1, source_target_pairs={{0,4},{4,0},{8,12},{12,8},{1,5},{5,1},{9,13},{13,9},{2,6},{6,2},{1... | collective-permute-start | bytes 1572872 | tf_op jit(solution)/shard_map/ppermute | solution.py:17
  75.4 9.0 %collective-permute-start.12 = (f32[64,1]{1,0:T(8,128)S(1)}, f32[64,1]{1,0:T(8,128)S(1)}, u32[]{:S(2)}, u32[]{:S(2)}) collective-permute-start(f32[64,1]{1,0:T(8,128)S(1)} %get-tuple-element.20), channel_id=1, source_target_pairs={{0,4},{4,0},{8,12},{12,8},{1,5},{5,1},{9,13},{13,9},{2,6},{6,2},{1... | collective-permute-start | bytes 776 | tf_op jit(solution)/shard_map/ppermute | solution.py:17
  82.5 13.4 %collective-permute-start.11 = (bf16[1,64,2048]{2,1,0:T(8,128)(2,1)S(1)}, bf16[1,64,2048]{2,1,0:T(8,128)(2,1)S(1)}, u32[]{:S(2)}, u32[]{:S(2)}) collective-permute-start(bf16[1,64,2048]{2,1,0:T(8,128)(2,1)S(1)} %add_convert_fusion), channel_id=1, source_target_pairs={{0,8},{4,12},{8,0},{12,4},{1,9},{5,13},{9,1},{13,5},{2,10},{6,14},... | collective-permute-start | bytes 786440 | tf_op jit(solution)/shard_map/ppermute | solution.py:17
  84.4 11.1 %collective-permute-start.13 = (f32[64,1]{1,0:T(8,128)S(1)}, f32[64,1]{1,0:T(8,128)S(1)}, u32[]{:S(2)}, u32[]{:S(2)}) collective-permute-start(f32[64,1]{1,0:T(8,128)S(1)} %add.69), channel_id=1, source_target_pairs={{0,8},{4,12},{8,0},{12,4},{1,9},{5,13},{9,1},{13,5},{2,10},{6,14},... | collective-permute-start | bytes 776 | tf_op jit(solution)/shard_map/ppermute | solution.py:17
  84.9 11.1 %copy-start.5 = (bf16[32,2,2048]{2,1,0:T(2,128)(2,1)S(1)}, bf16[32,2,2048]{2,1,0:T(2,128)(2,1)}, u32[]{:S(2)}) copy-start(bf16[32,2,2048]{2,1,0:T(2,128)(2,1)} %param.18) | copy-start | bytes 786436

commit v3 on v2

v3 whole, which is shorter than its diff:
```python
import functools

import jax
import jax.numpy as jnp
from jax import lax
from jax.experimental import pallas as pl
from jax.experimental.pallas import tpu as pltpu
from jax.sharding import PartitionSpec as P

BF16 = jnp.bfloat16
F32 = jnp.float32
VMEM_GRANT = 12 * 1024 * 1024


def swap(values, axis, distance):
    size = lax.axis_size(axis)
    return lax.ppermute(values, axis, [(i, i ^ distance) for i in range(size)])


def bits_of(size):
    return [1 << i for i in range(size.bit_length() - 1)]


def sum_over(values, axis):
    for distance in bits_of(lax.axis_size(axis)):
        values = values + swap(values, axis, distance)
    return values


def reverse_bits(value, size):
    result = 0
    for distance in bits_of(size):
        result = result * 2 + (1 if value & distance else 0)
    return result


def gather_relative(block, axis, beside):
    distances = list(reversed(bits_of(lax.axis_size(axis))))
    blocks, order = [block, swap(block, axis, distances[0])], [0, distances[0]]
    extra = beside(block)
    own = extra[0]
    for distance in distances[1:]:
        blocks = blocks + [swap(b, axis, distance) for b in [own] + blocks[1:]]
        order = order + [i ^ distance for i in order]
    return blocks, order, extra[1:]


def params(**more):
    return pltpu.CompilerParams(vmem_limit_bytes=VMEM_GRANT, **more)


def cost(flops, size):
    return pl.CostEstimate(flops=int(flops), bytes_accessed=int(size), transcendentals=0)


def in_hbm(values):
    return pltpu.with_memory_space_constraint(values, pltpu.HBM)


def load_body(pieces, after_ref, *refs):
    count = len(pieces)
    sources, targets, semaphores = refs[:count], refs[count : 2 * count], refs[2 * count]
    copies = []
    for source, target, parts in zip(sources, targets, pieces):
        step = source.shape[0] // parts
        for i in range(parts):
            at = pl.ds(i * step, step)
            copies.append(
                pltpu.make_async_copy(source.at[at], target.at[at], semaphores.at[len(copies)])
            )
    for copy in copies:
        copy.start()
    for copy in copies:
        copy.wait()


def load(after, passed, *weights):
    arrays = (passed, *weights)
    pieces = [1] + [8 if w.shape[0] % 128 == 0 else 1 for w in weights]
    size = sum(a.size * a.dtype.itemsize for a in arrays)
    return pl.pallas_call(
        functools.partial(load_body, pieces),
        out_shape=tuple(pltpu.VMEM(a.shape, a.dtype) for a in arrays),
        in_specs=[pl.BlockSpec(memory_space=pl.ANY)] * (1 + len(arrays)),
        out_specs=tuple(pl.BlockSpec(memory_space=pltpu.VMEM) for _ in arrays),
        scratch_shapes=[pltpu.SemaphoreType.DMA((sum(pieces),))],
        compiler_params=params(),
        cost_estimate=cost(0, 2 * size),
        name="load",
    )(after, passed, *[in_hbm(w) for w in weights])


def fill_rows(index_ref, blocks, lhs, semaphores):
    rows = blocks[0].shape[0]
    copies = []
    for i, block in enumerate(blocks):
        at = pl.multiple_of(index_ref[i] * rows, rows)
        copies.append(pltpu.make_async_copy(block, lhs.at[pl.ds(at, rows), :], semaphores.at[i]))
    for copy in copies:
        copy.start()
    for copy in copies:
        copy.wait()


def put_parts(acc, start, send_ref, keep_ref):
    rows = send_ref.shape[1]
    for k in range(acc.shape[0] // rows):
        target = send_ref if k % 2 else keep_ref
        target[k // 2, :, start : start + acc.shape[1]] = acc[k * rows : (k + 1) * rows].astype(
            target.dtype
        )


def project_signal_body(count, index_ref, *refs):
    blocks, refs = refs[:count], refs[count:]
    weight_ref, mix_ref, step_ref, send_ref, keep_ref, lhs_ref, semaphores = refs
    fill_rows(index_ref, blocks, lhs_ref, semaphores)
    lhs = lhs_ref[...]
    columns = weight_ref.shape[1]
    tile = min(columns, 512)
    for t in range(0, columns, tile):
        acc = jnp.dot(lhs, weight_ref[:, t : t + tile], preferred_element_type=F32)
        put_parts(acc, t, send_ref, keep_ref)
    acc = jnp.dot(lhs, mix_ref[...], preferred_element_type=F32)
    put_parts(acc, columns, send_ref, keep_ref)
    acc = lax.dot_general(lhs, step_ref[...], (((1,), (1,)), ((), ())), preferred_element_type=F32)
    put_parts(acc, columns + mix_ref.shape[1], send_ref, keep_ref)


def project_signal(index, blocks, weight, mix, step):
    count = len(blocks)
    rows, depth = blocks[0].shape
    columns = weight.shape[1] + mix.shape[1] + step.shape[0]
    half = jax.ShapeDtypeStruct((count // 2, rows, columns), BF16)
    whole = pl.BlockSpec(memory_space=pltpu.VMEM)
    return pl.pallas_call(
        functools.partial(project_signal_body, count),
        out_shape=(half, half, jax.ShapeDtypeStruct((count * rows, depth), BF16)),
        in_specs=[pl.BlockSpec(memory_space=pltpu.SMEM)]
        + [pl.BlockSpec(memory_space=pl.ANY)] * count
        + [whole] * 3,
        out_specs=(whole,) * 3,
        scratch_shapes=[pltpu.SemaphoreType.DMA((count,))],
        compiler_params=params(),
        cost_estimate=cost(2 * count * rows * depth * columns, 2 * depth * columns),
        name="project_signal",
    )(index, *blocks, weight, mix, step)


def project_gate_body(lhs_ref, weight_ref, sums_ref, after_ref, send_ref, keep_ref, out_ref):
    columns = weight_ref.shape[1]
    tile = min(columns, 512)
    for t in range(0, columns, tile):
        acc = jnp.dot(lhs_ref[...], weight_ref[:, t : t + tile], preferred_element_type=F32)
        put_parts(acc, t, send_ref, keep_ref)
    out_ref[...] = sums_ref[...]


def project_gate(rows, lhs, weight, sums, after):
    count = lhs.shape[0] // rows
    columns = weight.shape[1]
    half = jax.ShapeDtypeStruct((count // 2, rows, columns), BF16)
    whole = pl.BlockSpec(memory_space=pltpu.VMEM)
    return pl.pallas_call(
        project_gate_body,
        out_shape=(half, half, jax.ShapeDtypeStruct(sums.shape, sums.dtype)),
        in_specs=[whole, whole, whole, pl.BlockSpec(memory_space=pl.ANY)],
        out_specs=(whole,) * 3,
        compiler_params=params(),
        cost_estimate=cost(2 * lhs.size * columns, 2 * weight.size),
        name="project_gate",
    )(lhs, weight, sums, after)


def merge_body(terms, *refs):
    out_ref = refs[-1]
    for i in range(out_ref.shape[0]):
        total = sum(t[2 * i + 1].astype(F32) for t in refs[:terms])
        out_ref[i] = total.astype(out_ref.dtype)


def merge(terms, after):
    count, rows, columns = terms[0].shape
    whole = pl.BlockSpec(memory_space=pltpu.VMEM)
    return pl.pallas_call(
        functools.partial(merge_body, len(terms)),
        out_shape=jax.ShapeDtypeStruct((count // 2, rows, columns), BF16),
        in_specs=[whole] * len(terms) + [pl.BlockSpec(memory_space=pl.ANY)],
        out_specs=whole,
        compiler_params=params(),
        cost_estimate=cost(terms[0].size, 4 * terms[0].size),
        name="merge",
    )(*terms, after)


def scatter_rows(send, keep, axis, after=None):
    terms = [keep]
    for distance in bits_of(lax.axis_size(axis)):
        other = swap(send, axis, distance)
        now = [other] + terms
        if other.shape[0] == 1:
            return [t[0] for t in now], send
        if after is None:
            send = sum(t[1::2].astype(F32) for t in now).astype(BF16)
        else:
            send = merge(now, after)
        terms = [t[0::2] for t in now]
    return [t[0] for t in terms], send


def softplus(values):
    return jnp.maximum(values, 0.0) + jnp.log1p(jnp.exp(-jnp.abs(values)))


def silu(values):
    return values / (1.0 + jnp.exp(-values))


def recur_body(
    terms,
    group,
    live_ref,
    *refs,
):
    term_refs = refs[:terms]
    inverse_ref, adapted_ref, bias_ref, rate_ref, skip_ref, source_ref = refs[terms : terms + 6]
    result_ref, feeds_ref, b_ref, both_ref, state_ref, *scratch = refs[terms + 6 :]
    c_ref, read_ref, spread_ref, signal_ref, semaphores = scratch
    heads, head, width = state_ref.shape[1:]
    streams, inner = feeds_ref.shape[1:]
    step = pl.program_id(0)

    def fetch(i):
        at = pl.ds(i * group, group)
        return pltpu.make_async_copy(source_ref.at[at], state_ref.at[at], semaphores.at[i])

    @pl.when(step == 0)
    def _():
        for i in range(streams // group):
            fetch(i).start()
        total = sum(t[...].astype(F32) for t in term_refs) * inverse_ref[...]
        signal_ref[...] = silu(total[:, :inner] + adapted_ref[...])
        gates = silu(total[:, inner : inner + 2 * width])
        steps_dt = softplus(total[:, inner + 2 * width :] + bias_ref[...])
        b = [gates[p * streams : (p + 1) * streams, :width] for p in range(2)]
        c = [gates[p * streams : (p + 1) * streams, width:] for p in range(2)]
        for p in range(2):
            b_ref[p] = b[p]
            c_ref[p] = c[p]
        live = lax.broadcasted_iota(jnp.int32, (streams, heads), 0) < live_ref[0]
        dt = [steps_dt[p * streams : (p + 1) * streams] for p in range(2)]
        decay = [jnp.where(live, jnp.exp(-d * rate_ref[...]), 1.0) for d in dt]
        fed = [jnp.where(live, d, 0.0) for d in dt]

        def match(i, j):
            return jnp.sum(b[i] * c[j], -1, keepdims=True)

        both = decay[0] * decay[1]
        both_ref[...] = both
        late = decay[1] * fed[0]
        skip = skip_ref[...]
        factors = jnp.concatenate(
            [
                decay[0],
                both,
                fed[0] * match(0, 0) + skip,
                fed[1] * match(1, 1) + skip,
                late * match(0, 1),
                late,
                fed[1],
            ],
            0,
        )
        high, low = split(factors)
        place = lax.broadcasted_iota(jnp.int32, (heads, inner), 1) // head
        ones = (place == lax.broadcasted_iota(jnp.int32, (heads, inner), 0)).astype(BF16)
        spread_ref[...] = jnp.dot(high, ones, preferred_element_type=F32) + jnp.dot(
            low, ones, preferred_element_type=F32
        )

    fetch(step).wait()
    at = pl.multiple_of(step * group, group)
    c = jnp.concatenate([c_ref[p, pl.ds(at, group), :] for p in range(2)], 0)
    lhs = jnp.concatenate(split(c), 0)
    for g in range(group):
        state = state_ref[at + g].reshape(inner, width)
        found = lax.dot_general(lhs, state, (((1,), (1,)), ((), ())), preferred_element_type=F32)
        for p in range(2):
            row = p * group + g
            low = 2 * group + row
            read_ref[p, pl.ds(at + g, 1), :] = found[row : row + 1] + found[low : low + 1]

    @pl.when(step == pl.num_programs(0) - 1)
    def _():
        factor = [spread_ref[i * streams : (i + 1) * streams, :] for i in range(7)]
        first = signal_ref[:streams, :]
        second = signal_ref[streams:, :]
        result_ref[:streams, :] = factor[0] * read_ref[0] + factor[2] * first
        result_ref[streams:, :] = factor[1] * read_ref[1] + factor[4] * first + factor[3] * second
        feeds_ref[0] = factor[5] * first
        feeds_ref[1] = factor[6] * second


def recur(live_rows, terms, inverse, adapted, bias, rate, skip, state):
    streams, heads, head, width = state.shape
    group = 8
    inner = heads * head
    rows = 2 * streams
    whole = pl.BlockSpec(memory_space=pltpu.VMEM)
    return pl.pallas_call(
        functools.partial(recur_body, len(terms), group),
        out_shape=(
            jax.ShapeDtypeStruct((rows, inner), F32),
            jax.ShapeDtypeStruct((2, streams, inner), F32),
            jax.ShapeDtypeStruct((2, streams, width), F32),
            jax.ShapeDtypeStruct((streams, heads), F32),
            pltpu.VMEM(state.shape, state.dtype),
        ),
        grid=(streams // group,),
        in_specs=[pl.BlockSpec(memory_space=pltpu.SMEM)]
        + [whole] * (len(terms) + 5)
        + [pl.BlockSpec(memory_space=pl.ANY)],
        out_specs=(whole,) * 5,
        scratch_shapes=[
            pltpu.VMEM((2, streams, width), F32),
            pltpu.VMEM((2, streams, inner), F32),
            pltpu.VMEM((7 * streams, inner), F32),
            pltpu.VMEM((rows, inner), F32),
            pltpu.SemaphoreType.DMA((streams // group,)),
        ],
        compiler_params=params(),
        cost_estimate=cost(64 * state.size, 2 * state.size + 32 * rows * inner),
        name="recur",
    )(
        live_rows,
        *terms,
        inverse,
        adapted,
        bias[None],
        rate[None],
        skip[None],
        in_hbm(state),
    )


def state_write_body(left_ref, right_ref, decay_ref, state_ref, out_ref):
    group, heads, head, width = out_ref.shape
    at = pl.program_id(0) * group
    for g in range(group):
        outer = lax.dot_general(
            left_ref[g], right_ref[g], (((0,), (0,)), ((), ())), preferred_element_type=F32
        )
        scaled = state_ref[at + g].astype(F32) * decay_ref[g][:, None, :]
        out_ref[g] = (scaled + outer.reshape(heads, head, width)).astype(out_ref.dtype)


def state_write(left, right, decay, state):
    streams, heads, head, width = state.shape
    group = 4
    rank = left.shape[1]
    block = pl.BlockSpec((group, heads, head, width), lambda i: (i, 0, 0, 0))
    return pl.pallas_call(
        state_write_body,
        out_shape=jax.ShapeDtypeStruct(state.shape, state.dtype),
        grid=(streams // group,),
        in_specs=[
            pl.BlockSpec((group, rank, heads * head), lambda i: (i, 0, 0)),
            pl.BlockSpec((group, rank, width), lambda i: (i, 0, 0)),
            pl.BlockSpec((group, heads, width), lambda i: (i, 0, 0)),
            pl.BlockSpec(memory_space=pltpu.VMEM),
        ],
        out_specs=block,
        compiler_params=params(),
        cost_estimate=cost(32 * state.size, 4 * state.size),
        name="state_write",
    )(left, right, decay, state)


def output_tiles(index_ref, lhs_ref, weight_ref, out_ref):
    count, _, width = out_ref.shape
    tile = min(width, 512)
    for j in range(count):
        for t in range(0, width, tile):
            at = pl.multiple_of(index_ref[j] * width + t, tile)
            acc = jnp.dot(lhs_ref[...], weight_ref[:, pl.ds(at, tile)], preferred_element_type=F32)
            out_ref[j, :, t : t + tile] = acc.astype(out_ref.dtype)


def output_first_body(terms, index_ref, *refs):
    term_refs = refs[:terms]
    inverse_ref, result_ref, scale_ref, weight_ref, out_ref, lhs_ref, squares_ref = refs[terms:]
    total = sum(t[...].astype(F32) for t in term_refs) * inverse_ref[...]
    gated = result_ref[...] * silu(total)
    squares_ref[...] = jnp.sum(gated * gated, -1, keepdims=True)
    lhs_ref[...] = (gated * scale_ref[...]).astype(lhs_ref.dtype)
    output_tiles(index_ref, lhs_ref, weight_ref, out_ref)


def output_parts(index, weight, width, operands, first):
    rows, depth = operands[0].shape
    count = index.shape[0]
    whole = pl.BlockSpec(memory_space=pltpu.VMEM)
    out_shape = [jax.ShapeDtypeStruct((count, rows, width), BF16)]
    if first:
        out_shape += [
            jax.ShapeDtypeStruct((rows, depth), BF16),
            jax.ShapeDtypeStruct((rows, 1), F32),
        ]
    return pl.pallas_call(
        functools.partial(output_first_body, len(operands) - 3) if first else output_tiles,
        out_shape=tuple(out_shape),
        in_specs=[pl.BlockSpec(memory_space=pltpu.SMEM)] + [whole] * (len(operands) + 1),
        out_specs=(whole,) * len(out_shape),
        compiler_params=params(),
        cost_estimate=cost(2 * rows * depth * width * count, 2 * depth * width * count),
        name="output_first" if first else "output_second",
    )(index, *operands, weight)


def split(values):
    high = values.astype(BF16)
    return high, (values - high.astype(F32)).astype(BF16)


def on_device(
    hidden,
    input_norm_scale,
    projection_signal,
    projection_gate,
    projection_step,
    projection_input_output,
    step_bias,
    head_decay_rate,
    head_skip_weight,
    gated_norm_scale,
    adapter_down_weight,
    adapter_up_weight,
    output_weight,
    scan_state,
    stream_tenant_index,
    live_block_rows,
):
    epsilon = 1e-05
    streams, positions, feature_width = hidden.shape
    rows = streams * positions
    heads_n = lax.axis_size("head")
    rows_n = lax.axis_size("row")
    model_width = feature_width * heads_n
    depth, inner = projection_signal.shape
    inner_width = inner * heads_n
    heads_here = projection_step.shape[1]
    head_at = lax.axis_index("head")
    row_at = lax.axis_index("row")

    wide = jnp.swapaxes(hidden, 0, 1).astype(F32)
    scaled = (wide * input_norm_scale).astype(BF16)
    scaled_flat = scaled.reshape(rows, feature_width)

    in_weights = (projection_signal, projection_input_output, projection_gate)
    if heads_n == rows_n:
        turned = lax.ppermute(
            scaled_flat,
            ("head", "row"),
            [
                (h * rows_n + r, reverse_bits(r, rows_n) * rows_n + h)
                for h in range(heads_n)
                for r in range(rows_n)
            ],
        )
        blocks, order, weights = gather_relative(
            turned, "head", lambda block: load(block, block, *in_weights)
        )
        owner = jnp.asarray([reverse_bits(i, rows_n) for i in range(rows_n)], jnp.int32)
        index = owner[head_at ^ jnp.asarray(order, jnp.int32)] ^ row_at
    else:
        features = lax.all_gather(scaled_flat, "head", axis=1, tiled=True)
        blocks = lax.all_to_all(features, "row", split_axis=1, concat_axis=0, tiled=True)
        blocks = blocks.reshape(rows_n, rows, depth)
        blocks = [blocks[i] for i in range(rows_n)]
        weights = load(scaled_flat, scaled_flat, *in_weights)[1:]
        index = jnp.arange(rows_n, dtype=jnp.int32) ^ row_at

    tenant_local = stream_tenant_index - row_at * adapter_down_weight.shape[0]
    down_weight_rows = jnp.take(adapter_down_weight, tenant_local, axis=0)
    square_part = jnp.sum(wide * wide, -1)
    lowrank_part = jnp.einsum(
        "psd,sdr->psr", scaled, down_weight_rows, preferred_element_type=F32
    )
    sums = jnp.concatenate([lowrank_part, square_part[..., None]], -1).reshape(rows, -1)

    signal_weight, mix_weight, gate_weight = weights
    send, keep, lhs = project_signal(
        index, blocks, signal_weight, mix_weight, projection_step.T
    )
    gate_send, gate_keep, sums = project_gate(rows, lhs, gate_weight, sums, send)
    keep, out_weight = load(gate_send, keep, output_weight)
    signal_terms, last_send = scatter_rows(send, keep, "row")
    gate_terms, _ = scatter_rows(gate_send, gate_keep, "row", after=last_send)
    sums = sum_over(sums, "head")
    inverse = lax.rsqrt(sums[:, -1:] / model_width + epsilon)
    lowrank = (sums[:, :-1] * inverse).astype(BF16).reshape(positions, streams, -1)
    up_weight_rows = jnp.take(adapter_up_weight, tenant_local, axis=0)
    adapted = jnp.einsum("psr,srk->psk", lowrank, up_weight_rows, preferred_element_type=F32)

    result, feeds, bgate, both, state = recur(
        live_block_rows,
        signal_terms,
        inverse,
        adapted.reshape(rows, inner),
        step_bias,
        head_decay_rate,
        head_skip_weight,
        scan_state,
    )

    distances = jnp.arange(heads_n, dtype=jnp.int32) ^ head_at
    odd, out_lhs, gate_squares = output_parts(
        distances[1::2],
        out_weight,
        feature_width,
        [*gate_terms, inverse, result, gated_norm_scale[None]],
        True,
    )
    (even,) = output_parts(distances[0::2], out_weight, feature_width, [out_lhs], False)
    gate_squares = sum_over(gate_squares, "head")
    mixer = sum(t.astype(F32) for t in scatter_rows(odd, even, "head")[0])
    mixer = mixer * lax.rsqrt(gate_squares / inner_width + epsilon)
    mixer = mixer.reshape(positions, streams, feature_width)
    live = jnp.arange(streams) < live_block_rows[0]
    mixed = (wide + jnp.where(live[:, None], mixer, 0.0)).astype(BF16)

    b_high, b_low = split(jnp.swapaxes(bgate, 0, 1))
    f_high, f_low = split(jnp.swapaxes(feeds, 0, 1))
    left = jnp.concatenate([f_high, f_low, f_high, jnp.zeros_like(f_high)], 1)
    right = jnp.concatenate([b_high, b_high, b_low, jnp.zeros_like(b_high)], 1)
    spread = jnp.broadcast_to(both[..., None], both.shape + (bgate.shape[-1],))
    new_state = state_write(left, right, spread, state)
    return (jnp.swapaxes(mixed, 0, 1), new_state)


def solution(mesh):
    in_specs = (
        P(("rep", "row"), None, "head"),
        P("head"),
        P("row", "head"),
        P("row", "head"),
        P("row", "head"),
        P("row", None),
        P("head"),
        P("head"),
        P("head"),
        P("head"),
        P("row", "head", None),
        P("row", None, "head"),
        P("head", None),
        P(("rep", "row"), "head", None, None),
        P(("rep", "row")),
        P(("rep", "row")),
    )
    out_specs = (P(("rep", "row"), None, "head"), P(("rep", "row"), "head", None, None))
    return jax.shard_map(
        on_device, mesh=mesh, in_specs=in_specs, out_specs=out_specs, check_vma=False
    )
```

time: 97.8 us -> 92 us (0.941)
  Pallas kernels: 38.4 us -> 29.3 us
  waiting for transfers between devices: 25 us -> 16.9 us
  local copies, waits for them, and re-layouts: 8.98 us -> 15.1 us
  starting transfers between devices: 17.2 us -> 21.9 us
    ppermute x13, waiting for transfers between devices: 25 us -> 16.9 us  [swap(): return lax.ppermute(values, axis, [(i, i ^ distance) for i in range(size)])]
    pallas_call x2, Pallas kernels: 11.4 us -> 4.4 us  [output_parts(): pl.pallas_call(functools.partial(output_first_body, len(operands) - 3) if...]
    unnamed x12 -> x22, local copies, waits for them, and re-layouts: 0.03 us -> 6.18 us
    ppermute x13, starting transfers between devices: 16.5 us -> 21.2 us  [swap(): return lax.ppermute(values, axis, [(i, i ^ distance) for i in range(size)])]
    pallas_call x1, Pallas kernels: 10.7 us -> 6.34 us  [state_write(): pl.pallas_call(state_write_body, out_shape=jax.ShapeDtypeStruct(state.sha...]
    pallas_call x2 -> x5, Pallas kernels: 10.1 us -> 13.8 us  [the longest x2 10 us: load(): pl.pallas_call(functools.partial(load_body, pieces), out_shape=tuple((plt...]
    pallas_call x1, Pallas kernels: 6.36 us -> 4.83 us  [recur(): pl.pallas_call(functools.partial(recur_body, len(terms), group), out_shap...]
  transfers between devices with their start and end apart: 14 -> 14, of which waited for: 5 -> 4; matrix products, arithmetic and copies ran while one was open for 13% -> 14% of each run, Pallas kernels for 29% -> 27%
where the time goes in v3:
time: 92 us; the launch traced here: 91.8 us
  Pallas kernels  29.3 us (32%)
  starting transfers between devices  21.9 us (24%)
  waiting for transfers between devices  16.9 us (18%)
  local copies, waits for them, and re-layouts  15.1 us (16%)
  other arithmetic  5.46 us (6%)
  between operations  1.71 us (2%)
  matrix products  1.34 us (1%)
    ppermute x13, starting transfers between devices, swap(): return lax.ppermute(values, axis, [(i, i ^ distance) for i in range(size)])  21.2 us
    ppermute x13, waiting for transfers between devices, swap(): return lax.ppermute(values, axis, [(i, i ^ distance) for i in range(size)])  16.9 us
    pallas_call x2, Pallas kernels, load(): pl.pallas_call(functools.partial(load_body, pieces), out_shape=tuple((plt...  10 us
    pallas_call x1, Pallas kernels, state_write(): pl.pallas_call(state_write_body, out_shape=jax.ShapeDtypeStruct(state.sha...  6.34 us
    unnamed x22, local copies, waits for them, and re-layouts  6.18 us
    pallas_call x1, Pallas kernels, recur(): pl.pallas_call(functools.partial(recur_body, len(terms), group), out_shap...  4.83 us
    pallas_call x2, Pallas kernels, output_parts(): pl.pallas_call(functools.partial(output_first_body, len(operands) - 3) if...  4.4 us
    gather x1, local copies, waits for them, and re-layouts, on_device(): down_weight_rows = jnp.take(adapter_down_weight, tenant_local, axis=0)  4.06 us
  transfers between devices with their start and end apart: 14, of which 4 were waited for; matrix products, arithmetic and copies ran while one was open for 14% of the time, Pallas kernels for 27%

profile of v3, /device:TPU:0, one launch (start us, length us, event | category | flops | bytes accessed | tf_op | source)
XLA Modules:
  0.0 91.8 jit_solution(10049826259035243430)
XLA Ops:
  0.6 1.4 %fusion.10 = (f32[2,32]{0,1:T(8,128)S(1)}, bf16[2,32,2048]{2,0,1:T(2,128)(2,1)S(1)}) fusion(bf16[32,2,2048]{2,1,0:T(2,128)(2,1)} %param.18, f32[2048]{0:T(1024)} %param.19), kind=kLoop, calls=%fused_computation.16 | loop fusion | flops 655296 | bytes 532736 | tf_op jit(solution)/shard_map/reduce_sum | solution.py:485
  4.2 4.1 %gather_fusion.1 = bf16[32,2048,16]{1,2,0:T(8,128)(2,1)S(1)} fusion(bf16[128,2048,16]{1,2,0:T(8,128)(2,1)} %param.28, s32[1024]{0:T(1024)S(1)} %pad_clamp_fusion), kind=kCustom, calls=%fused_computation.1 | custom fusion | bytes 4194432 | tf_op jit(solution)/shard_map/jit(_take)/gather | solution.py:484
  9.2 7.4 %collective-permute-start.1 = (bf16[64,2048]{1,0:T(8,128)(2,1)S(1)}, bf16[64,2048]{1,0:T(8,128)(2,1)S(1)}, u32[]{:S(2)}, u32[]{:S(2)}) collective-permute-start(bf16[64,2048]{1,0:T(8,128)(2,1)S(1)} %collective-permute-done.after_ref.refs_0_), channel_id=1, source_target_pairs={{0,8},{4,12},{8,0},{12,4},{1,9},{5,13},{9,1},{13,5},{2,10},{6,14},... | collective-permute-start | bytes 786440 | tf_op jit(solution)/shard_map/ppermute | solution.py:17
  17.7 3.9 %load.2 = (bf16[64,2048]{1,0:T(8,128)(2,1)S(1)}, bf16[2048,1024]{1,0:T(8,128)(2,1)S(1)}, bf16[2048,256]{1,0:T(8,128)(2,1)S(1)}, bf16[2048,1024]{1,0:T(8,128)(2,1)S(1)}) custom-call(bf16[64,2048]{1,0:T(8,128)(2,1)S(1)} %collective-permute-done.after_ref.refs_0_, bf16[64,2048]{1,0:T(8,128)(2,1)S(1)} %collective-permute-done.after_ref.refs_0_, ...), custom_call_target="tpu_custom_call" | custom-call | bytes 19398656 | tf_op jit(solution)/shard_map/load/pallas_call | solution.py:81
  21.6 2.0 %copy-done = bf16[2048,1024]{1,0:T(8,128)(2,1)} copy-done((bf16[2048,1024]{1,0:T(8,128)(2,1)}, bf16[2048,1024]{1,0:T(8,128)(2,1)S(1)}, u32[]{:S(2)}) %copy-start) | copy-done | bytes 4194328
  23.6 1.9 %copy-done.2 = bf16[2048,1024]{1,0:T(8,128)(2,1)} copy-done((bf16[2048,1024]{1,0:T(8,128)(2,1)}, bf16[2048,1024]{1,0:T(8,128)(2,1)S(1)}, u32[]{:S(2)}) %copy-start.2) | copy-done | bytes 4194328
  25.6 3.3 %collective-permute-start.2 = (bf16[64,2048]{1,0:T(8,128)(2,1)S(1)}, bf16[64,2048]{1,0:T(8,128)(2,1)S(1)}, u32[]{:S(2)}, u32[]{:S(2)}) collective-permute-start(bf16[64,2048]{1,0:T(8,128)(2,1)S(1)} %get-tuple-element.22), channel_id=1, source_target_pairs={{0,4},{4,0},{8,12},{12,8},{1,5},{5,1},{9,13},{13,9},{2,6},{6,2},{1... | collective-permute-start | bytes 786440 | tf_op jit(solution)/shard_map/ppermute | solution.py:17
  29.8 2.8 %gather_fusion.2 = bf16[32,16,1024]{2,1,0:T(8,128)(2,1)S(1)} fusion(bf16[128,16,1024]{2,1,0:T(8,128)(2,1)} %param.29, s32[1024]{0:T(1024)S(1)} %pad_clamp_fusion), kind=kCustom, calls=%fused_computation.2 | custom fusion | bytes 2097280 | tf_op jit(solution)/shard_map/jit(_take)/gather | solution.py:502
  32.8 2.2 %copy-done.1 = bf16[2048,1024]{1,0:T(8,128)(2,1)S(1)} copy-done((bf16[2048,1024]{1,0:T(8,128)(2,1)S(1)}, bf16[2048,1024]{1,0:T(8,128)(2,1)}, u32[]{:S(2)}) %copy-start.1) | copy-done | bytes 4194328
  35.0 2.5 %project_signal.1 = (bf16[2,64,1296]{2,1,0:T(8,128)(2,1)S(1)}, bf16[2,64,1296]{2,1,0:T(8,128)(2,1)S(1)}, bf16[256,2048]{1,0:T(8,128)(2,1)S(1)}) custom-call(s32[4]{0:T(128)S(1)} %broadcast_xor_fusion.index_ref, bf16[64,2048]{1,0:T(8,128)(2,1)S(1)} %collective-permute-done.after_ref.refs_0_, bf16[64,2048]{1,0:T(8,128)(2,1)S(1)} %collective-permute-done.1.refs_1_, ...), custom_call_target="tpu_custom_call" | custom-call | flops 1358954496 | bytes 5308416 | tf_op jit(solution)/shard_map/project_signal/pallas_call | solution.py:136
  37.4 2.7 %collective-permute-start.5 = (bf16[2,64,1296]{2,1,0:T(8,128)(2,1)S(1)}, bf16[2,64,1296]{2,1,0:T(8,128)(2,1)S(1)}, u32[]{:S(2)}, u32[]{:S(2)}) collective-permute-start(bf16[2,64,1296]{2,1,0:T(8,128)(2,1)S(1)} %get-tuple-element.27.after_ref), channel_id=1, source_target_pairs={{0,1},{1,0},{2,3},{3,2},{4,5},{5,4},{6,7},{7,6},{8,9},{9,8},{10,11... | collective-permute-start | bytes 995336 | tf_op jit(solution)/shard_map/ppermute | solution.py:17
  40.1 1.2 %project_gate.1 = (bf16[2,64,1024]{2,1,0:T(8,128)(2,1)S(1)}, bf16[2,64,1024]{2,1,0:T(8,128)(2,1)S(1)}, f32[64,17]{1,0:T(8,128)S(1)}) custom-call(bf16[256,2048]{1,0:T(8,128)(2,1)S(1)} %get-tuple-element.25.lhs_ref, bf16[2048,1024]{1,0:T(8,128)(2,1)S(1)} %copy-done.3, f32[64,17]{1,0:T(8,128)S(1)} %copy.50.sums_ref, ...), custom_call_target="tpu_custom_call" | custom-call | flops 1073741824 | bytes 4194304 | tf_op jit(solution)/shard_map/project_gate/pallas_call | solution.py:164
  41.5 6.1 %load.3 = (bf16[2,64,1296]{2,1,0:T(8,128)(2,1)S(1)}, bf16[1024,8192]{1,0:T(8,128)(2,1)S(1)}) custom-call(bf16[2,64,1024]{2,1,0:T(8,128)(2,1)S(1)} %get-tuple-element.28.after_ref, bf16[2,64,1296]{2,1,0:T(8,128)(2,1)S(1)} %get-tuple-element.30.refs_0_, bf16[1024,8192]{1,0:T(8,128)(2,1)} %refs_1_.3), custom_call_target="tpu_custom_call" | custom-call | bytes 34217984 | tf_op jit(solution)/shard_map/load/pallas_call | solution.py:81
  47.7 1.1 %collective-permute-start.8 = (f32[64,17]{1,0:T(8,128)S(1)}, f32[64,17]{1,0:T(8,128)S(1)}, u32[]{:S(2)}, u32[]{:S(2)}) collective-permute-start(f32[64,17]{1,0:T(8,128)S(1)} %add.58), channel_id=1, source_target_pairs={{0,8},{4,12},{8,0},{12,4},{1,9},{5,13},{9,1},{13,5},{2,10},{6,14},... | collective-permute-start | bytes 13064 | tf_op jit(solution)/shard_map/ppermute | solution.py:17
  48.8 2.8 %collective-permute-done.8 = f32[64,17]{1,0:T(8,128)S(1)} collective-permute-done((f32[64,17]{1,0:T(8,128)S(1)}, f32[64,17]{1,0:T(8,128)S(1)}, u32[]{:S(2)}, u32[]{:S(2)}) %collective-permute-start.8) | collective-permute-done | bytes 4384 | tf_op jit(solution)/shard_map/ppermute | solution.py:17
  52.4 2.1 %collective-permute-done.4.refs_0_ = bf16[2,64,1024]{2,1,0:T(8,128)(2,1)S(1)} collective-permute-done((bf16[2,64,1024]{2,1,0:T(8,128)(2,1)S(1)}, bf16[2,64,1024]{2,1,0:T(8,128)(2,1)S(1)}, u32[]{:S(2)}, u32[]{:S(2)}) %collective-permute-start.4) | collective-permute-done | bytes 262176 | tf_op jit(solution)/shard_map/ppermute | solution.py:17
  54.6 3.6 %collective-permute-start.9 = (bf16[1,64,1296]{2,1,0:T(8,128)(2,1)S(1)}, bf16[1,64,1296]{2,1,0:T(8,128)(2,1)S(1)}, u32[]{:S(2)}, u32[]{:S(2)}) collective-permute-start(bf16[1,64,1296]{2,1,0:T(8,128)(2,1)S(1)} %add_convert_fusion.1.refs_2_), channel_id=1, source_target_pairs={{0,2},{1,3},{2,0},{3,1},{4,6},{5,7},{6,4},{7,5},{8,10},{9,11},{10,... | collective-permute-start | bytes 497672 | tf_op jit(solution)/shard_map/ppermute | solution.py:17
  58.3 11.7 %collective-permute-done.9 = bf16[1,64,1296]{2,1,0:T(8,128)(2,1)S(1)} collective-permute-done((bf16[1,64,1296]{2,1,0:T(8,128)(2,1)S(1)}, bf16[1,64,1296]{2,1,0:T(8,128)(2,1)S(1)}, u32[]{:S(2)}, u32[]{:S(2)}) %collective-permute-start.9) | collective-permute-done | bytes 165920 | tf_op jit(solution)/shard_map/ppermute | solution.py:17
  70.1 4.8 %recur.1 = (f32[64,1024]{1,0:T(8,128)S(1)}, f32[2,32,1024]{2,1,0:T(8,128)S(1)}, f32[2,32,128]{2,1,0:T(8,128)S(1)}, f32[32,16]{1,0:T(8,128)S(1)}, bf16[32,16,64,128]{3,2,1,0:T(8,128)(2,1)S(1)}) custom-call(s32[1]{0:T(128)} %copy.76.live_ref, bf16[64,1296]{1,0:T(8,128)(2,1)S(1)} %bitcast.59, bf16[64,1296]{1,0:T(8,128)(2,1)S(1)} %slice_bitcast_fusion.refs_1_, ...), custom_call_target="tpu_custom_call" | custom-call | flops 268435456 | bytes 10485760 | tf_op jit(solution)/shard_map/recur/pallas_call | solution.py:310
  74.9 2.3 %output_first.1 = (bf16[2,64,2048]{2,1,0:T(8,128)(2,1)S(1)}, bf16[64,1024]{1,0:T(8,128)(2,1)S(1)}, f32[64,1]{1,0:T(8,128)S(1)}) custom-call(s32[2]{0:T(128)S(1)} %slice.52.index_ref, bf16[64,1024]{1,0:T(8,128)(2,1)S(1)} %bitcast.60, bf16[64,1024]{1,0:T(8,128)(2,1)S(1)} %slice_bitcast_fusion.2.refs_1_, bf16[64,1024]{1,0:T(8,128)(2,1)S(1)} %slice_bitcast_fusion.3.refs_2_, ...), custom_call_target="tpu_custom_call" | custom-call | flops 536870912 | bytes 8388608 | tf_op jit(solution)/shard_map/output_first/pallas_call | solution.py:409
  78.1 2.1 %output_second.1 = bf16[2,64,2048]{2,1,0:T(8,128)(2,1)S(1)} custom-call(s32[2]{0:T(128)S(1)} %slice.62.index_ref, bf16[64,1024]{1,0:T(8,128)(2,1)S(1)} %get-tuple-element.36.lhs_ref, bf16[1024,8192]{1,0:T(8,128)(2,1)S(1)} %get-tuple-element.34.refs_6_.weight_ref), custom_call_target="tpu_custom_call" | custom-call | flops 536870912 | bytes 8388608 | tf_op jit(solution)/shard_map/output_second/pallas_call | solution.py:409
  81.2 2.1 %collective-permute-start.13 = (f32[64,1]{1,0:T(8,128)S(1)}, f32[64,1]{1,0:T(8,128)S(1)}, u32[]{:S(2)}, u32[]{:S(2)}) collective-permute-start(f32[64,1]{1,0:T(8,128)S(1)} %add.65), channel_id=1, source_target_pairs={{0,8},{4,12},{8,0},{12,4},{1,9},{5,13},{9,1},{13,5},{2,10},{6,14},... | collective-permute-start | bytes 776 | tf_op jit(solution)/shard_map/ppermute | solution.py:17
  83.4 6.3 %state_write.1 = bf16[32,16,64,128]{3,2,1,0:T(8,128)(2,1)} custom-call(bf16[32,8,1024]{2,1,0:T(8,128)(2,1)S(1)} %maximum_maximum_fusion.left_ref, bf16[32,8,128]{2,1,0:T(8,128)(2,1)S(1)} %maximum_maximum_fusion.1.right_ref, f32[32,16,128]{2,1,0:T(8,128)S(1)} %broadcast_in_dim.78.decay_ref, bf16[32,16,64,128]{3,2,1,0:T(8,128)(2,1)S(1)} %get-tuple-element.41.state_ref), custom_call_target="tpu_custom_call" | custom-call | flops 134217728 | bytes 16777216 | tf_op jit(solution)/shard_map/state_write/pallas_call | solution.py:362
  90.4 1.4 %fusion.15 = bf16[32,2,2048]{2,1,0:T(2,128)(2,1)} fusion(f32[2,32]{0,1:T(8,128)S(1)} %copy.53, f32[2,32,2048]{2,1,0:T(8,128)S(1)} %bitcast.66, pred[32]{0:T(512)(128)(4,1)S(1)} %iota_compare_fusion, bf16[32,2,2048]{2,1,0:T(2,128)(2,1)S(1)} %copy-done.10), kind=kLoop, calls=%fused_computation.27 | loop fusion | flops 655360 | bytes 1048864 | tf_op jit(solution)/shard_map/transpose | solution.py:538
  (83 shorter events, 8.1 us)
Async XLA Ops:
  2.1 7.1 %collective-permute-start = (bf16[64,2048]{1,0:T(8,128)(2,1)S(1)}, bf16[64,2048]{1,0:T(8,128)(2,1)S(1)}, u32[]{:S(2)}, u32[]{:S(2)}) collective-permute-start(bf16[64,2048]{1,0:T(8,128)(2,1)S(1)} %bitcast.68), channel_id=1, source_target_pairs={{0,0},{1,8},{2,4},{3,12},{4,1},{5,9},{6,5},{7,13},{8,2},{9,10},{10... | collective-permute-start | bytes 786440 | tf_op jit(solution)/shard_map/ppermute | solution.py:461
  9.2 19.7 %collective-permute-start.1 = (bf16[64,2048]{1,0:T(8,128)(2,1)S(1)}, bf16[64,2048]{1,0:T(8,128)(2,1)S(1)}, u32[]{:S(2)}, u32[]{:S(2)}) collective-permute-start(bf16[64,2048]{1,0:T(8,128)(2,1)S(1)} %collective-permute-done.after_ref.refs_0_), channel_id=1, source_target_pairs={{0,8},{4,12},{8,0},{12,4},{1,9},{5,13},{9,1},{13,5},{2,10},{6,14},... | collective-permute-start | bytes 786440 | tf_op jit(solution)/shard_map/ppermute | solution.py:17
  17.7 11.4 %copy-start.9 = (s32[4]{0:T(128)S(1)}, s32[4]{0:T(128)}, u32[]{:S(2)}) copy-start(s32[4]{0:T(128)} %constant.54.clone) | copy-start | bytes 52
  17.7 15.1 %copy-start.4 = (bf16[2048,16]{0,1:T(8,128)(2,1)S(1)}, bf16[2048,16]{0,1:T(8,128)(2,1)}, u32[]{:S(2)}) copy-start(bf16[2048,16]{0,1:T(8,128)(2,1)} %param.22) | copy-start | bytes 196612
  21.6 2.0 %copy-start = (bf16[2048,1024]{1,0:T(8,128)(2,1)}, bf16[2048,1024]{1,0:T(8,128)(2,1)S(1)}, u32[]{:S(2)}) copy-start(bf16[2048,1024]{1,0:T(8,128)(2,1)S(1)} %get-tuple-element.23.refs_4_) | copy-start | bytes 12582916
  25.6 7.2 %collective-permute-start.2 = (bf16[64,2048]{1,0:T(8,128)(2,1)S(1)}, bf16[64,2048]{1,0:T(8,128)(2,1)S(1)}, u32[]{:S(2)}, u32[]{:S(2)}) collective-permute-start(bf16[64,2048]{1,0:T(8,128)(2,1)S(1)} %get-tuple-element.22), channel_id=1, source_target_pairs={{0,4},{4,0},{8,12},{12,8},{1,5},{5,1},{9,13},{13,9},{2,6},{6,2},{1... | collective-permute-start | bytes 786440 | tf_op jit(solution)/shard_map/ppermute | solution.py:17
  28.9 3.8 %collective-permute-start.3 = (bf16[64,2048]{1,0:T(8,128)(2,1)S(1)}, bf16[64,2048]{1,0:T(8,128)(2,1)S(1)}, u32[]{:S(2)}, u32[]{:S(2)}) collective-permute-start(bf16[64,2048]{1,0:T(8,128)(2,1)S(1)} %collective-permute-done.1.refs_1_), channel_id=1, source_target_pairs={{0,4},{4,0},{8,12},{12,8},{1,5},{5,1},{9,13},{13,9},{2,6},{6,2},{1... | collective-permute-start | bytes 786440 | tf_op jit(solution)/shard_map/ppermute | solution.py:17
  32.8 2.2 %copy-start.1 = (bf16[2048,1024]{1,0:T(8,128)(2,1)S(1)}, bf16[2048,1024]{1,0:T(8,128)(2,1)}, u32[]{:S(2)}) copy-start(bf16[2048,1024]{1,0:T(8,128)(2,1)} %copy-done) | copy-start | bytes 12582916
  35.0 5.2 %copy-start.3 = (bf16[2048,1024]{1,0:T(8,128)(2,1)S(1)}, bf16[2048,1024]{1,0:T(8,128)(2,1)}, u32[]{:S(2)}) copy-start(bf16[2048,1024]{1,0:T(8,128)(2,1)} %copy-done.2) | copy-start | bytes 12582916
  37.4 17.1 %collective-permute-start.5 = (bf16[2,64,1296]{2,1,0:T(8,128)(2,1)S(1)}, bf16[2,64,1296]{2,1,0:T(8,128)(2,1)S(1)}, u32[]{:S(2)}, u32[]{:S(2)}) collective-permute-start(bf16[2,64,1296]{2,1,0:T(8,128)(2,1)S(1)} %get-tuple-element.27.after_ref), channel_id=1, source_target_pairs={{0,1},{1,0},{2,3},{3,2},{4,5},{5,4},{6,7},{7,6},{8,9},{9,8},{10,11... | collective-permute-start | bytes 995336 | tf_op jit(solution)/shard_map/ppermute | solution.py:17
  41.4 13.1 %collective-permute-start.4 = (bf16[2,64,1024]{2,1,0:T(8,128)(2,1)S(1)}, bf16[2,64,1024]{2,1,0:T(8,128)(2,1)S(1)}, u32[]{:S(2)}, u32[]{:S(2)}) collective-permute-start(bf16[2,64,1024]{2,1,0:T(8,128)(2,1)S(1)} %get-tuple-element.28.after_ref), channel_id=1, source_target_pairs={{0,1},{1,0},{2,3},{3,2},{4,5},{5,4},{6,7},{7,6},{8,9},{9,8},{10,11... | collective-permute-start | bytes 786440 | tf_op jit(solution)/shard_map/ppermute | solution.py:17
  41.4 6.2 %collective-permute-start.7 = (f32[64,17]{1,0:T(8,128)S(1)}, f32[64,17]{1,0:T(8,128)S(1)}, u32[]{:S(2)}, u32[]{:S(2)}) collective-permute-start(f32[64,17]{1,0:T(8,128)S(1)} %get-tuple-element.32), channel_id=1, source_target_pairs={{0,4},{4,0},{8,12},{12,8},{1,5},{5,1},{9,13},{13,9},{2,6},{6,2},{1... | collective-permute-start | bytes 13064 | tf_op jit(solution)/shard_map/ppermute | solution.py:17
  47.6 22.5 %copy-start.6 = (f32[16]{0:T(128)S(1)}, f32[16]{0:T(128)}, u32[]{:S(2)}) copy-start(f32[16]{0:T(128)} %param.24) | copy-start | bytes 196
  47.6 22.5 %copy-start.7 = (f32[16]{0:T(128)S(1)}, f32[16]{0:T(128)}, u32[]{:S(2)}) copy-start(f32[16]{0:T(128)} %param.25) | copy-start | bytes 196
  47.6 22.4 %copy-start.8 = (f32[16]{0:T(128)S(1)}, f32[16]{0:T(128)}, u32[]{:S(2)}) copy-start(f32[16]{0:T(128)} %param.26) | copy-start | bytes 196
  47.7 4.0 %collective-permute-start.8 = (f32[64,17]{1,0:T(8,128)S(1)}, f32[64,17]{1,0:T(8,128)S(1)}, u32[]{:S(2)}, u32[]{:S(2)}) collective-permute-start(f32[64,17]{1,0:T(8,128)S(1)} %add.58), channel_id=1, source_target_pairs={{0,8},{4,12},{8,0},{12,4},{1,9},{5,13},{9,1},{13,5},{2,10},{6,14},... | collective-permute-start | bytes 13064 | tf_op jit(solution)/shard_map/ppermute | solution.py:17
  54.6 15.5 %collective-permute-start.9 = (bf16[1,64,1296]{2,1,0:T(8,128)(2,1)S(1)}, bf16[1,64,1296]{2,1,0:T(8,128)(2,1)S(1)}, u32[]{:S(2)}, u32[]{:S(2)}) collective-permute-start(bf16[1,64,1296]{2,1,0:T(8,128)(2,1)S(1)} %add_convert_fusion.1.refs_2_), channel_id=1, source_target_pairs={{0,2},{1,3},{2,0},{3,1},{4,6},{5,7},{6,4},{7,5},{8,10},{9,11},{10,... | collective-permute-start | bytes 497672 | tf_op jit(solution)/shard_map/ppermute | solution.py:17
  58.2 16.7 %collective-permute-start.6 = (bf16[1,64,1024]{2,1,0:T(8,128)(2,1)S(1)}, bf16[1,64,1024]{2,1,0:T(8,128)(2,1)S(1)}, u32[]{:S(2)}, u32[]{:S(2)}) collective-permute-start(bf16[1,64,1024]{2,1,0:T(8,128)(2,1)S(1)} %merge.1), channel_id=1, source_target_pairs={{0,2},{1,3},{2,0},{3,1},{4,6},{5,7},{6,4},{7,5},{8,10},{9,11},{10,... | collective-permute-start | bytes 393224 | tf_op jit(solution)/shard_map/ppermute | solution.py:17
  70.1 4.9 %copy-start.5 = (f32[1024]{0:T(1024)S(1)}, f32[1024]{0:T(1024)}, u32[]{:S(2)}) copy-start(f32[1024]{0:T(1024)} %param.27) | copy-start | bytes 12292
  77.2 3.7 %collective-permute-start.10 = (bf16[2,64,2048]{2,1,0:T(8,128)(2,1)S(1)}, bf16[2,64,2048]{2,1,0:T(8,128)(2,1)S(1)}, u32[]{:S(2)}, u32[]{:S(2)}) collective-permute-start(bf16[2,64,2048]{2,1,0:T(8,128)(2,1)S(1)} %get-tuple-element.35), channel_id=1, source_target_pairs={{0,4},{4,0},{8,12},{12,8},{1,5},{5,1},{9,13},{13,9},{2,6},{6,2},{1... | collective-permute-start | bytes 1572872 | tf_op jit(solution)/shard_map/ppermute | solution.py:17
  77.4 3.8 %collective-permute-start.12 = (f32[64,1]{1,0:T(8,128)S(1)}, f32[64,1]{1,0:T(8,128)S(1)}, u32[]{:S(2)}, u32[]{:S(2)}) collective-permute-start(f32[64,1]{1,0:T(8,128)S(1)} %get-tuple-element.37), channel_id=1, source_target_pairs={{0,4},{4,0},{8,12},{12,8},{1,5},{5,1},{9,13},{13,9},{2,6},{6,2},{1... | collective-permute-start | bytes 776 | tf_op jit(solution)/shard_map/ppermute | solution.py:17
  81.0 9.3 %collective-permute-start.11 = (bf16[1,64,2048]{2,1,0:T(8,128)(2,1)S(1)}, bf16[1,64,2048]{2,1,0:T(8,128)(2,1)S(1)}, u32[]{:S(2)}, u32[]{:S(2)}) collective-permute-start(bf16[1,64,2048]{2,1,0:T(8,128)(2,1)S(1)} %add_convert_fusion), channel_id=1, source_target_pairs={{0,8},{4,12},{8,0},{12,4},{1,9},{5,13},{9,1},{13,5},{2,10},{6,14},... | collective-permute-start | bytes 786440 | tf_op jit(solution)/shard_map/ppermute | solution.py:17
  81.2 8.8 %collective-permute-start.13 = (f32[64,1]{1,0:T(8,128)S(1)}, f32[64,1]{1,0:T(8,128)S(1)}, u32[]{:S(2)}, u32[]{:S(2)}) collective-permute-start(f32[64,1]{1,0:T(8,128)S(1)} %add.65), channel_id=1, source_target_pairs={{0,8},{4,12},{8,0},{12,4},{1,9},{5,13},{9,1},{13,5},{2,10},{6,14},... | collective-permute-start | bytes 776 | tf_op jit(solution)/shard_map/ppermute | solution.py:17
  83.4 7.0 %copy-start.10 = (bf16[32,2,2048]{2,1,0:T(2,128)(2,1)S(1)}, bf16[32,2,2048]{2,1,0:T(2,128)(2,1)}, u32[]{:S(2)}) copy-start(bf16[32,2,2048]{2,1,0:T(2,128)(2,1)} %param.18) | copy-start | bytes 786436
  (1 other events, 1.9 us)

commit v4 on v3

--- a/solution.py
+++ b/solution.py
@@ -8,6 +8,7 @@
 from jax.sharding import PartitionSpec as P
 
 BF16 = jnp.bfloat16
+EPSILON = 1e-05
 F32 = jnp.float32
 VMEM_GRANT = 12 * 1024 * 1024
 
@@ -34,15 +35,17 @@
     return result
 
 
-def gather_relative(block, axis, beside):
+def gather_relative(parts, axis, beside):
     distances = list(reversed(bits_of(lax.axis_size(axis))))
-    blocks, order = [block, swap(block, axis, distances[0])], [0, distances[0]]
-    extra = beside(block)
-    own = extra[0]
+    blocks = [(0, p, part) for p, part in enumerate(parts)]
+    blocks += [(distances[0], p, swap(part, axis, distances[0])) for _, p, part in blocks]
+    passed, *extra = beside(parts[0])
     for distance in distances[1:]:
-        blocks = blocks + [swap(b, axis, distance) for b in [own] + blocks[1:]]
-        order = order + [i ^ distance for i in order]
-    return blocks, order, extra[1:]
+        blocks += [
+            (i ^ distance, p, swap(passed if (i, p) == (0, 0) else part, axis, distance))
+            for i, p, part in blocks
+        ]
+    return [part for _, _, part in blocks], [(i, p) for i, p, _ in blocks], extra
 
 
 def params(**more):
@@ -75,8 +78,8 @@
 
 
 def load(after, passed, *weights):
-    arrays = (passed, *weights)
-    pieces = [1] + [8 if w.shape[0] % 128 == 0 else 1 for w in weights]
+    arrays = (*passed, *weights)
+    pieces = [1] * len(passed) + [8 if w.shape[0] % 128 == 0 else 1 for w in weights]
     size = sum(a.size * a.dtype.itemsize for a in arrays)
     return pl.pallas_call(
         functools.partial(load_body, pieces),
@@ -87,7 +90,75 @@
         compiler_params=params(),
         cost_estimate=cost(0, 2 * size),
         name="load",
-    )(after, passed, *[in_hbm(w) for w in weights])
+    )(after, *passed, *[in_hbm(w) for w in weights])
+
+
+def own_columns(rows, streams, rank):
+    row = lax.broadcasted_iota(jnp.int32, (rows, streams * rank), 0) % streams
+    return row == lax.broadcasted_iota(jnp.int32, (rows, streams * rank), 1) // rank
+
+
+def adapt_body(tenant_ref, scaled_ref, squares_ref, down_ref, up_ref, sums_ref, up_rows_ref, *scratch):
+    down_rows_ref, semaphores = scratch
+    rank = down_ref.shape[1]
+    streams = tenant_ref.shape[0]
+    rows = scaled_ref.shape[0]
+    downs, ups = [], []
+    for s in range(streams):
+        at = pl.ds(s * rank, rank)
+        tenant = tenant_ref[s]
+        downs.append(
+            pltpu.make_async_copy(down_ref.at[tenant], down_rows_ref.at[at, :], semaphores.at[s])
+        )
+        ups.append(
+            pltpu.make_async_copy(
+                up_ref.at[tenant], up_rows_ref.at[at, :], semaphores.at[streams + s]
+            )
+        )
+    for copy in downs + ups:
+        copy.start()
+    for copy in downs:
+        copy.wait()
+    every = lax.dot_general(
+        scaled_ref[...],
+        down_rows_ref[...],
+        (((1,), (1,)), ((), ())),
+        preferred_element_type=F32,
+    )
+    own = jnp.where(own_columns(rows, streams, rank), every, 0.0)
+    fold = lax.broadcasted_iota(jnp.int32, (streams * rank, rank), 0) % rank
+    fold = (fold == lax.broadcasted_iota(jnp.int32, (streams * rank, rank), 1)).astype(BF16)
+    high, rest = split(own)
+    middle, low = rest, (own - high.astype(F32) - rest.astype(F32)).astype(BF16)
+    folded = sum(jnp.dot(x, fold, preferred_element_type=F32) for x in (high, middle, low))
+    sums_ref[:, :rank] = folded
+    sums_ref[:, rank:] = squares_ref[...]
+    for copy in ups:
+        copy.wait()
+
+
+def adapt(tenants, scaled, squares, down, up):
+    streams = tenants.shape[0]
+    rows, depth = scaled.shape
+    rank, inner = up.shape[1:]
+    whole = pl.BlockSpec(memory_space=pltpu.VMEM)
+    anywhere = pl.BlockSpec(memory_space=pl.ANY)
+    return pl.pallas_call(
+        adapt_body,
+        out_shape=(
+            jax.ShapeDtypeStruct((rows, rank + 1), F32),
+            pltpu.VMEM((streams * rank, inner), BF16),
+        ),
+        in_specs=[pl.BlockSpec(memory_space=pltpu.SMEM), whole, whole, anywhere, anywhere],
+        out_specs=(whole, whole),
+        scratch_shapes=[
+            pltpu.VMEM((streams * rank, depth), BF16),
+            pltpu.SemaphoreType.DMA((2 * streams,)),
+        ],
+        compiler_params=params(),
+        cost_estimate=cost(2 * rows * depth * streams * rank, 2 * streams * rank * (depth + inner)),
+        name="adapt",
+    )(tenants, scaled, squares, in_hbm(jnp.swapaxes(down, 1, 2)), in_hbm(up))
 
 
 def fill_rows(index_ref, blocks, lhs, semaphores):
@@ -113,7 +184,8 @@
 
 def project_signal_body(count, index_ref, *refs):
     blocks, refs = refs[:count], refs[count:]
-    weight_ref, mix_ref, step_ref, send_ref, keep_ref, lhs_ref, semaphores = refs
+    weight_ref, mix_ref, step_ref, sums_ref, send_ref, keep_ref, lhs_ref, out_ref, semaphores = refs
+    out_ref[...] = sums_ref[...]
     fill_rows(index_ref, blocks, lhs_ref, semaphores)
     lhs = lhs_ref[...]
     columns = weight_ref.shape[1]
@@ -127,84 +199,62 @@
     put_parts(acc, columns + mix_ref.shape[1], send_ref, keep_ref)
 
 
-def project_signal(index, blocks, weight, mix, step):
-    count = len(blocks)
-    rows, depth = blocks[0].shape
+def project_signal(index, blocks, owners, weight, mix, step, sums):
+    pieces = len(blocks)
+    depth = blocks[0].shape[1]
+    count, rows = owners, pieces * blocks[0].shape[0] // owners
     columns = weight.shape[1] + mix.shape[1] + step.shape[0]
     half = jax.ShapeDtypeStruct((count // 2, rows, columns), BF16)
     whole = pl.BlockSpec(memory_space=pltpu.VMEM)
     return pl.pallas_call(
-        functools.partial(project_signal_body, count),
-        out_shape=(half, half, jax.ShapeDtypeStruct((count * rows, depth), BF16)),
+        functools.partial(project_signal_body, pieces),
+        out_shape=(
+            half,
+            half,
+            jax.ShapeDtypeStruct((count * rows, depth), BF16),
+            jax.ShapeDtypeStruct(sums.shape, sums.dtype),
+        ),
         in_specs=[pl.BlockSpec(memory_space=pltpu.SMEM)]
-        + [pl.BlockSpec(memory_space=pl.ANY)] * count
-        + [whole] * 3,
-        out_specs=(whole,) * 3,
-        scratch_shapes=[pltpu.SemaphoreType.DMA((count,))],
+        + [pl.BlockSpec(memory_space=pl.ANY)] * pieces
+        + [whole] * 4,
+        out_specs=(whole,) * 4,
+        scratch_shapes=[pltpu.SemaphoreType.DMA((pieces,))],
         compiler_params=params(),
         cost_estimate=cost(2 * count * rows * depth * columns, 2 * depth * columns),
         name="project_signal",
-    )(index, *blocks, weight, mix, step)
-
-
-def project_gate_body(lhs_ref, weight_ref, sums_ref, after_ref, send_ref, keep_ref, out_ref):
+    )(index, *blocks, weight, mix, step, sums)
+
+
+def project_gate_body(lhs_ref, weight_ref, after_ref, send_ref, keep_ref):
     columns = weight_ref.shape[1]
     tile = min(columns, 512)
     for t in range(0, columns, tile):
         acc = jnp.dot(lhs_ref[...], weight_ref[:, t : t + tile], preferred_element_type=F32)
         put_parts(acc, t, send_ref, keep_ref)
-    out_ref[...] = sums_ref[...]
-
-
-def project_gate(rows, lhs, weight, sums, after):
+
+
+def project_gate(rows, lhs, weight, after):
     count = lhs.shape[0] // rows
     columns = weight.shape[1]
     half = jax.ShapeDtypeStruct((count // 2, rows, columns), BF16)
     whole = pl.BlockSpec(memory_space=pltpu.VMEM)
     return pl.pallas_call(
         project_gate_body,
-        out_shape=(half, half, jax.ShapeDtypeStruct(sums.shape, sums.dtype)),
-        in_specs=[whole, whole, whole, pl.BlockSpec(memory_space=pl.ANY)],
-        out_specs=(whole,) * 3,
+        out_shape=(half, half),
+        in_specs=[whole, whole, pl.BlockSpec(memory_space=pl.ANY)],
+        out_specs=(whole,) * 2,
         compiler_params=params(),
         cost_estimate=cost(2 * lhs.size * columns, 2 * weight.size),
         name="project_gate",
-    )(lhs, weight, sums, after)
-
-
-def merge_body(terms, *refs):
-    out_ref = refs[-1]
-    for i in range(out_ref.shape[0]):
-        total = sum(t[2 * i + 1].astype(F32) for t in refs[:terms])
-        out_ref[i] = total.astype(out_ref.dtype)
-
-
-def merge(terms, after):
-    count, rows, columns = terms[0].shape
-    whole = pl.BlockSpec(memory_space=pltpu.VMEM)
-    return pl.pallas_call(
-        functools.partial(merge_body, len(terms)),
-        out_shape=jax.ShapeDtypeStruct((count // 2, rows, columns), BF16),
-        in_specs=[whole] * len(terms) + [pl.BlockSpec(memory_space=pl.ANY)],
-        out_specs=whole,
-        compiler_params=params(),
-        cost_estimate=cost(terms[0].size, 4 * terms[0].size),
-        name="merge",
-    )(*terms, after)
-
-
-def scatter_rows(send, keep, axis, after=None):
-    terms = [keep]
-    for distance in bits_of(lax.axis_size(axis)):
-        other = swap(send, axis, distance)
-        now = [other] + terms
-        if other.shape[0] == 1:
-            return [t[0] for t in now], send
-        if after is None:
-            send = sum(t[1::2].astype(F32) for t in now).astype(BF16)
-        else:
-            send = merge(now, after)
-        terms = [t[0::2] for t in now]
+    )(lhs, weight, after)
+
+
+def scatter_rows(received, keep, axis, done=1):
+    send = received
+    terms = [received] + (keep if isinstance(keep, list) else [keep])
+    for distance in bits_of(lax.axis_size(axis))[done:]:
+        send = sum(t[1::2].astype(F32) for t in terms).astype(BF16)
+        terms = [swap(send, axis, distance)] + [t[0::2] for t in terms]
     return [t[0] for t in terms], send
 
 
@@ -214,17 +264,22 @@
 
 def silu(values):
     return values / (1.0 + jnp.exp(-values))
+
+
+def inverse_of(sums_ref, width):
+    return lax.rsqrt(sums_ref[:, sums_ref.shape[1] - 1 :] / width + EPSILON)
 
 
 def recur_body(
     terms,
     group,
+    model_width,
     live_ref,
     *refs,
 ):
     term_refs = refs[:terms]
-    inverse_ref, adapted_ref, bias_ref, rate_ref, skip_ref, source_ref = refs[terms : terms + 6]
-    result_ref, feeds_ref, b_ref, both_ref, state_ref, *scratch = refs[terms + 6 :]
+    sums_ref, up_ref, bias_ref, rate_ref, skip_ref, source_ref, _ = refs[terms : terms + 7]
+    result_ref, feeds_ref, b_ref, both_ref, state_ref, *scratch = refs[terms + 7 :]
     c_ref, read_ref, spread_ref, signal_ref, semaphores = scratch
     heads, head, width = state_ref.shape[1:]
     streams, inner = feeds_ref.shape[1:]
@@ -238,8 +293,17 @@
     def _():
         for i in range(streams // group):
             fetch(i).start()
-        total = sum(t[...].astype(F32) for t in term_refs) * inverse_ref[...]
-        signal_ref[...] = silu(total[:, :inner] + adapted_ref[...])
+        rows = sums_ref.shape[0]
+        rank = sums_ref.shape[1] - 1
+        inverse = inverse_of(sums_ref, model_width)
+        lowrank = (sums_ref[:, :rank] * inverse).astype(BF16)
+        repeat = lax.broadcasted_iota(jnp.int32, (rank, streams * rank), 1) % rank
+        repeat = (repeat == lax.broadcasted_iota(jnp.int32, (rank, streams * rank), 0)).astype(BF16)
+        every = jnp.dot(lowrank, repeat, preferred_element_type=F32)
+        own = jnp.where(own_columns(rows, streams, rank), every, 0.0).astype(BF16)
+        adapted = jnp.dot(own, up_ref[...], preferred_element_type=F32)
+        total = sum(t[...].astype(F32) for t in term_refs) * inverse
+        signal_ref[...] = silu(total[:, :inner] + adapted)
         gates = silu(total[:, inner : inner + 2 * width])
         steps_dt = softplus(total[:, inner + 2 * width :] + bias_ref[...])
         b = [gates[p * streams : (p + 1) * streams, :width] for p in range(2)]
@@ -301,14 +365,14 @@
         feeds_ref[1] = factor[6] * second
 
 
-def recur(live_rows, terms, inverse, adapted, bias, rate, skip, state):
+def recur(model_width, after, live_rows, terms, sums, up_rows, bias, rate, skip, state):
     streams, heads, head, width = state.shape
     group = 8
     inner = heads * head
     rows = 2 * streams
     whole = pl.BlockSpec(memory_space=pltpu.VMEM)
     return pl.pallas_call(
-        functools.partial(recur_body, len(terms), group),
+        functools.partial(recur_body, len(terms), group, model_width),
         out_shape=(
             jax.ShapeDtypeStruct((rows, inner), F32),
             jax.ShapeDtypeStruct((2, streams, inner), F32),
@@ -319,7 +383,7 @@
         grid=(streams // group,),
         in_specs=[pl.BlockSpec(memory_space=pltpu.SMEM)]
         + [whole] * (len(terms) + 5)
-        + [pl.BlockSpec(memory_space=pl.ANY)],
+        + [pl.BlockSpec(memory_space=pl.ANY)] * 2,
         out_specs=(whole,) * 5,
         scratch_shapes=[
             pltpu.VMEM((2, streams, width), F32),
@@ -334,12 +398,13 @@
     )(
         live_rows,
         *terms,
-        inverse,
-        adapted,
+        sums,
+        up_rows,
         bias[None],
         rate[None],
         skip[None],
         in_hbm(state),
+        after,
     )
 
 
@@ -386,34 +451,44 @@
             out_ref[j, :, t : t + tile] = acc.astype(out_ref.dtype)
 
 
-def output_first_body(terms, index_ref, *refs):
+def output_first_body(terms, model_width, index_ref, *refs):
     term_refs = refs[:terms]
-    inverse_ref, result_ref, scale_ref, weight_ref, out_ref, lhs_ref, squares_ref = refs[terms:]
-    total = sum(t[...].astype(F32) for t in term_refs) * inverse_ref[...]
+    sums_ref, result_ref, scale_ref, weight_ref, out_ref, lhs_ref, squares_ref = refs[terms:]
+    total = sum(t[...].astype(F32) for t in term_refs) * inverse_of(sums_ref, model_width)
     gated = result_ref[...] * silu(total)
     squares_ref[...] = jnp.sum(gated * gated, -1, keepdims=True)
     lhs_ref[...] = (gated * scale_ref[...]).astype(lhs_ref.dtype)
     output_tiles(index_ref, lhs_ref, weight_ref, out_ref)
 
 
-def output_parts(index, weight, width, operands, first):
+def output_rest_body(index_ref, lhs_ref, after_ref, weight_ref, out_ref):
+    output_tiles(index_ref, lhs_ref, weight_ref, out_ref)
+
+
+def output_parts(index, weight, width, operands, model_width=None):
+    first = model_width is not None
     rows, depth = operands[0].shape
     count = index.shape[0]
     whole = pl.BlockSpec(memory_space=pltpu.VMEM)
+    specs = [whole] * (len(operands) + 1)
+    body = output_rest_body
     out_shape = [jax.ShapeDtypeStruct((count, rows, width), BF16)]
     if first:
+        body = functools.partial(output_first_body, len(operands) - 3, model_width)
         out_shape += [
             jax.ShapeDtypeStruct((rows, depth), BF16),
             jax.ShapeDtypeStruct((rows, 1), F32),
         ]
+    else:
+        specs[1] = pl.BlockSpec(memory_space=pl.ANY)
     return pl.pallas_call(
-        functools.partial(output_first_body, len(operands) - 3) if first else output_tiles,
+        body,
         out_shape=tuple(out_shape),
-        in_specs=[pl.BlockSpec(memory_space=pltpu.SMEM)] + [whole] * (len(operands) + 1),
+        in_specs=[pl.BlockSpec(memory_space=pltpu.SMEM)] + specs,
         out_specs=(whole,) * len(out_shape),
         compiler_params=params(),
         cost_estimate=cost(2 * rows * depth * width * count, 2 * depth * width * count),
-        name="output_first" if first else "output_second",
+        name="output_first" if first else "output_rest",
     )(index, *operands, weight)
 
 
@@ -440,7 +515,6 @@
     stream_tenant_index,
     live_block_rows,
 ):
-    epsilon = 1e-05
     streams, positions, feature_width = hidden.shape
     rows = streams * positions
     heads_n = lax.axis_size("head")
@@ -448,7 +522,6 @@
     model_width = feature_width * heads_n
     depth, inner = projection_signal.shape
     inner_width = inner * heads_n
-    heads_here = projection_step.shape[1]
     head_at = lax.axis_index("head")
     row_at = lax.axis_index("row")
 
@@ -456,57 +529,51 @@
     scaled = (wide * input_norm_scale).astype(BF16)
     scaled_flat = scaled.reshape(rows, feature_width)
 
+    tenant_local = stream_tenant_index - row_at * adapter_down_weight.shape[0]
+    squares = jnp.sum(wide * wide, -1).reshape(rows, 1)
+    sums, up_rows = adapt(tenant_local, scaled_flat, squares, adapter_down_weight, adapter_up_weight)
+
     in_weights = (projection_signal, projection_input_output, projection_gate)
     if heads_n == rows_n:
-        turned = lax.ppermute(
-            scaled_flat,
-            ("head", "row"),
-            [
-                (h * rows_n + r, reverse_bits(r, rows_n) * rows_n + h)
-                for h in range(heads_n)
-                for r in range(rows_n)
-            ],
-        )
+        turn = [
+            (h * rows_n + r, reverse_bits(r, rows_n) * rows_n + h)
+            for h in range(heads_n)
+            for r in range(rows_n)
+        ]
         blocks, order, weights = gather_relative(
-            turned, "head", lambda block: load(block, block, *in_weights)
+            [lax.ppermute(scaled[p], ("head", "row"), turn) for p in range(positions)],
+            "head",
+            lambda block: load(sums, [block], *in_weights),
         )
         owner = jnp.asarray([reverse_bits(i, rows_n) for i in range(rows_n)], jnp.int32)
-        index = owner[head_at ^ jnp.asarray(order, jnp.int32)] ^ row_at
+        owner = owner[head_at ^ jnp.asarray([i for i, _ in order], jnp.int32)] ^ row_at
+        index = owner * positions + jnp.asarray([p for _, p in order], jnp.int32)
     else:
         features = lax.all_gather(scaled_flat, "head", axis=1, tiled=True)
         blocks = lax.all_to_all(features, "row", split_axis=1, concat_axis=0, tiled=True)
         blocks = blocks.reshape(rows_n, rows, depth)
         blocks = [blocks[i] for i in range(rows_n)]
-        weights = load(scaled_flat, scaled_flat, *in_weights)[1:]
+        weights = load(sums, [scaled_flat], *in_weights)[1:]
         index = jnp.arange(rows_n, dtype=jnp.int32) ^ row_at
 
-    tenant_local = stream_tenant_index - row_at * adapter_down_weight.shape[0]
-    down_weight_rows = jnp.take(adapter_down_weight, tenant_local, axis=0)
-    square_part = jnp.sum(wide * wide, -1)
-    lowrank_part = jnp.einsum(
-        "psd,sdr->psr", scaled, down_weight_rows, preferred_element_type=F32
+    signal_weight, mix_weight, gate_weight = weights
+    send, keep, lhs, sums = project_signal(
+        index, blocks, rows_n, signal_weight, mix_weight, projection_step.T, sums
     )
-    sums = jnp.concatenate([lowrank_part, square_part[..., None]], -1).reshape(rows, -1)
-
-    signal_weight, mix_weight, gate_weight = weights
-    send, keep, lhs = project_signal(
-        index, blocks, signal_weight, mix_weight, projection_step.T
-    )
-    gate_send, gate_keep, sums = project_gate(rows, lhs, gate_weight, sums, send)
-    keep, out_weight = load(gate_send, keep, output_weight)
-    signal_terms, last_send = scatter_rows(send, keep, "row")
-    gate_terms, _ = scatter_rows(gate_send, gate_keep, "row", after=last_send)
+    received = swap(send, "row", 1)
+    keep, out_weight = load(send, [keep], output_weight)
+    gate_send, gate_keep = project_gate(rows, lhs, gate_weight, received)
+    signal_terms, _ = scatter_rows(received, keep, "row")
+    gate_terms, gate_last = scatter_rows(swap(gate_send, "row", 1), gate_keep, "row")
     sums = sum_over(sums, "head")
-    inverse = lax.rsqrt(sums[:, -1:] / model_width + epsilon)
-    lowrank = (sums[:, :-1] * inverse).astype(BF16).reshape(positions, streams, -1)
-    up_weight_rows = jnp.take(adapter_up_weight, tenant_local, axis=0)
-    adapted = jnp.einsum("psr,srk->psk", lowrank, up_weight_rows, preferred_element_type=F32)
 
     result, feeds, bgate, both, state = recur(
+        model_width,
+        gate_last,
         live_block_rows,
         signal_terms,
-        inverse,
-        adapted.reshape(rows, inner),
+        sums,
+        up_rows,
         step_bias,
         head_decay_rate,
         head_skip_weight,
@@ -514,17 +581,23 @@
     )
 
     distances = jnp.arange(heads_n, dtype=jnp.int32) ^ head_at
-    odd, out_lhs, gate_squares = output_parts(
-        distances[1::2],
+    first, out_lhs, gate_squares = output_parts(
+        distances[3::4],
         out_weight,
         feature_width,
-        [*gate_terms, inverse, result, gated_norm_scale[None]],
-        True,
+        [*gate_terms, sums, result, gated_norm_scale[None]],
+        model_width,
     )
-    (even,) = output_parts(distances[0::2], out_weight, feature_width, [out_lhs], False)
+    (second,) = output_parts(distances[2::4], out_weight, feature_width, [out_lhs, first])
+    send = (swap(first, "head", 1).astype(F32) + second.astype(F32)).astype(BF16)
+    near = jnp.concatenate([distances[1::4], distances[0::4]])
+    (rest,) = output_parts(near, out_weight, feature_width, [out_lhs, send])
+    half = rest.shape[0] // 2
+    kept = [swap(rest[:half], "head", 1), rest[half:]]
+    mixer, _ = scatter_rows(swap(send, "head", 2), kept, "head", done=2)
+    mixer = sum(t.astype(F32) for t in mixer)
     gate_squares = sum_over(gate_squares, "head")
-    mixer = sum(t.astype(F32) for t in scatter_rows(odd, even, "head")[0])
-    mixer = mixer * lax.rsqrt(gate_squares / inner_width + epsilon)
+    mixer = mixer * lax.rsqrt(gate_squares / inner_width + EPSILON)
     mixer = mixer.reshape(positions, streams, feature_width)
     live = jnp.arange(streams) < live_block_rows[0]
     mixed = (wide + jnp.where(live[:, None], mixer, 0.0)).astype(BF16)

time: 92 us -> 87.1 us (0.947)
  local copies, waits for them, and re-layouts: 15.1 us -> 3.67 us
  Pallas kernels: 29.3 us -> 35.6 us
  starting transfers between devices: 21.9 us -> 27.7 us
  waiting for transfers between devices: 16.9 us -> 12.4 us
  matrix products: 1.34 us -> 0 us
    gather x3 -> x1, local copies, waits for them, and re-layouts: 7.5 us -> 1.29 us  [on_device(): owner[head_at ^ jnp.asarray([i for i, _ in order], jnp.int32)] ^ row_at]
    pallas_call x6 -> x7, Pallas kernels: 13 us -> 19.2 us  [the longest x3 5.21 us: output_parts(): pl.pallas_call(body, out_shape=tuple(out_shape), in_specs=[pl.BlockSpec(m...]
    ppermute x13 -> x17, starting transfers between devices: 21.2 us -> 26.4 us  [swap(): return lax.ppermute(values, axis, [(i, i ^ distance) for i in range(size)])]
    unnamed x22 -> x13, local copies, waits for them, and re-layouts: 6.18 us -> 1 us
    ppermute x13 -> x17, waiting for transfers between devices: 16.9 us -> 12.4 us  [swap(): return lax.ppermute(values, axis, [(i, i ^ distance) for i in range(size)])]
    concatenate x1, other arithmetic: 0.01 us -> 1.41 us  [on_device(): near = jnp.concatenate([distances[1::4], distances[0::4]])]
    dot_general x2 -> x0, matrix products: 1.34 us -> none  [the longest x1 0.98 us: on_device(): jnp.einsum('psd,sdr->psr', scaled, down_weight_rows, preferred_element_ty...]
    transpose x1, other arithmetic: 1.36 us -> 0.16 us  [on_device(): return (jnp.swapaxes(mixed, 0, 1), new_state)]
  transfers between devices with their start and end apart: 14 -> 19, of which waited for: 4 -> 6; matrix products, arithmetic and copies ran while one was open for 14% -> 8% of each run, Pallas kernels for 27% -> 33%
where the time goes in v4:
time: 87.1 us; the launch traced here: 86.9 us
  Pallas kernels  35.6 us (41%)
  starting transfers between devices  27.7 us (32%)
  waiting for transfers between devices  12.4 us (14%)
  other arithmetic  5.83 us (7%)
  local copies, waits for them, and re-layouts  3.67 us (4%)
  between operations  1.61 us (2%)
    ppermute x17, starting transfers between devices, swap(): return lax.ppermute(values, axis, [(i, i ^ distance) for i in range(size)])  26.4 us
    ppermute x17, waiting for transfers between devices, swap(): return lax.ppermute(values, axis, [(i, i ^ distance) for i in range(size)])  12.4 us
    pallas_call x2, Pallas kernels, load(): pl.pallas_call(functools.partial(load_body, pieces), out_shape=tuple((plt...  10.1 us
    pallas_call x1, Pallas kernels, state_write(): pl.pallas_call(state_write_body, out_shape=jax.ShapeDtypeStruct(state.sha...  6.34 us
    pallas_call x3, Pallas kernels, output_parts(): pl.pallas_call(body, out_shape=tuple(out_shape), in_specs=[pl.BlockSpec(m...  5.21 us
    pallas_call x1, Pallas kernels, recur(): pl.pallas_call(functools.partial(recur_body, len(terms), group, model_wid...  4.84 us
    pallas_call x1, Pallas kernels, project_signal(): pl.pallas_call(functools.partial(project_signal_body, pieces), out_shape=...  3.93 us
    pallas_call x1, Pallas kernels, adapt(): pl.pallas_call(adapt_body, out_shape=(jax.ShapeDtypeStruct((rows, rank +...  3.89 us
  transfers between devices with their start and end apart: 19, of which 6 were waited for; matrix products, arithmetic and copies ran while one was open for 8% of the time, Pallas kernels for 33%

profile of v4, /device:TPU:0, one launch (start us, length us, event | category | flops | bytes accessed | tf_op | source)
XLA Modules:
  0.0 86.9 jit_solution(8103214773836166135)
XLA Ops:
  0.6 1.1 %fusion.1 = (f32[2,32]{1,0:T(2,128)S(1)}, bf16[2,32,2048]{2,1,0:T(8,128)(2,1)S(1)}) fusion(bf16[32,2,2048]{2,1,0:T(2,128)(2,1)} %param.19, f32[2048]{0:T(1024)} %param.20), kind=kLoop, calls=%fused_computation.6 | loop fusion | flops 655296 | bytes 532736 | tf_op jit(solution)/shard_map/reduce_sum | solution.py:533
  3.8 1.3 %gather_fusion = s32[8]{0:T(128)S(1)} fusion(s32[4]{0:T(128)} %constant.31.clone, s32[1024]{0:T(1024)S(1)} %pad_clamp_fusion), kind=kCustom, calls=%fused_computation | custom fusion | bytes 96 | tf_op jit(solution)/shard_map/gather | solution.py:549
  5.8 8.0 %collective-permute-start.2 = (bf16[32,2048]{1,0:T(8,128)(2,1)S(1)}, bf16[32,2048]{1,0:T(8,128)(2,1)S(1)}, u32[]{:S(2)}, u32[]{:S(2)}) collective-permute-start(bf16[32,2048]{1,0:T(8,128)(2,1)S(1)} %collective-permute-done.refs_0_), channel_id=1, source_target_pairs={{0,8},{4,12},{8,0},{12,4},{1,9},{5,13},{9,1},{13,5},{2,10},{6,14},... | collective-permute-start | bytes 393224 | tf_op jit(solution)/shard_map/ppermute | solution.py:18
  13.8 3.8 %collective-permute-start.3 = (bf16[32,2048]{1,0:T(8,128)(2,1)S(1)}, bf16[32,2048]{1,0:T(8,128)(2,1)S(1)}, u32[]{:S(2)}, u32[]{:S(2)}) collective-permute-start(bf16[32,2048]{1,0:T(8,128)(2,1)S(1)} %collective-permute-done.1.refs_1_), channel_id=1, source_target_pairs={{0,8},{4,12},{8,0},{12,4},{1,9},{5,13},{9,1},{13,5},{2,10},{6,14},... | collective-permute-start | bytes 393224 | tf_op jit(solution)/shard_map/ppermute | solution.py:18
  19.0 3.9 %adapt.1 = (f32[64,17]{1,0:T(8,128)S(1)}, bf16[512,1024]{1,0:T(8,128)(2,1)S(1)}) custom-call(s32[32]{0:T(128)S(1)} %broadcast_subtract_fusion.tenant_ref, bf16[64,2048]{1,0:T(8,128)(2,1)S(1)} %bitcast.54, f32[64,1]{1,0:T(8,128)S(1)} %reshape.37.squares_ref, bf16[128,16,2048]{2,1,0:T(8,128)(2,1)} %bitcast.62, bf16[128,16,1024]{2,1,0:T(8,128)(2,1)} %up_ref.1), custom_call_target="tpu_custom_call" | custom-call | flops 134217728 | bytes 3145728 | tf_op jit(solution)/shard_map/adapt/pallas_call | solution.py:146
  22.9 4.1 %load.2 = (bf16[32,2048]{1,0:T(8,128)(2,1)S(1)}, bf16[2048,1024]{1,0:T(8,128)(2,1)S(1)}, bf16[2048,256]{1,0:T(8,128)(2,1)S(1)}, bf16[2048,1024]{1,0:T(8,128)(2,1)S(1)}) custom-call(f32[64,17]{1,0:T(8,128)S(1)} %get-tuple-element.24.after_ref.refs_11_, bf16[32,2048]{1,0:T(8,128)(2,1)S(1)} %collective-permute-done.refs_0_, bf16[2048,1024]{1,0:T(8,128)(2,1)} %refs_1_.2, ...), custom_call_target="tpu_custom_call" | custom-call | bytes 19136512 | tf_op jit(solution)/shard_map/load/pallas_call | solution.py:84
  27.0 2.1 %collective-permute-start.4 = (bf16[32,2048]{1,0:T(8,128)(2,1)S(1)}, bf16[32,2048]{1,0:T(8,128)(2,1)S(1)}, u32[]{:S(2)}, u32[]{:S(2)}) collective-permute-start(bf16[32,2048]{1,0:T(8,128)(2,1)S(1)} %get-tuple-element.25), channel_id=1, source_target_pairs={{0,4},{4,0},{8,12},{12,8},{1,5},{5,1},{9,13},{13,9},{2,6},{6,2},{1... | collective-permute-start | bytes 393224 | tf_op jit(solution)/shard_map/ppermute | solution.py:18
  31.0 3.9 %project_signal.1 = (bf16[2,64,1296]{2,1,0:T(8,128)(2,1)S(1)}, bf16[2,64,1296]{2,1,0:T(8,128)(2,1)S(1)}, bf16[256,2048]{1,0:T(8,128)(2,1)S(1)}, f32[64,17]{1,0:T(8,128)S(1)}) custom-call(s32[8]{0:T(128)S(1)} %multiply_add_fusion.index_ref, bf16[32,2048]{1,0:T(8,128)(2,1)S(1)} %collective-permute-done.refs_0_, ...), custom_call_target="tpu_custom_call" | custom-call | flops 1358954496 | bytes 5308416 | tf_op jit(solution)/shard_map/project_signal/pallas_call | solution.py:209
  35.2 1.4 %pad_add_fusion.index_ref = s32[2]{0:T(128)S(1)} fusion(s32[1]{0:T(128)} %get-tuple-element.55, s32[1]{0:T(128)} %get-tuple-element.56), kind=kLoop, calls=%fused_computation.29 | loop fusion | flops 2 | bytes 16 | tf_op jit(solution)/shard_map/concatenate | solution.py:593
  36.7 2.3 %collective-permute-start.8 = (bf16[2,64,1296]{2,1,0:T(8,128)(2,1)S(1)}, bf16[2,64,1296]{2,1,0:T(8,128)(2,1)S(1)}, u32[]{:S(2)}, u32[]{:S(2)}) collective-permute-start(bf16[2,64,1296]{2,1,0:T(8,128)(2,1)S(1)} %get-tuple-element.30.after_ref), channel_id=1, source_target_pairs={{0,1},{1,0},{2,3},{3,2},{4,5},{5,4},{6,7},{7,6},{8,9},{9,8},{10,11... | collective-permute-start | bytes 995336 | tf_op jit(solution)/shard_map/ppermute | solution.py:18
  39.0 6.1 %load.3 = (bf16[2,64,1296]{2,1,0:T(8,128)(2,1)S(1)}, bf16[1024,8192]{1,0:T(8,128)(2,1)S(1)}) custom-call(bf16[2,64,1296]{2,1,0:T(8,128)(2,1)S(1)} %get-tuple-element.30.after_ref, bf16[2,64,1296]{2,1,0:T(8,128)(2,1)S(1)} %get-tuple-element.34.refs_0_, bf16[1024,8192]{1,0:T(8,128)(2,1)} %refs_1_.3), custom_call_target="tpu_custom_call" | custom-call | bytes 34217984 | tf_op jit(solution)/shard_map/load/pallas_call | solution.py:84
  45.3 3.7 %collective-permute-done.12 = f32[64,17]{1,0:T(8,128)S(1)} collective-permute-done((f32[64,17]{1,0:T(8,128)S(1)}, f32[64,17]{1,0:T(8,128)S(1)}, u32[]{:S(2)}, u32[]{:S(2)}) %collective-permute-start.12) | collective-permute-done | bytes 4384 | tf_op jit(solution)/shard_map/ppermute | solution.py:18
  49.1 1.3 %project_gate.1 = (bf16[2,64,1024]{2,1,0:T(8,128)(2,1)S(1)}, bf16[2,64,1024]{2,1,0:T(8,128)(2,1)S(1)}) custom-call(bf16[256,2048]{1,0:T(8,128)(2,1)S(1)} %get-tuple-element.28.lhs_ref, bf16[2048,1024]{1,0:T(8,128)(2,1)S(1)} %get-tuple-element.29.weight_ref, bf16[2,64,1296]{2,1,0:T(8,128)(2,1)S(1)} %collective-permute-done.8.after_ref), custom_call_target="tpu_custom_call" | custom-call | flops 1073741824 | bytes 4194304 | tf_op jit(solution)/shard_map/project_gate/pallas_call | solution.py:241
  50.9 3.9 %collective-permute-start.13 = (bf16[1,64,1296]{2,1,0:T(8,128)(2,1)S(1)}, bf16[1,64,1296]{2,1,0:T(8,128)(2,1)S(1)}, u32[]{:S(2)}, u32[]{:S(2)}) collective-permute-start(bf16[1,64,1296]{2,1,0:T(8,128)(2,1)S(1)} %add_convert_fusion.1), channel_id=1, source_target_pairs={{0,2},{1,3},{2,0},{3,1},{4,6},{5,7},{6,4},{7,5},{8,10},{9,11},{10,... | collective-permute-start | bytes 497672 | tf_op jit(solution)/shard_map/ppermute | solution.py:18
  54.8 6.5 %collective-permute-done.9 = bf16[2,64,1024]{2,1,0:T(8,128)(2,1)S(1)} collective-permute-done((bf16[2,64,1024]{2,1,0:T(8,128)(2,1)S(1)}, bf16[2,64,1024]{2,1,0:T(8,128)(2,1)S(1)}, u32[]{:S(2)}, u32[]{:S(2)}) %collective-permute-start.9) | collective-permute-done | bytes 262176 | tf_op jit(solution)/shard_map/ppermute | solution.py:18
  61.4 1.9 %collective-permute-start.10 = (bf16[1,64,1024]{2,1,0:T(8,128)(2,1)S(1)}, bf16[1,64,1024]{2,1,0:T(8,128)(2,1)S(1)}, u32[]{:S(2)}, u32[]{:S(2)}) collective-permute-start(bf16[1,64,1024]{2,1,0:T(8,128)(2,1)S(1)} %add_convert_fusion.2.refs_9_), channel_id=1, source_target_pairs={{0,2},{1,3},{2,0},{3,1},{4,6},{5,7},{6,4},{7,5},{8,10},{9,11},{10,... | collective-permute-start | bytes 393224 | tf_op jit(solution)/shard_map/ppermute | solution.py:18
  63.3 4.8 %recur.1 = (f32[64,1024]{1,0:T(8,128)S(1)}, f32[2,32,1024]{2,1,0:T(8,128)S(1)}, f32[2,32,128]{2,1,0:T(8,128)S(1)}, f32[32,16]{1,0:T(8,128)S(1)}, bf16[32,16,64,128]{3,2,1,0:T(8,128)(2,1)S(1)}) custom-call(s32[1]{0:T(128)} %copy.44.live_ref, bf16[64,1296]{1,0:T(8,128)(2,1)S(1)} %bitcast.55, bf16[64,1296]{1,0:T(8,128)(2,1)S(1)} %slice_bitcast_fusion.refs_1_, ...), custom_call_target="tpu_custom_call" | custom-call | flops 268435456 | bytes 10485760 | tf_op jit(solution)/shard_map/recur/pallas_call | solution.py:374
  68.7 1.5 %collective-permute-done.10 = bf16[1,64,1024]{2,1,0:T(8,128)(2,1)S(1)} collective-permute-done((bf16[1,64,1024]{2,1,0:T(8,128)(2,1)S(1)}, bf16[1,64,1024]{2,1,0:T(8,128)(2,1)S(1)}, u32[]{:S(2)}, u32[]{:S(2)}) %collective-permute-start.10) | collective-permute-done | bytes 131104 | tf_op jit(solution)/shard_map/ppermute | solution.py:18
  70.2 1.6 %output_first.1 = (bf16[1,64,2048]{2,1,0:T(8,128)(2,1)S(1)}, bf16[64,1024]{1,0:T(8,128)(2,1)S(1)}, f32[64,1]{1,0:T(8,128)S(1)}) custom-call(s32[1]{0:T(128)} %get-tuple-element.57.index_ref, bf16[64,1024]{1,0:T(8,128)(2,1)S(1)} %bitcast.56, bf16[64,1024]{1,0:T(8,128)(2,1)S(1)} %slice_bitcast_fusion.2.refs_1_, ...), custom_call_target="tpu_custom_call" | custom-call | flops 268435456 | bytes 4194304 | tf_op jit(solution)/shard_map/output_first/pallas_call | solution.py:484
  72.8 1.5 %output_rest.2 = bf16[1,64,2048]{2,1,0:T(8,128)(2,1)S(1)} custom-call(s32[1]{0:T(128)} %get-tuple-element.54.index_ref, bf16[64,1024]{1,0:T(8,128)(2,1)S(1)} %get-tuple-element.40.lhs_ref, bf16[1,64,2048]{2,1,0:T(8,128)(2,1)S(1)} %get-tuple-element.39.after_ref, bf16[1024,8192]{1,0:T(8,128)(2,1)S(1)} %get-tuple-element.38.refs_6_.weight_ref), custom_call_target="tpu_custom_call" | custom-call | flops 268435456 | bytes 4194304 | tf_op jit(solution)/shard_map/output_rest/pallas_call | solution.py:484
  74.7 2.1 %output_rest.3 = bf16[2,64,2048]{2,1,0:T(8,128)(2,1)S(1)} custom-call(s32[2]{0:T(128)S(1)} %pad_add_fusion.index_ref, bf16[64,1024]{1,0:T(8,128)(2,1)S(1)} %get-tuple-element.40.lhs_ref, bf16[1,64,2048]{2,1,0:T(8,128)(2,1)S(1)} %add_convert_fusion.after_ref, bf16[1024,8192]{1,0:T(8,128)(2,1)S(1)} %get-tuple-element.38.refs_6_.weight_ref), custom_call_target="tpu_custom_call" | custom-call | flops 536870912 | bytes 8388608 | tf_op jit(solution)/shard_map/output_rest/pallas_call | solution.py:484
  77.1 1.8 %collective-permute-start.18 = (f32[64,1]{1,0:T(8,128)S(1)}, f32[64,1]{1,0:T(8,128)S(1)}, u32[]{:S(2)}, u32[]{:S(2)}) collective-permute-start(f32[64,1]{1,0:T(8,128)S(1)} %add.58), channel_id=1, source_target_pairs={{0,8},{4,12},{8,0},{12,4},{1,9},{5,13},{9,1},{13,5},{2,10},{6,14},... | collective-permute-start | bytes 776 | tf_op jit(solution)/shard_map/ppermute | solution.py:18
  79.1 6.3 %state_write.1 = bf16[32,16,64,128]{3,2,1,0:T(8,128)(2,1)} custom-call(bf16[32,8,1024]{2,1,0:T(8,128)(2,1)S(1)} %maximum_maximum_fusion.left_ref, bf16[32,8,128]{2,1,0:T(8,128)(2,1)S(1)} %maximum_maximum_fusion.1.right_ref, f32[32,16,128]{2,1,0:T(8,128)S(1)} %broadcast_in_dim.50.decay_ref, bf16[32,16,64,128]{3,2,1,0:T(8,128)(2,1)S(1)} %get-tuple-element.45.state_ref), custom_call_target="tpu_custom_call" | custom-call | flops 134217728 | bytes 16777216 | tf_op jit(solution)/shard_map/state_write/pallas_call | solution.py:427
  85.9 1.0 %copy.30 = bf16[32,2,2048]{2,1,0:T(2,128)(2,1)} copy(bf16[32,2,2048]{2,0,1:T(8,128)(2,1)S(1)} %fusion.3) | data formatting | bytes 524288
  (73 shorter events, 9.2 us)
Async XLA Ops:
  1.8 4.0 %collective-permute-start = (bf16[32,2048]{1,0:T(8,128)(2,1)S(1)}, bf16[32,2048]{1,0:T(8,128)(2,1)S(1)}, u32[]{:S(2)}, u32[]{:S(2)}) collective-permute-start(bf16[32,2048]{1,0:T(8,128)(2,1)S(1)} %get-tuple-element.53), channel_id=1, source_target_pairs={{0,0},{1,8},{2,4},{3,12},{4,1},{5,9},{6,5},{7,13},{8,2},{9,10},{10... | collective-permute-start | bytes 393224 | tf_op jit(solution)/shard_map/ppermute | solution.py:544
  2.5 11.3 %collective-permute-start.1 = (bf16[32,2048]{1,0:T(8,128)(2,1)S(1)}, bf16[32,2048]{1,0:T(8,128)(2,1)S(1)}, u32[]{:S(2)}, u32[]{:S(2)}) collective-permute-start(bf16[32,2048]{1,0:T(8,128)(2,1)S(1)} %get-tuple-element.52), channel_id=1, source_target_pairs={{0,0},{1,8},{2,4},{3,12},{4,1},{5,9},{6,5},{7,13},{8,2},{9,10},{10... | collective-permute-start | bytes 393224 | tf_op jit(solution)/shard_map/ppermute | solution.py:544
  5.8 23.4 %collective-permute-start.2 = (bf16[32,2048]{1,0:T(8,128)(2,1)S(1)}, bf16[32,2048]{1,0:T(8,128)(2,1)S(1)}, u32[]{:S(2)}, u32[]{:S(2)}) collective-permute-start(bf16[32,2048]{1,0:T(8,128)(2,1)S(1)} %collective-permute-done.refs_0_), channel_id=1, source_target_pairs={{0,8},{4,12},{8,0},{12,4},{1,9},{5,13},{9,1},{13,5},{2,10},{6,14},... | collective-permute-start | bytes 393224 | tf_op jit(solution)/shard_map/ppermute | solution.py:18
  13.8 15.9 %collective-permute-start.3 = (bf16[32,2048]{1,0:T(8,128)(2,1)S(1)}, bf16[32,2048]{1,0:T(8,128)(2,1)S(1)}, u32[]{:S(2)}, u32[]{:S(2)}) collective-permute-start(bf16[32,2048]{1,0:T(8,128)(2,1)S(1)} %collective-permute-done.1.refs_1_), channel_id=1, source_target_pairs={{0,8},{4,12},{8,0},{12,4},{1,9},{5,13},{9,1},{13,5},{2,10},{6,14},... | collective-permute-start | bytes 393224 | tf_op jit(solution)/shard_map/ppermute | solution.py:18
  19.0 12.0 %copy-start = (bf16[2048,16]{0,1:T(8,128)(2,1)S(1)}, bf16[2048,16]{0,1:T(8,128)(2,1)}, u32[]{:S(2)}) copy-start(bf16[2048,16]{0,1:T(8,128)(2,1)} %param.23) | copy-start | bytes 196612
  27.0 3.4 %collective-permute-start.4 = (bf16[32,2048]{1,0:T(8,128)(2,1)S(1)}, bf16[32,2048]{1,0:T(8,128)(2,1)S(1)}, u32[]{:S(2)}, u32[]{:S(2)}) collective-permute-start(bf16[32,2048]{1,0:T(8,128)(2,1)S(1)} %get-tuple-element.25), channel_id=1, source_target_pairs={{0,4},{4,0},{8,12},{12,8},{1,5},{5,1},{9,13},{13,9},{2,6},{6,2},{1... | collective-permute-start | bytes 393224 | tf_op jit(solution)/shard_map/ppermute | solution.py:18
  29.1 1.3 %collective-permute-start.5 = (bf16[32,2048]{1,0:T(8,128)(2,1)S(1)}, bf16[32,2048]{1,0:T(8,128)(2,1)S(1)}, u32[]{:S(2)}, u32[]{:S(2)}) collective-permute-start(bf16[32,2048]{1,0:T(8,128)(2,1)S(1)} %collective-permute-done.1.refs_1_), channel_id=1, source_target_pairs={{0,4},{4,0},{8,12},{12,8},{1,5},{5,1},{9,13},{13,9},{2,6},{6,2},{1... | collective-permute-start | bytes 393224 | tf_op jit(solution)/shard_map/ppermute | solution.py:18
  29.2 1.5 %collective-permute-start.6 = (bf16[32,2048]{1,0:T(8,128)(2,1)S(1)}, bf16[32,2048]{1,0:T(8,128)(2,1)S(1)}, u32[]{:S(2)}, u32[]{:S(2)}) collective-permute-start(bf16[32,2048]{1,0:T(8,128)(2,1)S(1)} %collective-permute-done.2.refs_2_), channel_id=1, source_target_pairs={{0,4},{4,0},{8,12},{12,8},{1,5},{5,1},{9,13},{13,9},{2,6},{6,2},{1... | collective-permute-start | bytes 393224 | tf_op jit(solution)/shard_map/ppermute | solution.py:18
  29.6 1.3 %collective-permute-start.7 = (bf16[32,2048]{1,0:T(8,128)(2,1)S(1)}, bf16[32,2048]{1,0:T(8,128)(2,1)S(1)}, u32[]{:S(2)}, u32[]{:S(2)}) collective-permute-start(bf16[32,2048]{1,0:T(8,128)(2,1)S(1)} %collective-permute-done.3.refs_3_), channel_id=1, source_target_pairs={{0,4},{4,0},{8,12},{12,8},{1,5},{5,1},{9,13},{13,9},{2,6},{6,2},{1... | collective-permute-start | bytes 393224 | tf_op jit(solution)/shard_map/ppermute | solution.py:18
  34.9 10.2 %collective-permute-start.11 = (f32[64,17]{1,0:T(8,128)S(1)}, f32[64,17]{1,0:T(8,128)S(1)}, u32[]{:S(2)}, u32[]{:S(2)}) collective-permute-start(f32[64,17]{1,0:T(8,128)S(1)} %get-tuple-element.33), channel_id=1, source_target_pairs={{0,4},{4,0},{8,12},{12,8},{1,5},{5,1},{9,13},{13,9},{2,6},{6,2},{1... | collective-permute-start | bytes 13064 | tf_op jit(solution)/shard_map/ppermute | solution.py:18
  36.7 12.4 %collective-permute-start.8 = (bf16[2,64,1296]{2,1,0:T(8,128)(2,1)S(1)}, bf16[2,64,1296]{2,1,0:T(8,128)(2,1)S(1)}, u32[]{:S(2)}, u32[]{:S(2)}) collective-permute-start(bf16[2,64,1296]{2,1,0:T(8,128)(2,1)S(1)} %get-tuple-element.30.after_ref), channel_id=1, source_target_pairs={{0,1},{1,0},{2,3},{3,2},{4,5},{5,4},{6,7},{7,6},{8,9},{9,8},{10,11... | collective-permute-start | bytes 995336 | tf_op jit(solution)/shard_map/ppermute | solution.py:18
  39.0 24.3 %copy-start.2 = (f32[16]{0:T(128)S(1)}, f32[16]{0:T(128)}, u32[]{:S(2)}) copy-start(f32[16]{0:T(128)} %param.25) | copy-start | bytes 196
  39.0 24.3 %copy-start.3 = (f32[16]{0:T(128)S(1)}, f32[16]{0:T(128)}, u32[]{:S(2)}) copy-start(f32[16]{0:T(128)} %param.26) | copy-start | bytes 196
  39.0 24.3 %copy-start.4 = (f32[16]{0:T(128)S(1)}, f32[16]{0:T(128)}, u32[]{:S(2)}) copy-start(f32[16]{0:T(128)} %param.27) | copy-start | bytes 196
  45.1 4.0 %collective-permute-start.12 = (f32[64,17]{1,0:T(8,128)S(1)}, f32[64,17]{1,0:T(8,128)S(1)}, u32[]{:S(2)}, u32[]{:S(2)}) collective-permute-start(f32[64,17]{1,0:T(8,128)S(1)} %add.51), channel_id=1, source_target_pairs={{0,8},{4,12},{8,0},{12,4},{1,9},{5,13},{9,1},{13,5},{2,10},{6,14},... | collective-permute-start | bytes 13064 | tf_op jit(solution)/shard_map/ppermute | solution.py:18
  49.1 21.1 %copy-start.1 = (f32[1024]{0:T(1024)S(1)}, f32[1024]{0:T(1024)}, u32[]{:S(2)}) copy-start(f32[1024]{0:T(1024)} %param.28) | copy-start | bytes 12292
  50.4 10.9 %collective-permute-start.9 = (bf16[2,64,1024]{2,1,0:T(8,128)(2,1)S(1)}, bf16[2,64,1024]{2,1,0:T(8,128)(2,1)S(1)}, u32[]{:S(2)}, u32[]{:S(2)}) collective-permute-start(bf16[2,64,1024]{2,1,0:T(8,128)(2,1)S(1)} %get-tuple-element.31), channel_id=1, source_target_pairs={{0,1},{1,0},{2,3},{3,2},{4,5},{5,4},{6,7},{7,6},{8,9},{9,8},{10,11... | collective-permute-start | bytes 786440 | tf_op jit(solution)/shard_map/ppermute | solution.py:18
  50.9 12.4 %collective-permute-start.13 = (bf16[1,64,1296]{2,1,0:T(8,128)(2,1)S(1)}, bf16[1,64,1296]{2,1,0:T(8,128)(2,1)S(1)}, u32[]{:S(2)}, u32[]{:S(2)}) collective-permute-start(bf16[1,64,1296]{2,1,0:T(8,128)(2,1)S(1)} %add_convert_fusion.1), channel_id=1, source_target_pairs={{0,2},{1,3},{2,0},{3,1},{4,6},{5,7},{6,4},{7,5},{8,10},{9,11},{10,... | collective-permute-start | bytes 497672 | tf_op jit(solution)/shard_map/ppermute | solution.py:18
  61.4 8.8 %collective-permute-start.10 = (bf16[1,64,1024]{2,1,0:T(8,128)(2,1)S(1)}, bf16[1,64,1024]{2,1,0:T(8,128)(2,1)S(1)}, u32[]{:S(2)}, u32[]{:S(2)}) collective-permute-start(bf16[1,64,1024]{2,1,0:T(8,128)(2,1)S(1)} %add_convert_fusion.2.refs_9_), channel_id=1, source_target_pairs={{0,2},{1,3},{2,0},{3,1},{4,6},{5,7},{6,4},{7,5},{8,10},{9,11},{10,... | collective-permute-start | bytes 393224 | tf_op jit(solution)/shard_map/ppermute | solution.py:18
  71.7 2.6 %collective-permute-start.14 = (bf16[1,64,2048]{2,1,0:T(8,128)(2,1)S(1)}, bf16[1,64,2048]{2,1,0:T(8,128)(2,1)S(1)}, u32[]{:S(2)}, u32[]{:S(2)}) collective-permute-start(bf16[1,64,2048]{2,1,0:T(8,128)(2,1)S(1)} %get-tuple-element.39.after_ref), channel_id=1, source_target_pairs={{0,4},{4,0},{8,12},{12,8},{1,5},{5,1},{9,13},{13,9},{2,6},{6,2},{1... | collective-permute-start | bytes 786440 | tf_op jit(solution)/shard_map/ppermute | solution.py:18
  72.3 4.8 %collective-permute-start.17 = (f32[64,1]{1,0:T(8,128)S(1)}, f32[64,1]{1,0:T(8,128)S(1)}, u32[]{:S(2)}, u32[]{:S(2)}) collective-permute-start(f32[64,1]{1,0:T(8,128)S(1)} %get-tuple-element.41), channel_id=1, source_target_pairs={{0,4},{4,0},{8,12},{12,8},{1,5},{5,1},{9,13},{13,9},{2,6},{6,2},{1... | collective-permute-start | bytes 776 | tf_op jit(solution)/shard_map/ppermute | solution.py:18
  74.4 11.2 %collective-permute-start.15 = (bf16[1,64,2048]{2,1,0:T(8,128)(2,1)S(1)}, bf16[1,64,2048]{2,1,0:T(8,128)(2,1)S(1)}, u32[]{:S(2)}, u32[]{:S(2)}) collective-permute-start(bf16[1,64,2048]{2,1,0:T(8,128)(2,1)S(1)} %add_convert_fusion.after_ref), channel_id=1, source_target_pairs={{0,8},{4,12},{8,0},{12,4},{1,9},{5,13},{9,1},{13,5},{2,10},{6,14},... | collective-permute-start | bytes 786440 | tf_op jit(solution)/shard_map/ppermute | solution.py:18
  76.9 8.7 %collective-permute-start.16 = (bf16[1,64,2048]{2,1,0:T(8,128)(2,1)S(1)}, bf16[1,64,2048]{2,1,0:T(8,128)(2,1)S(1)}, u32[]{:S(2)}, u32[]{:S(2)}) collective-permute-start(bf16[1,64,2048]{2,1,0:T(8,128)(2,1)S(1)} %slice.84), channel_id=1, source_target_pairs={{0,4},{4,0},{8,12},{12,8},{1,5},{5,1},{9,13},{13,9},{2,6},{6,2},{1... | collective-permute-start | bytes 786440 | tf_op jit(solution)/shard_map/ppermute | solution.py:18
  77.1 8.3 %collective-permute-start.18 = (f32[64,1]{1,0:T(8,128)S(1)}, f32[64,1]{1,0:T(8,128)S(1)}, u32[]{:S(2)}, u32[]{:S(2)}) collective-permute-start(f32[64,1]{1,0:T(8,128)S(1)} %add.58), channel_id=1, source_target_pairs={{0,8},{4,12},{8,0},{12,4},{1,9},{5,13},{9,1},{13,5},{2,10},{6,14},... | collective-permute-start | bytes 776 | tf_op jit(solution)/shard_map/ppermute | solution.py:18
  (1 other events, 6.7 us)

commit v5 on v4

--- a/solution.py
+++ b/solution.py
@@ -29,23 +29,17 @@
 
 
 def reverse_bits(value, size):
-    result = 0
-    for distance in bits_of(size):
-        result = result * 2 + (1 if value & distance else 0)
-    return result
-
-
-def gather_relative(parts, axis, beside):
+    bits = size.bit_length() - 1
+    return sum(((value >> i) & 1) << (bits - 1 - i) for i in range(bits))
+
+
+def gather_relative(parts, axis, order_after):
     distances = list(reversed(bits_of(lax.axis_size(axis))))
+    parts = [lax.optimization_barrier((part, order_after))[0] for part in parts]
     blocks = [(0, p, part) for p, part in enumerate(parts)]
-    blocks += [(distances[0], p, swap(part, axis, distances[0])) for _, p, part in blocks]
-    passed, *extra = beside(parts[0])
-    for distance in distances[1:]:
-        blocks += [
-            (i ^ distance, p, swap(passed if (i, p) == (0, 0) else part, axis, distance))
-            for i, p, part in blocks
-        ]
-    return [part for _, _, part in blocks], [(i, p) for i, p, _ in blocks], extra
+    for distance in distances:
+        blocks += [(i ^ distance, p, swap(part, axis, distance)) for i, p, part in blocks]
+    return [part for _, _, part in blocks], [(i, p) for i, p, _ in blocks]
 
 
 def params(**more):
@@ -103,10 +97,11 @@
     rank = down_ref.shape[1]
     streams = tenant_ref.shape[0]
     rows = scaled_ref.shape[0]
+    first = lax.axis_index("row") * down_ref.shape[0]
     downs, ups = [], []
     for s in range(streams):
         at = pl.ds(s * rank, rank)
-        tenant = tenant_ref[s]
+        tenant = tenant_ref[s] - first
         downs.append(
             pltpu.make_async_copy(down_ref.at[tenant], down_rows_ref.at[at, :], semaphores.at[s])
         )
@@ -161,11 +156,18 @@
     )(tenants, scaled, squares, in_hbm(jnp.swapaxes(down, 1, 2)), in_hbm(up))
 
 
-def fill_rows(index_ref, blocks, lhs, semaphores):
+def fill_rows(owners, order, blocks, lhs, semaphores):
     rows = blocks[0].shape[0]
+    parts = len(blocks) // owners
     copies = []
     for i, block in enumerate(blocks):
-        at = pl.multiple_of(index_ref[i] * rows, rows)
+        if order is None:
+            owner, part = i, 0
+        else:
+            distance, part = order[i]
+            owner = reverse_bits(lax.axis_index("head") ^ distance, owners)
+        at = ((owner ^ lax.axis_index("row")) * parts + part) * rows
+        at = pl.multiple_of(at, rows)
         copies.append(pltpu.make_async_copy(block, lhs.at[pl.ds(at, rows), :], semaphores.at[i]))
     for copy in copies:
         copy.start()
@@ -182,11 +184,10 @@
         )
 
 
-def project_signal_body(count, index_ref, *refs):
+def project_signal_body(owners, order, count, *refs):
     blocks, refs = refs[:count], refs[count:]
-    weight_ref, mix_ref, step_ref, sums_ref, send_ref, keep_ref, lhs_ref, out_ref, semaphores = refs
-    out_ref[...] = sums_ref[...]
-    fill_rows(index_ref, blocks, lhs_ref, semaphores)
+    weight_ref, mix_ref, step_ref, send_ref, keep_ref, lhs_ref, semaphores = refs
+    fill_rows(owners, order, blocks, lhs_ref, semaphores)
     lhs = lhs_ref[...]
     columns = weight_ref.shape[1]
     tile = min(columns, 512)
@@ -199,7 +200,7 @@
     put_parts(acc, columns + mix_ref.shape[1], send_ref, keep_ref)
 
 
-def project_signal(index, blocks, owners, weight, mix, step, sums):
+def project_signal(blocks, order, owners, weight, mix, step):
     pieces = len(blocks)
     depth = blocks[0].shape[1]
     count, rows = owners, pieces * blocks[0].shape[0] // owners
@@ -207,25 +208,23 @@
     half = jax.ShapeDtypeStruct((count // 2, rows, columns), BF16)
     whole = pl.BlockSpec(memory_space=pltpu.VMEM)
     return pl.pallas_call(
-        functools.partial(project_signal_body, pieces),
+        functools.partial(project_signal_body, owners, order, pieces),
         out_shape=(
             half,
             half,
             jax.ShapeDtypeStruct((count * rows, depth), BF16),
-            jax.ShapeDtypeStruct(sums.shape, sums.dtype),
         ),
-        in_specs=[pl.BlockSpec(memory_space=pltpu.SMEM)]
-        + [pl.BlockSpec(memory_space=pl.ANY)] * pieces
-        + [whole] * 4,
-        out_specs=(whole,) * 4,
+        in_specs=[pl.BlockSpec(memory_space=pl.ANY)] * pieces + [whole] * 3,
+        out_specs=(whole,) * 3,
         scratch_shapes=[pltpu.SemaphoreType.DMA((pieces,))],
         compiler_params=params(),
         cost_estimate=cost(2 * count * rows * depth * columns, 2 * depth * columns),
         name="project_signal",
-    )(index, *blocks, weight, mix, step, sums)
-
-
-def project_gate_body(lhs_ref, weight_ref, after_ref, send_ref, keep_ref):
+    )(*blocks, weight, mix, step)
+
+
+def project_gate_body(lhs_ref, weight_ref, sums_ref, after_ref, send_ref, keep_ref, out_ref):
+    out_ref[...] = sums_ref[...]
     columns = weight_ref.shape[1]
     tile = min(columns, 512)
     for t in range(0, columns, tile):
@@ -233,20 +232,20 @@
         put_parts(acc, t, send_ref, keep_ref)
 
 
-def project_gate(rows, lhs, weight, after):
+def project_gate(rows, lhs, weight, sums, after):
     count = lhs.shape[0] // rows
     columns = weight.shape[1]
     half = jax.ShapeDtypeStruct((count // 2, rows, columns), BF16)
     whole = pl.BlockSpec(memory_space=pltpu.VMEM)
     return pl.pallas_call(
         project_gate_body,
-        out_shape=(half, half),
-        in_specs=[whole, whole, pl.BlockSpec(memory_space=pl.ANY)],
-        out_specs=(whole,) * 2,
+        out_shape=(half, half, jax.ShapeDtypeStruct(sums.shape, sums.dtype)),
+        in_specs=[whole, whole, whole, pl.BlockSpec(memory_space=pl.ANY)],
+        out_specs=(whole,) * 3,
         compiler_params=params(),
         cost_estimate=cost(2 * lhs.size * columns, 2 * weight.size),
         name="project_gate",
-    )(lhs, weight, after)
+    )(lhs, weight, sums, after)
 
 
 def scatter_rows(received, keep, axis, done=1):
@@ -408,73 +407,82 @@
     )
 
 
-def state_write_body(left_ref, right_ref, decay_ref, state_ref, out_ref):
+def state_write_body(feeds_ref, b_ref, decay_ref, state_ref, out_ref):
     group, heads, head, width = out_ref.shape
-    at = pl.program_id(0) * group
-    for g in range(group):
+    at = pl.multiple_of(pl.program_id(0) * group, group)
+    feeds = [split(feeds_ref[p, pl.ds(at, group), :]) for p in range(2)]
+    rights = [split(b_ref[p, pl.ds(at, group), :]) for p in range(2)]
+    left = [f.astype(F32) for pair in feeds for f in (pair[0], pair[1], pair[0])]
+    right = [f.astype(F32) for pair in rights for f in (pair[0], pair[0], pair[1])]
+    left = jnp.concatenate(left, 0).astype(BF16)
+    right = jnp.concatenate(right, 0)
+    stream = lax.broadcasted_iota(jnp.int32, right.shape, 0) % group
+    for g in range(0, group, 2):
+        pair = jnp.concatenate([jnp.where(stream == g + i, right, 0.0) for i in range(2)], 1)
         outer = lax.dot_general(
-            left_ref[g], right_ref[g], (((0,), (0,)), ((), ())), preferred_element_type=F32
+            left, pair.astype(BF16), (((0,), (0,)), ((), ())), preferred_element_type=F32
         )
-        scaled = state_ref[at + g].astype(F32) * decay_ref[g][:, None, :]
-        out_ref[g] = (scaled + outer.reshape(heads, head, width)).astype(out_ref.dtype)
-
-
-def state_write(left, right, decay, state):
+        for i in range(2):
+            scaled = state_ref[at + g + i].astype(F32) * decay_ref[g + i][:, None, :]
+            own = outer[:, i * width : (i + 1) * width].reshape(heads, head, width)
+            out_ref[g + i] = (scaled + own).astype(out_ref.dtype)
+
+
+def state_write(feeds, b, decay, state):
     streams, heads, head, width = state.shape
-    group = 4
-    rank = left.shape[1]
-    block = pl.BlockSpec((group, heads, head, width), lambda i: (i, 0, 0, 0))
+    group = 8
+    whole = pl.BlockSpec(memory_space=pltpu.VMEM)
     return pl.pallas_call(
         state_write_body,
         out_shape=jax.ShapeDtypeStruct(state.shape, state.dtype),
         grid=(streams // group,),
         in_specs=[
-            pl.BlockSpec((group, rank, heads * head), lambda i: (i, 0, 0)),
-            pl.BlockSpec((group, rank, width), lambda i: (i, 0, 0)),
+            whole,
+            whole,
             pl.BlockSpec((group, heads, width), lambda i: (i, 0, 0)),
-            pl.BlockSpec(memory_space=pltpu.VMEM),
+            whole,
         ],
-        out_specs=block,
+        out_specs=pl.BlockSpec((group, heads, head, width), lambda i: (i, 0, 0, 0)),
         compiler_params=params(),
         cost_estimate=cost(32 * state.size, 4 * state.size),
         name="state_write",
-    )(left, right, decay, state)
-
-
-def output_tiles(index_ref, lhs_ref, weight_ref, out_ref):
-    count, _, width = out_ref.shape
+    )(feeds, b, decay, state)
+
+
+def output_tiles(distances, lhs_ref, weight_ref, out_ref):
+    width = out_ref.shape[2]
     tile = min(width, 512)
-    for j in range(count):
+    for j, distance in enumerate(distances):
         for t in range(0, width, tile):
-            at = pl.multiple_of(index_ref[j] * width + t, tile)
+            at = pl.multiple_of((lax.axis_index("head") ^ distance) * width + t, tile)
             acc = jnp.dot(lhs_ref[...], weight_ref[:, pl.ds(at, tile)], preferred_element_type=F32)
             out_ref[j, :, t : t + tile] = acc.astype(out_ref.dtype)
 
 
-def output_first_body(terms, model_width, index_ref, *refs):
+def output_first_body(distances, terms, model_width, *refs):
     term_refs = refs[:terms]
     sums_ref, result_ref, scale_ref, weight_ref, out_ref, lhs_ref, squares_ref = refs[terms:]
     total = sum(t[...].astype(F32) for t in term_refs) * inverse_of(sums_ref, model_width)
     gated = result_ref[...] * silu(total)
     squares_ref[...] = jnp.sum(gated * gated, -1, keepdims=True)
     lhs_ref[...] = (gated * scale_ref[...]).astype(lhs_ref.dtype)
-    output_tiles(index_ref, lhs_ref, weight_ref, out_ref)
-
-
-def output_rest_body(index_ref, lhs_ref, after_ref, weight_ref, out_ref):
-    output_tiles(index_ref, lhs_ref, weight_ref, out_ref)
-
-
-def output_parts(index, weight, width, operands, model_width=None):
+    output_tiles(distances, lhs_ref, weight_ref, out_ref)
+
+
+def output_rest_body(distances, lhs_ref, after_ref, weight_ref, out_ref):
+    output_tiles(distances, lhs_ref, weight_ref, out_ref)
+
+
+def output_parts(distances, weight, width, operands, model_width=None):
     first = model_width is not None
     rows, depth = operands[0].shape
-    count = index.shape[0]
+    count = len(distances)
     whole = pl.BlockSpec(memory_space=pltpu.VMEM)
     specs = [whole] * (len(operands) + 1)
-    body = output_rest_body
+    body = functools.partial(output_rest_body, distances)
     out_shape = [jax.ShapeDtypeStruct((count, rows, width), BF16)]
     if first:
-        body = functools.partial(output_first_body, len(operands) - 3, model_width)
+        body = functools.partial(output_first_body, distances, len(operands) - 3, model_width)
         out_shape += [
             jax.ShapeDtypeStruct((rows, depth), BF16),
             jax.ShapeDtypeStruct((rows, 1), F32),
@@ -484,12 +492,12 @@
     return pl.pallas_call(
         body,
         out_shape=tuple(out_shape),
-        in_specs=[pl.BlockSpec(memory_space=pltpu.SMEM)] + specs,
+        in_specs=specs,
         out_specs=(whole,) * len(out_shape),
         compiler_params=params(),
         cost_estimate=cost(2 * rows * depth * width * count, 2 * depth * width * count),
         name="output_first" if first else "output_rest",
-    )(index, *operands, weight)
+    )(*operands, weight)
 
 
 def split(values):
@@ -522,47 +530,40 @@
     model_width = feature_width * heads_n
     depth, inner = projection_signal.shape
     inner_width = inner * heads_n
-    head_at = lax.axis_index("head")
-    row_at = lax.axis_index("row")
 
     wide = jnp.swapaxes(hidden, 0, 1).astype(F32)
     scaled = (wide * input_norm_scale).astype(BF16)
     scaled_flat = scaled.reshape(rows, feature_width)
 
-    tenant_local = stream_tenant_index - row_at * adapter_down_weight.shape[0]
     squares = jnp.sum(wide * wide, -1).reshape(rows, 1)
-    sums, up_rows = adapt(tenant_local, scaled_flat, squares, adapter_down_weight, adapter_up_weight)
-
-    in_weights = (projection_signal, projection_input_output, projection_gate)
+    sums, up_rows = adapt(stream_tenant_index, scaled_flat, squares, adapter_down_weight, adapter_up_weight)
+
+    weights = load(sums, [], projection_signal, projection_input_output, projection_gate)
     if heads_n == rows_n:
         turn = [
             (h * rows_n + r, reverse_bits(r, rows_n) * rows_n + h)
             for h in range(heads_n)
             for r in range(rows_n)
         ]
-        blocks, order, weights = gather_relative(
+        blocks, order = gather_relative(
             [lax.ppermute(scaled[p], ("head", "row"), turn) for p in range(positions)],
             "head",
-            lambda block: load(sums, [block], *in_weights),
+            weights[0],
         )
-        owner = jnp.asarray([reverse_bits(i, rows_n) for i in range(rows_n)], jnp.int32)
-        owner = owner[head_at ^ jnp.asarray([i for i, _ in order], jnp.int32)] ^ row_at
-        index = owner * positions + jnp.asarray([p for _, p in order], jnp.int32)
     else:
         features = lax.all_gather(scaled_flat, "head", axis=1, tiled=True)
         blocks = lax.all_to_all(features, "row", split_axis=1, concat_axis=0, tiled=True)
         blocks = blocks.reshape(rows_n, rows, depth)
         blocks = [blocks[i] for i in range(rows_n)]
-        weights = load(sums, [scaled_flat], *in_weights)[1:]
-        index = jnp.arange(rows_n, dtype=jnp.int32) ^ row_at
+        order = None
 
     signal_weight, mix_weight, gate_weight = weights
-    send, keep, lhs, sums = project_signal(
-        index, blocks, rows_n, signal_weight, mix_weight, projection_step.T, sums
+    send, keep, lhs = project_signal(
+        blocks, order, rows_n, signal_weight, mix_weight, projection_step.T
     )
     received = swap(send, "row", 1)
     keep, out_weight = load(send, [keep], output_weight)
-    gate_send, gate_keep = project_gate(rows, lhs, gate_weight, received)
+    gate_send, gate_keep, sums = project_gate(rows, lhs, gate_weight, sums, received)
     signal_terms, _ = scatter_rows(received, keep, "row")
     gate_terms, gate_last = scatter_rows(swap(gate_send, "row", 1), gate_keep, "row")
     sums = sum_over(sums, "head")
@@ -580,7 +581,7 @@
         scan_state,
     )
 
-    distances = jnp.arange(heads_n, dtype=jnp.int32) ^ head_at
+    distances = list(range(heads_n))
     first, out_lhs, gate_squares = output_parts(
         distances[3::4],
         out_weight,
@@ -588,13 +589,15 @@
         [*gate_terms, sums, result, gated_norm_scale[None]],
         model_width,
     )
-    (second,) = output_parts(distances[2::4], out_weight, feature_width, [out_lhs, first])
-    send = (swap(first, "head", 1).astype(F32) + second.astype(F32)).astype(BF16)
-    near = jnp.concatenate([distances[1::4], distances[0::4]])
-    (rest,) = output_parts(near, out_weight, feature_width, [out_lhs, send])
-    half = rest.shape[0] // 2
-    kept = [swap(rest[:half], "head", 1), rest[half:]]
-    mixer, _ = scatter_rows(swap(send, "head", 2), kept, "head", done=2)
+    (second,) = output_parts(
+        distances[2::4] + distances[1::4], out_weight, feature_width, [out_lhs, first]
+    )
+    half = second.shape[0] // 2
+    send = (swap(first, "head", 1).astype(F32) + second[:half].astype(F32)).astype(BF16)
+    received = swap(send, "head", 2)
+    (rest,) = output_parts(distances[0::4], out_weight, feature_width, [out_lhs, send])
+    kept = [swap(second[half:], "head", 1), rest]
+    mixer, _ = scatter_rows(received, kept, "head", done=2)
     mixer = sum(t.astype(F32) for t in mixer)
     gate_squares = sum_over(gate_squares, "head")
     mixer = mixer * lax.rsqrt(gate_squares / inner_width + EPSILON)
@@ -602,12 +605,8 @@
     live = jnp.arange(streams) < live_block_rows[0]
     mixed = (wide + jnp.where(live[:, None], mixer, 0.0)).astype(BF16)
 
-    b_high, b_low = split(jnp.swapaxes(bgate, 0, 1))
-    f_high, f_low = split(jnp.swapaxes(feeds, 0, 1))
-    left = jnp.concatenate([f_high, f_low, f_high, jnp.zeros_like(f_high)], 1)
-    right = jnp.concatenate([b_high, b_high, b_low, jnp.zeros_like(b_high)], 1)
     spread = jnp.broadcast_to(both[..., None], both.shape + (bgate.shape[-1],))
-    new_state = state_write(left, right, spread, state)
+    new_state = state_write(feeds, bgate, spread, state)
     return (jnp.swapaxes(mixed, 0, 1), new_state)
 
 

time: 87.1 us -> 85 us (0.976)
  other arithmetic: 5.83 us -> 1.66 us
  local copies, waits for them, and re-layouts: 3.67 us -> 7.82 us
  Pallas kernels: 35.6 us -> 31.6 us
  waiting for transfers between devices: 12.4 us -> 16.3 us
  starting transfers between devices: 27.7 us -> 25.8 us
    unnamed x13 -> x19, local copies, waits for them, and re-layouts: 1 us -> 7.43 us
    ppermute x17, waiting for transfers between devices: 12.4 us -> 16.3 us  [swap(): return lax.ppermute(values, axis, [(i, i ^ distance) for i in range(size)])]
    pallas_call x5, Pallas kernels: 10.4 us -> 8.01 us  [the longest x3 3.45 us: output_parts(): pl.pallas_call(body, out_shape=tuple(out_shape), in_specs=specs, out_spec...]
    concatenate x3 -> x0, other arithmetic: 1.92 us -> none  [the longest x1 1.41 us: on_device(): near = jnp.concatenate([distances[1::4], distances[0::4]])]
    ppermute x17, starting transfers between devices: 26.4 us -> 24.5 us  [swap(): return lax.ppermute(values, axis, [(i, i ^ distance) for i in range(size)])]
    pallas_call x1, Pallas kernels: 6.34 us -> 4.89 us  [state_write(): pl.pallas_call(state_write_body, out_shape=jax.ShapeDtypeStruct(state.sha...]
    gather x1 -> x0, local copies, waits for them, and re-layouts: 1.29 us -> none  [on_device(): owner[head_at ^ jnp.asarray([i for i, _ in order], jnp.int32)] ^ row_at]
  transfers between devices with their start and end apart: 19 -> 19, of which waited for: 6 -> 8; matrix products, arithmetic and copies ran while one was open for 8% -> 1% of each run, Pallas kernels for 33% -> 31%
where the time goes in v5:
time: 85 us; the launch traced here: 84.7 us
  Pallas kernels  31.6 us (37%)
  starting transfers between devices  25.8 us (30%)
  waiting for transfers between devices  16.3 us (19%)
  local copies, waits for them, and re-layouts  7.82 us (9%)
  other arithmetic  1.66 us (2%)
  between operations  1.58 us (2%)
    ppermute x17, starting transfers between devices, swap(): return lax.ppermute(values, axis, [(i, i ^ distance) for i in range(size)])  24.5 us
    ppermute x17, waiting for transfers between devices, swap(): return lax.ppermute(values, axis, [(i, i ^ distance) for i in range(size)])  16.3 us
    pallas_call x2, Pallas kernels, load(): pl.pallas_call(functools.partial(load_body, pieces), out_shape=tuple((plt...  10 us
    unnamed x19, local copies, waits for them, and re-layouts  7.43 us
    pallas_call x1, Pallas kernels, state_write(): pl.pallas_call(state_write_body, out_shape=jax.ShapeDtypeStruct(state.sha...  4.89 us
    pallas_call x1, Pallas kernels, recur(): pl.pallas_call(functools.partial(recur_body, len(terms), group, model_wid...  4.84 us
    pallas_call x1, Pallas kernels, adapt(): pl.pallas_call(adapt_body, out_shape=(jax.ShapeDtypeStruct((rows, rank +...  3.81 us
    pallas_call x3, Pallas kernels, output_parts(): pl.pallas_call(body, out_shape=tuple(out_shape), in_specs=specs, out_spec...  3.45 us
  transfers between devices with their start and end apart: 19, of which 8 were waited for; matrix products, arithmetic and copies ran while one was open for 1% of the time, Pallas kernels for 31%

profile of v5, /device:TPU:0, one launch (start us, length us, event | category | flops | bytes accessed | tf_op | source)
XLA Modules:
  0.0 84.7 jit_solution(2619080909643731676)
XLA Ops:
  0.6 1.1 %fusion.1 = (f32[2,32]{1,0:T(2,128)S(1)}, bf16[2,32,2048]{2,1,0:T(8,128)(2,1)S(1)}) fusion(bf16[32,2,2048]{2,1,0:T(2,128)(2,1)} %param.16, f32[2048]{0:T(1024)} %param.17), kind=kLoop, calls=%fused_computation.4 | loop fusion | flops 655296 | bytes 532736 | tf_op jit(solution)/shard_map/reduce_sum | solution.py:538
  3.9 3.8 %adapt.1 = (f32[64,17]{1,0:T(8,128)S(1)}, bf16[512,1024]{1,0:T(8,128)(2,1)S(1)}) custom-call(s32[32]{0:T(128)S(1)} %copy-done.4, bf16[64,2048]{1,0:T(8,128)(2,1)S(1)} %bitcast.38, f32[64,1]{1,0:T(8,128)S(1)} %reshape.28.squares_ref, bf16[128,16,2048]{2,1,0:T(8,128)(2,1)} %bitcast.46, bf16[128,16,1024]{2,1,0:T(8,128)(2,1)} %up_ref.1), custom_call_target="tpu_custom_call" | custom-call | flops 134217728 | bytes 3145728 | tf_op jit(solution)/shard_map/adapt/pallas_call | solution.py:141
  7.7 3.9 %load.2 = (bf16[2048,1024]{1,0:T(8,128)(2,1)S(1)}, bf16[2048,256]{1,0:T(8,128)(2,1)S(1)}, bf16[2048,1024]{1,0:T(8,128)(2,1)S(1)}) custom-call(f32[64,17]{1,0:T(8,128)S(1)} %get-tuple-element.25.after_ref.sums_ref, bf16[2048,1024]{1,0:T(8,128)(2,1)} %refs_0_.1, bf16[2048,256]{1,0:T(8,128)(2,1)} %refs_1_.2, bf16[2048,1024]{1,0:T(8,128)(2,1)} %refs_2_.1), custom_call_target="tpu_custom_call" | custom-call | bytes 18874368 | tf_op jit(solution)/shard_map/load/pallas_call | solution.py:78
  11.7 8.1 %collective-permute-start.2 = (bf16[32,2048]{1,0:T(8,128)(2,1)S(1)}, bf16[32,2048]{1,0:T(8,128)(2,1)S(1)}, u32[]{:S(2)}, u32[]{:S(2)}) collective-permute-start(bf16[32,2048]{1,0:T(8,128)(2,1)S(1)} %collective-permute-done.refs_0_), channel_id=1, source_target_pairs={{0,8},{4,12},{8,0},{12,4},{1,9},{5,13},{9,1},{13,5},{2,10},{6,14},... | collective-permute-start | bytes 393224 | tf_op jit(solution)/shard_map/ppermute | solution.py:18
  19.8 1.4 %collective-permute-start.4 = (bf16[32,2048]{1,0:T(8,128)(2,1)S(1)}, bf16[32,2048]{1,0:T(8,128)(2,1)S(1)}, u32[]{:S(2)}, u32[]{:S(2)}) collective-permute-start(bf16[32,2048]{1,0:T(8,128)(2,1)S(1)} %collective-permute-done.refs_0_), channel_id=1, source_target_pairs={{0,4},{4,0},{8,12},{12,8},{1,5},{5,1},{9,13},{13,9},{2,6},{6,2},{1... | collective-permute-start | bytes 393224 | tf_op jit(solution)/shard_map/ppermute | solution.py:18
  21.3 1.8 %collective-permute-done.2.refs_2_ = bf16[32,2048]{1,0:T(8,128)(2,1)S(1)} collective-permute-done((bf16[32,2048]{1,0:T(8,128)(2,1)S(1)}, bf16[32,2048]{1,0:T(8,128)(2,1)S(1)}, u32[]{:S(2)}, u32[]{:S(2)}) %collective-permute-start.2) | collective-permute-done | bytes 131104 | tf_op jit(solution)/shard_map/ppermute | solution.py:18
  23.1 1.9 %collective-permute-start.6 = (bf16[32,2048]{1,0:T(8,128)(2,1)S(1)}, bf16[32,2048]{1,0:T(8,128)(2,1)S(1)}, u32[]{:S(2)}, u32[]{:S(2)}) collective-permute-start(bf16[32,2048]{1,0:T(8,128)(2,1)S(1)} %collective-permute-done.2.refs_2_), channel_id=1, source_target_pairs={{0,4},{4,0},{8,12},{12,8},{1,5},{5,1},{9,13},{13,9},{2,6},{6,2},{1... | collective-permute-start | bytes 393224 | tf_op jit(solution)/shard_map/ppermute | solution.py:18
  25.0 1.1 %collective-permute-done.3.refs_3_ = bf16[32,2048]{1,0:T(8,128)(2,1)S(1)} collective-permute-done((bf16[32,2048]{1,0:T(8,128)(2,1)S(1)}, bf16[32,2048]{1,0:T(8,128)(2,1)S(1)}, u32[]{:S(2)}, u32[]{:S(2)}) %collective-permute-start.3) | collective-permute-done | bytes 131104 | tf_op jit(solution)/shard_map/ppermute | solution.py:18
  27.7 3.3 %project_signal.1 = (bf16[2,64,1296]{2,1,0:T(8,128)(2,1)S(1)}, bf16[2,64,1296]{2,1,0:T(8,128)(2,1)S(1)}, bf16[256,2048]{1,0:T(8,128)(2,1)S(1)}) custom-call(bf16[32,2048]{1,0:T(8,128)(2,1)S(1)} %collective-permute-done.refs_0_, bf16[32,2048]{1,0:T(8,128)(2,1)S(1)} %collective-permute-done.1.refs_1_, bf16[32,2048]{1,0:T(8,128)(2,1)S(1)} %collective-permute-done.2.refs_2_, ...), custom_call_target="tpu_custom_call" | custom-call | flops 1358954496 | bytes 5308416 | tf_op jit(solution)/shard_map/project_signal/pallas_call | solution.py:210
  31.0 2.4 %collective-permute-start.8 = (bf16[2,64,1296]{2,1,0:T(8,128)(2,1)S(1)}, bf16[2,64,1296]{2,1,0:T(8,128)(2,1)S(1)}, u32[]{:S(2)}, u32[]{:S(2)}) collective-permute-start(bf16[2,64,1296]{2,1,0:T(8,128)(2,1)S(1)} %get-tuple-element.32.after_ref), channel_id=1, source_target_pairs={{0,1},{1,0},{2,3},{3,2},{4,5},{5,4},{6,7},{7,6},{8,9},{9,8},{10,11... | collective-permute-start | bytes 995336 | tf_op jit(solution)/shard_map/ppermute | solution.py:18
  33.5 6.1 %load.3 = (bf16[2,64,1296]{2,1,0:T(8,128)(2,1)S(1)}, bf16[1024,8192]{1,0:T(8,128)(2,1)S(1)}) custom-call(bf16[2,64,1296]{2,1,0:T(8,128)(2,1)S(1)} %get-tuple-element.32.after_ref, bf16[2,64,1296]{2,1,0:T(8,128)(2,1)S(1)} %get-tuple-element.36.refs_0_, bf16[1024,8192]{1,0:T(8,128)(2,1)} %refs_1_.3), custom_call_target="tpu_custom_call" | custom-call | bytes 34217984 | tf_op jit(solution)/shard_map/load/pallas_call | solution.py:78
  39.6 2.6 %collective-permute-done.8.after_ref = bf16[2,64,1296]{2,1,0:T(8,128)(2,1)S(1)} collective-permute-done((bf16[2,64,1296]{2,1,0:T(8,128)(2,1)S(1)}, bf16[2,64,1296]{2,1,0:T(8,128)(2,1)S(1)}, u32[]{:S(2)}, u32[]{:S(2)}) %collective-permute-start.8) | collective-permute-done | bytes 331808 | tf_op jit(solution)/shard_map/ppermute | solution.py:18
  42.2 1.2 %project_gate.1 = (bf16[2,64,1024]{2,1,0:T(8,128)(2,1)S(1)}, bf16[2,64,1024]{2,1,0:T(8,128)(2,1)S(1)}, f32[64,17]{1,0:T(8,128)S(1)}) custom-call(bf16[256,2048]{1,0:T(8,128)(2,1)S(1)} %get-tuple-element.30.lhs_ref, bf16[2048,1024]{1,0:T(8,128)(2,1)S(1)} %get-tuple-element.31.weight_ref, f32[64,17]{1,0:T(8,128)S(1)} %get-tuple-element.25.after_ref.sums_ref, ...), custom_call_target="tpu_custom_call" | custom-call | flops 1073741824 | bytes 4194304 | tf_op jit(solution)/shard_map/project_gate/pallas_call | solution.py:240
  43.4 1.8 %collective-permute-start.9 = (bf16[2,64,1024]{2,1,0:T(8,128)(2,1)S(1)}, bf16[2,64,1024]{2,1,0:T(8,128)(2,1)S(1)}, u32[]{:S(2)}, u32[]{:S(2)}) collective-permute-start(bf16[2,64,1024]{2,1,0:T(8,128)(2,1)S(1)} %get-tuple-element.33), channel_id=1, source_target_pairs={{0,1},{1,0},{2,3},{3,2},{4,5},{5,4},{6,7},{7,6},{8,9},{9,8},{10,11... | collective-permute-start | bytes 786440 | tf_op jit(solution)/shard_map/ppermute | solution.py:18
  45.3 3.1 %collective-permute-start.13 = (bf16[1,64,1296]{2,1,0:T(8,128)(2,1)S(1)}, bf16[1,64,1296]{2,1,0:T(8,128)(2,1)S(1)}, u32[]{:S(2)}, u32[]{:S(2)}) collective-permute-start(bf16[1,64,1296]{2,1,0:T(8,128)(2,1)S(1)} %add_convert_fusion.1), channel_id=1, source_target_pairs={{0,2},{1,3},{2,0},{3,1},{4,6},{5,7},{6,4},{7,5},{8,10},{9,11},{10,... | collective-permute-start | bytes 497672 | tf_op jit(solution)/shard_map/ppermute | solution.py:18
  48.8 3.6 %collective-permute-done.12 = f32[64,17]{1,0:T(8,128)S(1)} collective-permute-done((f32[64,17]{1,0:T(8,128)S(1)}, f32[64,17]{1,0:T(8,128)S(1)}, u32[]{:S(2)}, u32[]{:S(2)}) %collective-permute-start.12) | collective-permute-done | bytes 4384 | tf_op jit(solution)/shard_map/ppermute | solution.py:18
  52.4 2.8 %collective-permute-done.9 = bf16[2,64,1024]{2,1,0:T(8,128)(2,1)S(1)} collective-permute-done((bf16[2,64,1024]{2,1,0:T(8,128)(2,1)S(1)}, bf16[2,64,1024]{2,1,0:T(8,128)(2,1)S(1)}, u32[]{:S(2)}, u32[]{:S(2)}) %collective-permute-start.9) | collective-permute-done | bytes 262176 | tf_op jit(solution)/shard_map/ppermute | solution.py:18
  55.9 4.8 %recur.1 = (f32[64,1024]{1,0:T(8,128)S(1)}, f32[2,32,1024]{2,1,0:T(8,128)S(1)}, f32[2,32,128]{2,1,0:T(8,128)S(1)}, f32[32,16]{1,0:T(8,128)S(1)}, bf16[32,16,64,128]{3,2,1,0:T(8,128)(2,1)S(1)}) custom-call(s32[1]{0:T(128)} %copy.27.live_ref, bf16[64,1296]{1,0:T(8,128)(2,1)S(1)} %bitcast.39, bf16[64,1296]{1,0:T(8,128)(2,1)S(1)} %slice_bitcast_fusion.refs_1_, ...), custom_call_target="tpu_custom_call" | custom-call | flops 268435456 | bytes 10485760 | tf_op jit(solution)/shard_map/recur/pallas_call | solution.py:373
  60.8 2.5 %collective-permute-done.10 = bf16[1,64,1024]{2,1,0:T(8,128)(2,1)S(1)} collective-permute-done((bf16[1,64,1024]{2,1,0:T(8,128)(2,1)S(1)}, bf16[1,64,1024]{2,1,0:T(8,128)(2,1)S(1)}, u32[]{:S(2)}, u32[]{:S(2)}) %collective-permute-start.10) | collective-permute-done | bytes 131104 | tf_op jit(solution)/shard_map/ppermute | solution.py:18
  64.4 1.6 %output_rest.2 = bf16[2,64,2048]{2,1,0:T(8,128)(2,1)S(1)} custom-call(bf16[64,1024]{1,0:T(8,128)(2,1)S(1)} %get-tuple-element.42.lhs_ref, bf16[1,64,2048]{2,1,0:T(8,128)(2,1)S(1)} %get-tuple-element.41.after_ref, bf16[1024,8192]{1,0:T(8,128)(2,1)S(1)} %get-tuple-element.40.refs_6_.weight_ref), custom_call_target="tpu_custom_call" | custom-call | flops 536870912 | bytes 8388608 | tf_op jit(solution)/shard_map/output_rest/pallas_call | solution.py:492
  66.7 2.3 %collective-permute-start.15 = (bf16[1,64,2048]{2,1,0:T(8,128)(2,1)S(1)}, bf16[1,64,2048]{2,1,0:T(8,128)(2,1)S(1)}, u32[]{:S(2)}, u32[]{:S(2)}) collective-permute-start(bf16[1,64,2048]{2,1,0:T(8,128)(2,1)S(1)} %add_convert_fusion.after_ref), channel_id=1, source_target_pairs={{0,8},{4,12},{8,0},{12,4},{1,9},{5,13},{9,1},{13,5},{2,10},{6,14},... | collective-permute-start | bytes 786440 | tf_op jit(solution)/shard_map/ppermute | solution.py:18
  70.2 4.9 %state_write.1 = bf16[32,16,64,128]{3,2,1,0:T(8,128)(2,1)} custom-call(f32[2,32,1024]{2,1,0:T(8,128)S(1)} %get-tuple-element.44.feeds_ref, f32[2,32,128]{2,1,0:T(8,128)S(1)} %get-tuple-element.45.b_ref, f32[32,16,128]{2,1,0:T(8,128)S(1)} %broadcast_in_dim.38.decay_ref, bf16[32,16,64,128]{3,2,1,0:T(8,128)(2,1)S(1)} %get-tuple-element.47.state_ref), custom_call_target="tpu_custom_call" | custom-call | flops 134217728 | bytes 16777216 | tf_op jit(solution)/shard_map/state_write/pallas_call | solution.py:435
  75.1 1.6 %collective-permute-done.18 = f32[64,1]{1,0:T(8,128)S(1)} collective-permute-done((f32[64,1]{1,0:T(8,128)S(1)}, f32[64,1]{1,0:T(8,128)S(1)}, u32[]{:S(2)}, u32[]{:S(2)}) %collective-permute-start.18) | collective-permute-done | bytes 288 | tf_op jit(solution)/shard_map/ppermute | solution.py:18
  76.8 5.8 %copy-done.1 = bf16[1024,8192]{1,0:T(8,128)(2,1)S(1)} copy-done((bf16[1024,8192]{1,0:T(8,128)(2,1)S(1)}, bf16[1024,8192]{1,0:T(8,128)(2,1)}, u32[]{:S(2)}) %copy-start.1) | copy-done | bytes 16777240
  (63 shorter events, 9.5 us)
Async XLA Ops:
  1.8 9.9 %collective-permute-start = (bf16[32,2048]{1,0:T(8,128)(2,1)S(1)}, bf16[32,2048]{1,0:T(8,128)(2,1)S(1)}, u32[]{:S(2)}, u32[]{:S(2)}) collective-permute-start(bf16[32,2048]{1,0:T(8,128)(2,1)S(1)} %get-tuple-element.53), channel_id=1, source_target_pairs={{0,0},{1,8},{2,4},{3,12},{4,1},{5,9},{6,5},{7,13},{8,2},{9,10},{10... | collective-permute-start | bytes 393224 | tf_op jit(solution)/shard_map/ppermute | solution.py:549
  2.5 9.2 %collective-permute-start.1 = (bf16[32,2048]{1,0:T(8,128)(2,1)S(1)}, bf16[32,2048]{1,0:T(8,128)(2,1)S(1)}, u32[]{:S(2)}, u32[]{:S(2)}) collective-permute-start(bf16[32,2048]{1,0:T(8,128)(2,1)S(1)} %get-tuple-element.52), channel_id=1, source_target_pairs={{0,0},{1,8},{2,4},{3,12},{4,1},{5,9},{6,5},{7,13},{8,2},{9,10},{10... | collective-permute-start | bytes 393224 | tf_op jit(solution)/shard_map/ppermute | solution.py:549
  3.9 23.8 %copy-start.2 = (bf16[2048,16]{0,1:T(8,128)(2,1)S(1)}, bf16[2048,16]{0,1:T(8,128)(2,1)}, u32[]{:S(2)}) copy-start(bf16[2048,16]{0,1:T(8,128)(2,1)} %param.20) | copy-start | bytes 196612
  11.7 11.4 %collective-permute-start.2 = (bf16[32,2048]{1,0:T(8,128)(2,1)S(1)}, bf16[32,2048]{1,0:T(8,128)(2,1)S(1)}, u32[]{:S(2)}, u32[]{:S(2)}) collective-permute-start(bf16[32,2048]{1,0:T(8,128)(2,1)S(1)} %collective-permute-done.refs_0_), channel_id=1, source_target_pairs={{0,8},{4,12},{8,0},{12,4},{1,9},{5,13},{9,1},{13,5},{2,10},{6,14},... | collective-permute-start | bytes 393224 | tf_op jit(solution)/shard_map/ppermute | solution.py:18
  19.8 6.4 %collective-permute-start.3 = (bf16[32,2048]{1,0:T(8,128)(2,1)S(1)}, bf16[32,2048]{1,0:T(8,128)(2,1)S(1)}, u32[]{:S(2)}, u32[]{:S(2)}) collective-permute-start(bf16[32,2048]{1,0:T(8,128)(2,1)S(1)} %collective-permute-done.1.refs_1_), channel_id=1, source_target_pairs={{0,8},{4,12},{8,0},{12,4},{1,9},{5,13},{9,1},{13,5},{2,10},{6,14},... | collective-permute-start | bytes 393224 | tf_op jit(solution)/shard_map/ppermute | solution.py:18
  19.8 7.6 %collective-permute-start.4 = (bf16[32,2048]{1,0:T(8,128)(2,1)S(1)}, bf16[32,2048]{1,0:T(8,128)(2,1)S(1)}, u32[]{:S(2)}, u32[]{:S(2)}) collective-permute-start(bf16[32,2048]{1,0:T(8,128)(2,1)S(1)} %collective-permute-done.refs_0_), channel_id=1, source_target_pairs={{0,4},{4,0},{8,12},{12,8},{1,5},{5,1},{9,13},{13,9},{2,6},{6,2},{1... | collective-permute-start | bytes 393224 | tf_op jit(solution)/shard_map/ppermute | solution.py:18
  21.3 6.1 %collective-permute-start.5 = (bf16[32,2048]{1,0:T(8,128)(2,1)S(1)}, bf16[32,2048]{1,0:T(8,128)(2,1)S(1)}, u32[]{:S(2)}, u32[]{:S(2)}) collective-permute-start(bf16[32,2048]{1,0:T(8,128)(2,1)S(1)} %collective-permute-done.1.refs_1_), channel_id=1, source_target_pairs={{0,4},{4,0},{8,12},{12,8},{1,5},{5,1},{9,13},{13,9},{2,6},{6,2},{1... | collective-permute-start | bytes 393224 | tf_op jit(solution)/shard_map/ppermute | solution.py:18
  23.1 4.3 %collective-permute-start.6 = (bf16[32,2048]{1,0:T(8,128)(2,1)S(1)}, bf16[32,2048]{1,0:T(8,128)(2,1)S(1)}, u32[]{:S(2)}, u32[]{:S(2)}) collective-permute-start(bf16[32,2048]{1,0:T(8,128)(2,1)S(1)} %collective-permute-done.2.refs_2_), channel_id=1, source_target_pairs={{0,4},{4,0},{8,12},{12,8},{1,5},{5,1},{9,13},{13,9},{2,6},{6,2},{1... | collective-permute-start | bytes 393224 | tf_op jit(solution)/shard_map/ppermute | solution.py:18
  26.1 1.6 %collective-permute-start.7 = (bf16[32,2048]{1,0:T(8,128)(2,1)S(1)}, bf16[32,2048]{1,0:T(8,128)(2,1)S(1)}, u32[]{:S(2)}, u32[]{:S(2)}) collective-permute-start(bf16[32,2048]{1,0:T(8,128)(2,1)S(1)} %collective-permute-done.3.refs_3_), channel_id=1, source_target_pairs={{0,4},{4,0},{8,12},{12,8},{1,5},{5,1},{9,13},{13,9},{2,6},{6,2},{1... | collective-permute-start | bytes 393224 | tf_op jit(solution)/shard_map/ppermute | solution.py:18
  31.0 11.1 %collective-permute-start.8 = (bf16[2,64,1296]{2,1,0:T(8,128)(2,1)S(1)}, bf16[2,64,1296]{2,1,0:T(8,128)(2,1)S(1)}, u32[]{:S(2)}, u32[]{:S(2)}) collective-permute-start(bf16[2,64,1296]{2,1,0:T(8,128)(2,1)S(1)} %get-tuple-element.32.after_ref), channel_id=1, source_target_pairs={{0,1},{1,0},{2,3},{3,2},{4,5},{5,4},{6,7},{7,6},{8,9},{9,8},{10,11... | collective-permute-start | bytes 995336 | tf_op jit(solution)/shard_map/ppermute | solution.py:18
  33.5 22.5 %copy-start.5 = (f32[16]{0:T(128)S(1)}, f32[16]{0:T(128)}, u32[]{:S(2)}) copy-start(f32[16]{0:T(128)} %param.22) | copy-start | bytes 196
  33.5 22.5 %copy-start.6 = (f32[16]{0:T(128)S(1)}, f32[16]{0:T(128)}, u32[]{:S(2)}) copy-start(f32[16]{0:T(128)} %param.23) | copy-start | bytes 196
  33.5 22.5 %copy-start.7 = (f32[16]{0:T(128)S(1)}, f32[16]{0:T(128)}, u32[]{:S(2)}) copy-start(f32[16]{0:T(128)} %param.24) | copy-start | bytes 196
  39.6 24.8 %copy-start = (bf16[1024,8192]{1,0:T(8,128)(2,1)}, bf16[1024,8192]{1,0:T(8,128)(2,1)S(1)}, u32[]{:S(2)}) copy-start(bf16[1024,8192]{1,0:T(8,128)(2,1)S(1)} %get-tuple-element.40.refs_6_.weight_ref) | copy-start | bytes 50331652
  43.4 11.8 %collective-permute-start.9 = (bf16[2,64,1024]{2,1,0:T(8,128)(2,1)S(1)}, bf16[2,64,1024]{2,1,0:T(8,128)(2,1)S(1)}, u32[]{:S(2)}, u32[]{:S(2)}) collective-permute-start(bf16[2,64,1024]{2,1,0:T(8,128)(2,1)S(1)} %get-tuple-element.33), channel_id=1, source_target_pairs={{0,1},{1,0},{2,3},{3,2},{4,5},{5,4},{6,7},{7,6},{8,9},{9,8},{10,11... | collective-permute-start | bytes 786440 | tf_op jit(solution)/shard_map/ppermute | solution.py:18
  45.3 3.2 %collective-permute-start.11 = (f32[64,17]{1,0:T(8,128)S(1)}, f32[64,17]{1,0:T(8,128)S(1)}, u32[]{:S(2)}, u32[]{:S(2)}) collective-permute-start(f32[64,17]{1,0:T(8,128)S(1)} %get-tuple-element.35), channel_id=1, source_target_pairs={{0,4},{4,0},{8,12},{12,8},{1,5},{5,1},{9,13},{13,9},{2,6},{6,2},{1... | collective-permute-start | bytes 13064 | tf_op jit(solution)/shard_map/ppermute | solution.py:18
  45.3 10.6 %collective-permute-start.13 = (bf16[1,64,1296]{2,1,0:T(8,128)(2,1)S(1)}, bf16[1,64,1296]{2,1,0:T(8,128)(2,1)S(1)}, u32[]{:S(2)}, u32[]{:S(2)}) collective-permute-start(bf16[1,64,1296]{2,1,0:T(8,128)(2,1)S(1)} %add_convert_fusion.1), channel_id=1, source_target_pairs={{0,2},{1,3},{2,0},{3,1},{4,6},{5,7},{6,4},{7,5},{8,10},{9,11},{10,... | collective-permute-start | bytes 497672 | tf_op jit(solution)/shard_map/ppermute | solution.py:18
  48.4 4.0 %collective-permute-start.12 = (f32[64,17]{1,0:T(8,128)S(1)}, f32[64,17]{1,0:T(8,128)S(1)}, u32[]{:S(2)}, u32[]{:S(2)}) collective-permute-start(f32[64,17]{1,0:T(8,128)S(1)} %add.43), channel_id=1, source_target_pairs={{0,8},{4,12},{8,0},{12,4},{1,9},{5,13},{9,1},{13,5},{2,10},{6,14},... | collective-permute-start | bytes 13064 | tf_op jit(solution)/shard_map/ppermute | solution.py:18
  55.3 8.0 %collective-permute-start.10 = (bf16[1,64,1024]{2,1,0:T(8,128)(2,1)S(1)}, bf16[1,64,1024]{2,1,0:T(8,128)(2,1)S(1)}, u32[]{:S(2)}, u32[]{:S(2)}) collective-permute-start(bf16[1,64,1024]{2,1,0:T(8,128)(2,1)S(1)} %add_convert_fusion.2.refs_9_), channel_id=1, source_target_pairs={{0,2},{1,3},{2,0},{3,1},{4,6},{5,7},{6,4},{7,5},{8,10},{9,11},{10,... | collective-permute-start | bytes 393224 | tf_op jit(solution)/shard_map/ppermute | solution.py:18
  64.3 2.4 %collective-permute-start.14 = (bf16[1,64,2048]{2,1,0:T(8,128)(2,1)S(1)}, bf16[1,64,2048]{2,1,0:T(8,128)(2,1)S(1)}, u32[]{:S(2)}, u32[]{:S(2)}) collective-permute-start(bf16[1,64,2048]{2,1,0:T(8,128)(2,1)S(1)} %get-tuple-element.41.after_ref), channel_id=1, source_target_pairs={{0,4},{4,0},{8,12},{12,8},{1,5},{5,1},{9,13},{13,9},{2,6},{6,2},{1... | collective-permute-start | bytes 786440 | tf_op jit(solution)/shard_map/ppermute | solution.py:18
  66.0 17.4 %collective-permute-start.16 = (bf16[1,64,2048]{2,1,0:T(8,128)(2,1)S(1)}, bf16[1,64,2048]{2,1,0:T(8,128)(2,1)S(1)}, u32[]{:S(2)}, u32[]{:S(2)}) collective-permute-start(bf16[1,64,2048]{2,1,0:T(8,128)(2,1)S(1)} %slice.63), channel_id=1, source_target_pairs={{0,4},{4,0},{8,12},{12,8},{1,5},{5,1},{9,13},{13,9},{2,6},{6,2},{1... | collective-permute-start | bytes 786440 | tf_op jit(solution)/shard_map/ppermute | solution.py:18
  66.6 2.5 %collective-permute-start.17 = (f32[64,1]{1,0:T(8,128)S(1)}, f32[64,1]{1,0:T(8,128)S(1)}, u32[]{:S(2)}, u32[]{:S(2)}) collective-permute-start(f32[64,1]{1,0:T(8,128)S(1)} %get-tuple-element.43), channel_id=1, source_target_pairs={{0,4},{4,0},{8,12},{12,8},{1,5},{5,1},{9,13},{13,9},{2,6},{6,2},{1... | collective-permute-start | bytes 776 | tf_op jit(solution)/shard_map/ppermute | solution.py:18
  66.7 16.8 %collective-permute-start.15 = (bf16[1,64,2048]{2,1,0:T(8,128)(2,1)S(1)}, bf16[1,64,2048]{2,1,0:T(8,128)(2,1)S(1)}, u32[]{:S(2)}, u32[]{:S(2)}) collective-permute-start(bf16[1,64,2048]{2,1,0:T(8,128)(2,1)S(1)} %add_convert_fusion.after_ref), channel_id=1, source_target_pairs={{0,8},{4,12},{8,0},{12,4},{1,9},{5,13},{9,1},{13,5},{2,10},{6,14},... | collective-permute-start | bytes 786440 | tf_op jit(solution)/shard_map/ppermute | solution.py:18
  69.0 7.6 %collective-permute-start.18 = (f32[64,1]{1,0:T(8,128)S(1)}, f32[64,1]{1,0:T(8,128)S(1)}, u32[]{:S(2)}, u32[]{:S(2)}) collective-permute-start(f32[64,1]{1,0:T(8,128)S(1)} %add.50), channel_id=1, source_target_pairs={{0,8},{4,12},{8,0},{12,4},{1,9},{5,13},{9,1},{13,5},{2,10},{6,14},... | collective-permute-start | bytes 776 | tf_op jit(solution)/shard_map/ppermute | solution.py:18
  (4 other events, 28.5 us)

commit v6 on v5

--- a/solution.py
+++ b/solution.py
@@ -33,15 +33,6 @@
     return sum(((value >> i) & 1) << (bits - 1 - i) for i in range(bits))
 
 
-def gather_relative(parts, axis, order_after):
-    distances = list(reversed(bits_of(lax.axis_size(axis))))
-    parts = [lax.optimization_barrier((part, order_after))[0] for part in parts]
-    blocks = [(0, p, part) for p, part in enumerate(parts)]
-    for distance in distances:
-        blocks += [(i ^ distance, p, swap(part, axis, distance)) for i, p, part in blocks]
-    return [part for _, _, part in blocks], [(i, p) for i, p, _ in blocks]
-
-
 def params(**more):
     return pltpu.CompilerParams(vmem_limit_bytes=VMEM_GRANT, **more)
 
@@ -54,16 +45,19 @@
     return pltpu.with_memory_space_constraint(values, pltpu.HBM)
 
 
-def load_body(pieces, after_ref, *refs):
-    count = len(pieces)
+def load_body(spans, after_ref, *refs):
+    count = len(spans)
     sources, targets, semaphores = refs[:count], refs[count : 2 * count], refs[2 * count]
     copies = []
-    for source, target, parts in zip(sources, targets, pieces):
-        step = source.shape[0] // parts
+    for source, target, (start, rows, parts) in zip(sources, targets, spans):
+        step = rows // parts
         for i in range(parts):
-            at = pl.ds(i * step, step)
             copies.append(
-                pltpu.make_async_copy(source.at[at], target.at[at], semaphores.at[len(copies)])
+                pltpu.make_async_copy(
+                    source.at[pl.ds(start + i * step, step)],
+                    target.at[pl.ds(i * step, step)],
+                    semaphores.at[len(copies)],
+                )
             )
     for copy in copies:
         copy.start()
@@ -72,19 +66,21 @@
 
 
 def load(after, passed, *weights):
-    arrays = (*passed, *weights)
-    pieces = [1] * len(passed) + [8 if w.shape[0] % 128 == 0 else 1 for w in weights]
-    size = sum(a.size * a.dtype.itemsize for a in arrays)
+    weights = [w if isinstance(w, tuple) else (w, 0, w.shape[0]) for w in weights]
+    shapes = [p.shape for p in passed] + [(rows, *w.shape[1:]) for w, _, rows in weights]
+    spans = [(0, p.shape[0], 1) for p in passed]
+    spans += [(start, rows, 8 if rows % 128 == 0 else 1) for _, start, rows in weights]
+    size = sum(rows * w.shape[1] * w.dtype.itemsize for w, _, rows in weights)
     return pl.pallas_call(
-        functools.partial(load_body, pieces),
-        out_shape=tuple(pltpu.VMEM(a.shape, a.dtype) for a in arrays),
-        in_specs=[pl.BlockSpec(memory_space=pl.ANY)] * (1 + len(arrays)),
-        out_specs=tuple(pl.BlockSpec(memory_space=pltpu.VMEM) for _ in arrays),
-        scratch_shapes=[pltpu.SemaphoreType.DMA((sum(pieces),))],
+        functools.partial(load_body, spans),
+        out_shape=tuple(pltpu.VMEM(shape, BF16) for shape in shapes),
+        in_specs=[pl.BlockSpec(memory_space=pl.ANY)] * (1 + len(shapes)),
+        out_specs=tuple(pl.BlockSpec(memory_space=pltpu.VMEM) for _ in shapes),
+        scratch_shapes=[pltpu.SemaphoreType.DMA((sum(parts for _, _, parts in spans),))],
         compiler_params=params(),
         cost_estimate=cost(0, 2 * size),
         name="load",
-    )(after, *passed, *[in_hbm(w) for w in weights])
+    )(after, *passed, *[in_hbm(w) for w, _, _ in weights])
 
 
 def own_columns(rows, streams, rank):
@@ -156,96 +152,104 @@
     )(tenants, scaled, squares, in_hbm(jnp.swapaxes(down, 1, 2)), in_hbm(up))
 
 
-def fill_rows(owners, order, blocks, lhs, semaphores):
+def project_signal_body(owners, order, *refs):
+    blocks, refs = refs[: len(order)], refs[len(order) :]
+    weight_ref, mix_ref, step_ref, send_ref, keep_ref, lhs_ref, semaphores = refs
     rows = blocks[0].shape[0]
     parts = len(blocks) // owners
     copies = []
     for i, block in enumerate(blocks):
-        if order is None:
-            owner, part = i, 0
-        else:
-            distance, part = order[i]
-            owner = reverse_bits(lax.axis_index("head") ^ distance, owners)
-        at = ((owner ^ lax.axis_index("row")) * parts + part) * rows
-        at = pl.multiple_of(at, rows)
-        copies.append(pltpu.make_async_copy(block, lhs.at[pl.ds(at, rows), :], semaphores.at[i]))
+        owner, part = order[i]
+        away = (owner() ^ lax.axis_index("row")) % owners
+        at = pl.multiple_of((away * parts + part) * rows, rows)
+        copies.append(
+            pltpu.make_async_copy(block, lhs_ref.at[pl.ds(at, rows), :], semaphores.at[i])
+        )
     for copy in copies:
         copy.start()
     for copy in copies:
         copy.wait()
-
-
-def put_parts(acc, start, send_ref, keep_ref):
-    rows = send_ref.shape[1]
-    for k in range(acc.shape[0] // rows):
-        target = send_ref if k % 2 else keep_ref
-        target[k // 2, :, start : start + acc.shape[1]] = acc[k * rows : (k + 1) * rows].astype(
-            target.dtype
-        )
-
-
-def project_signal_body(owners, order, count, *refs):
-    blocks, refs = refs[:count], refs[count:]
-    weight_ref, mix_ref, step_ref, send_ref, keep_ref, lhs_ref, semaphores = refs
-    fill_rows(owners, order, blocks, lhs_ref, semaphores)
     lhs = lhs_ref[...]
+
+    def put(acc, start):
+        step = send_ref.shape[1]
+        for k in range(owners):
+            target = send_ref if k % 2 else keep_ref
+            target[k // 2, :, start : start + acc.shape[1]] = acc[k * step : (k + 1) * step].astype(
+                target.dtype
+            )
+
     columns = weight_ref.shape[1]
     tile = min(columns, 512)
     for t in range(0, columns, tile):
-        acc = jnp.dot(lhs, weight_ref[:, t : t + tile], preferred_element_type=F32)
-        put_parts(acc, t, send_ref, keep_ref)
-    acc = jnp.dot(lhs, mix_ref[...], preferred_element_type=F32)
-    put_parts(acc, columns, send_ref, keep_ref)
+        put(jnp.dot(lhs, weight_ref[:, t : t + tile], preferred_element_type=F32), t)
+    put(jnp.dot(lhs, mix_ref[...], preferred_element_type=F32), columns)
     acc = lax.dot_general(lhs, step_ref[...], (((1,), (1,)), ((), ())), preferred_element_type=F32)
-    put_parts(acc, columns + mix_ref.shape[1], send_ref, keep_ref)
-
-
-def project_signal(blocks, order, owners, weight, mix, step):
+    put(acc, columns + mix_ref.shape[1])
+
+
+def project_signal(blocks, order, owners, weight, mix, step, after):
     pieces = len(blocks)
     depth = blocks[0].shape[1]
-    count, rows = owners, pieces * blocks[0].shape[0] // owners
+    rows = pieces * blocks[0].shape[0]
     columns = weight.shape[1] + mix.shape[1] + step.shape[0]
-    half = jax.ShapeDtypeStruct((count // 2, rows, columns), BF16)
+    half = jax.ShapeDtypeStruct((owners // 2, rows // owners, columns), BF16)
     whole = pl.BlockSpec(memory_space=pltpu.VMEM)
+    anywhere = pl.BlockSpec(memory_space=pl.ANY)
+
+    def body(*refs):
+        project_signal_body(owners, order, *refs[:pieces], *refs[pieces + 1 :])
+
     return pl.pallas_call(
-        functools.partial(project_signal_body, owners, order, pieces),
-        out_shape=(
-            half,
-            half,
-            jax.ShapeDtypeStruct((count * rows, depth), BF16),
-        ),
-        in_specs=[pl.BlockSpec(memory_space=pl.ANY)] * pieces + [whole] * 3,
+        body,
+        out_shape=(half, half, jax.ShapeDtypeStruct((rows, depth), BF16)),
+        in_specs=[anywhere] * (pieces + 1) + [whole] * 3,
         out_specs=(whole,) * 3,
         scratch_shapes=[pltpu.SemaphoreType.DMA((pieces,))],
         compiler_params=params(),
-        cost_estimate=cost(2 * count * rows * depth * columns, 2 * depth * columns),
+        cost_estimate=cost(2 * rows * depth * columns, 2 * depth * columns),
         name="project_signal",
-    )(*blocks, weight, mix, step)
-
-
-def project_gate_body(lhs_ref, weight_ref, sums_ref, after_ref, send_ref, keep_ref, out_ref):
+    )(*blocks, after, weight, mix, step)
+
+
+def project_gate_body(groups, *refs):
+    lhs_refs, refs = refs[:groups], refs[groups:]
+    weight_ref, sums_ref, after_ref, send_ref, keep_ref, out_ref = refs
     out_ref[...] = sums_ref[...]
+    rows = send_ref.shape[1]
     columns = weight_ref.shape[1]
     tile = min(columns, 512)
+    first = group_of_own(groups)
     for t in range(0, columns, tile):
-        acc = jnp.dot(lhs_ref[...], weight_ref[:, t : t + tile], preferred_element_type=F32)
-        put_parts(acc, t, send_ref, keep_ref)
+        for g, lhs_ref in enumerate(lhs_refs):
+            acc = jnp.dot(lhs_ref[...], weight_ref[:, t : t + tile], preferred_element_type=F32)
+            pairs = lhs_ref.shape[0] // (2 * rows)
+            for k in range(2 * pairs):
+                target = send_ref if k % 2 else keep_ref
+                at = (first ^ g) * pairs + k // 2
+                target[at, :, t : t + tile] = acc[k * rows : (k + 1) * rows].astype(target.dtype)
+
+
+def group_of_own(groups):
+    if groups == 1:
+        return 0
+    return (lax.axis_index("head") ^ lax.axis_index("row")) // 2
 
 
 def project_gate(rows, lhs, weight, sums, after):
-    count = lhs.shape[0] // rows
+    count = sum(part.shape[0] for part in lhs) // rows
     columns = weight.shape[1]
     half = jax.ShapeDtypeStruct((count // 2, rows, columns), BF16)
     whole = pl.BlockSpec(memory_space=pltpu.VMEM)
     return pl.pallas_call(
-        project_gate_body,
+        functools.partial(project_gate_body, len(lhs)),
         out_shape=(half, half, jax.ShapeDtypeStruct(sums.shape, sums.dtype)),
-        in_specs=[whole, whole, whole, pl.BlockSpec(memory_space=pl.ANY)],
+        in_specs=[whole] * (len(lhs) + 2) + [pl.BlockSpec(memory_space=pl.ANY)],
         out_specs=(whole,) * 3,
         compiler_params=params(),
-        cost_estimate=cost(2 * lhs.size * columns, 2 * weight.size),
+        cost_estimate=cost(2 * count * rows * lhs[0].shape[1] * columns, 2 * weight.size),
         name="project_gate",
-    )(lhs, weight, sums, after)
+    )(*lhs, weight, sums, after)
 
 
 def scatter_rows(received, keep, axis, done=1):
@@ -449,36 +453,44 @@
     )(feeds, b, decay, state)
 
 
-def output_tiles(distances, lhs_ref, weight_ref, out_ref):
+def output_tiles(distances, lhs_ref, weight_refs, out_ref):
     width = out_ref.shape[2]
     tile = min(width, 512)
     for j, distance in enumerate(distances):
         for t in range(0, width, tile):
             at = pl.multiple_of((lax.axis_index("head") ^ distance) * width + t, tile)
-            acc = jnp.dot(lhs_ref[...], weight_ref[:, pl.ds(at, tile)], preferred_element_type=F32)
+            acc, start = 0.0, 0
+            for weight_ref in weight_refs:
+                stop = start + weight_ref.shape[0]
+                acc += jnp.dot(
+                    lhs_ref[:, start:stop],
+                    weight_ref[:, pl.ds(at, tile)],
+                    preferred_element_type=F32,
+                )
+                start = stop
             out_ref[j, :, t : t + tile] = acc.astype(out_ref.dtype)
 
 
 def output_first_body(distances, terms, model_width, *refs):
     term_refs = refs[:terms]
-    sums_ref, result_ref, scale_ref, weight_ref, out_ref, lhs_ref, squares_ref = refs[terms:]
+    sums_ref, result_ref, scale_ref, *weight_refs, out_ref, lhs_ref, squares_ref = refs[terms:]
     total = sum(t[...].astype(F32) for t in term_refs) * inverse_of(sums_ref, model_width)
     gated = result_ref[...] * silu(total)
     squares_ref[...] = jnp.sum(gated * gated, -1, keepdims=True)
     lhs_ref[...] = (gated * scale_ref[...]).astype(lhs_ref.dtype)
-    output_tiles(distances, lhs_ref, weight_ref, out_ref)
-
-
-def output_rest_body(distances, lhs_ref, after_ref, weight_ref, out_ref):
-    output_tiles(distances, lhs_ref, weight_ref, out_ref)
-
-
-def output_parts(distances, weight, width, operands, model_width=None):
+    output_tiles(distances, lhs_ref, weight_refs, out_ref)
+
+
+def output_rest_body(distances, lhs_ref, after_ref, *refs):
+    output_tiles(distances, lhs_ref, refs[:-1], refs[-1])
+
+
+def output_parts(distances, weights, width, operands, model_width=None):
     first = model_width is not None
     rows, depth = operands[0].shape
     count = len(distances)
     whole = pl.BlockSpec(memory_space=pltpu.VMEM)
-    specs = [whole] * (len(operands) + 1)
+    specs = [whole] * (len(operands) + len(weights))
     body = functools.partial(output_rest_body, distances)
     out_shape = [jax.ShapeDtypeStruct((count, rows, width), BF16)]
     if first:
@@ -497,7 +509,7 @@
         compiler_params=params(),
         cost_estimate=cost(2 * rows * depth * width * count, 2 * depth * width * count),
         name="output_first" if first else "output_rest",
-    )(*operands, weight)
+    )(*operands, *weights)
 
 
 def split(values):
@@ -539,32 +551,52 @@
     sums, up_rows = adapt(stream_tenant_index, scaled_flat, squares, adapter_down_weight, adapter_up_weight)
 
     weights = load(sums, [], projection_signal, projection_input_output, projection_gate)
-    if heads_n == rows_n:
-        turn = [
-            (h * rows_n + r, reverse_bits(r, rows_n) * rows_n + h)
-            for h in range(heads_n)
-            for r in range(rows_n)
-        ]
-        blocks, order = gather_relative(
-            [lax.ppermute(scaled[p], ("head", "row"), turn) for p in range(positions)],
-            "head",
-            weights[0],
-        )
+    signal_weights = (*weights[:2], projection_step.T)
+    middle = output_weight.shape[0] // 2
+    if heads_n == rows_n and len(bits_of(rows_n)) == 2:
+        turn = [(h * rows_n + r, r * rows_n + h) for h in range(heads_n) for r in range(rows_n)]
+        turned = [lax.ppermute(scaled[p], ("head", "row"), turn) for p in range(positions)]
+        turned, _ = lax.optimization_barrier((turned, weights[0]))
+        crossed = [swap(part, "head", 2) for part in turned]
+
+        def order(distance):
+            return [
+                (lambda d=d: lax.axis_index("head") ^ d, p)
+                for d in (distance, distance ^ 1)
+                for p in range(positions)
+            ]
+
+        near = turned + [swap(part, "head", 1) for part in turned]
+        near_send, near_keep, near_lhs = project_signal(near, order(0), 2, *signal_weights, sums)
+        (out_early,) = load(near_send, [], (output_weight, 0, middle))
+        near_other = swap(near_send, "row", 1)
+        crossed, _ = lax.optimization_barrier((crossed, near_send))
+        far = crossed + [swap(part, "head", 1) for part in crossed]
+        far_send, far_keep, far_lhs = project_signal(far, order(2), 2, *signal_weights, out_early)
+        far_other = swap(far_send, "row", 1)
+        gate_send, gate_keep, sums = project_gate(
+            rows, [near_lhs, far_lhs], weights[2], sums, far_send
+        )
+        far_keep, out_late = load(gate_send, [far_keep], (output_weight, middle, middle))
+        own = group_of_own(2) == 0
+        pick = [(near_keep, far_keep), (near_other, far_other)]
+        last_send = sum(jnp.where(own, f, n).astype(F32) for n, f in pick).astype(BF16)
+        signal_terms = [jnp.where(own, n, f)[0] for n, f in pick]
+        signal_terms = [swap(last_send, "row", 2)[0]] + signal_terms
     else:
         features = lax.all_gather(scaled_flat, "head", axis=1, tiled=True)
         blocks = lax.all_to_all(features, "row", split_axis=1, concat_axis=0, tiled=True)
         blocks = blocks.reshape(rows_n, rows, depth)
         blocks = [blocks[i] for i in range(rows_n)]
-        order = None
-
-    signal_weight, mix_weight, gate_weight = weights
-    send, keep, lhs = project_signal(
-        blocks, order, rows_n, signal_weight, mix_weight, projection_step.T
-    )
-    received = swap(send, "row", 1)
-    keep, out_weight = load(send, [keep], output_weight)
-    gate_send, gate_keep, sums = project_gate(rows, lhs, gate_weight, sums, received)
-    signal_terms, _ = scatter_rows(received, keep, "row")
+        order = [(lambda i=i: i, 0) for i in range(rows_n)]
+        send, keep, lhs = project_signal(blocks, order, rows_n, *signal_weights, sums)
+        received = swap(send, "row", 1)
+        gate_send, gate_keep, sums = project_gate(rows, [lhs], weights[2], sums, send)
+        keep, out_early, out_late = load(
+            gate_send, [keep], (output_weight, 0, middle), (output_weight, middle, middle)
+        )
+        signal_terms, _ = scatter_rows(received, keep, "row")
+    out_weights = [out_early, out_late]
     gate_terms, gate_last = scatter_rows(swap(gate_send, "row", 1), gate_keep, "row")
     sums = sum_over(sums, "head")
 
@@ -584,20 +616,22 @@
     distances = list(range(heads_n))
     first, out_lhs, gate_squares = output_parts(
         distances[3::4],
-        out_weight,
+        out_weights,
         feature_width,
         [*gate_terms, sums, result, gated_norm_scale[None]],
         model_width,
     )
-    (second,) = output_parts(
-        distances[2::4] + distances[1::4], out_weight, feature_width, [out_lhs, first]
+    (rest,) = output_parts(
+        distances[2::4] + distances[1::4] + distances[0::4],
+        out_weights,
+        feature_width,
+        [out_lhs, first],
     )
-    half = second.shape[0] // 2
-    send = (swap(first, "head", 1).astype(F32) + second[:half].astype(F32)).astype(BF16)
-    received = swap(send, "head", 2)
-    (rest,) = output_parts(distances[0::4], out_weight, feature_width, [out_lhs, send])
-    kept = [swap(second[half:], "head", 1), rest]
-    mixer, _ = scatter_rows(received, kept, "head", done=2)
+    quarter = rest.shape[0] // 3
+    second, third, fourth = (rest[i * quarter : (i + 1) * quarter] for i in range(3))
+    send = (swap(first, "head", 1).astype(F32) + second.astype(F32)).astype(BF16)
+    kept = [swap(third, "head", 1), fourth]
+    mixer, _ = scatter_rows(swap(send, "head", 2), kept, "head", done=2)
     mixer = sum(t.astype(F32) for t in mixer)
     gate_squares = sum_over(gate_squares, "head")
     mixer = mixer * lax.rsqrt(gate_squares / inner_width + EPSILON)

time: 85 us -> 84.7 us (level)
  starting transfers between devices: 25.8 us -> 23.1 us
  Pallas kernels: 31.6 us -> 34 us
  local copies, waits for them, and re-layouts: 7.82 us -> 6.53 us
  waiting for transfers between devices: 16.3 us -> 17.4 us
    ppermute x17 -> x18, starting transfers between devices: 24.5 us -> 21.2 us  [swap(): return lax.ppermute(values, axis, [(i, i ^ distance) for i in range(size)])]
    pallas_call x4 -> x6, Pallas kernels: 14.6 us -> 17.2 us  [the longest x3 11.3 us: load(): pl.pallas_call(functools.partial(load_body, spans), out_shape=tuple((pltp...]
    unnamed x19 -> x23, local copies, waits for them, and re-layouts: 7.43 us -> 6.17 us
    ppermute x17 -> x18, waiting for transfers between devices: 16.3 us -> 17.4 us  [swap(): return lax.ppermute(values, axis, [(i, i ^ distance) for i in range(size)])]
    pallas_call x3 -> x2, Pallas kernels: 3.45 us -> 3.32 us  [output_parts(): pl.pallas_call(body, out_shape=tuple(out_shape), in_specs=specs, out_spec...]
  transfers between devices with their start and end apart: 19 -> 20, of which waited for: 8 -> 5; matrix products, arithmetic and copies ran while one was open for 1% -> 1% of each run, Pallas kernels for 31% -> 39%
where the time goes in v6:
time: 84.7 us; the launch traced here: 84.4 us
  Pallas kernels  34 us (40%)
  starting transfers between devices  23.1 us (27%)
  waiting for transfers between devices  17.4 us (21%)
  local copies, waits for them, and re-layouts  6.53 us (8%)
  other arithmetic  1.79 us (2%)
  between operations  1.63 us (2%)
    ppermute x18, starting transfers between devices, swap(): return lax.ppermute(values, axis, [(i, i ^ distance) for i in range(size)])  21.2 us
    ppermute x18, waiting for transfers between devices, swap(): return lax.ppermute(values, axis, [(i, i ^ distance) for i in range(size)])  17.4 us
    pallas_call x3, Pallas kernels, load(): pl.pallas_call(functools.partial(load_body, spans), out_shape=tuple((pltp...  11.3 us
    unnamed x23, local copies, waits for them, and re-layouts  6.17 us
    pallas_call x1, Pallas kernels, state_write(): pl.pallas_call(state_write_body, out_shape=jax.ShapeDtypeStruct(state.sha...  4.88 us
    pallas_call x1, Pallas kernels, recur(): pl.pallas_call(functools.partial(recur_body, len(terms), group, model_wid...  4.84 us
    pallas_call x2, Pallas kernels, project_signal(): pl.pallas_call(body, out_shape=(half, half, jax.ShapeDtypeStruct((rows, d...  4.69 us
    pallas_call x1, Pallas kernels, adapt(): pl.pallas_call(adapt_body, out_shape=(jax.ShapeDtypeStruct((rows, rank +...  3.72 us
  transfers between devices with their start and end apart: 20, of which 5 were waited for; matrix products, arithmetic and copies ran while one was open for 1% of the time, Pallas kernels for 39%

profile of v6, /device:TPU:0, one launch (start us, length us, event | category | flops | bytes accessed | tf_op | source)
XLA Modules:
  0.0 84.4 jit_solution(16947328850521756705)
XLA Ops:
  0.6 1.1 %fusion.1 = (f32[2,32]{1,0:T(2,128)S(1)}, bf16[2,32,2048]{2,1,0:T(8,128)(2,1)S(1)}) fusion(bf16[32,2,2048]{2,1,0:T(2,128)(2,1)} %param.16, f32[2048]{0:T(1024)} %param.17), kind=kLoop, calls=%fused_computation.4 | loop fusion | flops 655296 | bytes 532736 | tf_op jit(solution)/shard_map/reduce_sum | solution.py:550
  2.5 1.3 %collective-permute-start.1 = (bf16[32,2048]{1,0:T(8,128)(2,1)S(1)}, bf16[32,2048]{1,0:T(8,128)(2,1)}, u32[]{:S(2)}, u32[]{:S(2)}) collective-permute-start(bf16[32,2048]{1,0:T(8,128)(2,1)S(1)} %get-tuple-element.64), channel_id=1, source_target_pairs={{0,0},{1,4},{2,8},{3,12},{4,1},{5,5},{6,9},{7,13},{8,2},{9,6},{10,... | collective-permute-start | bytes 393224 | tf_op jit(solution)/shard_map/ppermute | solution.py:558
  4.5 3.7 %adapt.1 = (f32[64,17]{1,0:T(8,128)S(1)}, bf16[512,1024]{1,0:T(8,128)(2,1)S(1)}) custom-call(s32[32]{0:T(128)S(1)} %copy-done.6, bf16[64,2048]{1,0:T(8,128)(2,1)S(1)} %bitcast.38, f32[64,1]{1,0:T(8,128)S(1)} %reshape.28.squares_ref, bf16[128,16,2048]{2,1,0:T(8,128)(2,1)} %bitcast.47, bf16[128,16,1024]{2,1,0:T(8,128)(2,1)} %up_ref.1), custom_call_target="tpu_custom_call" | custom-call | flops 134217728 | bytes 3145728 | tf_op jit(solution)/shard_map/adapt/pallas_call | solution.py:137
  8.3 3.9 %load.3 = (bf16[2048,1024]{1,0:T(8,128)(2,1)S(1)}, bf16[2048,256]{1,0:T(8,128)(2,1)S(1)}, bf16[2048,1024]{1,0:T(8,128)(2,1)S(1)}) custom-call(f32[64,17]{1,0:T(8,128)S(1)} %get-tuple-element.30.after_ref.refs_4_.refs_3_, bf16[2048,1024]{1,0:T(8,128)(2,1)} %refs_0_.2, bf16[2048,256]{1,0:T(8,128)(2,1)} %refs_1_.2, bf16[2048,1024]{1,0:T(8,128)(2,1)} %refs_2_.1), custom_call_target="tpu_custom_call" | custom-call | bytes 18874368 | tf_op jit(solution)/shard_map/load/pallas_call | solution.py:74
  12.2 2.0 %copy-done.2 = bf16[2048,1024]{1,0:T(8,128)(2,1)} copy-done((bf16[2048,1024]{1,0:T(8,128)(2,1)}, bf16[2048,1024]{1,0:T(8,128)(2,1)S(1)}, u32[]{:S(2)}) %copy-start.2) | copy-done | bytes 4194328
  14.1 5.0 %collective-permute-start.2 = (bf16[32,2048]{1,0:T(8,128)(2,1)S(1)}, bf16[32,2048]{1,0:T(8,128)(2,1)S(1)}, u32[]{:S(2)}, u32[]{:S(2)}) collective-permute-start(bf16[32,2048]{1,0:T(8,128)(2,1)S(1)} %collective-permute-done.refs_0_), channel_id=1, source_target_pairs={{0,4},{4,0},{8,12},{12,8},{1,5},{5,1},{9,13},{13,9},{2,6},{6,2},{1... | collective-permute-start | bytes 393224 | tf_op jit(solution)/shard_map/ppermute | solution.py:18
  19.2 4.2 %collective-permute-start.4 = (bf16[32,2048]{1,0:T(8,128)(2,1)S(1)}, bf16[32,2048]{1,0:T(8,128)(2,1)S(1)}, u32[]{:S(2)}, u32[]{:S(2)}) collective-permute-start(bf16[32,2048]{1,0:T(8,128)(2,1)S(1)} %collective-permute-done.refs_0_), channel_id=1, source_target_pairs={{0,8},{4,12},{8,0},{12,4},{1,9},{5,13},{9,1},{13,5},{2,10},{6,14},... | collective-permute-start | bytes 393224 | tf_op jit(solution)/shard_map/ppermute | solution.py:18
  23.4 2.1 %project_signal.2 = (bf16[1,64,1296]{2,1,0:T(8,128)(2,1)S(1)}, bf16[1,64,1296]{2,1,0:T(8,128)(2,1)S(1)}, bf16[128,2048]{1,0:T(8,128)(2,1)S(1)}) custom-call(bf16[32,2048]{1,0:T(8,128)(2,1)S(1)} %collective-permute-done.refs_0_, bf16[32,2048]{1,0:T(8,128)(2,1)} %collective-permute-done.1.refs_1_, bf16[32,2048]{1,0:T(8,128)(2,1)S(1)} %collective-permute-done.2.refs_2_, ...), custom_call_target="tpu_custom_call" | custom-call | flops 679477248 | bytes 5308416 | tf_op jit(solution)/shard_map/project_signal/pallas_call | solution.py:203
  25.6 2.0 %copy-done = bf16[2048,1024]{1,0:T(8,128)(2,1)} copy-done((bf16[2048,1024]{1,0:T(8,128)(2,1)}, bf16[2048,1024]{1,0:T(8,128)(2,1)S(1)}, u32[]{:S(2)}) %copy-start) | copy-done | bytes 4194328
  27.6 2.6 %collective-permute-done.5.refs_1_ = bf16[32,2048]{1,0:T(8,128)(2,1)S(1)} collective-permute-done((bf16[32,2048]{1,0:T(8,128)(2,1)}, bf16[32,2048]{1,0:T(8,128)(2,1)S(1)}, u32[]{:S(2)}, u32[]{:S(2)}) %collective-permute-start.5) | collective-permute-done | bytes 131104 | tf_op jit(solution)/shard_map/ppermute | solution.py:18
  31.8 3.7 %load.4.refs_4_.refs_6_.refs_0_ = bf16[512,8192]{1,0:T(8,128)(2,1)S(1)} custom-call(bf16[1,64,1296]{2,1,0:T(8,128)(2,1)S(1)} %get-tuple-element.36.after_ref, bf16[1024,8192]{1,0:T(8,128)(2,1)} %refs_1_.3), custom_call_target="tpu_custom_call" | custom-call | bytes 16777216 | tf_op jit(solution)/shard_map/load/pallas_call | solution.py:74
  36.0 2.6 %project_signal.3 = (bf16[1,64,1296]{2,1,0:T(8,128)(2,1)S(1)}, bf16[1,64,1296]{2,1,0:T(8,128)(2,1)S(1)}, bf16[128,2048]{1,0:T(8,128)(2,1)S(1)}) custom-call(bf16[32,2048]{1,0:T(8,128)(2,1)S(1)} %collective-permute-done.4.refs_0_, bf16[32,2048]{1,0:T(8,128)(2,1)S(1)} %collective-permute-done.5.refs_1_, bf16[32,2048]{1,0:T(8,128)(2,1)S(1)} %collective-permute-done.6.refs_2_, ...), custom_call_target="tpu_custom_call" | custom-call | flops 679477248 | bytes 5308416 | tf_op jit(solution)/shard_map/project_signal/pallas_call | solution.py:203
  38.6 1.2 %collective-permute-start.12 = (bf16[1,64,1296]{2,1,0:T(8,128)(2,1)S(1)}, bf16[1,64,1296]{2,1,0:T(8,128)(2,1)S(1)}, u32[]{:S(2)}, u32[]{:S(2)}) collective-permute-start(bf16[1,64,1296]{2,1,0:T(8,128)(2,1)S(1)} %get-tuple-element.41.refs_4_), channel_id=1, source_target_pairs={{0,1},{1,0},{2,3},{3,2},{4,5},{5,4},{6,7},{7,6},{8,9},{9,8},{10,11... | collective-permute-start | bytes 497672 | tf_op jit(solution)/shard_map/ppermute | solution.py:18
  39.8 1.3 %project_gate.1 = (bf16[2,64,1024]{2,1,0:T(8,128)(2,1)S(1)}, bf16[2,64,1024]{2,1,0:T(8,128)(2,1)S(1)}, f32[64,17]{1,0:T(8,128)S(1)}) custom-call(bf16[128,2048]{1,0:T(8,128)(2,1)S(1)} %get-tuple-element.35.refs_0_, bf16[128,2048]{1,0:T(8,128)(2,1)S(1)} %get-tuple-element.39.refs_1_, bf16[2048,1024]{1,0:T(8,128)(2,1)S(1)} %copy-done.3, ...), custom_call_target="tpu_custom_call" | custom-call | flops 1073741824 | bytes 4194304 | tf_op jit(solution)/shard_map/project_gate/pallas_call | solution.py:244
  42.0 3.7 %load.5 = (bf16[1,64,1296]{2,1,0:T(8,128)(2,1)S(1)}, bf16[512,8192]{1,0:T(8,128)(2,1)S(1)}) custom-call(bf16[2,64,1024]{2,1,0:T(8,128)(2,1)S(1)} %get-tuple-element.42.after_ref, bf16[1,64,1296]{2,1,0:T(8,128)(2,1)S(1)} %get-tuple-element.45.refs_0_, bf16[1024,8192]{1,0:T(8,128)(2,1)} %refs_1_.3), custom_call_target="tpu_custom_call" | custom-call | bytes 16777216 | tf_op jit(solution)/shard_map/load/pallas_call | solution.py:74
  45.8 1.8 %collective-permute-start.11 = (f32[64,17]{1,0:T(8,128)S(1)}, f32[64,17]{1,0:T(8,128)S(1)}, u32[]{:S(2)}, u32[]{:S(2)}) collective-permute-start(f32[64,17]{1,0:T(8,128)S(1)} %add.44), channel_id=1, source_target_pairs={{0,8},{4,12},{8,0},{12,4},{1,9},{5,13},{9,1},{13,5},{2,10},{6,14},... | collective-permute-start | bytes 13064 | tf_op jit(solution)/shard_map/ppermute | solution.py:18
  47.7 2.1 %collective-permute-done.11 = f32[64,17]{1,0:T(8,128)S(1)} collective-permute-done((f32[64,17]{1,0:T(8,128)S(1)}, f32[64,17]{1,0:T(8,128)S(1)}, u32[]{:S(2)}, u32[]{:S(2)}) %collective-permute-start.11) | collective-permute-done | bytes 4384 | tf_op jit(solution)/shard_map/ppermute | solution.py:18
  49.9 3.8 %collective-permute-start.14 = (bf16[1,64,1296]{2,1,0:T(8,128)(2,1)S(1)}, bf16[1,64,1296]{2,1,0:T(8,128)(2,1)S(1)}, u32[]{:S(2)}, u32[]{:S(2)}) collective-permute-start(bf16[1,64,1296]{2,1,0:T(8,128)(2,1)S(1)} %add_convert_fusion.1), channel_id=1, source_target_pairs={{0,2},{1,3},{2,0},{3,1},{4,6},{5,7},{6,4},{7,5},{8,10},{9,11},{10,... | collective-permute-start | bytes 497672 | tf_op jit(solution)/shard_map/ppermute | solution.py:18
  54.3 10.7 %collective-permute-done.14 = bf16[1,64,1296]{2,1,0:T(8,128)(2,1)S(1)} collective-permute-done((bf16[1,64,1296]{2,1,0:T(8,128)(2,1)S(1)}, bf16[1,64,1296]{2,1,0:T(8,128)(2,1)S(1)}, u32[]{:S(2)}, u32[]{:S(2)}) %collective-permute-start.14) | collective-permute-done | bytes 165920 | tf_op jit(solution)/shard_map/ppermute | solution.py:18
  65.1 4.8 %recur.1 = (f32[64,1024]{1,0:T(8,128)S(1)}, f32[2,32,1024]{2,1,0:T(8,128)S(1)}, f32[2,32,128]{2,1,0:T(8,128)S(1)}, f32[32,16]{1,0:T(8,128)S(1)}, bf16[32,16,64,128]{3,2,1,0:T(8,128)(2,1)S(1)}) custom-call(s32[1]{0:T(128)} %copy.27.live_ref, bf16[64,1296]{1,0:T(8,128)(2,1)S(1)} %bitcast.41, bf16[64,1296]{1,0:T(8,128)(2,1)S(1)} %select_bitcast_fusion.1.refs_1_, ...), custom_call_target="tpu_custom_call" | custom-call | flops 268435456 | bytes 10485760 | tf_op jit(solution)/shard_map/recur/pallas_call | solution.py:377
  71.0 2.3 %output_rest.1 = bf16[3,64,2048]{2,1,0:T(8,128)(2,1)S(1)} custom-call(bf16[64,1024]{1,0:T(8,128)(2,1)S(1)} %get-tuple-element.52.lhs_ref, bf16[1,64,2048]{2,1,0:T(8,128)(2,1)S(1)} %get-tuple-element.51.after_ref, bf16[512,8192]{1,0:T(8,128)(2,1)S(1)} %load.4.refs_4_.refs_6_.refs_0_, bf16[512,8192]{1,0:T(8,128)(2,1)S(1)} %get-tuple-element.50.refs_7_.refs_1_), custom_call_target="tpu_custom_call" | custom-call | flops 805306368 | bytes 12582912 | tf_op jit(solution)/shard_map/output_rest/pallas_call | solution.py:504
  74.0 1.2 %collective-permute-start.16 = (bf16[1,64,2048]{2,1,0:T(8,128)(2,1)S(1)}, bf16[1,64,2048]{2,1,0:T(8,128)(2,1)S(1)}, u32[]{:S(2)}, u32[]{:S(2)}) collective-permute-start(bf16[1,64,2048]{2,1,0:T(8,128)(2,1)S(1)} %add_convert_fusion), channel_id=1, source_target_pairs={{0,8},{4,12},{8,0},{12,4},{1,9},{5,13},{9,1},{13,5},{2,10},{6,14},... | collective-permute-start | bytes 786440 | tf_op jit(solution)/shard_map/ppermute | solution.py:18
  75.1 1.2 %collective-permute-done.18 = f32[64,1]{1,0:T(8,128)S(1)} collective-permute-done((f32[64,1]{1,0:T(8,128)S(1)}, f32[64,1]{1,0:T(8,128)S(1)}, u32[]{:S(2)}, u32[]{:S(2)}) %collective-permute-start.18) | collective-permute-done | bytes 288 | tf_op jit(solution)/shard_map/ppermute | solution.py:18
  77.4 4.9 %state_write.1 = bf16[32,16,64,128]{3,2,1,0:T(8,128)(2,1)} custom-call(f32[2,32,1024]{2,1,0:T(8,128)S(1)} %get-tuple-element.54.feeds_ref, f32[2,32,128]{2,1,0:T(8,128)S(1)} %get-tuple-element.55.b_ref, f32[32,16,128]{2,1,0:T(8,128)S(1)} %broadcast_in_dim.38.decay_ref, bf16[32,16,64,128]{3,2,1,0:T(8,128)(2,1)S(1)} %get-tuple-element.57.state_ref), custom_call_target="tpu_custom_call" | custom-call | flops 134217728 | bytes 16777216 | tf_op jit(solution)/shard_map/state_write/pallas_call | solution.py:439
  (70 shorter events, 9.6 us)
Async XLA Ops:
  1.8 12.3 %collective-permute-start = (bf16[32,2048]{1,0:T(8,128)(2,1)S(1)}, bf16[32,2048]{1,0:T(8,128)(2,1)S(1)}, u32[]{:S(2)}, u32[]{:S(2)}) collective-permute-start(bf16[32,2048]{1,0:T(8,128)(2,1)S(1)} %get-tuple-element.65), channel_id=1, source_target_pairs={{0,0},{1,4},{2,8},{3,12},{4,1},{5,5},{6,9},{7,13},{8,2},{9,6},{10,... | collective-permute-start | bytes 393224 | tf_op jit(solution)/shard_map/ppermute | solution.py:558
  2.5 11.7 %collective-permute-start.1 = (bf16[32,2048]{1,0:T(8,128)(2,1)S(1)}, bf16[32,2048]{1,0:T(8,128)(2,1)}, u32[]{:S(2)}, u32[]{:S(2)}) collective-permute-start(bf16[32,2048]{1,0:T(8,128)(2,1)S(1)} %get-tuple-element.64), channel_id=1, source_target_pairs={{0,0},{1,4},{2,8},{3,12},{4,1},{5,5},{6,9},{7,13},{8,2},{9,6},{10,... | collective-permute-start | bytes 393224 | tf_op jit(solution)/shard_map/ppermute | solution.py:558
  14.1 9.3 %collective-permute-start.2 = (bf16[32,2048]{1,0:T(8,128)(2,1)S(1)}, bf16[32,2048]{1,0:T(8,128)(2,1)S(1)}, u32[]{:S(2)}, u32[]{:S(2)}) collective-permute-start(bf16[32,2048]{1,0:T(8,128)(2,1)S(1)} %collective-permute-done.refs_0_), channel_id=1, source_target_pairs={{0,4},{4,0},{8,12},{12,8},{1,5},{5,1},{9,13},{13,9},{2,6},{6,2},{1... | collective-permute-start | bytes 393224 | tf_op jit(solution)/shard_map/ppermute | solution.py:18
  19.1 4.3 %collective-permute-start.3 = (bf16[32,2048]{1,0:T(8,128)(2,1)}, bf16[32,2048]{1,0:T(8,128)(2,1)S(1)}, u32[]{:S(2)}, u32[]{:S(2)}) collective-permute-start(bf16[32,2048]{1,0:T(8,128)(2,1)} %collective-permute-done.1.refs_1_), channel_id=1, source_target_pairs={{0,4},{4,0},{8,12},{12,8},{1,5},{5,1},{9,13},{13,9},{2,6},{6,2},{1... | collective-permute-start | bytes 393224 | tf_op jit(solution)/shard_map/ppermute | solution.py:18
  19.2 8.4 %collective-permute-start.4 = (bf16[32,2048]{1,0:T(8,128)(2,1)S(1)}, bf16[32,2048]{1,0:T(8,128)(2,1)S(1)}, u32[]{:S(2)}, u32[]{:S(2)}) collective-permute-start(bf16[32,2048]{1,0:T(8,128)(2,1)S(1)} %collective-permute-done.refs_0_), channel_id=1, source_target_pairs={{0,8},{4,12},{8,0},{12,4},{1,9},{5,13},{9,1},{13,5},{2,10},{6,14},... | collective-permute-start | bytes 393224 | tf_op jit(solution)/shard_map/ppermute | solution.py:18
  23.4 6.8 %collective-permute-start.5 = (bf16[32,2048]{1,0:T(8,128)(2,1)}, bf16[32,2048]{1,0:T(8,128)(2,1)S(1)}, u32[]{:S(2)}, u32[]{:S(2)}) collective-permute-start(bf16[32,2048]{1,0:T(8,128)(2,1)} %collective-permute-done.1.refs_1_), channel_id=1, source_target_pairs={{0,8},{4,12},{8,0},{12,4},{1,9},{5,13},{9,1},{13,5},{2,10},{6,14},... | collective-permute-start | bytes 393224 | tf_op jit(solution)/shard_map/ppermute | solution.py:18
  30.2 5.3 %collective-permute-start.6 = (bf16[32,2048]{1,0:T(8,128)(2,1)S(1)}, bf16[32,2048]{1,0:T(8,128)(2,1)S(1)}, u32[]{:S(2)}, u32[]{:S(2)}) collective-permute-start(bf16[32,2048]{1,0:T(8,128)(2,1)S(1)} %collective-permute-done.4.refs_0_), channel_id=1, source_target_pairs={{0,4},{4,0},{8,12},{12,8},{1,5},{5,1},{9,13},{13,9},{2,6},{6,2},{1... | collective-permute-start | bytes 393224 | tf_op jit(solution)/shard_map/ppermute | solution.py:18
  30.2 5.3 %collective-permute-start.7 = (bf16[32,2048]{1,0:T(8,128)(2,1)S(1)}, bf16[32,2048]{1,0:T(8,128)(2,1)}, u32[]{:S(2)}, u32[]{:S(2)}) collective-permute-start(bf16[32,2048]{1,0:T(8,128)(2,1)S(1)} %collective-permute-done.5.refs_1_), channel_id=1, source_target_pairs={{0,4},{4,0},{8,12},{12,8},{1,5},{5,1},{9,13},{13,9},{2,6},{6,2},{1... | collective-permute-start | bytes 393224 | tf_op jit(solution)/shard_map/ppermute | solution.py:18
  31.4 18.4 %collective-permute-start.13 = (bf16[1,64,1296]{2,1,0:T(8,128)(2,1)S(1)}, bf16[1,64,1296]{2,1,0:T(8,128)(2,1)S(1)}, u32[]{:S(2)}, u32[]{:S(2)}) collective-permute-start(bf16[1,64,1296]{2,1,0:T(8,128)(2,1)S(1)} %get-tuple-element.36.after_ref), channel_id=1, source_target_pairs={{0,1},{1,0},{2,3},{3,2},{4,5},{5,4},{6,7},{7,6},{8,9},{9,8},{10,11... | collective-permute-start | bytes 497672 | tf_op jit(solution)/shard_map/ppermute | solution.py:18
  38.6 11.2 %collective-permute-start.12 = (bf16[1,64,1296]{2,1,0:T(8,128)(2,1)S(1)}, bf16[1,64,1296]{2,1,0:T(8,128)(2,1)S(1)}, u32[]{:S(2)}, u32[]{:S(2)}) collective-permute-start(bf16[1,64,1296]{2,1,0:T(8,128)(2,1)S(1)} %get-tuple-element.41.refs_4_), channel_id=1, source_target_pairs={{0,1},{1,0},{2,3},{3,2},{4,5},{5,4},{6,7},{7,6},{8,9},{9,8},{10,11... | collective-permute-start | bytes 497672 | tf_op jit(solution)/shard_map/ppermute | solution.py:18
  41.1 12.7 %collective-permute-start.8 = (bf16[2,64,1024]{2,1,0:T(8,128)(2,1)S(1)}, bf16[2,64,1024]{2,1,0:T(8,128)(2,1)S(1)}, u32[]{:S(2)}, u32[]{:S(2)}) collective-permute-start(bf16[2,64,1024]{2,1,0:T(8,128)(2,1)S(1)} %get-tuple-element.42.after_ref), channel_id=1, source_target_pairs={{0,1},{1,0},{2,3},{3,2},{4,5},{5,4},{6,7},{7,6},{8,9},{9,8},{10,11... | collective-permute-start | bytes 786440 | tf_op jit(solution)/shard_map/ppermute | solution.py:18
  42.0 3.8 %collective-permute-start.10 = (f32[64,17]{1,0:T(8,128)S(1)}, f32[64,17]{1,0:T(8,128)S(1)}, u32[]{:S(2)}, u32[]{:S(2)}) collective-permute-start(f32[64,17]{1,0:T(8,128)S(1)} %get-tuple-element.44), channel_id=1, source_target_pairs={{0,4},{4,0},{8,12},{12,8},{1,5},{5,1},{9,13},{13,9},{2,6},{6,2},{1... | collective-permute-start | bytes 13064 | tf_op jit(solution)/shard_map/ppermute | solution.py:18
  42.0 23.0 %copy-start.7 = (f32[16]{0:T(128)S(1)}, f32[16]{0:T(128)}, u32[]{:S(2)}) copy-start(f32[16]{0:T(128)} %param.22) | copy-start | bytes 196
  42.0 23.0 %copy-start.8 = (f32[16]{0:T(128)S(1)}, f32[16]{0:T(128)}, u32[]{:S(2)}) copy-start(f32[16]{0:T(128)} %param.23) | copy-start | bytes 196
  42.0 23.0 %copy-start.9 = (f32[16]{0:T(128)S(1)}, f32[16]{0:T(128)}, u32[]{:S(2)}) copy-start(f32[16]{0:T(128)} %param.24) | copy-start | bytes 196
  45.8 24.2 %copy-start.5 = (f32[1024]{0:T(1024)S(1)}, f32[1024]{0:T(1024)}, u32[]{:S(2)}) copy-start(f32[1024]{0:T(1024)} %param.25) | copy-start | bytes 12292
  45.8 4.0 %collective-permute-start.11 = (f32[64,17]{1,0:T(8,128)S(1)}, f32[64,17]{1,0:T(8,128)S(1)}, u32[]{:S(2)}, u32[]{:S(2)}) collective-permute-start(f32[64,17]{1,0:T(8,128)S(1)} %add.44), channel_id=1, source_target_pairs={{0,8},{4,12},{8,0},{12,4},{1,9},{5,13},{9,1},{13,5},{2,10},{6,14},... | collective-permute-start | bytes 13064 | tf_op jit(solution)/shard_map/ppermute | solution.py:18
  49.9 15.1 %collective-permute-start.14 = (bf16[1,64,1296]{2,1,0:T(8,128)(2,1)S(1)}, bf16[1,64,1296]{2,1,0:T(8,128)(2,1)S(1)}, u32[]{:S(2)}, u32[]{:S(2)}) collective-permute-start(bf16[1,64,1296]{2,1,0:T(8,128)(2,1)S(1)} %add_convert_fusion.1), channel_id=1, source_target_pairs={{0,2},{1,3},{2,0},{3,1},{4,6},{5,7},{6,4},{7,5},{8,10},{9,11},{10,... | collective-permute-start | bytes 497672 | tf_op jit(solution)/shard_map/ppermute | solution.py:18
  53.9 16.1 %collective-permute-start.9 = (bf16[1,64,1024]{2,1,0:T(8,128)(2,1)S(1)}, bf16[1,64,1024]{2,1,0:T(8,128)(2,1)S(1)}, u32[]{:S(2)}, u32[]{:S(2)}) collective-permute-start(bf16[1,64,1024]{2,1,0:T(8,128)(2,1)S(1)} %add_convert_fusion.2.refs_9_), channel_id=1, source_target_pairs={{0,2},{1,3},{2,0},{3,1},{4,6},{5,7},{6,4},{7,5},{8,10},{9,11},{10,... | collective-permute-start | bytes 393224 | tf_op jit(solution)/shard_map/ppermute | solution.py:18
  70.9 3.0 %collective-permute-start.15 = (bf16[1,64,2048]{2,1,0:T(8,128)(2,1)S(1)}, bf16[1,64,2048]{2,1,0:T(8,128)(2,1)S(1)}, u32[]{:S(2)}, u32[]{:S(2)}) collective-permute-start(bf16[1,64,2048]{2,1,0:T(8,128)(2,1)S(1)} %get-tuple-element.51.after_ref), channel_id=1, source_target_pairs={{0,4},{4,0},{8,12},{12,8},{1,5},{5,1},{9,13},{13,9},{2,6},{6,2},{1... | collective-permute-start | bytes 786440 | tf_op jit(solution)/shard_map/ppermute | solution.py:18
  73.4 9.8 %collective-permute-start.17 = (bf16[1,64,2048]{2,1,0:T(8,128)(2,1)S(1)}, bf16[1,64,2048]{2,1,0:T(8,128)(2,1)S(1)}, u32[]{:S(2)}, u32[]{:S(2)}) collective-permute-start(bf16[1,64,2048]{2,1,0:T(8,128)(2,1)S(1)} %slice.45), channel_id=1, source_target_pairs={{0,4},{4,0},{8,12},{12,8},{1,5},{5,1},{9,13},{13,9},{2,6},{6,2},{1... | collective-permute-start | bytes 786440 | tf_op jit(solution)/shard_map/ppermute | solution.py:18
  74.0 9.2 %collective-permute-start.16 = (bf16[1,64,2048]{2,1,0:T(8,128)(2,1)S(1)}, bf16[1,64,2048]{2,1,0:T(8,128)(2,1)S(1)}, u32[]{:S(2)}, u32[]{:S(2)}) collective-permute-start(bf16[1,64,2048]{2,1,0:T(8,128)(2,1)S(1)} %add_convert_fusion), channel_id=1, source_target_pairs={{0,8},{4,12},{8,0},{12,4},{1,9},{5,13},{9,1},{13,5},{2,10},{6,14},... | collective-permute-start | bytes 786440 | tf_op jit(solution)/shard_map/ppermute | solution.py:18
  75.1 1.2 %collective-permute-start.18 = (f32[64,1]{1,0:T(8,128)S(1)}, f32[64,1]{1,0:T(8,128)S(1)}, u32[]{:S(2)}, u32[]{:S(2)}) collective-permute-start(f32[64,1]{1,0:T(8,128)S(1)} %get-tuple-element.53), channel_id=1, source_target_pairs={{0,4},{4,0},{8,12},{12,8},{1,5},{5,1},{9,13},{13,9},{2,6},{6,2},{1... | collective-permute-start | bytes 776 | tf_op jit(solution)/shard_map/ppermute | solution.py:18
  76.4 6.6 %collective-permute-start.19 = (f32[64,1]{1,0:T(8,128)S(1)}, f32[64,1]{1,0:T(8,128)S(1)}, u32[]{:S(2)}, u32[]{:S(2)}) collective-permute-start(f32[64,1]{1,0:T(8,128)S(1)} %add.51), channel_id=1, source_target_pairs={{0,8},{4,12},{8,0},{12,4},{1,9},{5,13},{9,1},{13,5},{2,10},{6,14},... | collective-permute-start | bytes 776 | tf_op jit(solution)/shard_map/ppermute | solution.py:18
  (7 other events, 38.4 us)

commit v7 on v6

--- a/solution.py
+++ b/solution.py
@@ -43,6 +43,10 @@
 
 def in_hbm(values):
     return pltpu.with_memory_space_constraint(values, pltpu.HBM)
+
+
+def in_vmem(values):
+    return pltpu.with_memory_space_constraint(values, pltpu.VMEM)
 
 
 def load_body(spans, after_ref, *refs):
@@ -209,13 +213,12 @@
         compiler_params=params(),
         cost_estimate=cost(2 * rows * depth * columns, 2 * depth * columns),
         name="project_signal",
-    )(*blocks, after, weight, mix, step)
+    )(*blocks, after, in_vmem(weight), in_vmem(mix), step)
 
 
 def project_gate_body(groups, *refs):
     lhs_refs, refs = refs[:groups], refs[groups:]
-    weight_ref, sums_ref, after_ref, send_ref, keep_ref, out_ref = refs
-    out_ref[...] = sums_ref[...]
+    weight_ref, after_ref, send_ref, keep_ref = refs
     rows = send_ref.shape[1]
     columns = weight_ref.shape[1]
     tile = min(columns, 512)
@@ -236,20 +239,20 @@
     return (lax.axis_index("head") ^ lax.axis_index("row")) // 2
 
 
-def project_gate(rows, lhs, weight, sums, after):
+def project_gate(rows, lhs, weight, after):
     count = sum(part.shape[0] for part in lhs) // rows
     columns = weight.shape[1]
     half = jax.ShapeDtypeStruct((count // 2, rows, columns), BF16)
     whole = pl.BlockSpec(memory_space=pltpu.VMEM)
     return pl.pallas_call(
         functools.partial(project_gate_body, len(lhs)),
-        out_shape=(half, half, jax.ShapeDtypeStruct(sums.shape, sums.dtype)),
-        in_specs=[whole] * (len(lhs) + 2) + [pl.BlockSpec(memory_space=pl.ANY)],
-        out_specs=(whole,) * 3,
+        out_shape=(half, half),
+        in_specs=[whole] * (len(lhs) + 1) + [pl.BlockSpec(memory_space=pl.ANY)],
+        out_specs=(whole,) * 2,
         compiler_params=params(),
         cost_estimate=cost(2 * count * rows * lhs[0].shape[1] * columns, 2 * weight.size),
         name="project_gate",
-    )(*lhs, weight, sums, after)
+    )(*lhs, in_vmem(weight), after)
 
 
 def scatter_rows(received, keep, axis, done=1):
@@ -509,7 +512,7 @@
         compiler_params=params(),
         cost_estimate=cost(2 * rows * depth * width * count, 2 * depth * width * count),
         name="output_first" if first else "output_rest",
-    )(*operands, *weights)
+    )(*operands, *[in_vmem(w) for w in weights])
 
 
 def split(values):
@@ -555,34 +558,32 @@
     middle = output_weight.shape[0] // 2
     if heads_n == rows_n and len(bits_of(rows_n)) == 2:
         turn = [(h * rows_n + r, r * rows_n + h) for h in range(heads_n) for r in range(rows_n)]
-        turned = [lax.ppermute(scaled[p], ("head", "row"), turn) for p in range(positions)]
+        turned = lax.ppermute(scaled_flat, ("head", "row"), turn)
         turned, _ = lax.optimization_barrier((turned, weights[0]))
-        crossed = [swap(part, "head", 2) for part in turned]
+        crossed = swap(turned, "head", 2)
 
         def order(distance):
             return [
-                (lambda d=d: lax.axis_index("head") ^ d, p)
-                for d in (distance, distance ^ 1)
-                for p in range(positions)
+                (lambda d=d: lax.axis_index("head") ^ d, 0) for d in (distance, distance ^ 1)
             ]
 
-        near = turned + [swap(part, "head", 1) for part in turned]
-        near_send, near_keep, near_lhs = project_signal(near, order(0), 2, *signal_weights, sums)
-        (out_early,) = load(near_send, [], (output_weight, 0, middle))
+        near = [turned, swap(turned, "head", 1)]
+        far = [crossed, swap(crossed, "head", 1)]
+        (out_early,) = load(turned, [], (output_weight, 0, middle))
+        after, _ = lax.optimization_barrier((crossed, out_early))
+        near_send, near_keep, near_lhs = project_signal(near, order(0), 2, *signal_weights, after)
         near_other = swap(near_send, "row", 1)
-        crossed, _ = lax.optimization_barrier((crossed, near_send))
-        far = crossed + [swap(part, "head", 1) for part in crossed]
-        far_send, far_keep, far_lhs = project_signal(far, order(2), 2, *signal_weights, out_early)
+        far_send, far_keep, far_lhs = project_signal(far, order(2), 2, *signal_weights, near_send)
         far_other = swap(far_send, "row", 1)
-        gate_send, gate_keep, sums = project_gate(
-            rows, [near_lhs, far_lhs], weights[2], sums, far_send
-        )
+        gate_send, gate_keep = project_gate(rows, [near_lhs, far_lhs], weights[2], far_send)
         far_keep, out_late = load(gate_send, [far_keep], (output_weight, middle, middle))
         own = group_of_own(2) == 0
         pick = [(near_keep, far_keep), (near_other, far_other)]
         last_send = sum(jnp.where(own, f, n).astype(F32) for n, f in pick).astype(BF16)
         signal_terms = [jnp.where(own, n, f)[0] for n, f in pick]
         signal_terms = [swap(last_send, "row", 2)[0]] + signal_terms
+        sums, _ = lax.optimization_barrier((sums, last_send))
+        sums = sum_over(sums, "head")
     else:
         features = lax.all_gather(scaled_flat, "head", axis=1, tiled=True)
         blocks = lax.all_to_all(features, "row", split_axis=1, concat_axis=0, tiled=True)
@@ -591,14 +592,14 @@
         order = [(lambda i=i: i, 0) for i in range(rows_n)]
         send, keep, lhs = project_signal(blocks, order, rows_n, *signal_weights, sums)
         received = swap(send, "row", 1)
-        gate_send, gate_keep, sums = project_gate(rows, [lhs], weights[2], sums, send)
+        gate_send, gate_keep = project_gate(rows, [lhs], weights[2], send)
+        sums = sum_over(sums, "head")
         keep, out_early, out_late = load(
             gate_send, [keep], (output_weight, 0, middle), (output_weight, middle, middle)
         )
         signal_terms, _ = scatter_rows(received, keep, "row")
     out_weights = [out_early, out_late]
     gate_terms, gate_last = scatter_rows(swap(gate_send, "row", 1), gate_keep, "row")
-    sums = sum_over(sums, "head")
 
     result, feeds, bgate, both, state = recur(
         model_width,

time: 84.7 us -> 81.6 us (0.963)
  starting transfers between devices: 23.1 us -> 16.9 us
  waiting for transfers between devices: 17.4 us -> 22.8 us
  Pallas kernels: 34 us -> 31.3 us
    ppermute x18 -> x15, waiting for transfers between devices: 17.4 us -> 22.8 us  [swap(): return lax.ppermute(values, axis, [(i, i ^ distance) for i in range(size)])]
    ppermute x18 -> x15, starting transfers between devices: 21.2 us -> 16.3 us  [swap(): return lax.ppermute(values, axis, [(i, i ^ distance) for i in range(size)])]
    pallas_call x2, Pallas kernels: 4.69 us -> 2.12 us  [project_signal(): pl.pallas_call(body, out_shape=(half, half, jax.ShapeDtypeStruct((rows, d...]
    ppermute x2 -> x1, starting transfers between devices: 1.97 us -> 0.67 us  [on_device(): turned = lax.ppermute(scaled_flat, ('head', 'row'), turn)]
  transfers between devices with their start and end apart: 20 -> 16, of which waited for: 5 -> 7; matrix products, arithmetic and copies ran while one was open for 1% -> 1% of each run, Pallas kernels for 39% -> 37%
where the time goes in v7:
time: 81.6 us; the launch traced here: 81.3 us
  Pallas kernels  31.3 us (38%)
  waiting for transfers between devices  22.8 us (28%)
  starting transfers between devices  16.9 us (21%)
  local copies, waits for them, and re-layouts  6.95 us (9%)
  other arithmetic  1.76 us (2%)
  between operations  1.58 us (2%)
    ppermute x15, waiting for transfers between devices, swap(): return lax.ppermute(values, axis, [(i, i ^ distance) for i in range(size)])  22.8 us
    ppermute x15, starting transfers between devices, swap(): return lax.ppermute(values, axis, [(i, i ^ distance) for i in range(size)])  16.3 us
    pallas_call x3, Pallas kernels, load(): pl.pallas_call(functools.partial(load_body, spans), out_shape=tuple((pltp...  11.2 us
    unnamed x23, local copies, waits for them, and re-layouts  6.61 us
    pallas_call x1, Pallas kernels, state_write(): pl.pallas_call(state_write_body, out_shape=jax.ShapeDtypeStruct(state.sha...  4.88 us
    pallas_call x1, Pallas kernels, recur(): pl.pallas_call(functools.partial(recur_body, len(terms), group, model_wid...  4.84 us
    pallas_call x1, Pallas kernels, adapt(): pl.pallas_call(adapt_body, out_shape=(jax.ShapeDtypeStruct((rows, rank +...  3.65 us
    pallas_call x2, Pallas kernels, output_parts(): pl.pallas_call(body, out_shape=tuple(out_shape), in_specs=specs, out_spec...  3.29 us
  transfers between devices with their start and end apart: 16, of which 7 were waited for; matrix products, arithmetic and copies ran while one was open for 1% of the time, Pallas kernels for 37%

profile of v7, /device:TPU:0, one launch (start us, length us, event | category | flops | bytes accessed | tf_op | source)
XLA Modules:
  0.0 81.3 jit_solution(15874999084039308662)
XLA Ops:
  0.6 1.1 %fusion.1 = (f32[2,32]{1,0:T(2,128)S(1)}, bf16[2,32,2048]{2,1,0:T(8,128)(2,1)S(1)}) fusion(bf16[32,2,2048]{2,1,0:T(2,128)(2,1)} %param.16, f32[2048]{0:T(1024)} %param.17), kind=kLoop, calls=%fused_computation.4 | loop fusion | flops 655296 | bytes 532736 | tf_op jit(solution)/shard_map/reduce_sum | solution.py:553
  3.2 3.7 %adapt.1 = (f32[64,17]{1,0:T(8,128)S(1)}, bf16[512,1024]{1,0:T(8,128)(2,1)S(1)}) custom-call(s32[32]{0:T(128)S(1)} %copy-done.6, bf16[64,2048]{1,0:T(8,128)(2,1)S(1)} %bitcast.35, f32[64,1]{1,0:T(8,128)S(1)} %reshape.28.squares_ref, bf16[128,16,2048]{2,1,0:T(8,128)(2,1)} %bitcast.44, bf16[128,16,1024]{2,1,0:T(8,128)(2,1)} %up_ref.1), custom_call_target="tpu_custom_call" | custom-call | flops 134217728 | bytes 3145728 | tf_op jit(solution)/shard_map/adapt/pallas_call | solution.py:141
  6.9 3.9 %load.3 = (bf16[2048,1024]{1,0:T(8,128)(2,1)S(1)}, bf16[2048,256]{1,0:T(8,128)(2,1)S(1)}, bf16[2048,1024]{1,0:T(8,128)(2,1)S(1)}) custom-call(f32[64,17]{1,0:T(8,128)S(1)} %get-tuple-element.43.after_ref, bf16[2048,1024]{1,0:T(8,128)(2,1)} %refs_0_.2, bf16[2048,256]{1,0:T(8,128)(2,1)} %refs_1_.2, bf16[2048,1024]{1,0:T(8,128)(2,1)} %refs_2_.1), custom_call_target="tpu_custom_call" | custom-call | bytes 18874368 | tf_op jit(solution)/shard_map/load/pallas_call | solution.py:78
  10.8 2.0 %copy-done = bf16[2048,1024]{1,0:T(8,128)(2,1)} copy-done((bf16[2048,1024]{1,0:T(8,128)(2,1)}, bf16[2048,1024]{1,0:T(8,128)(2,1)S(1)}, u32[]{:S(2)}) %copy-start) | copy-done | bytes 4194328
  12.8 2.0 %copy-done.2 = bf16[2048,1024]{1,0:T(8,128)(2,1)} copy-done((bf16[2048,1024]{1,0:T(8,128)(2,1)}, bf16[2048,1024]{1,0:T(8,128)(2,1)S(1)}, u32[]{:S(2)}) %copy-start.2) | copy-done | bytes 4194328
  14.7 8.0 %collective-permute-start.2 = (bf16[64,2048]{1,0:T(8,128)(2,1)S(1)}, bf16[64,2048]{1,0:T(8,128)(2,1)S(1)}, u32[]{:S(2)}, u32[]{:S(2)}) collective-permute-start(bf16[64,2048]{1,0:T(8,128)(2,1)S(1)} %collective-permute-done.after_ref.refs_0_), channel_id=1, source_target_pairs={{0,8},{4,12},{8,0},{12,4},{1,9},{5,13},{9,1},{13,5},{2,10},{6,14},... | collective-permute-start | bytes 786440 | tf_op jit(solution)/shard_map/ppermute | solution.py:18
  22.7 6.3 %collective-permute-done.2.refs_2_.refs_0_ = bf16[64,2048]{1,0:T(8,128)(2,1)S(1)} collective-permute-done((bf16[64,2048]{1,0:T(8,128)(2,1)S(1)}, bf16[64,2048]{1,0:T(8,128)(2,1)S(1)}, u32[]{:S(2)}, u32[]{:S(2)}) %collective-permute-start.2) | collective-permute-done | bytes 262176 | tf_op jit(solution)/shard_map/ppermute | solution.py:18
  29.7 3.6 %load.4.refs_6_.refs_0_ = bf16[512,8192]{1,0:T(8,128)(2,1)S(1)} custom-call(bf16[64,2048]{1,0:T(8,128)(2,1)S(1)} %collective-permute-done.after_ref.refs_0_, bf16[1024,8192]{1,0:T(8,128)(2,1)} %refs_1_.3), custom_call_target="tpu_custom_call" | custom-call | bytes 16777216 | tf_op jit(solution)/shard_map/load/pallas_call | solution.py:78
  34.4 1.1 %project_signal.2 = (bf16[1,64,1296]{2,1,0:T(8,128)(2,1)S(1)}, bf16[1,64,1296]{2,1,0:T(8,128)(2,1)S(1)}, bf16[128,2048]{1,0:T(8,128)(2,1)S(1)}) custom-call(bf16[64,2048]{1,0:T(8,128)(2,1)S(1)} %collective-permute-done.after_ref.refs_0_, bf16[64,2048]{1,0:T(8,128)(2,1)S(1)} %collective-permute-done.1.refs_1_, ...), custom_call_target="tpu_custom_call" | custom-call | flops 679477248 | bytes 5308416 | tf_op jit(solution)/shard_map/project_signal/pallas_call | solution.py:207
  35.7 1.1 %project_signal.3 = (bf16[1,64,1296]{2,1,0:T(8,128)(2,1)S(1)}, bf16[1,64,1296]{2,1,0:T(8,128)(2,1)S(1)}, bf16[128,2048]{1,0:T(8,128)(2,1)S(1)}) custom-call(bf16[64,2048]{1,0:T(8,128)(2,1)S(1)} %collective-permute-done.2.refs_2_.refs_0_, bf16[64,2048]{1,0:T(8,128)(2,1)S(1)} %collective-permute-done.3.refs_1_, ...), custom_call_target="tpu_custom_call" | custom-call | flops 679477248 | bytes 5308416 | tf_op jit(solution)/shard_map/project_signal/pallas_call | solution.py:207
  36.8 1.9 %collective-permute-start.6 = (bf16[1,64,1296]{2,1,0:T(8,128)(2,1)S(1)}, bf16[1,64,1296]{2,1,0:T(8,128)(2,1)S(1)}, u32[]{:S(2)}, u32[]{:S(2)}) collective-permute-start(bf16[1,64,1296]{2,1,0:T(8,128)(2,1)S(1)} %get-tuple-element.37.refs_3_), channel_id=1, source_target_pairs={{0,1},{1,0},{2,3},{3,2},{4,5},{5,4},{6,7},{7,6},{8,9},{9,8},{10,11... | collective-permute-start | bytes 497672 | tf_op jit(solution)/shard_map/ppermute | solution.py:18
  38.7 1.3 %project_gate.1 = (bf16[2,64,1024]{2,1,0:T(8,128)(2,1)S(1)}, bf16[2,64,1024]{2,1,0:T(8,128)(2,1)S(1)}) custom-call(bf16[128,2048]{1,0:T(8,128)(2,1)S(1)} %get-tuple-element.33.refs_0_, bf16[128,2048]{1,0:T(8,128)(2,1)S(1)} %get-tuple-element.35.refs_1_, bf16[2048,1024]{1,0:T(8,128)(2,1)S(1)} %copy-done.3, bf16[1,64,1296]{2,1,0:T(8,128)(2,1)S(1)} %get-tuple-element.37.refs_3_), custom_call_target="tpu_custom_call" | custom-call | flops 1073741824 | bytes 4194304 | tf_op jit(solution)/shard_map/project_gate/pallas_call | solution.py:247
  40.2 3.7 %load.5 = (bf16[1,64,1296]{2,1,0:T(8,128)(2,1)S(1)}, bf16[512,8192]{1,0:T(8,128)(2,1)S(1)}) custom-call(bf16[2,64,1024]{2,1,0:T(8,128)(2,1)S(1)} %get-tuple-element.38.after_ref, bf16[1,64,1296]{2,1,0:T(8,128)(2,1)S(1)} %get-tuple-element.40.refs_0_, bf16[1024,8192]{1,0:T(8,128)(2,1)} %refs_1_.3), custom_call_target="tpu_custom_call" | custom-call | bytes 16777216 | tf_op jit(solution)/shard_map/load/pallas_call | solution.py:78
  44.0 2.7 %collective-permute-done.6 = bf16[1,64,1296]{2,1,0:T(8,128)(2,1)S(1)} collective-permute-done((bf16[1,64,1296]{2,1,0:T(8,128)(2,1)S(1)}, bf16[1,64,1296]{2,1,0:T(8,128)(2,1)S(1)}, u32[]{:S(2)}, u32[]{:S(2)}) %collective-permute-start.6) | collective-permute-done | bytes 165920 | tf_op jit(solution)/shard_map/ppermute | solution.py:18
  46.9 1.5 %collective-permute-start.10 = (bf16[1,64,1296]{2,1,0:T(8,128)(2,1)S(1)}, bf16[1,64,1296]{2,1,0:T(8,128)(2,1)S(1)}, u32[]{:S(2)}, u32[]{:S(2)}) collective-permute-start(bf16[1,64,1296]{2,1,0:T(8,128)(2,1)S(1)} %add_convert_fusion.1), channel_id=1, source_target_pairs={{0,2},{1,3},{2,0},{3,1},{4,6},{5,7},{6,4},{7,5},{8,10},{9,11},{10,... | collective-permute-start | bytes 497672 | tf_op jit(solution)/shard_map/ppermute | solution.py:18
  48.5 1.4 %collective-permute-start.9 = (f32[64,17]{1,0:T(8,128)S(1)}, f32[64,17]{1,0:T(8,128)S(1)}, u32[]{:S(2)}, u32[]{:S(2)}) collective-permute-start(f32[64,17]{1,0:T(8,128)S(1)} %add.45), channel_id=1, source_target_pairs={{0,8},{4,12},{8,0},{12,4},{1,9},{5,13},{9,1},{13,5},{2,10},{6,14},... | collective-permute-start | bytes 13064 | tf_op jit(solution)/shard_map/ppermute | solution.py:18
  49.9 2.6 %collective-permute-done.9 = f32[64,17]{1,0:T(8,128)S(1)} collective-permute-done((f32[64,17]{1,0:T(8,128)S(1)}, f32[64,17]{1,0:T(8,128)S(1)}, u32[]{:S(2)}, u32[]{:S(2)}) %collective-permute-start.9) | collective-permute-done | bytes 4384 | tf_op jit(solution)/shard_map/ppermute | solution.py:18
  52.4 1.4 %collective-permute-done.4 = bf16[2,64,1024]{2,1,0:T(8,128)(2,1)S(1)} collective-permute-done((bf16[2,64,1024]{2,1,0:T(8,128)(2,1)S(1)}, bf16[2,64,1024]{2,1,0:T(8,128)(2,1)S(1)}, u32[]{:S(2)}, u32[]{:S(2)}) %collective-permute-start.4) | collective-permute-done | bytes 262176 | tf_op jit(solution)/shard_map/ppermute | solution.py:18
  54.0 7.9 %collective-permute-done.10 = bf16[1,64,1296]{2,1,0:T(8,128)(2,1)S(1)} collective-permute-done((bf16[1,64,1296]{2,1,0:T(8,128)(2,1)S(1)}, bf16[1,64,1296]{2,1,0:T(8,128)(2,1)S(1)}, u32[]{:S(2)}, u32[]{:S(2)}) %collective-permute-start.10) | collective-permute-done | bytes 165920 | tf_op jit(solution)/shard_map/ppermute | solution.py:18
  62.0 4.8 %recur.1 = (f32[64,1024]{1,0:T(8,128)S(1)}, f32[2,32,1024]{2,1,0:T(8,128)S(1)}, f32[2,32,128]{2,1,0:T(8,128)S(1)}, f32[32,16]{1,0:T(8,128)S(1)}, bf16[32,16,64,128]{3,2,1,0:T(8,128)(2,1)S(1)}) custom-call(s32[1]{0:T(128)} %copy.40.live_ref, bf16[64,1296]{1,0:T(8,128)(2,1)S(1)} %bitcast.38, bf16[64,1296]{1,0:T(8,128)(2,1)S(1)} %select_bitcast_fusion.1.refs_1_, ...), custom_call_target="tpu_custom_call" | custom-call | flops 268435456 | bytes 10485760 | tf_op jit(solution)/shard_map/recur/pallas_call | solution.py:380
  67.9 2.3 %output_rest.1 = bf16[3,64,2048]{2,1,0:T(8,128)(2,1)S(1)} custom-call(bf16[64,1024]{1,0:T(8,128)(2,1)S(1)} %get-tuple-element.48.lhs_ref, bf16[1,64,2048]{2,1,0:T(8,128)(2,1)S(1)} %get-tuple-element.47.after_ref, bf16[512,8192]{1,0:T(8,128)(2,1)S(1)} %load.4.refs_6_.refs_0_, bf16[512,8192]{1,0:T(8,128)(2,1)S(1)} %get-tuple-element.46.refs_7_.refs_1_), custom_call_target="tpu_custom_call" | custom-call | flops 805306368 | bytes 12582912 | tf_op jit(solution)/shard_map/output_rest/pallas_call | solution.py:507
  70.9 1.6 %collective-permute-start.12 = (bf16[1,64,2048]{2,1,0:T(8,128)(2,1)S(1)}, bf16[1,64,2048]{2,1,0:T(8,128)(2,1)S(1)}, u32[]{:S(2)}, u32[]{:S(2)}) collective-permute-start(bf16[1,64,2048]{2,1,0:T(8,128)(2,1)S(1)} %add_convert_fusion), channel_id=1, source_target_pairs={{0,8},{4,12},{8,0},{12,4},{1,9},{5,13},{9,1},{13,5},{2,10},{6,14},... | collective-permute-start | bytes 786440 | tf_op jit(solution)/shard_map/ppermute | solution.py:18
  72.4 1.2 %collective-permute-done.14 = f32[64,1]{1,0:T(8,128)S(1)} collective-permute-done((f32[64,1]{1,0:T(8,128)S(1)}, f32[64,1]{1,0:T(8,128)S(1)}, u32[]{:S(2)}, u32[]{:S(2)}) %collective-permute-start.14) | collective-permute-done | bytes 288 | tf_op jit(solution)/shard_map/ppermute | solution.py:18
  74.3 4.9 %state_write.1 = bf16[32,16,64,128]{3,2,1,0:T(8,128)(2,1)} custom-call(f32[2,32,1024]{2,1,0:T(8,128)S(1)} %get-tuple-element.50.feeds_ref, f32[2,32,128]{2,1,0:T(8,128)S(1)} %get-tuple-element.51.b_ref, f32[32,16,128]{2,1,0:T(8,128)S(1)} %broadcast_in_dim.38.decay_ref, bf16[32,16,64,128]{3,2,1,0:T(8,128)(2,1)S(1)} %get-tuple-element.53.state_ref), custom_call_target="tpu_custom_call" | custom-call | flops 134217728 | bytes 16777216 | tf_op jit(solution)/shard_map/state_write/pallas_call | solution.py:442
  (61 shorter events, 7.9 us)
Async XLA Ops:
  1.8 13.0 %collective-permute-start = (bf16[64,2048]{1,0:T(8,128)(2,1)S(1)}, bf16[64,2048]{1,0:T(8,128)(2,1)S(1)}, u32[]{:S(2)}, u32[]{:S(2)}) collective-permute-start(bf16[64,2048]{1,0:T(8,128)(2,1)S(1)} %bitcast.34), channel_id=1, source_target_pairs={{0,0},{1,4},{2,8},{3,12},{4,1},{5,5},{6,9},{7,13},{8,2},{9,6},{10,... | collective-permute-start | bytes 786440 | tf_op jit(solution)/shard_map/ppermute | solution.py:561
  14.7 14.3 %collective-permute-start.2 = (bf16[64,2048]{1,0:T(8,128)(2,1)S(1)}, bf16[64,2048]{1,0:T(8,128)(2,1)S(1)}, u32[]{:S(2)}, u32[]{:S(2)}) collective-permute-start(bf16[64,2048]{1,0:T(8,128)(2,1)S(1)} %collective-permute-done.after_ref.refs_0_), channel_id=1, source_target_pairs={{0,8},{4,12},{8,0},{12,4},{1,9},{5,13},{9,1},{13,5},{2,10},{6,14},... | collective-permute-start | bytes 786440 | tf_op jit(solution)/shard_map/ppermute | solution.py:18
  22.7 10.7 %collective-permute-start.1 = (bf16[64,2048]{1,0:T(8,128)(2,1)S(1)}, bf16[64,2048]{1,0:T(8,128)(2,1)S(1)}, u32[]{:S(2)}, u32[]{:S(2)}) collective-permute-start(bf16[64,2048]{1,0:T(8,128)(2,1)S(1)} %collective-permute-done.after_ref.refs_0_), channel_id=1, source_target_pairs={{0,4},{4,0},{8,12},{12,8},{1,5},{5,1},{9,13},{13,9},{2,6},{6,2},{1... | collective-permute-start | bytes 786440 | tf_op jit(solution)/shard_map/ppermute | solution.py:18
  29.1 6.6 %collective-permute-start.3 = (bf16[64,2048]{1,0:T(8,128)(2,1)S(1)}, bf16[64,2048]{1,0:T(8,128)(2,1)S(1)}, u32[]{:S(2)}, u32[]{:S(2)}) collective-permute-start(bf16[64,2048]{1,0:T(8,128)(2,1)S(1)} %collective-permute-done.2.refs_2_.refs_0_), channel_id=1, source_target_pairs={{0,4},{4,0},{8,12},{12,8},{1,5},{5,1},{9,13},{13,9},{2,6},{6,2},{1... | collective-permute-start | bytes 786440 | tf_op jit(solution)/shard_map/ppermute | solution.py:18
  29.7 4.7 %copy-start.1 = (bf16[2048,1024]{1,0:T(8,128)(2,1)S(1)}, bf16[2048,1024]{1,0:T(8,128)(2,1)}, u32[]{:S(2)}) copy-start(bf16[2048,1024]{1,0:T(8,128)(2,1)} %copy-done) | copy-start | bytes 12582916
  29.7 4.7 %copy-start.4 = (bf16[2048,16]{0,1:T(8,128)(2,1)S(1)}, bf16[2048,16]{0,1:T(8,128)(2,1)}, u32[]{:S(2)}) copy-start(bf16[2048,16]{0,1:T(8,128)(2,1)} %param.20) | copy-start | bytes 196612
  33.4 5.3 %copy-start.3 = (bf16[2048,1024]{1,0:T(8,128)(2,1)S(1)}, bf16[2048,1024]{1,0:T(8,128)(2,1)}, u32[]{:S(2)}) copy-start(bf16[2048,1024]{1,0:T(8,128)(2,1)} %copy-done.2) | copy-start | bytes 12582916
  35.5 8.5 %collective-permute-start.7 = (bf16[1,64,1296]{2,1,0:T(8,128)(2,1)S(1)}, bf16[1,64,1296]{2,1,0:T(8,128)(2,1)S(1)}, u32[]{:S(2)}, u32[]{:S(2)}) collective-permute-start(bf16[1,64,1296]{2,1,0:T(8,128)(2,1)S(1)} %get-tuple-element.34.refs_2_), channel_id=1, source_target_pairs={{0,1},{1,0},{2,3},{3,2},{4,5},{5,4},{6,7},{7,6},{8,9},{9,8},{10,11... | collective-permute-start | bytes 497672 | tf_op jit(solution)/shard_map/ppermute | solution.py:18
  36.8 10.0 %collective-permute-start.6 = (bf16[1,64,1296]{2,1,0:T(8,128)(2,1)S(1)}, bf16[1,64,1296]{2,1,0:T(8,128)(2,1)S(1)}, u32[]{:S(2)}, u32[]{:S(2)}) collective-permute-start(bf16[1,64,1296]{2,1,0:T(8,128)(2,1)S(1)} %get-tuple-element.37.refs_3_), channel_id=1, source_target_pairs={{0,1},{1,0},{2,3},{3,2},{4,5},{5,4},{6,7},{7,6},{8,9},{9,8},{10,11... | collective-permute-start | bytes 497672 | tf_op jit(solution)/shard_map/ppermute | solution.py:18
  39.9 13.9 %collective-permute-start.4 = (bf16[2,64,1024]{2,1,0:T(8,128)(2,1)S(1)}, bf16[2,64,1024]{2,1,0:T(8,128)(2,1)S(1)}, u32[]{:S(2)}, u32[]{:S(2)}) collective-permute-start(bf16[2,64,1024]{2,1,0:T(8,128)(2,1)S(1)} %get-tuple-element.38.after_ref), channel_id=1, source_target_pairs={{0,1},{1,0},{2,3},{3,2},{4,5},{5,4},{6,7},{7,6},{8,9},{9,8},{10,11... | collective-permute-start | bytes 786440 | tf_op jit(solution)/shard_map/ppermute | solution.py:18
  40.2 21.7 %copy-start.7 = (f32[16]{0:T(128)S(1)}, f32[16]{0:T(128)}, u32[]{:S(2)}) copy-start(f32[16]{0:T(128)} %param.22) | copy-start | bytes 196
  40.2 21.7 %copy-start.8 = (f32[16]{0:T(128)S(1)}, f32[16]{0:T(128)}, u32[]{:S(2)}) copy-start(f32[16]{0:T(128)} %param.23) | copy-start | bytes 196
  40.2 21.7 %copy-start.9 = (f32[16]{0:T(128)S(1)}, f32[16]{0:T(128)}, u32[]{:S(2)}) copy-start(f32[16]{0:T(128)} %param.24) | copy-start | bytes 196
  43.9 22.9 %copy-start.5 = (f32[1024]{0:T(1024)S(1)}, f32[1024]{0:T(1024)}, u32[]{:S(2)}) copy-start(f32[1024]{0:T(1024)} %param.25) | copy-start | bytes 12292
  46.8 1.6 %collective-permute-start.8 = (f32[64,17]{1,0:T(8,128)S(1)}, f32[64,17]{1,0:T(8,128)S(1)}, u32[]{:S(2)}, u32[]{:S(2)}) collective-permute-start(f32[64,17]{1,0:T(8,128)S(1)} %get-tuple-element.43.after_ref), channel_id=1, source_target_pairs={{0,4},{4,0},{8,12},{12,8},{1,5},{5,1},{9,13},{13,9},{2,6},{6,2},{1... | collective-permute-start | bytes 13064 | tf_op jit(solution)/shard_map/ppermute | solution.py:18
  46.9 15.0 %collective-permute-start.10 = (bf16[1,64,1296]{2,1,0:T(8,128)(2,1)S(1)}, bf16[1,64,1296]{2,1,0:T(8,128)(2,1)S(1)}, u32[]{:S(2)}, u32[]{:S(2)}) collective-permute-start(bf16[1,64,1296]{2,1,0:T(8,128)(2,1)S(1)} %add_convert_fusion.1), channel_id=1, source_target_pairs={{0,2},{1,3},{2,0},{3,1},{4,6},{5,7},{6,4},{7,5},{8,10},{9,11},{10,... | collective-permute-start | bytes 497672 | tf_op jit(solution)/shard_map/ppermute | solution.py:18
  48.5 4.0 %collective-permute-start.9 = (f32[64,17]{1,0:T(8,128)S(1)}, f32[64,17]{1,0:T(8,128)S(1)}, u32[]{:S(2)}, u32[]{:S(2)}) collective-permute-start(f32[64,17]{1,0:T(8,128)S(1)} %add.45), channel_id=1, source_target_pairs={{0,8},{4,12},{8,0},{12,4},{1,9},{5,13},{9,1},{13,5},{2,10},{6,14},... | collective-permute-start | bytes 13064 | tf_op jit(solution)/shard_map/ppermute | solution.py:18
  53.9 13.0 %collective-permute-start.5 = (bf16[1,64,1024]{2,1,0:T(8,128)(2,1)S(1)}, bf16[1,64,1024]{2,1,0:T(8,128)(2,1)S(1)}, u32[]{:S(2)}, u32[]{:S(2)}) collective-permute-start(bf16[1,64,1024]{2,1,0:T(8,128)(2,1)S(1)} %add_convert_fusion.2.refs_9_), channel_id=1, source_target_pairs={{0,2},{1,3},{2,0},{3,1},{4,6},{5,7},{6,4},{7,5},{8,10},{9,11},{10,... | collective-permute-start | bytes 393224 | tf_op jit(solution)/shard_map/ppermute | solution.py:18
  67.8 3.0 %collective-permute-start.11 = (bf16[1,64,2048]{2,1,0:T(8,128)(2,1)S(1)}, bf16[1,64,2048]{2,1,0:T(8,128)(2,1)S(1)}, u32[]{:S(2)}, u32[]{:S(2)}) collective-permute-start(bf16[1,64,2048]{2,1,0:T(8,128)(2,1)S(1)} %get-tuple-element.47.after_ref), channel_id=1, source_target_pairs={{0,4},{4,0},{8,12},{12,8},{1,5},{5,1},{9,13},{13,9},{2,6},{6,2},{1... | collective-permute-start | bytes 786440 | tf_op jit(solution)/shard_map/ppermute | solution.py:18
  70.2 9.8 %collective-permute-start.13 = (bf16[1,64,2048]{2,1,0:T(8,128)(2,1)S(1)}, bf16[1,64,2048]{2,1,0:T(8,128)(2,1)S(1)}, u32[]{:S(2)}, u32[]{:S(2)}) collective-permute-start(bf16[1,64,2048]{2,1,0:T(8,128)(2,1)S(1)} %slice.35), channel_id=1, source_target_pairs={{0,4},{4,0},{8,12},{12,8},{1,5},{5,1},{9,13},{13,9},{2,6},{6,2},{1... | collective-permute-start | bytes 786440 | tf_op jit(solution)/shard_map/ppermute | solution.py:18
  70.9 9.2 %collective-permute-start.12 = (bf16[1,64,2048]{2,1,0:T(8,128)(2,1)S(1)}, bf16[1,64,2048]{2,1,0:T(8,128)(2,1)S(1)}, u32[]{:S(2)}, u32[]{:S(2)}) collective-permute-start(bf16[1,64,2048]{2,1,0:T(8,128)(2,1)S(1)} %add_convert_fusion), channel_id=1, source_target_pairs={{0,8},{4,12},{8,0},{12,4},{1,9},{5,13},{9,1},{13,5},{2,10},{6,14},... | collective-permute-start | bytes 786440 | tf_op jit(solution)/shard_map/ppermute | solution.py:18
  72.4 1.2 %collective-permute-start.14 = (f32[64,1]{1,0:T(8,128)S(1)}, f32[64,1]{1,0:T(8,128)S(1)}, u32[]{:S(2)}, u32[]{:S(2)}) collective-permute-start(f32[64,1]{1,0:T(8,128)S(1)} %get-tuple-element.49), channel_id=1, source_target_pairs={{0,4},{4,0},{8,12},{12,8},{1,5},{5,1},{9,13},{13,9},{2,6},{6,2},{1... | collective-permute-start | bytes 776 | tf_op jit(solution)/shard_map/ppermute | solution.py:18
  73.6 6.2 %collective-permute-start.15 = (f32[64,1]{1,0:T(8,128)S(1)}, f32[64,1]{1,0:T(8,128)S(1)}, u32[]{:S(2)}, u32[]{:S(2)}) collective-permute-start(f32[64,1]{1,0:T(8,128)S(1)} %add.51), channel_id=1, source_target_pairs={{0,8},{4,12},{8,0},{12,4},{1,9},{5,13},{9,1},{13,5},{2,10},{6,14},... | collective-permute-start | bytes 776 | tf_op jit(solution)/shard_map/ppermute | solution.py:18
  74.3 5.9 %copy-start.10 = (bf16[32,2,2048]{2,1,0:T(2,128)(2,1)S(1)}, bf16[32,2,2048]{2,1,0:T(2,128)(2,1)}, u32[]{:S(2)}) copy-start(bf16[32,2,2048]{2,1,0:T(2,128)(2,1)} %param.16) | copy-start | bytes 786436
  (3 other events, 4.6 us)

commit v8 on v7

--- a/solution.py
+++ b/solution.py
@@ -236,7 +236,7 @@
 def group_of_own(groups):
     if groups == 1:
         return 0
-    return (lax.axis_index("head") ^ lax.axis_index("row")) // 2
+    return (lax.axis_index("head") ^ lax.axis_index("row")) >> 1
 
 
 def project_gate(rows, lhs, weight, after):
@@ -553,6 +553,8 @@
     squares = jnp.sum(wide * wide, -1).reshape(rows, 1)
     sums, up_rows = adapt(stream_tenant_index, scaled_flat, squares, adapter_down_weight, adapter_up_weight)
 
+    own = group_of_own(2) == 0
+    sums, own = lax.optimization_barrier((sums, own))
     weights = load(sums, [], projection_signal, projection_input_output, projection_gate)
     signal_weights = (*weights[:2], projection_step.T)
     middle = output_weight.shape[0] // 2
@@ -568,20 +570,24 @@
             ]
 
         near = [turned, swap(turned, "head", 1)]
+        (out_early,) = load(turned, [], (output_weight, 0, middle))
+        crossed, _ = lax.optimization_barrier((crossed, out_early))
         far = [crossed, swap(crossed, "head", 1)]
-        (out_early,) = load(turned, [], (output_weight, 0, middle))
-        after, _ = lax.optimization_barrier((crossed, out_early))
-        near_send, near_keep, near_lhs = project_signal(near, order(0), 2, *signal_weights, after)
+        near_send, near_keep, near_lhs = project_signal(near, order(0), 2, *signal_weights, crossed)
         near_other = swap(near_send, "row", 1)
         far_send, far_keep, far_lhs = project_signal(far, order(2), 2, *signal_weights, near_send)
         far_other = swap(far_send, "row", 1)
         gate_send, gate_keep = project_gate(rows, [near_lhs, far_lhs], weights[2], far_send)
         far_keep, out_late = load(gate_send, [far_keep], (output_weight, middle, middle))
-        own = group_of_own(2) == 0
         pick = [(near_keep, far_keep), (near_other, far_other)]
         last_send = sum(jnp.where(own, f, n).astype(F32) for n, f in pick).astype(BF16)
         signal_terms = [jnp.where(own, n, f)[0] for n, f in pick]
-        signal_terms = [swap(last_send, "row", 2)[0]] + signal_terms
+        last_other = swap(last_send, "row", 2)
+        signal_terms = [last_other[0]] + signal_terms
+        gate_terms = [swap(gate_send, "row", 1), gate_keep]
+        gate_last = sum(t[1:].astype(F32) for t in gate_terms).astype(BF16)
+        gate_last, _ = lax.optimization_barrier((gate_last, last_other))
+        gate_terms = [t[0] for t in [swap(gate_last, "row", 2)] + gate_terms]
         sums, _ = lax.optimization_barrier((sums, last_send))
         sums = sum_over(sums, "head")
     else:
@@ -598,8 +604,8 @@
             gate_send, [keep], (output_weight, 0, middle), (output_weight, middle, middle)
         )
         signal_terms, _ = scatter_rows(received, keep, "row")
+        gate_terms, gate_last = scatter_rows(swap(gate_send, "row", 1), gate_keep, "row")
     out_weights = [out_early, out_late]
-    gate_terms, gate_last = scatter_rows(swap(gate_send, "row", 1), gate_keep, "row")
 
     result, feeds, bgate, both, state = recur(
         model_width,
@@ -622,17 +628,16 @@
         [*gate_terms, sums, result, gated_norm_scale[None]],
         model_width,
     )
-    (rest,) = output_parts(
-        distances[2::4] + distances[1::4] + distances[0::4],
-        out_weights,
-        feature_width,
-        [out_lhs, first],
+    (second,) = output_parts(
+        distances[2::4] + distances[1::4], out_weights, feature_width, [out_lhs, first]
     )
-    quarter = rest.shape[0] // 3
-    second, third, fourth = (rest[i * quarter : (i + 1) * quarter] for i in range(3))
-    send = (swap(first, "head", 1).astype(F32) + second.astype(F32)).astype(BF16)
-    kept = [swap(third, "head", 1), fourth]
-    mixer, _ = scatter_rows(swap(send, "head", 2), kept, "head", done=2)
+    half = second.shape[0] // 2
+    send = (swap(first, "head", 1).astype(F32) + second[:half].astype(F32)).astype(BF16)
+    received = swap(send, "head", 2)
+    (rest,) = output_parts(distances[0::4], out_weights, feature_width, [out_lhs, send])
+    feeds, _ = lax.optimization_barrier((feeds, rest))
+    kept = [swap(second[half:], "head", 1), rest]
+    mixer, _ = scatter_rows(received, kept, "head", done=2)
     mixer = sum(t.astype(F32) for t in mixer)
     gate_squares = sum_over(gate_squares, "head")
     mixer = mixer * lax.rsqrt(gate_squares / inner_width + EPSILON)

time: 81.6 us -> 84.6 us (1.037)
  waiting for transfers between devices: 22.8 us -> 13.3 us
  local copies, waits for them, and re-layouts: 6.95 us -> 14.4 us
  starting transfers between devices: 16.9 us -> 21.7 us
    ppermute x15, waiting for transfers between devices: 22.8 us -> 13.3 us  [swap(): return lax.ppermute(values, axis, [(i, i ^ distance) for i in range(size)])]
    unnamed x23 -> x27, local copies, waits for them, and re-layouts: 6.61 us -> 14.1 us
    ppermute x15, starting transfers between devices: 16.3 us -> 21 us  [swap(): return lax.ppermute(values, axis, [(i, i ^ distance) for i in range(size)])]
    pallas_call x2 -> x3, Pallas kernels: 3.29 us -> 3.41 us  [output_parts(): pl.pallas_call(body, out_shape=tuple(out_shape), in_specs=specs, out_spec...]
  transfers between devices with their start and end apart: 16 -> 16, of which waited for: 7 -> 7; matrix products, arithmetic and copies ran while one was open for 1% -> 1% of each run, Pallas kernels for 37% -> 36%
where the time goes in v8:
time: 84.6 us; the launch traced here: 84.3 us
  Pallas kernels  31.4 us (37%)
  starting transfers between devices  21.7 us (26%)
  local copies, waits for them, and re-layouts  14.4 us (17%)
  waiting for transfers between devices  13.3 us (16%)
  other arithmetic  1.75 us (2%)
  between operations  1.65 us (2%)
    ppermute x15, starting transfers between devices, swap(): return lax.ppermute(values, axis, [(i, i ^ distance) for i in range(size)])  21 us
    unnamed x27, local copies, waits for them, and re-layouts  14.1 us
    ppermute x15, waiting for transfers between devices, swap(): return lax.ppermute(values, axis, [(i, i ^ distance) for i in range(size)])  13.3 us
    pallas_call x3, Pallas kernels, load(): pl.pallas_call(functools.partial(load_body, spans), out_shape=tuple((pltp...  11.1 us
    pallas_call x1, Pallas kernels, state_write(): pl.pallas_call(state_write_body, out_shape=jax.ShapeDtypeStruct(state.sha...  4.86 us
    pallas_call x1, Pallas kernels, recur(): pl.pallas_call(functools.partial(recur_body, len(terms), group, model_wid...  4.84 us
    pallas_call x1, Pallas kernels, adapt(): pl.pallas_call(adapt_body, out_shape=(jax.ShapeDtypeStruct((rows, rank +...  3.81 us
    pallas_call x3, Pallas kernels, output_parts(): pl.pallas_call(body, out_shape=tuple(out_shape), in_specs=specs, out_spec...  3.41 us
  transfers between devices with their start and end apart: 16, of which 7 were waited for; matrix products, arithmetic and copies ran while one was open for 1% of the time, Pallas kernels for 36%

profile of v8, /device:TPU:0, one launch (start us, length us, event | category | flops | bytes accessed | tf_op | source)
XLA Modules:
  0.0 84.3 jit_solution(17109203753447699806)
XLA Ops:
  0.6 1.1 %fusion.1 = (f32[2,32]{1,0:T(2,128)S(1)}, bf16[2,32,2048]{2,1,0:T(8,128)(2,1)S(1)}) fusion(bf16[32,2,2048]{2,1,0:T(2,128)(2,1)} %param.16, f32[2048]{0:T(1024)} %param.17), kind=kLoop, calls=%fused_computation.4 | loop fusion | flops 655296 | bytes 532736 | tf_op jit(solution)/shard_map/reduce_sum | solution.py:553
  3.2 3.8 %adapt.1 = (f32[64,17]{1,0:T(8,128)S(1)}, bf16[512,1024]{1,0:T(8,128)(2,1)S(1)}) custom-call(s32[32]{0:T(128)S(1)} %copy-done.8, bf16[64,2048]{1,0:T(8,128)(2,1)S(1)} %bitcast.35, f32[64,1]{1,0:T(8,128)S(1)} %reshape.28.squares_ref, bf16[128,16,2048]{2,1,0:T(8,128)(2,1)} %bitcast.44, bf16[128,16,1024]{2,1,0:T(8,128)(2,1)} %up_ref.1), custom_call_target="tpu_custom_call" | custom-call | flops 134217728 | bytes 3145728 | tf_op jit(solution)/shard_map/adapt/pallas_call | solution.py:141
  7.0 3.9 %load.3 = (bf16[2048,1024]{1,0:T(8,128)(2,1)S(1)}, bf16[2048,256]{1,0:T(8,128)(2,1)S(1)}, bf16[2048,1024]{1,0:T(8,128)(2,1)S(1)}) custom-call(f32[64,17]{1,0:T(8,128)S(1)} %get-tuple-element.50.after_ref, bf16[2048,1024]{1,0:T(8,128)(2,1)} %refs_0_.2, bf16[2048,256]{1,0:T(8,128)(2,1)} %refs_1_.2, bf16[2048,1024]{1,0:T(8,128)(2,1)} %refs_2_.1), custom_call_target="tpu_custom_call" | custom-call | bytes 18874368 | tf_op jit(solution)/shard_map/load/pallas_call | solution.py:78
  11.0 11.8 %collective-permute-start.2 = (bf16[64,2048]{1,0:T(8,128)(2,1)S(1)}, bf16[64,2048]{1,0:T(8,128)(2,1)S(1)}, u32[]{:S(2)}, u32[]{:S(2)}) collective-permute-start(bf16[64,2048]{1,0:T(8,128)(2,1)S(1)} %collective-permute-done.after_ref.refs_0_), channel_id=1, source_target_pairs={{0,8},{4,12},{8,0},{12,4},{1,9},{5,13},{9,1},{13,5},{2,10},{6,14},... | collective-permute-start | bytes 786440 | tf_op jit(solution)/shard_map/ppermute | solution.py:18
  22.8 3.5 %load.4.refs_6_.refs_0_ = bf16[512,8192]{1,0:T(8,128)(2,1)S(1)} custom-call(bf16[64,2048]{1,0:T(8,128)(2,1)S(1)} %collective-permute-done.after_ref.refs_0_, bf16[1024,8192]{1,0:T(8,128)(2,1)} %refs_1_.3), custom_call_target="tpu_custom_call" | custom-call | bytes 16777216 | tf_op jit(solution)/shard_map/load/pallas_call | solution.py:78
  27.9 1.1 %project_signal.2 = (bf16[1,64,1296]{2,1,0:T(8,128)(2,1)S(1)}, bf16[1,64,1296]{2,1,0:T(8,128)(2,1)S(1)}, bf16[128,2048]{1,0:T(8,128)(2,1)S(1)}) custom-call(bf16[64,2048]{1,0:T(8,128)(2,1)S(1)} %collective-permute-done.after_ref.refs_0_, bf16[64,2048]{1,0:T(8,128)(2,1)S(1)} %collective-permute-done.1.refs_1_, ...), custom_call_target="tpu_custom_call" | custom-call | flops 679477248 | bytes 5308416 | tf_op jit(solution)/shard_map/project_signal/pallas_call | solution.py:207
  29.9 1.1 %project_signal.3 = (bf16[1,64,1296]{2,1,0:T(8,128)(2,1)S(1)}, bf16[1,64,1296]{2,1,0:T(8,128)(2,1)S(1)}, bf16[128,2048]{1,0:T(8,128)(2,1)S(1)}) custom-call(bf16[64,2048]{1,0:T(8,128)(2,1)S(1)} %collective-permute-done.2.refs_2_.refs_0_, bf16[64,2048]{1,0:T(8,128)(2,1)S(1)} %collective-permute-done.3.refs_1_, ...), custom_call_target="tpu_custom_call" | custom-call | flops 679477248 | bytes 5308416 | tf_op jit(solution)/shard_map/project_signal/pallas_call | solution.py:207
  31.0 1.2 %collective-permute-start.5 = (bf16[1,64,1296]{2,1,0:T(8,128)(2,1)S(1)}, bf16[1,64,1296]{2,1,0:T(8,128)(2,1)S(1)}, u32[]{:S(2)}, u32[]{:S(2)}) collective-permute-start(bf16[1,64,1296]{2,1,0:T(8,128)(2,1)S(1)} %get-tuple-element.42.refs_3_), channel_id=1, source_target_pairs={{0,1},{1,0},{2,3},{3,2},{4,5},{5,4},{6,7},{7,6},{8,9},{9,8},{10,11... | collective-permute-start | bytes 497672 | tf_op jit(solution)/shard_map/ppermute | solution.py:18
  32.2 1.3 %project_gate.1 = (bf16[2,64,1024]{2,1,0:T(8,128)(2,1)S(1)}, bf16[2,64,1024]{2,1,0:T(8,128)(2,1)S(1)}) custom-call(bf16[128,2048]{1,0:T(8,128)(2,1)S(1)} %get-tuple-element.38.refs_0_, bf16[128,2048]{1,0:T(8,128)(2,1)S(1)} %get-tuple-element.40.refs_1_, bf16[2048,1024]{1,0:T(8,128)(2,1)S(1)} %get-tuple-element.41.refs_2_, ...), custom_call_target="tpu_custom_call" | custom-call | flops 1073741824 | bytes 4194304 | tf_op jit(solution)/shard_map/project_gate/pallas_call | solution.py:247
  34.4 3.7 %load.5 = (bf16[1,64,1296]{2,1,0:T(8,128)(2,1)S(1)}, bf16[512,8192]{1,0:T(8,128)(2,1)S(1)}) custom-call(bf16[2,64,1024]{2,1,0:T(8,128)(2,1)S(1)} %get-tuple-element.43.after_ref, bf16[1,64,1296]{2,1,0:T(8,128)(2,1)S(1)} %get-tuple-element.46.refs_0_, bf16[1024,8192]{1,0:T(8,128)(2,1)} %refs_1_.3), custom_call_target="tpu_custom_call" | custom-call | bytes 16777216 | tf_op jit(solution)/shard_map/load/pallas_call | solution.py:78
  38.2 2.1 %collective-permute-done.5 = bf16[1,64,1296]{2,1,0:T(8,128)(2,1)S(1)} collective-permute-done((bf16[1,64,1296]{2,1,0:T(8,128)(2,1)S(1)}, bf16[1,64,1296]{2,1,0:T(8,128)(2,1)S(1)}, u32[]{:S(2)}, u32[]{:S(2)}) %collective-permute-start.5) | collective-permute-done | bytes 165920 | tf_op jit(solution)/shard_map/ppermute | solution.py:18
  40.5 2.7 %collective-permute-start.7 = (bf16[1,64,1296]{2,1,0:T(8,128)(2,1)S(1)}, bf16[1,64,1296]{2,1,0:T(8,128)(2,1)S(1)}, u32[]{:S(2)}, u32[]{:S(2)}) collective-permute-start(bf16[1,64,1296]{2,1,0:T(8,128)(2,1)S(1)} %add_convert_fusion.1), channel_id=1, source_target_pairs={{0,2},{1,3},{2,0},{3,1},{4,6},{5,7},{6,4},{7,5},{8,10},{9,11},{10,... | collective-permute-start | bytes 497672 | tf_op jit(solution)/shard_map/ppermute | solution.py:18
  43.6 3.5 %collective-permute-done.10 = f32[64,17]{1,0:T(8,128)S(1)} collective-permute-done((f32[64,17]{1,0:T(8,128)S(1)}, f32[64,17]{1,0:T(8,128)S(1)}, u32[]{:S(2)}, u32[]{:S(2)}) %collective-permute-start.10) | collective-permute-done | bytes 4384 | tf_op jit(solution)/shard_map/ppermute | solution.py:18
  47.1 1.2 %collective-permute-done.4 = bf16[2,64,1024]{2,1,0:T(8,128)(2,1)S(1)} collective-permute-done((bf16[2,64,1024]{2,1,0:T(8,128)(2,1)S(1)}, bf16[2,64,1024]{2,1,0:T(8,128)(2,1)S(1)}, u32[]{:S(2)}, u32[]{:S(2)}) %collective-permute-start.4) | collective-permute-done | bytes 262176 | tf_op jit(solution)/shard_map/ppermute | solution.py:18
  48.3 4.0 %collective-permute-done.7 = bf16[1,64,1296]{2,1,0:T(8,128)(2,1)S(1)} collective-permute-done((bf16[1,64,1296]{2,1,0:T(8,128)(2,1)S(1)}, bf16[1,64,1296]{2,1,0:T(8,128)(2,1)S(1)}, u32[]{:S(2)}, u32[]{:S(2)}) %collective-permute-start.7) | collective-permute-done | bytes 165920 | tf_op jit(solution)/shard_map/ppermute | solution.py:18
  52.3 4.8 %recur.1 = (f32[64,1024]{1,0:T(8,128)S(1)}, f32[2,32,1024]{2,1,0:T(8,128)S(1)}, f32[2,32,128]{2,1,0:T(8,128)S(1)}, f32[32,16]{1,0:T(8,128)S(1)}, bf16[32,16,64,128]{3,2,1,0:T(8,128)(2,1)S(1)}) custom-call(s32[1]{0:T(128)} %copy.40.live_ref, bf16[64,1296]{1,0:T(8,128)(2,1)S(1)} %bitcast.38, bf16[64,1296]{1,0:T(8,128)(2,1)S(1)} %select_bitcast_fusion.1.refs_1_, ...), custom_call_target="tpu_custom_call" | custom-call | flops 268435456 | bytes 10485760 | tf_op jit(solution)/shard_map/recur/pallas_call | solution.py:380
  57.2 3.2 %copy-done.4 = bf16[32,16,64,128]{3,2,1,0:T(8,128)(2,1)} copy-done((bf16[32,16,64,128]{3,2,1,0:T(8,128)(2,1)}, bf16[32,16,64,128]{3,2,1,0:T(8,128)(2,1)S(1)}, u32[]{:S(2)}) %copy-start.4) | copy-done | bytes 8388632
  62.0 1.6 %output_rest.2 = bf16[2,64,2048]{2,1,0:T(8,128)(2,1)S(1)} custom-call(bf16[64,1024]{1,0:T(8,128)(2,1)S(1)} %get-tuple-element.55.lhs_ref, bf16[1,64,2048]{2,1,0:T(8,128)(2,1)S(1)} %get-tuple-element.54.after_ref, bf16[512,8192]{1,0:T(8,128)(2,1)S(1)} %load.4.refs_6_.refs_0_, bf16[512,8192]{1,0:T(8,128)(2,1)S(1)} %get-tuple-element.53.refs_7_.refs_1_), custom_call_target="tpu_custom_call" | custom-call | flops 536870912 | bytes 8388608 | tf_op jit(solution)/shard_map/output_rest/pallas_call | solution.py:507
  63.8 1.9 %collective-permute-start.15 = (f32[64,1]{1,0:T(8,128)S(1)}, f32[64,1]{1,0:T(8,128)S(1)}, u32[]{:S(2)}, u32[]{:S(2)}) collective-permute-start(f32[64,1]{1,0:T(8,128)S(1)} %add.50), channel_id=1, source_target_pairs={{0,8},{4,12},{8,0},{12,4},{1,9},{5,13},{9,1},{13,5},{2,10},{6,14},... | collective-permute-start | bytes 776 | tf_op jit(solution)/shard_map/ppermute | solution.py:18
  66.0 1.7 %collective-permute-done.15 = f32[64,1]{1,0:T(8,128)S(1)} collective-permute-done((f32[64,1]{1,0:T(8,128)S(1)}, f32[64,1]{1,0:T(8,128)S(1)}, u32[]{:S(2)}, u32[]{:S(2)}) %collective-permute-start.15) | collective-permute-done | bytes 288 | tf_op jit(solution)/shard_map/ppermute | solution.py:18
  68.0 3.4 %copy-done.1 = bf16[512,8192]{1,0:T(8,128)(2,1)S(1)} copy-done((bf16[512,8192]{1,0:T(8,128)(2,1)S(1)}, bf16[512,8192]{1,0:T(8,128)(2,1)}, u32[]{:S(2)}) %copy-start.1) | copy-done | bytes 8388632
  71.4 3.4 %copy-done.3 = bf16[512,8192]{1,0:T(8,128)(2,1)S(1)} copy-done((bf16[512,8192]{1,0:T(8,128)(2,1)S(1)}, bf16[512,8192]{1,0:T(8,128)(2,1)}, u32[]{:S(2)}) %copy-start.3) | copy-done | bytes 8388632
  75.7 2.4 %copy-done.5 = bf16[32,16,64,128]{3,2,1,0:T(8,128)(2,1)S(1)} copy-done((bf16[32,16,64,128]{3,2,1,0:T(8,128)(2,1)S(1)}, bf16[32,16,64,128]{3,2,1,0:T(8,128)(2,1)}, u32[]{:S(2)}) %copy-start.5) | copy-done | bytes 8388632
  78.1 4.9 %state_write.1 = bf16[32,16,64,128]{3,2,1,0:T(8,128)(2,1)} custom-call(f32[2,32,1024]{2,1,0:T(8,128)S(1)} %get-tuple-element.58.feeds_ref, f32[2,32,128]{2,1,0:T(8,128)S(1)} %get-tuple-element.59.b_ref, f32[32,16,128]{2,1,0:T(8,128)S(1)} %broadcast_in_dim.38.decay_ref, bf16[32,16,64,128]{3,2,1,0:T(8,128)(2,1)S(1)} %copy-done.5), custom_call_target="tpu_custom_call" | custom-call | flops 134217728 | bytes 16777216 | tf_op jit(solution)/shard_map/state_write/pallas_call | solution.py:442
  (66 shorter events, 9.4 us)
Async XLA Ops:
  1.8 9.2 %collective-permute-start = (bf16[64,2048]{1,0:T(8,128)(2,1)S(1)}, bf16[64,2048]{1,0:T(8,128)(2,1)S(1)}, u32[]{:S(2)}, u32[]{:S(2)}) collective-permute-start(bf16[64,2048]{1,0:T(8,128)(2,1)S(1)} %bitcast.34), channel_id=1, source_target_pairs={{0,0},{1,4},{2,8},{3,12},{4,1},{5,5},{6,9},{7,13},{8,2},{9,6},{10,... | collective-permute-start | bytes 786440 | tf_op jit(solution)/shard_map/ppermute | solution.py:563
  11.0 16.9 %copy-start.6 = (bf16[2048,16]{0,1:T(8,128)(2,1)S(1)}, bf16[2048,16]{0,1:T(8,128)(2,1)}, u32[]{:S(2)}) copy-start(bf16[2048,16]{0,1:T(8,128)(2,1)} %param.20) | copy-start | bytes 196612
  11.0 16.2 %collective-permute-start.2 = (bf16[64,2048]{1,0:T(8,128)(2,1)S(1)}, bf16[64,2048]{1,0:T(8,128)(2,1)S(1)}, u32[]{:S(2)}, u32[]{:S(2)}) collective-permute-start(bf16[64,2048]{1,0:T(8,128)(2,1)S(1)} %collective-permute-done.after_ref.refs_0_), channel_id=1, source_target_pairs={{0,8},{4,12},{8,0},{12,4},{1,9},{5,13},{9,1},{13,5},{2,10},{6,14},... | collective-permute-start | bytes 786440 | tf_op jit(solution)/shard_map/ppermute | solution.py:18
  22.8 5.1 %collective-permute-start.1 = (bf16[64,2048]{1,0:T(8,128)(2,1)S(1)}, bf16[64,2048]{1,0:T(8,128)(2,1)S(1)}, u32[]{:S(2)}, u32[]{:S(2)}) collective-permute-start(bf16[64,2048]{1,0:T(8,128)(2,1)S(1)} %collective-permute-done.after_ref.refs_0_), channel_id=1, source_target_pairs={{0,4},{4,0},{8,12},{12,8},{1,5},{5,1},{9,13},{13,9},{2,6},{6,2},{1... | collective-permute-start | bytes 786440 | tf_op jit(solution)/shard_map/ppermute | solution.py:18
  26.3 35.7 %copy-start = (bf16[512,8192]{1,0:T(8,128)(2,1)}, bf16[512,8192]{1,0:T(8,128)(2,1)S(1)}, u32[]{:S(2)}) copy-start(bf16[512,8192]{1,0:T(8,128)(2,1)S(1)} %load.4.refs_6_.refs_0_) | copy-start | bytes 25165828
  27.2 2.8 %collective-permute-start.3 = (bf16[64,2048]{1,0:T(8,128)(2,1)S(1)}, bf16[64,2048]{1,0:T(8,128)(2,1)S(1)}, u32[]{:S(2)}, u32[]{:S(2)}) collective-permute-start(bf16[64,2048]{1,0:T(8,128)(2,1)S(1)} %collective-permute-done.2.refs_2_.refs_0_), channel_id=1, source_target_pairs={{0,4},{4,0},{8,12},{12,8},{1,5},{5,1},{9,13},{13,9},{2,6},{6,2},{1... | collective-permute-start | bytes 786440 | tf_op jit(solution)/shard_map/ppermute | solution.py:18
  29.0 9.2 %collective-permute-start.6 = (bf16[1,64,1296]{2,1,0:T(8,128)(2,1)S(1)}, bf16[1,64,1296]{2,1,0:T(8,128)(2,1)S(1)}, u32[]{:S(2)}, u32[]{:S(2)}) collective-permute-start(bf16[1,64,1296]{2,1,0:T(8,128)(2,1)S(1)} %get-tuple-element.39.refs_2_), channel_id=1, source_target_pairs={{0,1},{1,0},{2,3},{3,2},{4,5},{5,4},{6,7},{7,6},{8,9},{9,8},{10,11... | collective-permute-start | bytes 497672 | tf_op jit(solution)/shard_map/ppermute | solution.py:18
  31.0 9.3 %collective-permute-start.5 = (bf16[1,64,1296]{2,1,0:T(8,128)(2,1)S(1)}, bf16[1,64,1296]{2,1,0:T(8,128)(2,1)S(1)}, u32[]{:S(2)}, u32[]{:S(2)}) collective-permute-start(bf16[1,64,1296]{2,1,0:T(8,128)(2,1)S(1)} %get-tuple-element.42.refs_3_), channel_id=1, source_target_pairs={{0,1},{1,0},{2,3},{3,2},{4,5},{5,4},{6,7},{7,6},{8,9},{9,8},{10,11... | collective-permute-start | bytes 497672 | tf_op jit(solution)/shard_map/ppermute | solution.py:18
  33.5 14.8 %collective-permute-start.4 = (bf16[2,64,1024]{2,1,0:T(8,128)(2,1)S(1)}, bf16[2,64,1024]{2,1,0:T(8,128)(2,1)S(1)}, u32[]{:S(2)}, u32[]{:S(2)}) collective-permute-start(bf16[2,64,1024]{2,1,0:T(8,128)(2,1)S(1)} %get-tuple-element.43.after_ref), channel_id=1, source_target_pairs={{0,1},{1,0},{2,3},{3,2},{4,5},{5,4},{6,7},{7,6},{8,9},{9,8},{10,11... | collective-permute-start | bytes 786440 | tf_op jit(solution)/shard_map/ppermute | solution.py:18
  34.4 17.9 %copy-start.9 = (f32[16]{0:T(128)S(1)}, f32[16]{0:T(128)}, u32[]{:S(2)}) copy-start(f32[16]{0:T(128)} %param.22) | copy-start | bytes 196
  34.4 17.9 %copy-start.10 = (f32[16]{0:T(128)S(1)}, f32[16]{0:T(128)}, u32[]{:S(2)}) copy-start(f32[16]{0:T(128)} %param.23) | copy-start | bytes 196
  34.4 17.9 %copy-start.11 = (f32[16]{0:T(128)S(1)}, f32[16]{0:T(128)}, u32[]{:S(2)}) copy-start(f32[16]{0:T(128)} %param.24) | copy-start | bytes 196
  38.1 23.9 %copy-start.2 = (bf16[512,8192]{1,0:T(8,128)(2,1)}, bf16[512,8192]{1,0:T(8,128)(2,1)S(1)}, u32[]{:S(2)}) copy-start(bf16[512,8192]{1,0:T(8,128)(2,1)S(1)} %get-tuple-element.53.refs_7_.refs_1_) | copy-start | bytes 25165828
  38.2 22.3 %copy-start.7 = (f32[1024]{0:T(1024)S(1)}, f32[1024]{0:T(1024)}, u32[]{:S(2)}) copy-start(f32[1024]{0:T(1024)} %param.25) | copy-start | bytes 12292
  40.4 2.8 %collective-permute-start.9 = (f32[64,17]{1,0:T(8,128)S(1)}, f32[64,17]{1,0:T(8,128)S(1)}, u32[]{:S(2)}, u32[]{:S(2)}) collective-permute-start(f32[64,17]{1,0:T(8,128)S(1)} %get-tuple-element.50.after_ref), channel_id=1, source_target_pairs={{0,4},{4,0},{8,12},{12,8},{1,5},{5,1},{9,13},{13,9},{2,6},{6,2},{1... | collective-permute-start | bytes 13064 | tf_op jit(solution)/shard_map/ppermute | solution.py:18
  40.5 11.8 %collective-permute-start.7 = (bf16[1,64,1296]{2,1,0:T(8,128)(2,1)S(1)}, bf16[1,64,1296]{2,1,0:T(8,128)(2,1)S(1)}, u32[]{:S(2)}, u32[]{:S(2)}) collective-permute-start(bf16[1,64,1296]{2,1,0:T(8,128)(2,1)S(1)} %add_convert_fusion.1), channel_id=1, source_target_pairs={{0,2},{1,3},{2,0},{3,1},{4,6},{5,7},{6,4},{7,5},{8,10},{9,11},{10,... | collective-permute-start | bytes 497672 | tf_op jit(solution)/shard_map/ppermute | solution.py:18
  43.1 4.0 %collective-permute-start.10 = (f32[64,17]{1,0:T(8,128)S(1)}, f32[64,17]{1,0:T(8,128)S(1)}, u32[]{:S(2)}, u32[]{:S(2)}) collective-permute-start(f32[64,17]{1,0:T(8,128)S(1)} %add.44), channel_id=1, source_target_pairs={{0,8},{4,12},{8,0},{12,4},{1,9},{5,13},{9,1},{13,5},{2,10},{6,14},... | collective-permute-start | bytes 13064 | tf_op jit(solution)/shard_map/ppermute | solution.py:18
  52.3 8.2 %collective-permute-start.8 = (bf16[1,64,1024]{2,1,0:T(8,128)(2,1)S(1)}, bf16[1,64,1024]{2,1,0:T(8,128)(2,1)S(1)}, u32[]{:S(2)}, u32[]{:S(2)}) collective-permute-start(bf16[1,64,1024]{2,1,0:T(8,128)(2,1)S(1)} %add_convert_fusion.2.refs_9_), channel_id=1, source_target_pairs={{0,2},{1,3},{2,0},{3,1},{4,6},{5,7},{6,4},{7,5},{8,10},{9,11},{10,... | collective-permute-start | bytes 393224 | tf_op jit(solution)/shard_map/ppermute | solution.py:18
  61.5 4.3 %collective-permute-start.11 = (bf16[1,64,2048]{2,1,0:T(8,128)(2,1)S(1)}, bf16[1,64,2048]{2,1,0:T(8,128)(2,1)S(1)}, u32[]{:S(2)}, u32[]{:S(2)}) collective-permute-start(bf16[1,64,2048]{2,1,0:T(8,128)(2,1)S(1)} %get-tuple-element.54.after_ref), channel_id=1, source_target_pairs={{0,4},{4,0},{8,12},{12,8},{1,5},{5,1},{9,13},{13,9},{2,6},{6,2},{1... | collective-permute-start | bytes 786440 | tf_op jit(solution)/shard_map/ppermute | solution.py:18
  61.5 2.3 %collective-permute-start.14 = (f32[64,1]{1,0:T(8,128)S(1)}, f32[64,1]{1,0:T(8,128)S(1)}, u32[]{:S(2)}, u32[]{:S(2)}) collective-permute-start(f32[64,1]{1,0:T(8,128)S(1)} %get-tuple-element.56), channel_id=1, source_target_pairs={{0,4},{4,0},{8,12},{12,8},{1,5},{5,1},{9,13},{13,9},{2,6},{6,2},{1... | collective-permute-start | bytes 776 | tf_op jit(solution)/shard_map/ppermute | solution.py:18
  63.7 19.4 %collective-permute-start.13 = (bf16[1,64,2048]{2,1,0:T(8,128)(2,1)S(1)}, bf16[1,64,2048]{2,1,0:T(8,128)(2,1)S(1)}, u32[]{:S(2)}, u32[]{:S(2)}) collective-permute-start(bf16[1,64,2048]{2,1,0:T(8,128)(2,1)S(1)} %slice.27), channel_id=1, source_target_pairs={{0,4},{4,0},{8,12},{12,8},{1,5},{5,1},{9,13},{13,9},{2,6},{6,2},{1... | collective-permute-start | bytes 786440 | tf_op jit(solution)/shard_map/ppermute | solution.py:18
  63.8 4.0 %collective-permute-start.15 = (f32[64,1]{1,0:T(8,128)S(1)}, f32[64,1]{1,0:T(8,128)S(1)}, u32[]{:S(2)}, u32[]{:S(2)}) collective-permute-start(f32[64,1]{1,0:T(8,128)S(1)} %add.50), channel_id=1, source_target_pairs={{0,8},{4,12},{8,0},{12,4},{1,9},{5,13},{9,1},{13,5},{2,10},{6,14},... | collective-permute-start | bytes 776 | tf_op jit(solution)/shard_map/ppermute | solution.py:18
  65.8 17.2 %collective-permute-start.12 = (bf16[1,64,2048]{2,1,0:T(8,128)(2,1)S(1)}, bf16[1,64,2048]{2,1,0:T(8,128)(2,1)S(1)}, u32[]{:S(2)}, u32[]{:S(2)}) collective-permute-start(bf16[1,64,2048]{2,1,0:T(8,128)(2,1)S(1)} %add_convert_fusion.after_ref), channel_id=1, source_target_pairs={{0,8},{4,12},{8,0},{12,4},{1,9},{5,13},{9,1},{13,5},{2,10},{6,14},... | collective-permute-start | bytes 786440 | tf_op jit(solution)/shard_map/ppermute | solution.py:18
  78.1 5.0 %copy-start.12 = (bf16[32,2,2048]{2,1,0:T(2,128)(2,1)S(1)}, bf16[32,2,2048]{2,1,0:T(2,128)(2,1)}, u32[]{:S(2)}) copy-start(bf16[32,2,2048]{2,1,0:T(2,128)(2,1)} %param.16) | copy-start | bytes 786436
  (5 other events, 14.1 us)

commit v9 on v8

--- a/solution.py
+++ b/solution.py
@@ -640,6 +640,7 @@
     mixer, _ = scatter_rows(received, kept, "head", done=2)
     mixer = sum(t.astype(F32) for t in mixer)
     gate_squares = sum_over(gate_squares, "head")
+    gate_squares, _ = lax.optimization_barrier((gate_squares, received))
     mixer = mixer * lax.rsqrt(gate_squares / inner_width + EPSILON)
     mixer = mixer.reshape(positions, streams, feature_width)
     live = jnp.arange(streams) < live_block_rows[0]

time: 84.6 us -> 80.2 us (0.948)
  local copies, waits for them, and re-layouts: 14.4 us -> 1.99 us
  waiting for transfers between devices: 13.3 us -> 21.6 us
    unnamed x27 -> x15, local copies, waits for them, and re-layouts: 14.1 us -> 1.65 us
    ppermute x15, waiting for transfers between devices: 13.3 us -> 21.6 us  [swap(): return lax.ppermute(values, axis, [(i, i ^ distance) for i in range(size)])]
  transfers between devices with their start and end apart: 16 -> 16, of which waited for: 7 -> 8; matrix products, arithmetic and copies ran while one was open for 1% -> 1% of each run, Pallas kernels for 36% -> 38%
where the time goes in v9:
time: 80.2 us; the launch traced here: 80 us
  Pallas kernels  31.4 us (39%)
  starting transfers between devices  21.7 us (27%)
  waiting for transfers between devices  21.6 us (27%)
  local copies, waits for them, and re-layouts  1.99 us (2%)
  other arithmetic  1.77 us (2%)
  between operations  1.59 us (2%)
    ppermute x15, waiting for transfers between devices, swap(): return lax.ppermute(values, axis, [(i, i ^ distance) for i in range(size)])  21.6 us
    ppermute x15, starting transfers between devices, swap(): return lax.ppermute(values, axis, [(i, i ^ distance) for i in range(size)])  21 us
    pallas_call x3, Pallas kernels, load(): pl.pallas_call(functools.partial(load_body, spans), out_shape=tuple((pltp...  11.1 us
    pallas_call x1, Pallas kernels, state_write(): pl.pallas_call(state_write_body, out_shape=jax.ShapeDtypeStruct(state.sha...  4.89 us
    pallas_call x1, Pallas kernels, recur(): pl.pallas_call(functools.partial(recur_body, len(terms), group, model_wid...  4.84 us
    pallas_call x1, Pallas kernels, adapt(): pl.pallas_call(adapt_body, out_shape=(jax.ShapeDtypeStruct((rows, rank +...  3.78 us
    pallas_call x3, Pallas kernels, output_parts(): pl.pallas_call(body, out_shape=tuple(out_shape), in_specs=specs, out_spec...  3.41 us
    pallas_call x2, Pallas kernels, project_signal(): pl.pallas_call(body, out_shape=(half, half, jax.ShapeDtypeStruct((rows, d...  2.13 us
  transfers between devices with their start and end apart: 16, of which 8 were waited for; matrix products, arithmetic and copies ran while one was open for 1% of the time, Pallas kernels for 38%

profile of v9, /device:TPU:0, one launch (start us, length us, event | category | flops | bytes accessed | tf_op | source)
XLA Modules:
  0.0 80.0 jit_solution(5601560437933641161)
XLA Ops:
  0.6 1.1 %fusion.1 = (f32[2,32]{1,0:T(2,128)S(1)}, bf16[2,32,2048]{2,1,0:T(8,128)(2,1)S(1)}) fusion(bf16[32,2,2048]{2,1,0:T(2,128)(2,1)} %param.16, f32[2048]{0:T(1024)} %param.17), kind=kLoop, calls=%fused_computation.4 | loop fusion | flops 655296 | bytes 532736 | tf_op jit(solution)/shard_map/reduce_sum | solution.py:553
  3.2 3.8 %adapt.1 = (f32[64,17]{1,0:T(8,128)S(1)}, bf16[512,1024]{1,0:T(8,128)(2,1)S(1)}) custom-call(s32[32]{0:T(128)S(1)} %copy-done.2, bf16[64,2048]{1,0:T(8,128)(2,1)S(1)} %bitcast.35, f32[64,1]{1,0:T(8,128)S(1)} %reshape.28.squares_ref, bf16[128,16,2048]{2,1,0:T(8,128)(2,1)} %bitcast.44, bf16[128,16,1024]{2,1,0:T(8,128)(2,1)} %up_ref.1), custom_call_target="tpu_custom_call" | custom-call | flops 134217728 | bytes 3145728 | tf_op jit(solution)/shard_map/adapt/pallas_call | solution.py:141
  7.0 3.9 %load.3 = (bf16[2048,1024]{1,0:T(8,128)(2,1)S(1)}, bf16[2048,256]{1,0:T(8,128)(2,1)S(1)}, bf16[2048,1024]{1,0:T(8,128)(2,1)S(1)}) custom-call(f32[64,17]{1,0:T(8,128)S(1)} %get-tuple-element.51.after_ref, bf16[2048,1024]{1,0:T(8,128)(2,1)} %refs_0_.2, bf16[2048,256]{1,0:T(8,128)(2,1)} %refs_1_.2, bf16[2048,1024]{1,0:T(8,128)(2,1)} %refs_2_.1), custom_call_target="tpu_custom_call" | custom-call | bytes 18874368 | tf_op jit(solution)/shard_map/load/pallas_call | solution.py:78
  10.9 11.9 %collective-permute-start.2 = (bf16[64,2048]{1,0:T(8,128)(2,1)S(1)}, bf16[64,2048]{1,0:T(8,128)(2,1)S(1)}, u32[]{:S(2)}, u32[]{:S(2)}) collective-permute-start(bf16[64,2048]{1,0:T(8,128)(2,1)S(1)} %collective-permute-done.after_ref.refs_0_), channel_id=1, source_target_pairs={{0,8},{4,12},{8,0},{12,4},{1,9},{5,13},{9,1},{13,5},{2,10},{6,14},... | collective-permute-start | bytes 786440 | tf_op jit(solution)/shard_map/ppermute | solution.py:18
  22.8 3.5 %load.4.refs_6_.refs_0_ = bf16[512,8192]{1,0:T(8,128)(2,1)S(1)} custom-call(bf16[64,2048]{1,0:T(8,128)(2,1)S(1)} %collective-permute-done.after_ref.refs_0_, bf16[1024,8192]{1,0:T(8,128)(2,1)} %refs_1_.3), custom_call_target="tpu_custom_call" | custom-call | bytes 16777216 | tf_op jit(solution)/shard_map/load/pallas_call | solution.py:78
  27.9 1.1 %project_signal.2 = (bf16[1,64,1296]{2,1,0:T(8,128)(2,1)S(1)}, bf16[1,64,1296]{2,1,0:T(8,128)(2,1)S(1)}, bf16[128,2048]{1,0:T(8,128)(2,1)S(1)}) custom-call(bf16[64,2048]{1,0:T(8,128)(2,1)S(1)} %collective-permute-done.after_ref.refs_0_, bf16[64,2048]{1,0:T(8,128)(2,1)S(1)} %collective-permute-done.1.refs_1_, ...), custom_call_target="tpu_custom_call" | custom-call | flops 679477248 | bytes 5308416 | tf_op jit(solution)/shard_map/project_signal/pallas_call | solution.py:207
  29.9 1.1 %project_signal.3 = (bf16[1,64,1296]{2,1,0:T(8,128)(2,1)S(1)}, bf16[1,64,1296]{2,1,0:T(8,128)(2,1)S(1)}, bf16[128,2048]{1,0:T(8,128)(2,1)S(1)}) custom-call(bf16[64,2048]{1,0:T(8,128)(2,1)S(1)} %collective-permute-done.2.refs_2_.refs_0_, bf16[64,2048]{1,0:T(8,128)(2,1)S(1)} %collective-permute-done.3.refs_1_, ...), custom_call_target="tpu_custom_call" | custom-call | flops 679477248 | bytes 5308416 | tf_op jit(solution)/shard_map/project_signal/pallas_call | solution.py:207
  30.9 1.2 %collective-permute-start.5 = (bf16[1,64,1296]{2,1,0:T(8,128)(2,1)S(1)}, bf16[1,64,1296]{2,1,0:T(8,128)(2,1)S(1)}, u32[]{:S(2)}, u32[]{:S(2)}) collective-permute-start(bf16[1,64,1296]{2,1,0:T(8,128)(2,1)S(1)} %get-tuple-element.43.refs_3_), channel_id=1, source_target_pairs={{0,1},{1,0},{2,3},{3,2},{4,5},{5,4},{6,7},{7,6},{8,9},{9,8},{10,11... | collective-permute-start | bytes 497672 | tf_op jit(solution)/shard_map/ppermute | solution.py:18
  32.2 1.3 %project_gate.1 = (bf16[2,64,1024]{2,1,0:T(8,128)(2,1)S(1)}, bf16[2,64,1024]{2,1,0:T(8,128)(2,1)S(1)}) custom-call(bf16[128,2048]{1,0:T(8,128)(2,1)S(1)} %get-tuple-element.39.refs_0_, bf16[128,2048]{1,0:T(8,128)(2,1)S(1)} %get-tuple-element.41.refs_1_, bf16[2048,1024]{1,0:T(8,128)(2,1)S(1)} %get-tuple-element.42.refs_2_, ...), custom_call_target="tpu_custom_call" | custom-call | flops 1073741824 | bytes 4194304 | tf_op jit(solution)/shard_map/project_gate/pallas_call | solution.py:247
  33.4 0.9 %collective-permute-start.4 = (bf16[2,64,1024]{2,1,0:T(8,128)(2,1)S(1)}, bf16[2,64,1024]{2,1,0:T(8,128)(2,1)S(1)}, u32[]{:S(2)}, u32[]{:S(2)}) collective-permute-start(bf16[2,64,1024]{2,1,0:T(8,128)(2,1)S(1)} %get-tuple-element.44.after_ref), channel_id=1, source_target_pairs={{0,1},{1,0},{2,3},{3,2},{4,5},{5,4},{6,7},{7,6},{8,9},{9,8},{10,11... | collective-permute-start | bytes 786440 | tf_op jit(solution)/shard_map/ppermute | solution.py:18
  34.4 3.7 %load.5 = (bf16[1,64,1296]{2,1,0:T(8,128)(2,1)S(1)}, bf16[512,8192]{1,0:T(8,128)(2,1)S(1)}) custom-call(bf16[2,64,1024]{2,1,0:T(8,128)(2,1)S(1)} %get-tuple-element.44.after_ref, bf16[1,64,1296]{2,1,0:T(8,128)(2,1)S(1)} %get-tuple-element.47.refs_0_, bf16[1024,8192]{1,0:T(8,128)(2,1)} %refs_1_.3), custom_call_target="tpu_custom_call" | custom-call | bytes 16777216 | tf_op jit(solution)/shard_map/load/pallas_call | solution.py:78
  38.1 2.1 %collective-permute-done.5 = bf16[1,64,1296]{2,1,0:T(8,128)(2,1)S(1)} collective-permute-done((bf16[1,64,1296]{2,1,0:T(8,128)(2,1)S(1)}, bf16[1,64,1296]{2,1,0:T(8,128)(2,1)S(1)}, u32[]{:S(2)}, u32[]{:S(2)}) %collective-permute-start.5) | collective-permute-done | bytes 165920 | tf_op jit(solution)/shard_map/ppermute | solution.py:18
  40.4 2.7 %collective-permute-start.7 = (bf16[1,64,1296]{2,1,0:T(8,128)(2,1)S(1)}, bf16[1,64,1296]{2,1,0:T(8,128)(2,1)S(1)}, u32[]{:S(2)}, u32[]{:S(2)}) collective-permute-start(bf16[1,64,1296]{2,1,0:T(8,128)(2,1)S(1)} %add_convert_fusion.1), channel_id=1, source_target_pairs={{0,2},{1,3},{2,0},{3,1},{4,6},{5,7},{6,4},{7,5},{8,10},{9,11},{10,... | collective-permute-start | bytes 497672 | tf_op jit(solution)/shard_map/ppermute | solution.py:18
  43.6 3.5 %collective-permute-done.10 = f32[64,17]{1,0:T(8,128)S(1)} collective-permute-done((f32[64,17]{1,0:T(8,128)S(1)}, f32[64,17]{1,0:T(8,128)S(1)}, u32[]{:S(2)}, u32[]{:S(2)}) %collective-permute-start.10) | collective-permute-done | bytes 4384 | tf_op jit(solution)/shard_map/ppermute | solution.py:18
  47.1 1.1 %collective-permute-done.4 = bf16[2,64,1024]{2,1,0:T(8,128)(2,1)S(1)} collective-permute-done((bf16[2,64,1024]{2,1,0:T(8,128)(2,1)S(1)}, bf16[2,64,1024]{2,1,0:T(8,128)(2,1)S(1)}, u32[]{:S(2)}, u32[]{:S(2)}) %collective-permute-start.4) | collective-permute-done | bytes 262176 | tf_op jit(solution)/shard_map/ppermute | solution.py:18
  48.3 3.9 %collective-permute-done.7 = bf16[1,64,1296]{2,1,0:T(8,128)(2,1)S(1)} collective-permute-done((bf16[1,64,1296]{2,1,0:T(8,128)(2,1)S(1)}, bf16[1,64,1296]{2,1,0:T(8,128)(2,1)S(1)}, u32[]{:S(2)}, u32[]{:S(2)}) %collective-permute-start.7) | collective-permute-done | bytes 165920 | tf_op jit(solution)/shard_map/ppermute | solution.py:18
  52.3 4.8 %recur.1 = (f32[64,1024]{1,0:T(8,128)S(1)}, f32[2,32,1024]{2,1,0:T(8,128)S(1)}, f32[2,32,128]{2,1,0:T(8,128)S(1)}, f32[32,16]{1,0:T(8,128)S(1)}, bf16[32,16,64,128]{3,2,1,0:T(8,128)(2,1)S(1)}) custom-call(s32[1]{0:T(128)} %copy.40.live_ref, bf16[64,1296]{1,0:T(8,128)(2,1)S(1)} %bitcast.38, bf16[64,1296]{1,0:T(8,128)(2,1)S(1)} %select_bitcast_fusion.1.refs_1_, ...), custom_call_target="tpu_custom_call" | custom-call | flops 268435456 | bytes 10485760 | tf_op jit(solution)/shard_map/recur/pallas_call | solution.py:380
  57.1 3.3 %collective-permute-done.8 = bf16[1,64,1024]{2,1,0:T(8,128)(2,1)S(1)} collective-permute-done((bf16[1,64,1024]{2,1,0:T(8,128)(2,1)S(1)}, bf16[1,64,1024]{2,1,0:T(8,128)(2,1)S(1)}, u32[]{:S(2)}, u32[]{:S(2)}) %collective-permute-start.8) | collective-permute-done | bytes 131104 | tf_op jit(solution)/shard_map/ppermute | solution.py:18
  60.5 1.0 %output_first.1 = (bf16[1,64,2048]{2,1,0:T(8,128)(2,1)S(1)}, bf16[64,1024]{1,0:T(8,128)(2,1)S(1)}, f32[64,1]{1,0:T(8,128)S(1)}) custom-call(bf16[64,1024]{1,0:T(8,128)(2,1)S(1)} %bitcast.39, bf16[64,1024]{1,0:T(8,128)(2,1)S(1)} %slice_bitcast_fusion.refs_1_, bf16[64,1024]{1,0:T(8,128)(2,1)S(1)} %slice_bitcast_fusion.1.refs_2_, f32[64,17]{1,0:T(8,128)S(1)} %add.45.refs_3_, ...), custom_call_target="tpu_custom_call" | custom-call | flops 268435456 | bytes 4194304 | tf_op jit(solution)/shard_map/output_first/pallas_call | solution.py:507
  61.5 1.6 %output_rest.2 = bf16[2,64,2048]{2,1,0:T(8,128)(2,1)S(1)} custom-call(bf16[64,1024]{1,0:T(8,128)(2,1)S(1)} %get-tuple-element.56.lhs_ref, bf16[1,64,2048]{2,1,0:T(8,128)(2,1)S(1)} %get-tuple-element.55.after_ref, bf16[512,8192]{1,0:T(8,128)(2,1)S(1)} %load.4.refs_6_.refs_0_, bf16[512,8192]{1,0:T(8,128)(2,1)S(1)} %get-tuple-element.54.refs_7_.refs_1_), custom_call_target="tpu_custom_call" | custom-call | flops 536870912 | bytes 8388608 | tf_op jit(solution)/shard_map/output_rest/pallas_call | solution.py:507
  64.9 1.6 %collective-permute-start.15 = (f32[64,1]{1,0:T(8,128)S(1)}, f32[64,1]{1,0:T(8,128)S(1)}, u32[]{:S(2)}, u32[]{:S(2)}) collective-permute-start(f32[64,1]{1,0:T(8,128)S(1)} %add.50), channel_id=1, source_target_pairs={{0,8},{4,12},{8,0},{12,4},{1,9},{5,13},{9,1},{13,5},{2,10},{6,14},... | collective-permute-start | bytes 776 | tf_op jit(solution)/shard_map/ppermute | solution.py:18
  66.5 6.2 %collective-permute-done.15 = f32[64,1]{1,0:T(8,128)S(1)} collective-permute-done((f32[64,1]{1,0:T(8,128)S(1)}, f32[64,1]{1,0:T(8,128)S(1)}, u32[]{:S(2)}, u32[]{:S(2)}) %collective-permute-start.15) | collective-permute-done | bytes 288 | tf_op jit(solution)/shard_map/ppermute | solution.py:18
  73.7 4.9 %state_write.1 = bf16[32,16,64,128]{3,2,1,0:T(8,128)(2,1)} custom-call(f32[2,32,1024]{2,1,0:T(8,128)S(1)} %get-tuple-element.60.feeds_ref, f32[2,32,128]{2,1,0:T(8,128)S(1)} %get-tuple-element.61.b_ref, f32[32,16,128]{2,1,0:T(8,128)S(1)} %broadcast_in_dim.38.decay_ref, bf16[32,16,64,128]{3,2,1,0:T(8,128)(2,1)S(1)} %get-tuple-element.63.state_ref), custom_call_target="tpu_custom_call" | custom-call | flops 134217728 | bytes 16777216 | tf_op jit(solution)/shard_map/state_write/pallas_call | solution.py:442
  79.0 1.0 %copy.35 = bf16[32,2,2048]{2,1,0:T(2,128)(2,1)} copy(bf16[32,2,2048]{2,0,1:T(8,128)(2,1)S(1)} %fusion.3) | data formatting | bytes 524288
  (55 shorter events, 7.3 us)
Async XLA Ops:
  1.8 9.1 %collective-permute-start = (bf16[64,2048]{1,0:T(8,128)(2,1)S(1)}, bf16[64,2048]{1,0:T(8,128)(2,1)S(1)}, u32[]{:S(2)}, u32[]{:S(2)}) collective-permute-start(bf16[64,2048]{1,0:T(8,128)(2,1)S(1)} %bitcast.34), channel_id=1, source_target_pairs={{0,0},{1,4},{2,8},{3,12},{4,1},{5,5},{6,9},{7,13},{8,2},{9,6},{10,... | collective-permute-start | bytes 786440 | tf_op jit(solution)/shard_map/ppermute | solution.py:563
  2.6 0.7 copy-start.2
  10.9 16.9 %copy-start = (bf16[2048,16]{0,1:T(8,128)(2,1)S(1)}, bf16[2048,16]{0,1:T(8,128)(2,1)}, u32[]{:S(2)}) copy-start(bf16[2048,16]{0,1:T(8,128)(2,1)} %param.20) | copy-start | bytes 196612
  10.9 16.3 %collective-permute-start.2 = (bf16[64,2048]{1,0:T(8,128)(2,1)S(1)}, bf16[64,2048]{1,0:T(8,128)(2,1)S(1)}, u32[]{:S(2)}, u32[]{:S(2)}) collective-permute-start(bf16[64,2048]{1,0:T(8,128)(2,1)S(1)} %collective-permute-done.after_ref.refs_0_), channel_id=1, source_target_pairs={{0,8},{4,12},{8,0},{12,4},{1,9},{5,13},{9,1},{13,5},{2,10},{6,14},... | collective-permute-start | bytes 786440 | tf_op jit(solution)/shard_map/ppermute | solution.py:18
  22.8 5.0 %collective-permute-start.1 = (bf16[64,2048]{1,0:T(8,128)(2,1)S(1)}, bf16[64,2048]{1,0:T(8,128)(2,1)S(1)}, u32[]{:S(2)}, u32[]{:S(2)}) collective-permute-start(bf16[64,2048]{1,0:T(8,128)(2,1)S(1)} %collective-permute-done.after_ref.refs_0_), channel_id=1, source_target_pairs={{0,4},{4,0},{8,12},{12,8},{1,5},{5,1},{9,13},{13,9},{2,6},{6,2},{1... | collective-permute-start | bytes 786440 | tf_op jit(solution)/shard_map/ppermute | solution.py:18
  27.2 2.7 %collective-permute-start.3 = (bf16[64,2048]{1,0:T(8,128)(2,1)S(1)}, bf16[64,2048]{1,0:T(8,128)(2,1)S(1)}, u32[]{:S(2)}, u32[]{:S(2)}) collective-permute-start(bf16[64,2048]{1,0:T(8,128)(2,1)S(1)} %collective-permute-done.2.refs_2_.refs_0_), channel_id=1, source_target_pairs={{0,4},{4,0},{8,12},{12,8},{1,5},{5,1},{9,13},{13,9},{2,6},{6,2},{1... | collective-permute-start | bytes 786440 | tf_op jit(solution)/shard_map/ppermute | solution.py:18
  28.9 9.2 %collective-permute-start.6 = (bf16[1,64,1296]{2,1,0:T(8,128)(2,1)S(1)}, bf16[1,64,1296]{2,1,0:T(8,128)(2,1)S(1)}, u32[]{:S(2)}, u32[]{:S(2)}) collective-permute-start(bf16[1,64,1296]{2,1,0:T(8,128)(2,1)S(1)} %get-tuple-element.40.refs_2_), channel_id=1, source_target_pairs={{0,1},{1,0},{2,3},{3,2},{4,5},{5,4},{6,7},{7,6},{8,9},{9,8},{10,11... | collective-permute-start | bytes 497672 | tf_op jit(solution)/shard_map/ppermute | solution.py:18
  30.9 9.3 %collective-permute-start.5 = (bf16[1,64,1296]{2,1,0:T(8,128)(2,1)S(1)}, bf16[1,64,1296]{2,1,0:T(8,128)(2,1)S(1)}, u32[]{:S(2)}, u32[]{:S(2)}) collective-permute-start(bf16[1,64,1296]{2,1,0:T(8,128)(2,1)S(1)} %get-tuple-element.43.refs_3_), channel_id=1, source_target_pairs={{0,1},{1,0},{2,3},{3,2},{4,5},{5,4},{6,7},{7,6},{8,9},{9,8},{10,11... | collective-permute-start | bytes 497672 | tf_op jit(solution)/shard_map/ppermute | solution.py:18
  33.4 14.8 %collective-permute-start.4 = (bf16[2,64,1024]{2,1,0:T(8,128)(2,1)S(1)}, bf16[2,64,1024]{2,1,0:T(8,128)(2,1)S(1)}, u32[]{:S(2)}, u32[]{:S(2)}) collective-permute-start(bf16[2,64,1024]{2,1,0:T(8,128)(2,1)S(1)} %get-tuple-element.44.after_ref), channel_id=1, source_target_pairs={{0,1},{1,0},{2,3},{3,2},{4,5},{5,4},{6,7},{7,6},{8,9},{9,8},{10,11... | collective-permute-start | bytes 786440 | tf_op jit(solution)/shard_map/ppermute | solution.py:18
  34.4 17.9 %copy-start.3 = (f32[16]{0:T(128)S(1)}, f32[16]{0:T(128)}, u32[]{:S(2)}) copy-start(f32[16]{0:T(128)} %param.22) | copy-start | bytes 196
  34.4 17.9 %copy-start.4 = (f32[16]{0:T(128)S(1)}, f32[16]{0:T(128)}, u32[]{:S(2)}) copy-start(f32[16]{0:T(128)} %param.23) | copy-start | bytes 196
  34.4 17.9 %copy-start.5 = (f32[16]{0:T(128)S(1)}, f32[16]{0:T(128)}, u32[]{:S(2)}) copy-start(f32[16]{0:T(128)} %param.24) | copy-start | bytes 196
  38.1 22.4 %copy-start.1 = (f32[1024]{0:T(1024)S(1)}, f32[1024]{0:T(1024)}, u32[]{:S(2)}) copy-start(f32[1024]{0:T(1024)} %param.25) | copy-start | bytes 12292
  40.3 2.8 %collective-permute-start.9 = (f32[64,17]{1,0:T(8,128)S(1)}, f32[64,17]{1,0:T(8,128)S(1)}, u32[]{:S(2)}, u32[]{:S(2)}) collective-permute-start(f32[64,17]{1,0:T(8,128)S(1)} %get-tuple-element.51.after_ref), channel_id=1, source_target_pairs={{0,4},{4,0},{8,12},{12,8},{1,5},{5,1},{9,13},{13,9},{2,6},{6,2},{1... | collective-permute-start | bytes 13064 | tf_op jit(solution)/shard_map/ppermute | solution.py:18
  40.4 11.8 %collective-permute-start.7 = (bf16[1,64,1296]{2,1,0:T(8,128)(2,1)S(1)}, bf16[1,64,1296]{2,1,0:T(8,128)(2,1)S(1)}, u32[]{:S(2)}, u32[]{:S(2)}) collective-permute-start(bf16[1,64,1296]{2,1,0:T(8,128)(2,1)S(1)} %add_convert_fusion.1), channel_id=1, source_target_pairs={{0,2},{1,3},{2,0},{3,1},{4,6},{5,7},{6,4},{7,5},{8,10},{9,11},{10,... | collective-permute-start | bytes 497672 | tf_op jit(solution)/shard_map/ppermute | solution.py:18
  43.1 4.0 %collective-permute-start.10 = (f32[64,17]{1,0:T(8,128)S(1)}, f32[64,17]{1,0:T(8,128)S(1)}, u32[]{:S(2)}, u32[]{:S(2)}) collective-permute-start(f32[64,17]{1,0:T(8,128)S(1)} %add.44), channel_id=1, source_target_pairs={{0,8},{4,12},{8,0},{12,4},{1,9},{5,13},{9,1},{13,5},{2,10},{6,14},... | collective-permute-start | bytes 13064 | tf_op jit(solution)/shard_map/ppermute | solution.py:18
  52.2 8.2 %collective-permute-start.8 = (bf16[1,64,1024]{2,1,0:T(8,128)(2,1)S(1)}, bf16[1,64,1024]{2,1,0:T(8,128)(2,1)S(1)}, u32[]{:S(2)}, u32[]{:S(2)}) collective-permute-start(bf16[1,64,1024]{2,1,0:T(8,128)(2,1)S(1)} %add_convert_fusion.2.refs_9_), channel_id=1, source_target_pairs={{0,2},{1,3},{2,0},{3,1},{4,6},{5,7},{6,4},{7,5},{8,10},{9,11},{10,... | collective-permute-start | bytes 393224 | tf_op jit(solution)/shard_map/ppermute | solution.py:18
  61.4 1.7 %collective-permute-start.11 = (bf16[1,64,2048]{2,1,0:T(8,128)(2,1)S(1)}, bf16[1,64,2048]{2,1,0:T(8,128)(2,1)S(1)}, u32[]{:S(2)}, u32[]{:S(2)}) collective-permute-start(bf16[1,64,2048]{2,1,0:T(8,128)(2,1)S(1)} %get-tuple-element.55.after_ref), channel_id=1, source_target_pairs={{0,4},{4,0},{8,12},{12,8},{1,5},{5,1},{9,13},{13,9},{2,6},{6,2},{1... | collective-permute-start | bytes 786440 | tf_op jit(solution)/shard_map/ppermute | solution.py:18
  63.2 15.4 %collective-permute-start.12 = (bf16[1,64,2048]{2,1,0:T(8,128)(2,1)S(1)}, bf16[1,64,2048]{2,1,0:T(8,128)(2,1)S(1)}, u32[]{:S(2)}, u32[]{:S(2)}) collective-permute-start(bf16[1,64,2048]{2,1,0:T(8,128)(2,1)S(1)} %add_convert_fusion.after_ref), channel_id=1, source_target_pairs={{0,8},{4,12},{8,0},{12,4},{1,9},{5,13},{9,1},{13,5},{2,10},{6,14},... | collective-permute-start | bytes 786440 | tf_op jit(solution)/shard_map/ppermute | solution.py:18
  63.7 1.2 %collective-permute-start.14 = (f32[64,1]{1,0:T(8,128)S(1)}, f32[64,1]{1,0:T(8,128)S(1)}, u32[]{:S(2)}, u32[]{:S(2)}) collective-permute-start(f32[64,1]{1,0:T(8,128)S(1)} %get-tuple-element.57), channel_id=1, source_target_pairs={{0,4},{4,0},{8,12},{12,8},{1,5},{5,1},{9,13},{13,9},{2,6},{6,2},{1... | collective-permute-start | bytes 776 | tf_op jit(solution)/shard_map/ppermute | solution.py:18
  63.9 14.8 %collective-permute-start.13 = (bf16[1,64,2048]{2,1,0:T(8,128)(2,1)S(1)}, bf16[1,64,2048]{2,1,0:T(8,128)(2,1)S(1)}, u32[]{:S(2)}, u32[]{:S(2)}) collective-permute-start(bf16[1,64,2048]{2,1,0:T(8,128)(2,1)S(1)} %slice.27), channel_id=1, source_target_pairs={{0,4},{4,0},{8,12},{12,8},{1,5},{5,1},{9,13},{13,9},{2,6},{6,2},{1... | collective-permute-start | bytes 786440 | tf_op jit(solution)/shard_map/ppermute | solution.py:18
  64.9 7.8 %collective-permute-start.15 = (f32[64,1]{1,0:T(8,128)S(1)}, f32[64,1]{1,0:T(8,128)S(1)}, u32[]{:S(2)}, u32[]{:S(2)}) collective-permute-start(f32[64,1]{1,0:T(8,128)S(1)} %add.50), channel_id=1, source_target_pairs={{0,8},{4,12},{8,0},{12,4},{1,9},{5,13},{9,1},{13,5},{2,10},{6,14},... | collective-permute-start | bytes 776 | tf_op jit(solution)/shard_map/ppermute | solution.py:18
  73.7 5.2 %copy-start.6 = (bf16[32,2,2048]{2,1,0:T(2,128)(2,1)S(1)}, bf16[32,2,2048]{2,1,0:T(2,128)(2,1)}, u32[]{:S(2)}) copy-start(bf16[32,2,2048]{2,1,0:T(2,128)(2,1)} %param.16) | copy-start | bytes 786436

commit v10 on v8

--- a/solution.py
+++ b/solution.py
@@ -457,7 +457,7 @@
 
 
 def output_tiles(distances, lhs_ref, weight_refs, out_ref):
-    width = out_ref.shape[2]
+    width = out_ref.shape[2] // 256 * 256
     tile = min(width, 512)
     for j, distance in enumerate(distances):
         for t in range(0, width, tile):
@@ -474,6 +474,50 @@
             out_ref[j, :, t : t + tile] = acc.astype(out_ref.dtype)
 
 
+LANES = 128
+
+
+def put_lanes(values, out_ref, j):
+    lane = lax.broadcasted_iota(jnp.int32, (values.shape[0], LANES), 1)
+    tail = jnp.zeros(lane.shape, F32)
+    for i in range(3):
+        term = values.astype(BF16).astype(F32)
+        tail = jnp.where(lane == i, term, tail)
+        values = values - term
+    out_ref[j, :, out_ref.shape[2] - LANES :] = tail.astype(out_ref.dtype)
+
+
+def meet_body(met_ref, own_ref, squares_ref, out_ref, total_ref):
+    count = met_ref.shape[0]
+    width = own_ref.shape[2]
+    total = squares_ref[...] + join_lanes(met_ref[0, :, width:])
+    total_ref[...] = total
+    for j in range(count):
+        both = met_ref[j, :, :width].astype(F32) + own_ref[j].astype(F32)
+        out_ref[j, :, :width] = both.astype(out_ref.dtype)
+        put_lanes(total, out_ref, j)
+
+
+def meet(met, own, squares):
+    whole = pl.BlockSpec(memory_space=pltpu.VMEM)
+    return pl.pallas_call(
+        meet_body,
+        out_shape=(
+            jax.ShapeDtypeStruct(met.shape, met.dtype),
+            jax.ShapeDtypeStruct(squares.shape, squares.dtype),
+        ),
+        in_specs=[whole] * 3,
+        out_specs=(whole, whole),
+        compiler_params=params(),
+        cost_estimate=cost(met.size, 6 * met.size),
+        name="meet",
+    )(met, own, squares)
+
+
+def join_lanes(values):
+    return jnp.sum(values.astype(F32), -1, keepdims=True)
+
+
 def output_first_body(distances, terms, model_width, *refs):
     term_refs = refs[:terms]
     sums_ref, result_ref, scale_ref, *weight_refs, out_ref, lhs_ref, squares_ref = refs[terms:]
@@ -482,6 +526,8 @@
     squares_ref[...] = jnp.sum(gated * gated, -1, keepdims=True)
     lhs_ref[...] = (gated * scale_ref[...]).astype(lhs_ref.dtype)
     output_tiles(distances, lhs_ref, weight_refs, out_ref)
+    for j in range(len(distances)):
+        put_lanes(squares_ref[...], out_ref, j)
 
 
 def output_rest_body(distances, lhs_ref, after_ref, *refs):
@@ -495,7 +541,8 @@
     whole = pl.BlockSpec(memory_space=pltpu.VMEM)
     specs = [whole] * (len(operands) + len(weights))
     body = functools.partial(output_rest_body, distances)
-    out_shape = [jax.ShapeDtypeStruct((count, rows, width), BF16)]
+    extra = LANES if first else 0
+    out_shape = [jax.ShapeDtypeStruct((count, rows, width + extra), BF16)]
     if first:
         body = functools.partial(output_first_body, distances, len(operands) - 3, model_width)
         out_shape += [
@@ -584,6 +631,7 @@
         signal_terms = [jnp.where(own, n, f)[0] for n, f in pick]
         last_other = swap(last_send, "row", 2)
         signal_terms = [last_other[0]] + signal_terms
+        gate_send, _ = lax.optimization_barrier((gate_send, last_send))
         gate_terms = [swap(gate_send, "row", 1), gate_keep]
         gate_last = sum(t[1:].astype(F32) for t in gate_terms).astype(BF16)
         gate_last, _ = lax.optimization_barrier((gate_last, last_other))
@@ -632,14 +680,20 @@
         distances[2::4] + distances[1::4], out_weights, feature_width, [out_lhs, first]
     )
     half = second.shape[0] // 2
-    send = (swap(first, "head", 1).astype(F32) + second[:half].astype(F32)).astype(BF16)
-    received = swap(send, "head", 2)
+    send, gate_squares = meet(swap(first, "head", 1), second, gate_squares)
     (rest,) = output_parts(distances[0::4], out_weights, feature_width, [out_lhs, send])
     feeds, _ = lax.optimization_barrier((feeds, rest))
     kept = [swap(second[half:], "head", 1), rest]
-    mixer, _ = scatter_rows(received, kept, "head", done=2)
-    mixer = sum(t.astype(F32) for t in mixer)
-    gate_squares = sum_over(gate_squares, "head")
+    if len(bits_of(heads_n)) == 2:
+        received = swap(send, "head", 2)
+        mixer = sum(t[0].astype(F32) for t in [received[..., :feature_width]] + kept)
+        gate_squares = gate_squares + join_lanes(received[0, :, feature_width:])
+    else:
+        received = swap(send[..., :feature_width], "head", 2)
+        mixer, _ = scatter_rows(received, kept, "head", done=2)
+        mixer = sum(t.astype(F32) for t in mixer)
+        for distance in bits_of(heads_n)[1:]:
+            gate_squares = gate_squares + swap(gate_squares, "head", distance)
     mixer = mixer * lax.rsqrt(gate_squares / inner_width + EPSILON)
     mixer = mixer.reshape(positions, streams, feature_width)
     live = jnp.arange(streams) < live_block_rows[0]

time: 84.6 us -> 76.9 us (0.909)
  local copies, waits for them, and re-layouts: 14.4 us -> 2.1 us
  waiting for transfers between devices: 13.3 us -> 20.3 us
  starting transfers between devices: 21.7 us -> 19.1 us
    unnamed x27 -> x15, local copies, waits for them, and re-layouts: 14.1 us -> 1.66 us
    ppermute x15 -> x13, waiting for transfers between devices: 13.3 us -> 20.3 us  [swap(): return lax.ppermute(values, axis, [(i, i ^ distance) for i in range(size)])]
    ppermute x15 -> x13, starting transfers between devices: 21 us -> 18.5 us  [swap(): return lax.ppermute(values, axis, [(i, i ^ distance) for i in range(size)])]
  transfers between devices with their start and end apart: 16 -> 14, of which waited for: 7 -> 6; matrix products, arithmetic and copies ran while one was open for 1% -> 1% of each run, Pallas kernels for 36% -> 40%
where the time goes in v10:
time: 76.9 us; the launch traced here: 76.6 us
  Pallas kernels  31.7 us (41%)
  waiting for transfers between devices  20.3 us (26%)
  starting transfers between devices  19.1 us (25%)
  local copies, waits for them, and re-layouts  2.1 us (3%)
  other arithmetic  1.81 us (2%)
  between operations  1.61 us (2%)
    ppermute x13, waiting for transfers between devices, swap(): return lax.ppermute(values, axis, [(i, i ^ distance) for i in range(size)])  20.3 us
    ppermute x13, starting transfers between devices, swap(): return lax.ppermute(values, axis, [(i, i ^ distance) for i in range(size)])  18.5 us
    pallas_call x3, Pallas kernels, load(): pl.pallas_call(functools.partial(load_body, spans), out_shape=tuple((pltp...  11.1 us
    pallas_call x1, Pallas kernels, state_write(): pl.pallas_call(state_write_body, out_shape=jax.ShapeDtypeStruct(state.sha...  4.88 us
    pallas_call x1, Pallas kernels, recur(): pl.pallas_call(functools.partial(recur_body, len(terms), group, model_wid...  4.83 us
    pallas_call x1, Pallas kernels, adapt(): pl.pallas_call(adapt_body, out_shape=(jax.ShapeDtypeStruct((rows, rank +...  3.84 us
    pallas_call x3, Pallas kernels, output_parts(): pl.pallas_call(body, out_shape=tuple(out_shape), in_specs=specs, out_spec...  3.42 us
    pallas_call x2, Pallas kernels, project_signal(): pl.pallas_call(body, out_shape=(half, half, jax.ShapeDtypeStruct((rows, d...  2.13 us
  transfers between devices with their start and end apart: 14, of which 6 were waited for; matrix products, arithmetic and copies ran while one was open for 1% of the time, Pallas kernels for 40%

profile of v10, /device:TPU:0, one launch (start us, length us, event | category | flops | bytes accessed | tf_op | source)
XLA Modules:
  0.0 76.6 jit_solution(11661276949414665674)
XLA Ops:
  0.6 1.1 %fusion.1 = (f32[2,32]{1,0:T(2,128)S(1)}, bf16[2,32,2048]{2,1,0:T(8,128)(2,1)S(1)}) fusion(bf16[32,2,2048]{2,1,0:T(2,128)(2,1)} %param.16, f32[2048]{0:T(1024)} %param.17), kind=kLoop, calls=%fused_computation.4 | loop fusion | flops 655296 | bytes 532736 | tf_op jit(solution)/shard_map/reduce_sum | solution.py:600
  3.2 3.8 %adapt.1 = (f32[64,17]{1,0:T(8,128)S(1)}, bf16[512,1024]{1,0:T(8,128)(2,1)S(1)}) custom-call(s32[32]{0:T(128)S(1)} %copy-done.2, bf16[64,2048]{1,0:T(8,128)(2,1)S(1)} %bitcast.36, f32[64,1]{1,0:T(8,128)S(1)} %reshape.29.squares_ref, bf16[128,16,2048]{2,1,0:T(8,128)(2,1)} %bitcast.45, bf16[128,16,1024]{2,1,0:T(8,128)(2,1)} %up_ref.1), custom_call_target="tpu_custom_call" | custom-call | flops 134217728 | bytes 3145728 | tf_op jit(solution)/shard_map/adapt/pallas_call | solution.py:141
  7.1 3.9 %load.3 = (bf16[2048,1024]{1,0:T(8,128)(2,1)S(1)}, bf16[2048,256]{1,0:T(8,128)(2,1)S(1)}, bf16[2048,1024]{1,0:T(8,128)(2,1)S(1)}) custom-call(f32[64,17]{1,0:T(8,128)S(1)} %get-tuple-element.54.after_ref, bf16[2048,1024]{1,0:T(8,128)(2,1)} %refs_0_.2, bf16[2048,256]{1,0:T(8,128)(2,1)} %refs_1_.2, bf16[2048,1024]{1,0:T(8,128)(2,1)} %refs_2_.1), custom_call_target="tpu_custom_call" | custom-call | bytes 18874368 | tf_op jit(solution)/shard_map/load/pallas_call | solution.py:78
  11.0 11.8 %collective-permute-start.2 = (bf16[64,2048]{1,0:T(8,128)(2,1)S(1)}, bf16[64,2048]{1,0:T(8,128)(2,1)S(1)}, u32[]{:S(2)}, u32[]{:S(2)}) collective-permute-start(bf16[64,2048]{1,0:T(8,128)(2,1)S(1)} %collective-permute-done.after_ref.refs_0_), channel_id=1, source_target_pairs={{0,8},{4,12},{8,0},{12,4},{1,9},{5,13},{9,1},{13,5},{2,10},{6,14},... | collective-permute-start | bytes 786440 | tf_op jit(solution)/shard_map/ppermute | solution.py:18
  22.8 3.5 %load.4.refs_6_.refs_0_ = bf16[512,8192]{1,0:T(8,128)(2,1)S(1)} custom-call(bf16[64,2048]{1,0:T(8,128)(2,1)S(1)} %collective-permute-done.after_ref.refs_0_, bf16[1024,8192]{1,0:T(8,128)(2,1)} %refs_1_.3), custom_call_target="tpu_custom_call" | custom-call | bytes 16777216 | tf_op jit(solution)/shard_map/load/pallas_call | solution.py:78
  26.3 0.9 %collective-permute-done.2.refs_2_.refs_0_ = bf16[64,2048]{1,0:T(8,128)(2,1)S(1)} collective-permute-done((bf16[64,2048]{1,0:T(8,128)(2,1)S(1)}, bf16[64,2048]{1,0:T(8,128)(2,1)S(1)}, u32[]{:S(2)}, u32[]{:S(2)}) %collective-permute-start.2) | collective-permute-done | bytes 262176 | tf_op jit(solution)/shard_map/ppermute | solution.py:18
  27.9 1.1 %project_signal.2 = (bf16[1,64,1296]{2,1,0:T(8,128)(2,1)S(1)}, bf16[1,64,1296]{2,1,0:T(8,128)(2,1)S(1)}, bf16[128,2048]{1,0:T(8,128)(2,1)S(1)}) custom-call(bf16[64,2048]{1,0:T(8,128)(2,1)S(1)} %collective-permute-done.after_ref.refs_0_, bf16[64,2048]{1,0:T(8,128)(2,1)S(1)} %collective-permute-done.1.refs_1_, ...), custom_call_target="tpu_custom_call" | custom-call | flops 679477248 | bytes 5308416 | tf_op jit(solution)/shard_map/project_signal/pallas_call | solution.py:207
  28.9 0.9 %collective-permute-start.5 = (bf16[1,64,1296]{2,1,0:T(8,128)(2,1)S(1)}, bf16[1,64,1296]{2,1,0:T(8,128)(2,1)S(1)}, u32[]{:S(2)}, u32[]{:S(2)}) collective-permute-start(bf16[1,64,1296]{2,1,0:T(8,128)(2,1)S(1)} %get-tuple-element.42.refs_2_), channel_id=1, source_target_pairs={{0,1},{1,0},{2,3},{3,2},{4,5},{5,4},{6,7},{7,6},{8,9},{9,8},{10,11... | collective-permute-start | bytes 497672 | tf_op jit(solution)/shard_map/ppermute | solution.py:18
  29.9 1.1 %project_signal.3 = (bf16[1,64,1296]{2,1,0:T(8,128)(2,1)S(1)}, bf16[1,64,1296]{2,1,0:T(8,128)(2,1)S(1)}, bf16[128,2048]{1,0:T(8,128)(2,1)S(1)}) custom-call(bf16[64,2048]{1,0:T(8,128)(2,1)S(1)} %collective-permute-done.2.refs_2_.refs_0_, bf16[64,2048]{1,0:T(8,128)(2,1)S(1)} %collective-permute-done.3.refs_1_, ...), custom_call_target="tpu_custom_call" | custom-call | flops 679477248 | bytes 5308416 | tf_op jit(solution)/shard_map/project_signal/pallas_call | solution.py:207
  30.9 1.2 %collective-permute-start.4 = (bf16[1,64,1296]{2,1,0:T(8,128)(2,1)S(1)}, bf16[1,64,1296]{2,1,0:T(8,128)(2,1)S(1)}, u32[]{:S(2)}, u32[]{:S(2)}) collective-permute-start(bf16[1,64,1296]{2,1,0:T(8,128)(2,1)S(1)} %get-tuple-element.45.refs_3_), channel_id=1, source_target_pairs={{0,1},{1,0},{2,3},{3,2},{4,5},{5,4},{6,7},{7,6},{8,9},{9,8},{10,11... | collective-permute-start | bytes 497672 | tf_op jit(solution)/shard_map/ppermute | solution.py:18
  32.2 1.3 %project_gate.1 = (bf16[2,64,1024]{2,1,0:T(8,128)(2,1)S(1)}, bf16[2,64,1024]{2,1,0:T(8,128)(2,1)S(1)}) custom-call(bf16[128,2048]{1,0:T(8,128)(2,1)S(1)} %get-tuple-element.41.refs_0_, bf16[128,2048]{1,0:T(8,128)(2,1)S(1)} %get-tuple-element.43.refs_1_, bf16[2048,1024]{1,0:T(8,128)(2,1)S(1)} %get-tuple-element.44.refs_2_, ...), custom_call_target="tpu_custom_call" | custom-call | flops 1073741824 | bytes 4194304 | tf_op jit(solution)/shard_map/project_gate/pallas_call | solution.py:247
  33.5 3.7 %load.5 = (bf16[1,64,1296]{2,1,0:T(8,128)(2,1)S(1)}, bf16[512,8192]{1,0:T(8,128)(2,1)S(1)}) custom-call(bf16[2,64,1024]{2,1,0:T(8,128)(2,1)S(1)} %get-tuple-element.51.after_ref, bf16[1,64,1296]{2,1,0:T(8,128)(2,1)S(1)} %get-tuple-element.48.refs_0_, bf16[1024,8192]{1,0:T(8,128)(2,1)} %refs_1_.3), custom_call_target="tpu_custom_call" | custom-call | bytes 16777216 | tf_op jit(solution)/shard_map/load/pallas_call | solution.py:78
  37.2 2.6 %collective-permute-done.4 = bf16[1,64,1296]{2,1,0:T(8,128)(2,1)S(1)} collective-permute-done((bf16[1,64,1296]{2,1,0:T(8,128)(2,1)S(1)}, bf16[1,64,1296]{2,1,0:T(8,128)(2,1)S(1)}, u32[]{:S(2)}, u32[]{:S(2)}) %collective-permute-start.4) | collective-permute-done | bytes 165920 | tf_op jit(solution)/shard_map/ppermute | solution.py:18
  40.0 2.4 %collective-permute-start.7 = (bf16[1,64,1296]{2,1,0:T(8,128)(2,1)S(1)}, bf16[1,64,1296]{2,1,0:T(8,128)(2,1)S(1)}, u32[]{:S(2)}, u32[]{:S(2)}) collective-permute-start(bf16[1,64,1296]{2,1,0:T(8,128)(2,1)S(1)} %add_convert_fusion), channel_id=1, source_target_pairs={{0,2},{1,3},{2,0},{3,1},{4,6},{5,7},{6,4},{7,5},{8,10},{9,11},{10,... | collective-permute-start | bytes 497672 | tf_op jit(solution)/shard_map/ppermute | solution.py:18
  43.2 3.5 %collective-permute-done.10 = f32[64,17]{1,0:T(8,128)S(1)} collective-permute-done((f32[64,17]{1,0:T(8,128)S(1)}, f32[64,17]{1,0:T(8,128)S(1)}, u32[]{:S(2)}, u32[]{:S(2)}) %collective-permute-start.10) | collective-permute-done | bytes 4384 | tf_op jit(solution)/shard_map/ppermute | solution.py:18
  46.7 7.6 %collective-permute-done.6 = bf16[2,64,1024]{2,1,0:T(8,128)(2,1)S(1)} collective-permute-done((bf16[2,64,1024]{2,1,0:T(8,128)(2,1)S(1)}, bf16[2,64,1024]{2,1,0:T(8,128)(2,1)S(1)}, u32[]{:S(2)}, u32[]{:S(2)}) %collective-permute-start.6) | collective-permute-done | bytes 262176 | tf_op jit(solution)/shard_map/ppermute | solution.py:18
  54.6 4.8 %recur.1 = (f32[64,1024]{1,0:T(8,128)S(1)}, f32[2,32,1024]{2,1,0:T(8,128)S(1)}, f32[2,32,128]{2,1,0:T(8,128)S(1)}, f32[32,16]{1,0:T(8,128)S(1)}, bf16[32,16,64,128]{3,2,1,0:T(8,128)(2,1)S(1)}) custom-call(s32[1]{0:T(128)} %copy.44.live_ref, bf16[64,1296]{1,0:T(8,128)(2,1)S(1)} %bitcast.39, bf16[64,1296]{1,0:T(8,128)(2,1)S(1)} %select_bitcast_fusion.1.refs_1_, ...), custom_call_target="tpu_custom_call" | custom-call | flops 268435456 | bytes 10485760 | tf_op jit(solution)/shard_map/recur/pallas_call | solution.py:380
  59.4 3.5 %collective-permute-done.8 = bf16[1,64,1024]{2,1,0:T(8,128)(2,1)S(1)} collective-permute-done((bf16[1,64,1024]{2,1,0:T(8,128)(2,1)S(1)}, bf16[1,64,1024]{2,1,0:T(8,128)(2,1)S(1)}, u32[]{:S(2)}, u32[]{:S(2)}) %collective-permute-start.8) | collective-permute-done | bytes 131104 | tf_op jit(solution)/shard_map/ppermute | solution.py:18
  62.9 1.0 %output_first.1 = (bf16[1,64,2176]{2,1,0:T(8,128)(2,1)S(1)}, bf16[64,1024]{1,0:T(8,128)(2,1)S(1)}, f32[64,1]{1,0:T(8,128)S(1)}) custom-call(bf16[64,1024]{1,0:T(8,128)(2,1)S(1)} %bitcast.40, bf16[64,1024]{1,0:T(8,128)(2,1)S(1)} %slice_bitcast_fusion.refs_1_, bf16[64,1024]{1,0:T(8,128)(2,1)S(1)} %slice_bitcast_fusion.1.refs_2_, f32[64,17]{1,0:T(8,128)S(1)} %add.39.refs_3_, ...), custom_call_target="tpu_custom_call" | custom-call | flops 268435456 | bytes 4194304 | tf_op jit(solution)/shard_map/output_first/pallas_call | solution.py:554
  64.0 1.6 %output_rest.2.own_ref = bf16[2,64,2048]{2,1,0:T(8,128)(2,1)S(1)} custom-call(bf16[64,1024]{1,0:T(8,128)(2,1)S(1)} %get-tuple-element.59.lhs_ref, bf16[1,64,2176]{2,1,0:T(8,128)(2,1)S(1)} %get-tuple-element.58.after_ref, bf16[512,8192]{1,0:T(8,128)(2,1)S(1)} %load.4.refs_6_.refs_0_, bf16[512,8192]{1,0:T(8,128)(2,1)S(1)} %get-tuple-element.57.refs_7_.refs_1_), custom_call_target="tpu_custom_call" | custom-call | flops 536870912 | bytes 8388608 | tf_op jit(solution)/shard_map/output_rest/pallas_call | solution.py:554
  66.8 0.8 %output_rest.3 = bf16[1,64,2048]{2,1,0:T(8,128)(2,1)S(1)} custom-call(bf16[64,1024]{1,0:T(8,128)(2,1)S(1)} %get-tuple-element.59.lhs_ref, bf16[1,64,2176]{2,1,0:T(8,128)(2,1)S(1)} %get-tuple-element.61.after_ref, bf16[512,8192]{1,0:T(8,128)(2,1)S(1)} %load.4.refs_6_.refs_0_, bf16[512,8192]{1,0:T(8,128)(2,1)S(1)} %get-tuple-element.57.refs_7_.refs_1_), custom_call_target="tpu_custom_call" | custom-call | flops 268435456 | bytes 4194304 | tf_op jit(solution)/shard_map/output_rest/pallas_call | solution.py:554
  67.8 4.9 %state_write.1 = bf16[32,16,64,128]{3,2,1,0:T(8,128)(2,1)} custom-call(f32[2,32,1024]{2,1,0:T(8,128)S(1)} %get-tuple-element.64.feeds_ref, f32[2,32,128]{2,1,0:T(8,128)S(1)} %get-tuple-element.65.b_ref, f32[32,16,128]{2,1,0:T(8,128)S(1)} %broadcast_in_dim.42.decay_ref, bf16[32,16,64,128]{3,2,1,0:T(8,128)(2,1)S(1)} %get-tuple-element.67.state_ref), custom_call_target="tpu_custom_call" | custom-call | flops 134217728 | bytes 16777216 | tf_op jit(solution)/shard_map/state_write/pallas_call | solution.py:442
  72.7 2.3 %collective-permute-done.12 = bf16[1,64,2176]{2,1,0:T(8,128)(2,1)S(1)} collective-permute-done((bf16[1,64,2176]{2,1,0:T(8,128)(2,1)S(1)}, bf16[1,64,2176]{2,1,0:T(8,128)(2,1)S(1)}, u32[]{:S(2)}, u32[]{:S(2)}) %collective-permute-start.12) | collective-permute-done | bytes 278560 | tf_op jit(solution)/shard_map/ppermute | solution.py:18
  75.7 1.0 %copy.39 = bf16[32,2,2048]{2,1,0:T(2,128)(2,1)} copy(bf16[32,2,2048]{2,0,1:T(8,128)(2,1)S(1)} %fusion.3) | data formatting | bytes 524288
  (51 shorter events, 4.8 us)
Async XLA Ops:
  1.8 9.2 %collective-permute-start = (bf16[64,2048]{1,0:T(8,128)(2,1)S(1)}, bf16[64,2048]{1,0:T(8,128)(2,1)S(1)}, u32[]{:S(2)}, u32[]{:S(2)}) collective-permute-start(bf16[64,2048]{1,0:T(8,128)(2,1)S(1)} %bitcast.35), channel_id=1, source_target_pairs={{0,0},{1,4},{2,8},{3,12},{4,1},{5,5},{6,9},{7,13},{8,2},{9,6},{10,... | collective-permute-start | bytes 786440 | tf_op jit(solution)/shard_map/ppermute | solution.py:610
  2.6 0.7 copy-start.2
  11.0 16.9 %copy-start = (bf16[2048,16]{0,1:T(8,128)(2,1)S(1)}, bf16[2048,16]{0,1:T(8,128)(2,1)}, u32[]{:S(2)}) copy-start(bf16[2048,16]{0,1:T(8,128)(2,1)} %param.20) | copy-start | bytes 196612
  11.0 16.2 %collective-permute-start.2 = (bf16[64,2048]{1,0:T(8,128)(2,1)S(1)}, bf16[64,2048]{1,0:T(8,128)(2,1)S(1)}, u32[]{:S(2)}, u32[]{:S(2)}) collective-permute-start(bf16[64,2048]{1,0:T(8,128)(2,1)S(1)} %collective-permute-done.after_ref.refs_0_), channel_id=1, source_target_pairs={{0,8},{4,12},{8,0},{12,4},{1,9},{5,13},{9,1},{13,5},{2,10},{6,14},... | collective-permute-start | bytes 786440 | tf_op jit(solution)/shard_map/ppermute | solution.py:18
  22.8 5.0 %collective-permute-start.1 = (bf16[64,2048]{1,0:T(8,128)(2,1)S(1)}, bf16[64,2048]{1,0:T(8,128)(2,1)S(1)}, u32[]{:S(2)}, u32[]{:S(2)}) collective-permute-start(bf16[64,2048]{1,0:T(8,128)(2,1)S(1)} %collective-permute-done.after_ref.refs_0_), channel_id=1, source_target_pairs={{0,4},{4,0},{8,12},{12,8},{1,5},{5,1},{9,13},{13,9},{2,6},{6,2},{1... | collective-permute-start | bytes 786440 | tf_op jit(solution)/shard_map/ppermute | solution.py:18
  27.2 2.7 %collective-permute-start.3 = (bf16[64,2048]{1,0:T(8,128)(2,1)S(1)}, bf16[64,2048]{1,0:T(8,128)(2,1)S(1)}, u32[]{:S(2)}, u32[]{:S(2)}) collective-permute-start(bf16[64,2048]{1,0:T(8,128)(2,1)S(1)} %collective-permute-done.2.refs_2_.refs_0_), channel_id=1, source_target_pairs={{0,4},{4,0},{8,12},{12,8},{1,5},{5,1},{9,13},{13,9},{2,6},{6,2},{1... | collective-permute-start | bytes 786440 | tf_op jit(solution)/shard_map/ppermute | solution.py:18
  28.9 8.3 %collective-permute-start.5 = (bf16[1,64,1296]{2,1,0:T(8,128)(2,1)S(1)}, bf16[1,64,1296]{2,1,0:T(8,128)(2,1)S(1)}, u32[]{:S(2)}, u32[]{:S(2)}) collective-permute-start(bf16[1,64,1296]{2,1,0:T(8,128)(2,1)S(1)} %get-tuple-element.42.refs_2_), channel_id=1, source_target_pairs={{0,1},{1,0},{2,3},{3,2},{4,5},{5,4},{6,7},{7,6},{8,9},{9,8},{10,11... | collective-permute-start | bytes 497672 | tf_op jit(solution)/shard_map/ppermute | solution.py:18
  30.9 8.9 %collective-permute-start.4 = (bf16[1,64,1296]{2,1,0:T(8,128)(2,1)S(1)}, bf16[1,64,1296]{2,1,0:T(8,128)(2,1)S(1)}, u32[]{:S(2)}, u32[]{:S(2)}) collective-permute-start(bf16[1,64,1296]{2,1,0:T(8,128)(2,1)S(1)} %get-tuple-element.45.refs_3_), channel_id=1, source_target_pairs={{0,1},{1,0},{2,3},{3,2},{4,5},{5,4},{6,7},{7,6},{8,9},{9,8},{10,11... | collective-permute-start | bytes 497672 | tf_op jit(solution)/shard_map/ppermute | solution.py:18
  33.4 21.2 %copy-start.3 = (f32[16]{0:T(128)S(1)}, f32[16]{0:T(128)}, u32[]{:S(2)}) copy-start(f32[16]{0:T(128)} %param.22) | copy-start | bytes 196
  33.4 21.1 %copy-start.4 = (f32[16]{0:T(128)S(1)}, f32[16]{0:T(128)}, u32[]{:S(2)}) copy-start(f32[16]{0:T(128)} %param.23) | copy-start | bytes 196
  33.5 21.1 %copy-start.5 = (f32[16]{0:T(128)S(1)}, f32[16]{0:T(128)}, u32[]{:S(2)}) copy-start(f32[16]{0:T(128)} %param.24) | copy-start | bytes 196
  37.2 25.7 %copy-start.1 = (f32[1024]{0:T(1024)S(1)}, f32[1024]{0:T(1024)}, u32[]{:S(2)}) copy-start(f32[1024]{0:T(1024)} %param.25) | copy-start | bytes 12292
  39.9 2.8 %collective-permute-start.9 = (f32[64,17]{1,0:T(8,128)S(1)}, f32[64,17]{1,0:T(8,128)S(1)}, u32[]{:S(2)}, u32[]{:S(2)}) collective-permute-start(f32[64,17]{1,0:T(8,128)S(1)} %get-tuple-element.54.after_ref), channel_id=1, source_target_pairs={{0,4},{4,0},{8,12},{12,8},{1,5},{5,1},{9,13},{13,9},{2,6},{6,2},{1... | collective-permute-start | bytes 13064 | tf_op jit(solution)/shard_map/ppermute | solution.py:18
  40.0 14.3 %collective-permute-start.7 = (bf16[1,64,1296]{2,1,0:T(8,128)(2,1)S(1)}, bf16[1,64,1296]{2,1,0:T(8,128)(2,1)S(1)}, u32[]{:S(2)}, u32[]{:S(2)}) collective-permute-start(bf16[1,64,1296]{2,1,0:T(8,128)(2,1)S(1)} %add_convert_fusion), channel_id=1, source_target_pairs={{0,2},{1,3},{2,0},{3,1},{4,6},{5,7},{6,4},{7,5},{8,10},{9,11},{10,... | collective-permute-start | bytes 497672 | tf_op jit(solution)/shard_map/ppermute | solution.py:18
  42.4 11.9 %collective-permute-start.6 = (bf16[2,64,1024]{2,1,0:T(8,128)(2,1)S(1)}, bf16[2,64,1024]{2,1,0:T(8,128)(2,1)S(1)}, u32[]{:S(2)}, u32[]{:S(2)}) collective-permute-start(bf16[2,64,1024]{2,1,0:T(8,128)(2,1)S(1)} %get-tuple-element.51.after_ref), channel_id=1, source_target_pairs={{0,1},{1,0},{2,3},{3,2},{4,5},{5,4},{6,7},{7,6},{8,9},{9,8},{10,11... | collective-permute-start | bytes 786440 | tf_op jit(solution)/shard_map/ppermute | solution.py:18
  42.7 4.0 %collective-permute-start.10 = (f32[64,17]{1,0:T(8,128)S(1)}, f32[64,17]{1,0:T(8,128)S(1)}, u32[]{:S(2)}, u32[]{:S(2)}) collective-permute-start(f32[64,17]{1,0:T(8,128)S(1)} %add.38), channel_id=1, source_target_pairs={{0,8},{4,12},{8,0},{12,4},{1,9},{5,13},{9,1},{13,5},{2,10},{6,14},... | collective-permute-start | bytes 13064 | tf_op jit(solution)/shard_map/ppermute | solution.py:18
  54.4 8.6 %collective-permute-start.8 = (bf16[1,64,1024]{2,1,0:T(8,128)(2,1)S(1)}, bf16[1,64,1024]{2,1,0:T(8,128)(2,1)S(1)}, u32[]{:S(2)}, u32[]{:S(2)}) collective-permute-start(bf16[1,64,1024]{2,1,0:T(8,128)(2,1)S(1)} %add_convert_fusion.1.refs_9_), channel_id=1, source_target_pairs={{0,2},{1,3},{2,0},{3,1},{4,6},{5,7},{6,4},{7,5},{8,10},{9,11},{10,... | collective-permute-start | bytes 393224 | tf_op jit(solution)/shard_map/ppermute | solution.py:18
  63.9 1.7 %collective-permute-start.11 = (bf16[1,64,2176]{2,1,0:T(8,128)(2,1)S(1)}, bf16[1,64,2176]{2,1,0:T(8,128)(2,1)S(1)}, u32[]{:S(2)}, u32[]{:S(2)}) collective-permute-start(bf16[1,64,2176]{2,1,0:T(8,128)(2,1)S(1)} %get-tuple-element.58.after_ref), channel_id=1, source_target_pairs={{0,4},{4,0},{8,12},{12,8},{1,5},{5,1},{9,13},{13,9},{2,6},{6,2},{1... | collective-permute-start | bytes 835592 | tf_op jit(solution)/shard_map/ppermute | solution.py:18
  65.9 9.1 %collective-permute-start.12 = (bf16[1,64,2176]{2,1,0:T(8,128)(2,1)S(1)}, bf16[1,64,2176]{2,1,0:T(8,128)(2,1)S(1)}, u32[]{:S(2)}, u32[]{:S(2)}) collective-permute-start(bf16[1,64,2176]{2,1,0:T(8,128)(2,1)S(1)} %get-tuple-element.61.after_ref), channel_id=1, source_target_pairs={{0,8},{4,12},{8,0},{12,4},{1,9},{5,13},{9,1},{13,5},{2,10},{6,14},... | collective-permute-start | bytes 835592 | tf_op jit(solution)/shard_map/ppermute | solution.py:18
  66.5 8.9 %collective-permute-start.13 = (bf16[1,64,2048]{2,1,0:T(8,128)(2,1)S(1)}, bf16[1,64,2048]{2,1,0:T(8,128)(2,1)S(1)}, u32[]{:S(2)}, u32[]{:S(2)}) collective-permute-start(bf16[1,64,2048]{2,1,0:T(8,128)(2,1)S(1)} %slice.31), channel_id=1, source_target_pairs={{0,4},{4,0},{8,12},{12,8},{1,5},{5,1},{9,13},{13,9},{2,6},{6,2},{1... | collective-permute-start | bytes 786440 | tf_op jit(solution)/shard_map/ppermute | solution.py:18
  67.8 7.7 %copy-start.6 = (bf16[32,2,2048]{2,1,0:T(2,128)(2,1)S(1)}, bf16[32,2,2048]{2,1,0:T(2,128)(2,1)}, u32[]{:S(2)}) copy-start(bf16[32,2,2048]{2,1,0:T(2,128)(2,1)} %param.16) | copy-start | bytes 786436

commit v11 on v10

--- a/solution.py
+++ b/solution.py
@@ -16,6 +16,10 @@
 def swap(values, axis, distance):
     size = lax.axis_size(axis)
     return lax.ppermute(values, axis, [(i, i ^ distance) for i in range(size)])
+
+
+def swap_halves(values, axis, distance, dim):
+    return jnp.concatenate([swap(v, axis, distance) for v in jnp.split(values, 2, dim)], dim)
 
 
 def bits_of(size):
@@ -236,7 +240,7 @@
 def group_of_own(groups):
     if groups == 1:
         return 0
-    return (lax.axis_index("head") ^ lax.axis_index("row")) >> 1
+    return (lax.axis_index("head") ^ 2 ^ lax.axis_index("row")) >> 1
 
 
 def project_gate(rows, lhs, weight, after):
@@ -606,14 +610,16 @@
     signal_weights = (*weights[:2], projection_step.T)
     middle = output_weight.shape[0] // 2
     if heads_n == rows_n and len(bits_of(rows_n)) == 2:
-        turn = [(h * rows_n + r, r * rows_n + h) for h in range(heads_n) for r in range(rows_n)]
+        turn = [
+            (h * rows_n + r, (r ^ 2) * rows_n + h) for h in range(heads_n) for r in range(rows_n)
+        ]
         turned = lax.ppermute(scaled_flat, ("head", "row"), turn)
         turned, _ = lax.optimization_barrier((turned, weights[0]))
         crossed = swap(turned, "head", 2)
 
         def order(distance):
             return [
-                (lambda d=d: lax.axis_index("head") ^ d, 0) for d in (distance, distance ^ 1)
+                (lambda d=d: lax.axis_index("head") ^ 2 ^ d, 0) for d in (distance, distance ^ 1)
             ]
 
         near = [turned, swap(turned, "head", 1)]
@@ -629,13 +635,12 @@
         pick = [(near_keep, far_keep), (near_other, far_other)]
         last_send = sum(jnp.where(own, f, n).astype(F32) for n, f in pick).astype(BF16)
         signal_terms = [jnp.where(own, n, f)[0] for n, f in pick]
-        last_other = swap(last_send, "row", 2)
+        last_other = swap_halves(last_send, "row", 2, 1)
         signal_terms = [last_other[0]] + signal_terms
-        gate_send, _ = lax.optimization_barrier((gate_send, last_send))
-        gate_terms = [swap(gate_send, "row", 1), gate_keep]
+        gate_terms = [swap_halves(gate_send, "row", 1, 0), gate_keep]
         gate_last = sum(t[1:].astype(F32) for t in gate_terms).astype(BF16)
         gate_last, _ = lax.optimization_barrier((gate_last, last_other))
-        gate_terms = [t[0] for t in [swap(gate_last, "row", 2)] + gate_terms]
+        gate_terms = [t[0] for t in [swap_halves(gate_last, "row", 2, 1)] + gate_terms]
         sums, _ = lax.optimization_barrier((sums, last_send))
         sums = sum_over(sums, "head")
     else:
@@ -685,7 +690,7 @@
     feeds, _ = lax.optimization_barrier((feeds, rest))
     kept = [swap(second[half:], "head", 1), rest]
     if len(bits_of(heads_n)) == 2:
-        received = swap(send, "head", 2)
+        received = swap_halves(send, "head", 2, 1)
         mixer = sum(t[0].astype(F32) for t in [received[..., :feature_width]] + kept)
         gate_squares = gate_squares + join_lanes(received[0, :, feature_width:])
     else:

time: 76.9 us -> 72.2 us (0.939)
  waiting for transfers between devices: 20.3 us -> 17.5 us
  starting transfers between devices: 19.1 us -> 17.3 us
    ppermute x13 -> x17, waiting for transfers between devices: 20.3 us -> 12.1 us  [swap(): return lax.ppermute(values, axis, [(i, i ^ distance) for i in range(size)])]
    ppermute x1, waiting for transfers between devices: 0.01 us -> 5.4 us  [on_device(): turned = lax.ppermute(scaled_flat, ('head', 'row'), turn)]
    ppermute x13 -> x17, starting transfers between devices: 18.5 us -> 14.4 us  [swap(): return lax.ppermute(values, axis, [(i, i ^ distance) for i in range(size)])]
    ppermute x1, starting transfers between devices: 0.67 us -> 2.95 us  [on_device(): turned = lax.ppermute(scaled_flat, ('head', 'row'), turn)]
    unnamed x15 -> x17, local copies, waits for them, and re-layouts: 1.66 us -> 1.67 us
  transfers between devices with their start and end apart: 14 -> 18, of which waited for: 6 -> 8; matrix products, arithmetic and copies ran while one was open for 1% -> 1% of each run, Pallas kernels for 40% -> 42%
where the time goes in v11:
time: 72.2 us; the launch traced here: 72 us
  Pallas kernels  31.6 us (44%)
  waiting for transfers between devices  17.5 us (24%)
  starting transfers between devices  17.3 us (24%)
  local copies, waits for them, and re-layouts  2.19 us (3%)
  other arithmetic  1.82 us (3%)
  between operations  1.65 us (2%)
    ppermute x17, starting transfers between devices, swap(): return lax.ppermute(values, axis, [(i, i ^ distance) for i in range(size)])  14.4 us
    ppermute x17, waiting for transfers between devices, swap(): return lax.ppermute(values, axis, [(i, i ^ distance) for i in range(size)])  12.1 us
    pallas_call x3, Pallas kernels, load(): pl.pallas_call(functools.partial(load_body, spans), out_shape=tuple((pltp...  11.1 us
    ppermute x1, waiting for transfers between devices, on_device(): turned = lax.ppermute(scaled_flat, ('head', 'row'), turn)  5.4 us
    pallas_call x1, Pallas kernels, state_write(): pl.pallas_call(state_write_body, out_shape=jax.ShapeDtypeStruct(state.sha...  4.89 us
    pallas_call x1, Pallas kernels, recur(): pl.pallas_call(functools.partial(recur_body, len(terms), group, model_wid...  4.84 us
    pallas_call x1, Pallas kernels, adapt(): pl.pallas_call(adapt_body, out_shape=(jax.ShapeDtypeStruct((rows, rank +...  3.66 us
    pallas_call x3, Pallas kernels, output_parts(): pl.pallas_call(body, out_shape=tuple(out_shape), in_specs=specs, out_spec...  3.41 us
  transfers between devices with their start and end apart: 18, of which 8 were waited for; matrix products, arithmetic and copies ran while one was open for 1% of the time, Pallas kernels for 42%

profile of v11, /device:TPU:0, one launch (start us, length us, event | category | flops | bytes accessed | tf_op | source)
XLA Modules:
  0.0 72.0 jit_solution(17156676744491142958)
XLA Ops:
  0.6 1.1 %fusion.1 = (f32[2,32]{1,0:T(2,128)S(1)}, bf16[2,32,2048]{2,1,0:T(8,128)(2,1)S(1)}) fusion(bf16[32,2,2048]{2,1,0:T(2,128)(2,1)} %param.16, f32[2048]{0:T(1024)} %param.17), kind=kLoop, calls=%fused_computation.4 | loop fusion | flops 655296 | bytes 532736 | tf_op jit(solution)/shard_map/reduce_sum | solution.py:604
  1.8 3.0 %collective-permute-start = (bf16[64,2048]{1,0:T(8,128)(2,1)S(1)}, bf16[64,2048]{1,0:T(8,128)(2,1)S(1)}, u32[]{:S(2)}, u32[]{:S(2)}) collective-permute-start(bf16[64,2048]{1,0:T(8,128)(2,1)S(1)} %bitcast.35), channel_id=1, source_target_pairs={{0,8},{1,12},{2,0},{3,4},{4,9},{5,13},{6,1},{7,5},{8,10},{9,14},{1... | collective-permute-start | bytes 786440 | tf_op jit(solution)/shard_map/ppermute | solution.py:616
  5.5 3.7 %adapt.1 = (f32[64,17]{1,0:T(8,128)S(1)}, bf16[512,1024]{1,0:T(8,128)(2,1)S(1)}) custom-call(s32[32]{0:T(128)S(1)} %copy-done.2, bf16[64,2048]{1,0:T(8,128)(2,1)S(1)} %bitcast.36, f32[64,1]{1,0:T(8,128)S(1)} %reshape.29.squares_ref, bf16[128,16,2048]{2,1,0:T(8,128)(2,1)} %bitcast.45, bf16[128,16,1024]{2,1,0:T(8,128)(2,1)} %up_ref.1), custom_call_target="tpu_custom_call" | custom-call | flops 134217728 | bytes 3145728 | tf_op jit(solution)/shard_map/adapt/pallas_call | solution.py:145
  9.2 3.9 %load.3 = (bf16[2048,1024]{1,0:T(8,128)(2,1)S(1)}, bf16[2048,256]{1,0:T(8,128)(2,1)S(1)}, bf16[2048,1024]{1,0:T(8,128)(2,1)S(1)}) custom-call(f32[64,17]{1,0:T(8,128)S(1)} %get-tuple-element.52.after_ref, bf16[2048,1024]{1,0:T(8,128)(2,1)} %refs_0_.2, bf16[2048,256]{1,0:T(8,128)(2,1)} %refs_1_.2, bf16[2048,1024]{1,0:T(8,128)(2,1)} %refs_2_.1), custom_call_target="tpu_custom_call" | custom-call | bytes 18874368 | tf_op jit(solution)/shard_map/load/pallas_call | solution.py:82
  13.1 5.4 %collective-permute-done.after_ref.refs_0_ = bf16[64,2048]{1,0:T(8,128)(2,1)S(1)} collective-permute-done((bf16[64,2048]{1,0:T(8,128)(2,1)S(1)}, bf16[64,2048]{1,0:T(8,128)(2,1)S(1)}, u32[]{:S(2)}, u32[]{:S(2)}) %collective-permute-start) | collective-permute-done | bytes 262176 | tf_op jit(solution)/shard_map/ppermute | solution.py:616
  18.5 3.5 %load.4.refs_6_.refs_0_ = bf16[512,8192]{1,0:T(8,128)(2,1)S(1)} custom-call(bf16[64,2048]{1,0:T(8,128)(2,1)S(1)} %collective-permute-done.after_ref.refs_0_, bf16[1024,8192]{1,0:T(8,128)(2,1)} %refs_1_.3), custom_call_target="tpu_custom_call" | custom-call | bytes 16777216 | tf_op jit(solution)/shard_map/load/pallas_call | solution.py:82
  22.0 2.9 %collective-permute-done.2.refs_2_.refs_0_ = bf16[64,2048]{1,0:T(8,128)(2,1)S(1)} collective-permute-done((bf16[64,2048]{1,0:T(8,128)(2,1)S(1)}, bf16[64,2048]{1,0:T(8,128)(2,1)S(1)}, u32[]{:S(2)}, u32[]{:S(2)}) %collective-permute-start.2) | collective-permute-done | bytes 262176 | tf_op jit(solution)/shard_map/ppermute | solution.py:18
  25.5 1.1 %project_signal.2 = (bf16[1,64,1296]{2,1,0:T(8,128)(2,1)S(1)}, bf16[1,64,1296]{2,1,0:T(8,128)(2,1)S(1)}, bf16[128,2048]{1,0:T(8,128)(2,1)S(1)}) custom-call(bf16[64,2048]{1,0:T(8,128)(2,1)S(1)} %collective-permute-done.after_ref.refs_0_, bf16[64,2048]{1,0:T(8,128)(2,1)S(1)} %collective-permute-done.1.refs_1_, ...), custom_call_target="tpu_custom_call" | custom-call | flops 679477248 | bytes 5308416 | tf_op jit(solution)/shard_map/project_signal/pallas_call | solution.py:211
  26.6 1.4 %collective-permute-start.6 = (bf16[1,64,1296]{2,1,0:T(8,128)(2,1)S(1)}, bf16[1,64,1296]{2,1,0:T(8,128)(2,1)S(1)}, u32[]{:S(2)}, u32[]{:S(2)}) collective-permute-start(bf16[1,64,1296]{2,1,0:T(8,128)(2,1)S(1)} %get-tuple-element.41.refs_2_), channel_id=1, source_target_pairs={{0,1},{1,0},{2,3},{3,2},{4,5},{5,4},{6,7},{7,6},{8,9},{9,8},{10,11... | collective-permute-start | bytes 497672 | tf_op jit(solution)/shard_map/ppermute | solution.py:18
  28.0 1.1 %project_signal.3 = (bf16[1,64,1296]{2,1,0:T(8,128)(2,1)S(1)}, bf16[1,64,1296]{2,1,0:T(8,128)(2,1)S(1)}, bf16[128,2048]{1,0:T(8,128)(2,1)S(1)}) custom-call(bf16[64,2048]{1,0:T(8,128)(2,1)S(1)} %collective-permute-done.2.refs_2_.refs_0_, bf16[64,2048]{1,0:T(8,128)(2,1)S(1)} %collective-permute-done.3.refs_1_, ...), custom_call_target="tpu_custom_call" | custom-call | flops 679477248 | bytes 5308416 | tf_op jit(solution)/shard_map/project_signal/pallas_call | solution.py:211
  29.8 1.3 %project_gate.1 = (bf16[2,64,1024]{2,1,0:T(8,128)(2,1)S(1)}, bf16[2,64,1024]{2,1,0:T(8,128)(2,1)S(1)}) custom-call(bf16[128,2048]{1,0:T(8,128)(2,1)S(1)} %get-tuple-element.40.refs_0_, bf16[128,2048]{1,0:T(8,128)(2,1)S(1)} %get-tuple-element.42.refs_1_, bf16[2048,1024]{1,0:T(8,128)(2,1)S(1)} %get-tuple-element.43.refs_2_, ...), custom_call_target="tpu_custom_call" | custom-call | flops 1073741824 | bytes 4194304 | tf_op jit(solution)/shard_map/project_gate/pallas_call | solution.py:251
  31.1 1.4 %collective-permute-start.4 = (bf16[1,64,1024]{2,1,0:T(8,128)(2,1)S(1)}, bf16[1,64,1024]{2,1,0:T(8,128)(2,1)S(1)}, u32[]{:S(2)}, u32[]{:S(2)}) collective-permute-start(bf16[1,64,1024]{2,1,0:T(8,128)(2,1)S(1)} %get-tuple-element.71), channel_id=1, source_target_pairs={{0,1},{1,0},{2,3},{3,2},{4,5},{5,4},{6,7},{7,6},{8,9},{9,8},{10,11... | collective-permute-start | bytes 393224 | tf_op jit(solution)/shard_map/ppermute | solution.py:18
  32.6 3.7 %load.5 = (bf16[1,64,1296]{2,1,0:T(8,128)(2,1)S(1)}, bf16[512,8192]{1,0:T(8,128)(2,1)S(1)}) custom-call(bf16[2,64,1024]{2,1,0:T(8,128)(2,1)S(1)} %get-tuple-element.45.after_ref, bf16[1,64,1296]{2,1,0:T(8,128)(2,1)S(1)} %get-tuple-element.48.refs_0_, bf16[1024,8192]{1,0:T(8,128)(2,1)} %refs_1_.3), custom_call_target="tpu_custom_call" | custom-call | bytes 16777216 | tf_op jit(solution)/shard_map/load/pallas_call | solution.py:82
  38.0 2.2 %collective-permute-start.7 = (bf16[1,32,1296]{2,1,0:T(8,128)(2,1)S(1)}, bf16[1,32,1296]{2,1,0:T(8,128)(2,1)S(1)}, u32[]{:S(2)}, u32[]{:S(2)}) collective-permute-start(bf16[1,32,1296]{2,1,0:T(8,128)(2,1)S(1)} %get-tuple-element.75), channel_id=1, source_target_pairs={{0,2},{1,3},{2,0},{3,1},{4,6},{5,7},{6,4},{7,5},{8,10},{9,11},{10,... | collective-permute-start | bytes 248840 | tf_op jit(solution)/shard_map/ppermute | solution.py:18
  40.7 2.2 %collective-permute-start.8 = (bf16[1,32,1296]{2,1,0:T(8,128)(2,1)S(1)}, bf16[1,32,1296]{2,1,0:T(8,128)(2,1)S(1)}, u32[]{:S(2)}, u32[]{:S(2)}) collective-permute-start(bf16[1,32,1296]{2,1,0:T(8,128)(2,1)S(1)} %get-tuple-element.74), channel_id=1, source_target_pairs={{0,2},{1,3},{2,0},{3,1},{4,6},{5,7},{6,4},{7,5},{8,10},{9,11},{10,... | collective-permute-start | bytes 248840 | tf_op jit(solution)/shard_map/ppermute | solution.py:18
  43.1 1.3 %collective-permute-done.7 = bf16[1,32,1296]{2,1,0:T(8,128)(2,1)S(1)} collective-permute-done((bf16[1,32,1296]{2,1,0:T(8,128)(2,1)S(1)}, bf16[1,32,1296]{2,1,0:T(8,128)(2,1)S(1)}, u32[]{:S(2)}, u32[]{:S(2)}) %collective-permute-start.7) | collective-permute-done | bytes 82976 | tf_op jit(solution)/shard_map/ppermute | solution.py:18
  44.4 5.7 %collective-permute-done.8 = bf16[1,32,1296]{2,1,0:T(8,128)(2,1)S(1)} collective-permute-done((bf16[1,32,1296]{2,1,0:T(8,128)(2,1)S(1)}, bf16[1,32,1296]{2,1,0:T(8,128)(2,1)S(1)}, u32[]{:S(2)}, u32[]{:S(2)}) %collective-permute-start.8) | collective-permute-done | bytes 82976 | tf_op jit(solution)/shard_map/ppermute | solution.py:18
  50.2 2.9 %collective-permute-start.9 = (bf16[1,32,1024]{2,1,0:T(8,128)(2,1)S(1)}, bf16[1,32,1024]{2,1,0:T(8,128)(2,1)S(1)}, u32[]{:S(2)}, u32[]{:S(2)}) collective-permute-start(bf16[1,32,1024]{2,1,0:T(8,128)(2,1)S(1)} %get-tuple-element.76), channel_id=1, source_target_pairs={{0,2},{1,3},{2,0},{3,1},{4,6},{5,7},{6,4},{7,5},{8,10},{9,11},{10,... | collective-permute-start | bytes 196616 | tf_op jit(solution)/shard_map/ppermute | solution.py:18
  53.2 4.8 %recur.1 = (f32[64,1024]{1,0:T(8,128)S(1)}, f32[2,32,1024]{2,1,0:T(8,128)S(1)}, f32[2,32,128]{2,1,0:T(8,128)S(1)}, f32[32,16]{1,0:T(8,128)S(1)}, bf16[32,16,64,128]{3,2,1,0:T(8,128)(2,1)S(1)}) custom-call(s32[1]{0:T(128)} %copy.46.live_ref, bf16[64,1296]{1,0:T(8,128)(2,1)S(1)} %bitcast.37, bf16[64,1296]{1,0:T(8,128)(2,1)S(1)} %select_bitcast_fusion.1.refs_1_, ...), custom_call_target="tpu_custom_call" | custom-call | flops 268435456 | bytes 10485760 | tf_op jit(solution)/shard_map/recur/pallas_call | solution.py:384
  58.2 1.0 %output_first.1 = (bf16[1,64,2176]{2,1,0:T(8,128)(2,1)S(1)}, bf16[64,1024]{1,0:T(8,128)(2,1)S(1)}, f32[64,1]{1,0:T(8,128)S(1)}) custom-call(bf16[64,1024]{1,0:T(8,128)(2,1)S(1)} %maximum_bitcast_fusion.refs_0_, bf16[64,1024]{1,0:T(8,128)(2,1)S(1)} %bitcast.40, bf16[64,1024]{1,0:T(8,128)(2,1)S(1)} %slice_bitcast_fusion.refs_2_, f32[64,17]{1,0:T(8,128)S(1)} %add.39.refs_3_, ...), custom_call_target="tpu_custom_call" | custom-call | flops 268435456 | bytes 4194304 | tf_op jit(solution)/shard_map/output_first/pallas_call | solution.py:558
  59.3 1.6 %output_rest.2.own_ref = bf16[2,64,2048]{2,1,0:T(8,128)(2,1)S(1)} custom-call(bf16[64,1024]{1,0:T(8,128)(2,1)S(1)} %get-tuple-element.57.lhs_ref, bf16[1,64,2176]{2,1,0:T(8,128)(2,1)S(1)} %get-tuple-element.56.after_ref, bf16[512,8192]{1,0:T(8,128)(2,1)S(1)} %load.4.refs_6_.refs_0_, bf16[512,8192]{1,0:T(8,128)(2,1)S(1)} %get-tuple-element.55.refs_7_.refs_1_), custom_call_target="tpu_custom_call" | custom-call | flops 536870912 | bytes 8388608 | tf_op jit(solution)/shard_map/output_rest/pallas_call | solution.py:558
  61.2 1.3 %collective-permute-start.15 = (bf16[1,32,2176]{2,1,0:T(8,128)(2,1)S(1)}, bf16[1,32,2176]{2,1,0:T(8,128)(2,1)S(1)}, u32[]{:S(2)}, u32[]{:S(2)}) collective-permute-start(bf16[1,32,2176]{2,1,0:T(8,128)(2,1)S(1)} %get-tuple-element.69), channel_id=1, source_target_pairs={{0,8},{4,12},{8,0},{12,4},{1,9},{5,13},{9,1},{13,5},{2,10},{6,14},... | collective-permute-start | bytes 417800 | tf_op jit(solution)/shard_map/ppermute | solution.py:18
  64.6 4.9 %state_write.1 = bf16[32,16,64,128]{3,2,1,0:T(8,128)(2,1)} custom-call(f32[2,32,1024]{2,1,0:T(8,128)S(1)} %get-tuple-element.62.feeds_ref, f32[2,32,128]{2,1,0:T(8,128)S(1)} %get-tuple-element.63.b_ref, f32[32,16,128]{2,1,0:T(8,128)S(1)} %broadcast_in_dim.42.decay_ref, bf16[32,16,64,128]{3,2,1,0:T(8,128)(2,1)S(1)} %get-tuple-element.65.state_ref), custom_call_target="tpu_custom_call" | custom-call | flops 134217728 | bytes 16777216 | tf_op jit(solution)/shard_map/state_write/pallas_call | solution.py:446
  71.0 1.0 %copy.39 = bf16[32,2,2048]{2,1,0:T(2,128)(2,1)} copy(bf16[32,2,2048]{2,0,1:T(8,128)(2,1)S(1)} %fusion.3) | data formatting | bytes 524288
  (67 shorter events, 8.0 us)
Async XLA Ops:
  1.8 16.7 %collective-permute-start = (bf16[64,2048]{1,0:T(8,128)(2,1)S(1)}, bf16[64,2048]{1,0:T(8,128)(2,1)S(1)}, u32[]{:S(2)}, u32[]{:S(2)}) collective-permute-start(bf16[64,2048]{1,0:T(8,128)(2,1)S(1)} %bitcast.35), channel_id=1, source_target_pairs={{0,8},{1,12},{2,0},{3,4},{4,9},{5,13},{6,1},{7,5},{8,10},{9,14},{1... | collective-permute-start | bytes 786440 | tf_op jit(solution)/shard_map/ppermute | solution.py:616
  18.5 7.0 %copy-start = (bf16[2048,16]{0,1:T(8,128)(2,1)S(1)}, bf16[2048,16]{0,1:T(8,128)(2,1)}, u32[]{:S(2)}) copy-start(bf16[2048,16]{0,1:T(8,128)(2,1)} %param.20) | copy-start | bytes 196612
  18.5 6.4 %collective-permute-start.2 = (bf16[64,2048]{1,0:T(8,128)(2,1)S(1)}, bf16[64,2048]{1,0:T(8,128)(2,1)S(1)}, u32[]{:S(2)}, u32[]{:S(2)}) collective-permute-start(bf16[64,2048]{1,0:T(8,128)(2,1)S(1)} %collective-permute-done.after_ref.refs_0_), channel_id=1, source_target_pairs={{0,8},{4,12},{8,0},{12,4},{1,9},{5,13},{9,1},{13,5},{2,10},{6,14},... | collective-permute-start | bytes 786440 | tf_op jit(solution)/shard_map/ppermute | solution.py:18
  18.5 7.0 %collective-permute-start.1 = (bf16[64,2048]{1,0:T(8,128)(2,1)S(1)}, bf16[64,2048]{1,0:T(8,128)(2,1)S(1)}, u32[]{:S(2)}, u32[]{:S(2)}) collective-permute-start(bf16[64,2048]{1,0:T(8,128)(2,1)S(1)} %collective-permute-done.after_ref.refs_0_), channel_id=1, source_target_pairs={{0,4},{4,0},{8,12},{12,8},{1,5},{5,1},{9,13},{13,9},{2,6},{6,2},{1... | collective-permute-start | bytes 786440 | tf_op jit(solution)/shard_map/ppermute | solution.py:18
  24.8 3.2 %collective-permute-start.3 = (bf16[64,2048]{1,0:T(8,128)(2,1)S(1)}, bf16[64,2048]{1,0:T(8,128)(2,1)S(1)}, u32[]{:S(2)}, u32[]{:S(2)}) collective-permute-start(bf16[64,2048]{1,0:T(8,128)(2,1)S(1)} %collective-permute-done.2.refs_2_.refs_0_), channel_id=1, source_target_pairs={{0,4},{4,0},{8,12},{12,8},{1,5},{5,1},{9,13},{13,9},{2,6},{6,2},{1... | collective-permute-start | bytes 786440 | tf_op jit(solution)/shard_map/ppermute | solution.py:18
  26.6 10.5 %collective-permute-start.6 = (bf16[1,64,1296]{2,1,0:T(8,128)(2,1)S(1)}, bf16[1,64,1296]{2,1,0:T(8,128)(2,1)S(1)}, u32[]{:S(2)}, u32[]{:S(2)}) collective-permute-start(bf16[1,64,1296]{2,1,0:T(8,128)(2,1)S(1)} %get-tuple-element.41.refs_2_), channel_id=1, source_target_pairs={{0,1},{1,0},{2,3},{3,2},{4,5},{5,4},{6,7},{7,6},{8,9},{9,8},{10,11... | collective-permute-start | bytes 497672 | tf_op jit(solution)/shard_map/ppermute | solution.py:18
  29.1 8.8 %collective-permute-start.5 = (bf16[1,64,1296]{2,1,0:T(8,128)(2,1)S(1)}, bf16[1,64,1296]{2,1,0:T(8,128)(2,1)S(1)}, u32[]{:S(2)}, u32[]{:S(2)}) collective-permute-start(bf16[1,64,1296]{2,1,0:T(8,128)(2,1)S(1)} %get-tuple-element.44.refs_3_), channel_id=1, source_target_pairs={{0,1},{1,0},{2,3},{3,2},{4,5},{5,4},{6,7},{7,6},{8,9},{9,8},{10,11... | collective-permute-start | bytes 497672 | tf_op jit(solution)/shard_map/ppermute | solution.py:18
  31.1 9.6 %collective-permute-start.4 = (bf16[1,64,1024]{2,1,0:T(8,128)(2,1)S(1)}, bf16[1,64,1024]{2,1,0:T(8,128)(2,1)S(1)}, u32[]{:S(2)}, u32[]{:S(2)}) collective-permute-start(bf16[1,64,1024]{2,1,0:T(8,128)(2,1)S(1)} %get-tuple-element.71), channel_id=1, source_target_pairs={{0,1},{1,0},{2,3},{3,2},{4,5},{5,4},{6,7},{7,6},{8,9},{9,8},{10,11... | collective-permute-start | bytes 393224 | tf_op jit(solution)/shard_map/ppermute | solution.py:18
  32.6 20.6 %copy-start.3 = (f32[16]{0:T(128)S(1)}, f32[16]{0:T(128)}, u32[]{:S(2)}) copy-start(f32[16]{0:T(128)} %param.22) | copy-start | bytes 196
  32.6 20.6 %copy-start.4 = (f32[16]{0:T(128)S(1)}, f32[16]{0:T(128)}, u32[]{:S(2)}) copy-start(f32[16]{0:T(128)} %param.23) | copy-start | bytes 196
  32.6 20.6 %copy-start.5 = (f32[16]{0:T(128)S(1)}, f32[16]{0:T(128)}, u32[]{:S(2)}) copy-start(f32[16]{0:T(128)} %param.24) | copy-start | bytes 196
  36.3 22.0 %copy-start.1 = (f32[1024]{0:T(1024)S(1)}, f32[1024]{0:T(1024)}, u32[]{:S(2)}) copy-start(f32[1024]{0:T(1024)} %param.25) | copy-start | bytes 12292
  36.3 21.9 %collective-permute-start.11 = (bf16[1,64,1024]{2,1,0:T(8,128)(2,1)S(1)}, bf16[1,64,1024]{2,1,0:T(8,128)(2,1)S(1)}, u32[]{:S(2)}, u32[]{:S(2)}) collective-permute-start(bf16[1,64,1024]{2,1,0:T(8,128)(2,1)S(1)} %get-tuple-element.70), channel_id=1, source_target_pairs={{0,1},{1,0},{2,3},{3,2},{4,5},{5,4},{6,7},{7,6},{8,9},{9,8},{10,11... | collective-permute-start | bytes 393224 | tf_op jit(solution)/shard_map/ppermute | solution.py:18
  38.0 6.4 %collective-permute-start.7 = (bf16[1,32,1296]{2,1,0:T(8,128)(2,1)S(1)}, bf16[1,32,1296]{2,1,0:T(8,128)(2,1)S(1)}, u32[]{:S(2)}, u32[]{:S(2)}) collective-permute-start(bf16[1,32,1296]{2,1,0:T(8,128)(2,1)S(1)} %get-tuple-element.75), channel_id=1, source_target_pairs={{0,2},{1,3},{2,0},{3,1},{4,6},{5,7},{6,4},{7,5},{8,10},{9,11},{10,... | collective-permute-start | bytes 248840 | tf_op jit(solution)/shard_map/ppermute | solution.py:18
  40.2 2.7 %collective-permute-start.12 = (f32[64,17]{1,0:T(8,128)S(1)}, f32[64,17]{1,0:T(8,128)S(1)}, u32[]{:S(2)}, u32[]{:S(2)}) collective-permute-start(f32[64,17]{1,0:T(8,128)S(1)} %get-tuple-element.52.after_ref), channel_id=1, source_target_pairs={{0,4},{4,0},{8,12},{12,8},{1,5},{5,1},{9,13},{13,9},{2,6},{6,2},{1... | collective-permute-start | bytes 13064 | tf_op jit(solution)/shard_map/ppermute | solution.py:18
  40.7 9.3 %collective-permute-start.8 = (bf16[1,32,1296]{2,1,0:T(8,128)(2,1)S(1)}, bf16[1,32,1296]{2,1,0:T(8,128)(2,1)S(1)}, u32[]{:S(2)}, u32[]{:S(2)}) collective-permute-start(bf16[1,32,1296]{2,1,0:T(8,128)(2,1)S(1)} %get-tuple-element.74), channel_id=1, source_target_pairs={{0,2},{1,3},{2,0},{3,1},{4,6},{5,7},{6,4},{7,5},{8,10},{9,11},{10,... | collective-permute-start | bytes 248840 | tf_op jit(solution)/shard_map/ppermute | solution.py:18
  43.0 10.1 %collective-permute-start.13 = (f32[64,17]{1,0:T(8,128)S(1)}, f32[64,17]{1,0:T(8,128)S(1)}, u32[]{:S(2)}, u32[]{:S(2)}) collective-permute-start(f32[64,17]{1,0:T(8,128)S(1)} %add.38), channel_id=1, source_target_pairs={{0,8},{4,12},{8,0},{12,4},{1,9},{5,13},{9,1},{13,5},{2,10},{6,14},... | collective-permute-start | bytes 13064 | tf_op jit(solution)/shard_map/ppermute | solution.py:18
  50.1 7.9 %collective-permute-start.10 = (bf16[1,32,1024]{2,1,0:T(8,128)(2,1)S(1)}, bf16[1,32,1024]{2,1,0:T(8,128)(2,1)S(1)}, u32[]{:S(2)}, u32[]{:S(2)}) collective-permute-start(bf16[1,32,1024]{2,1,0:T(8,128)(2,1)S(1)} %get-tuple-element.77), channel_id=1, source_target_pairs={{0,2},{1,3},{2,0},{3,1},{4,6},{5,7},{6,4},{7,5},{8,10},{9,11},{10,... | collective-permute-start | bytes 196616 | tf_op jit(solution)/shard_map/ppermute | solution.py:18
  50.2 8.0 %collective-permute-start.9 = (bf16[1,32,1024]{2,1,0:T(8,128)(2,1)S(1)}, bf16[1,32,1024]{2,1,0:T(8,128)(2,1)S(1)}, u32[]{:S(2)}, u32[]{:S(2)}) collective-permute-start(bf16[1,32,1024]{2,1,0:T(8,128)(2,1)S(1)} %get-tuple-element.76), channel_id=1, source_target_pairs={{0,2},{1,3},{2,0},{3,1},{4,6},{5,7},{6,4},{7,5},{8,10},{9,11},{10,... | collective-permute-start | bytes 196616 | tf_op jit(solution)/shard_map/ppermute | solution.py:18
  59.2 1.7 %collective-permute-start.14 = (bf16[1,64,2176]{2,1,0:T(8,128)(2,1)S(1)}, bf16[1,64,2176]{2,1,0:T(8,128)(2,1)S(1)}, u32[]{:S(2)}, u32[]{:S(2)}) collective-permute-start(bf16[1,64,2176]{2,1,0:T(8,128)(2,1)S(1)} %get-tuple-element.56.after_ref), channel_id=1, source_target_pairs={{0,4},{4,0},{8,12},{12,8},{1,5},{5,1},{9,13},{13,9},{2,6},{6,2},{1... | collective-permute-start | bytes 835592 | tf_op jit(solution)/shard_map/ppermute | solution.py:18
  61.2 8.3 %collective-permute-start.15 = (bf16[1,32,2176]{2,1,0:T(8,128)(2,1)S(1)}, bf16[1,32,2176]{2,1,0:T(8,128)(2,1)S(1)}, u32[]{:S(2)}, u32[]{:S(2)}) collective-permute-start(bf16[1,32,2176]{2,1,0:T(8,128)(2,1)S(1)} %get-tuple-element.69), channel_id=1, source_target_pairs={{0,8},{4,12},{8,0},{12,4},{1,9},{5,13},{9,1},{13,5},{2,10},{6,14},... | collective-permute-start | bytes 417800 | tf_op jit(solution)/shard_map/ppermute | solution.py:18
  62.6 8.2 %collective-permute-start.17 = (bf16[1,64,2048]{2,1,0:T(8,128)(2,1)S(1)}, bf16[1,64,2048]{2,1,0:T(8,128)(2,1)S(1)}, u32[]{:S(2)}, u32[]{:S(2)}) collective-permute-start(bf16[1,64,2048]{2,1,0:T(8,128)(2,1)S(1)} %slice.21), channel_id=1, source_target_pairs={{0,4},{4,0},{8,12},{12,8},{1,5},{5,1},{9,13},{13,9},{2,6},{6,2},{1... | collective-permute-start | bytes 786440 | tf_op jit(solution)/shard_map/ppermute | solution.py:18
  62.8 7.5 %collective-permute-start.16 = (bf16[1,32,2176]{2,1,0:T(8,128)(2,1)S(1)}, bf16[1,32,2176]{2,1,0:T(8,128)(2,1)S(1)}, u32[]{:S(2)}, u32[]{:S(2)}) collective-permute-start(bf16[1,32,2176]{2,1,0:T(8,128)(2,1)S(1)} %get-tuple-element.68), channel_id=1, source_target_pairs={{0,8},{4,12},{8,0},{12,4},{1,9},{5,13},{9,1},{13,5},{2,10},{6,14},... | collective-permute-start | bytes 417800 | tf_op jit(solution)/shard_map/ppermute | solution.py:18
  64.6 6.3 %copy-start.6 = (bf16[32,2,2048]{2,1,0:T(2,128)(2,1)S(1)}, bf16[32,2,2048]{2,1,0:T(2,128)(2,1)}, u32[]{:S(2)}) copy-start(bf16[32,2,2048]{2,1,0:T(2,128)(2,1)} %param.16) | copy-start | bytes 786436
  (1 other events, 0.7 us)

commit v12 on v11

--- a/solution.py
+++ b/solution.py
@@ -630,19 +630,21 @@
         near_other = swap(near_send, "row", 1)
         far_send, far_keep, far_lhs = project_signal(far, order(2), 2, *signal_weights, near_send)
         far_other = swap(far_send, "row", 1)
+        sums, _ = lax.optimization_barrier((sums, far_send))
+        sums = sum_over(sums, "head")
         gate_send, gate_keep = project_gate(rows, [near_lhs, far_lhs], weights[2], far_send)
-        far_keep, out_late = load(gate_send, [far_keep], (output_weight, middle, middle))
+        gate_own, gate_far = [swap(part, "row", 1) for part in jnp.split(gate_send, 2, 0)]
         pick = [(near_keep, far_keep), (near_other, far_other)]
         last_send = sum(jnp.where(own, f, n).astype(F32) for n, f in pick).astype(BF16)
+        last_send, sums = lax.optimization_barrier((last_send, sums))
+        last_other = [swap(part, "row", 2) for part in jnp.split(last_send, 2, 1)]
+        (out_late,) = load(last_send, [], (output_weight, middle, middle))
         signal_terms = [jnp.where(own, n, f)[0] for n, f in pick]
-        last_other = swap_halves(last_send, "row", 2, 1)
-        signal_terms = [last_other[0]] + signal_terms
-        gate_terms = [swap_halves(gate_send, "row", 1, 0), gate_keep]
-        gate_last = sum(t[1:].astype(F32) for t in gate_terms).astype(BF16)
-        gate_last, _ = lax.optimization_barrier((gate_last, last_other))
-        gate_terms = [t[0] for t in [swap_halves(gate_last, "row", 2, 1)] + gate_terms]
-        sums, _ = lax.optimization_barrier((sums, last_send))
-        sums = sum_over(sums, "head")
+        signal_terms = [jnp.concatenate(last_other, 1)[0]] + signal_terms
+        gate_far, _ = lax.optimization_barrier((gate_far, last_other[0]))
+        gate_last = (gate_far.astype(F32) + gate_keep[1:].astype(F32)).astype(BF16)
+        gate_terms = [swap_halves(gate_last, "row", 2, 1)[0], gate_own[0], gate_keep[0]]
+        gate_last, out_late = lax.optimization_barrier((gate_last, out_late))
     else:
         features = lax.all_gather(scaled_flat, "head", axis=1, tiled=True)
         blocks = lax.all_to_all(features, "row", split_axis=1, concat_axis=0, tiled=True)

time: 72.2 us -> 70.8 us (0.981)
  waiting for transfers between devices: 17.5 us -> 15.3 us
  starting transfers between devices: 17.3 us -> 18.1 us
    ppermute x17, waiting for transfers between devices: 12.1 us -> 10 us  [swap(): return lax.ppermute(values, axis, [(i, i ^ distance) for i in range(size)])]
    ppermute x17, starting transfers between devices: 14.4 us -> 15.2 us  [swap(): return lax.ppermute(values, axis, [(i, i ^ distance) for i in range(size)])]
    unnamed x17 -> x16, local copies, waits for them, and re-layouts: 1.67 us -> 1.67 us
  transfers between devices with their start and end apart: 18 -> 18, of which waited for: 8 -> 8; matrix products, arithmetic and copies ran while one was open for 1% -> 1% of each run, Pallas kernels for 42% -> 43%
where the time goes in v12:
time: 70.8 us; the launch traced here: 70.6 us
  Pallas kernels  31.5 us (44%)
  starting transfers between devices  18.1 us (26%)
  waiting for transfers between devices  15.3 us (22%)
  local copies, waits for them, and re-layouts  2.18 us (3%)
  other arithmetic  1.84 us (3%)
  between operations  1.65 us (2%)
    ppermute x17, starting transfers between devices, swap(): return lax.ppermute(values, axis, [(i, i ^ distance) for i in range(size)])  15.2 us
    pallas_call x3, Pallas kernels, load(): pl.pallas_call(functools.partial(load_body, spans), out_shape=tuple((pltp...  10.9 us
    ppermute x17, waiting for transfers between devices, swap(): return lax.ppermute(values, axis, [(i, i ^ distance) for i in range(size)])  10 us
    ppermute x1, waiting for transfers between devices, on_device(): turned = lax.ppermute(scaled_flat, ('head', 'row'), turn)  5.27 us
    pallas_call x1, Pallas kernels, state_write(): pl.pallas_call(state_write_body, out_shape=jax.ShapeDtypeStruct(state.sha...  4.89 us
    pallas_call x1, Pallas kernels, recur(): pl.pallas_call(functools.partial(recur_body, len(terms), group, model_wid...  4.84 us
    pallas_call x1, Pallas kernels, adapt(): pl.pallas_call(adapt_body, out_shape=(jax.ShapeDtypeStruct((rows, rank +...  3.79 us
    pallas_call x3, Pallas kernels, output_parts(): pl.pallas_call(body, out_shape=tuple(out_shape), in_specs=specs, out_spec...  3.42 us
  transfers between devices with their start and end apart: 18, of which 8 were waited for; matrix products, arithmetic and copies ran while one was open for 1% of the time, Pallas kernels for 43%

profile of v12, /device:TPU:0, one launch (start us, length us, event | category | flops | bytes accessed | tf_op | source)
XLA Modules:
  0.0 70.6 jit_solution(16492571631340099117)
XLA Ops:
  0.6 1.1 %fusion.1 = (f32[2,32]{1,0:T(2,128)S(1)}, bf16[2,32,2048]{2,1,0:T(8,128)(2,1)S(1)}) fusion(bf16[32,2,2048]{2,1,0:T(2,128)(2,1)} %param.16, f32[2048]{0:T(1024)} %param.17), kind=kLoop, calls=%fused_computation.4 | loop fusion | flops 655296 | bytes 532736 | tf_op jit(solution)/shard_map/reduce_sum | solution.py:604
  1.8 3.0 %collective-permute-start = (bf16[64,2048]{1,0:T(8,128)(2,1)S(1)}, bf16[64,2048]{1,0:T(8,128)(2,1)S(1)}, u32[]{:S(2)}, u32[]{:S(2)}) collective-permute-start(bf16[64,2048]{1,0:T(8,128)(2,1)S(1)} %bitcast.36), channel_id=1, source_target_pairs={{0,8},{1,12},{2,0},{3,4},{4,9},{5,13},{6,1},{7,5},{8,10},{9,14},{1... | collective-permute-start | bytes 786440 | tf_op jit(solution)/shard_map/ppermute | solution.py:616
  5.5 3.8 %adapt.1 = (f32[64,17]{1,0:T(8,128)S(1)}, bf16[512,1024]{1,0:T(8,128)(2,1)S(1)}) custom-call(s32[32]{0:T(128)S(1)} %copy-done.2, bf16[64,2048]{1,0:T(8,128)(2,1)S(1)} %bitcast.37, f32[64,1]{1,0:T(8,128)S(1)} %reshape.29.squares_ref, bf16[128,16,2048]{2,1,0:T(8,128)(2,1)} %bitcast.45, bf16[128,16,1024]{2,1,0:T(8,128)(2,1)} %up_ref.1), custom_call_target="tpu_custom_call" | custom-call | flops 134217728 | bytes 3145728 | tf_op jit(solution)/shard_map/adapt/pallas_call | solution.py:145
  9.3 3.9 %load.3 = (bf16[2048,1024]{1,0:T(8,128)(2,1)S(1)}, bf16[2048,256]{1,0:T(8,128)(2,1)S(1)}, bf16[2048,1024]{1,0:T(8,128)(2,1)S(1)}) custom-call(f32[64,17]{1,0:T(8,128)S(1)} %get-tuple-element.51.after_ref, bf16[2048,1024]{1,0:T(8,128)(2,1)} %refs_0_.3, bf16[2048,256]{1,0:T(8,128)(2,1)} %refs_1_.1, bf16[2048,1024]{1,0:T(8,128)(2,1)} %refs_2_.1), custom_call_target="tpu_custom_call" | custom-call | bytes 18874368 | tf_op jit(solution)/shard_map/load/pallas_call | solution.py:82
  13.2 5.3 %collective-permute-done.after_ref.refs_0_ = bf16[64,2048]{1,0:T(8,128)(2,1)S(1)} collective-permute-done((bf16[64,2048]{1,0:T(8,128)(2,1)S(1)}, bf16[64,2048]{1,0:T(8,128)(2,1)S(1)}, u32[]{:S(2)}, u32[]{:S(2)}) %collective-permute-start) | collective-permute-done | bytes 262176 | tf_op jit(solution)/shard_map/ppermute | solution.py:616
  18.5 3.5 %load.4.refs_6_.refs_0_ = bf16[512,8192]{1,0:T(8,128)(2,1)S(1)} custom-call(bf16[64,2048]{1,0:T(8,128)(2,1)S(1)} %collective-permute-done.after_ref.refs_0_, bf16[1024,8192]{1,0:T(8,128)(2,1)} %refs_0_.5), custom_call_target="tpu_custom_call" | custom-call | bytes 16777216 | tf_op jit(solution)/shard_map/load/pallas_call | solution.py:82
  22.0 2.9 %collective-permute-done.2.refs_2_.refs_0_ = bf16[64,2048]{1,0:T(8,128)(2,1)S(1)} collective-permute-done((bf16[64,2048]{1,0:T(8,128)(2,1)S(1)}, bf16[64,2048]{1,0:T(8,128)(2,1)S(1)}, u32[]{:S(2)}, u32[]{:S(2)}) %collective-permute-start.2) | collective-permute-done | bytes 262176 | tf_op jit(solution)/shard_map/ppermute | solution.py:18
  25.5 1.1 %project_signal.2 = (bf16[1,64,1296]{2,1,0:T(8,128)(2,1)S(1)}, bf16[1,64,1296]{2,1,0:T(8,128)(2,1)S(1)}, bf16[128,2048]{1,0:T(8,128)(2,1)S(1)}) custom-call(bf16[64,2048]{1,0:T(8,128)(2,1)S(1)} %collective-permute-done.after_ref.refs_0_, bf16[64,2048]{1,0:T(8,128)(2,1)S(1)} %collective-permute-done.1.refs_1_, ...), custom_call_target="tpu_custom_call" | custom-call | flops 679477248 | bytes 5308416 | tf_op jit(solution)/shard_map/project_signal/pallas_call | solution.py:211
  26.6 1.4 %collective-permute-start.6 = (bf16[1,64,1296]{2,1,0:T(8,128)(2,1)S(1)}, bf16[1,64,1296]{2,1,0:T(8,128)(2,1)S(1)}, u32[]{:S(2)}, u32[]{:S(2)}) collective-permute-start(bf16[1,64,1296]{2,1,0:T(8,128)(2,1)S(1)} %get-tuple-element.43.refs_2_), channel_id=1, source_target_pairs={{0,1},{1,0},{2,3},{3,2},{4,5},{5,4},{6,7},{7,6},{8,9},{9,8},{10,11... | collective-permute-start | bytes 497672 | tf_op jit(solution)/shard_map/ppermute | solution.py:18
  28.0 1.1 %project_signal.3 = (bf16[1,64,1296]{2,1,0:T(8,128)(2,1)S(1)}, bf16[1,64,1296]{2,1,0:T(8,128)(2,1)S(1)}, bf16[128,2048]{1,0:T(8,128)(2,1)S(1)}) custom-call(bf16[64,2048]{1,0:T(8,128)(2,1)S(1)} %collective-permute-done.2.refs_2_.refs_0_, bf16[64,2048]{1,0:T(8,128)(2,1)S(1)} %collective-permute-done.3.refs_1_, ...), custom_call_target="tpu_custom_call" | custom-call | flops 679477248 | bytes 5308416 | tf_op jit(solution)/shard_map/project_signal/pallas_call | solution.py:211
  29.8 1.3 %project_gate.1 = (bf16[2,64,1024]{2,1,0:T(8,128)(2,1)S(1)}, bf16[2,64,1024]{2,1,0:T(8,128)(2,1)S(1)}) custom-call(bf16[128,2048]{1,0:T(8,128)(2,1)S(1)} %get-tuple-element.42.refs_0_, bf16[128,2048]{1,0:T(8,128)(2,1)S(1)} %get-tuple-element.44.refs_1_, bf16[2048,1024]{1,0:T(8,128)(2,1)S(1)} %get-tuple-element.45.refs_2_, ...), custom_call_target="tpu_custom_call" | custom-call | flops 1073741824 | bytes 4194304 | tf_op jit(solution)/shard_map/project_gate/pallas_call | solution.py:251
  31.1 1.4 %collective-permute-start.4 = (bf16[1,64,1024]{2,1,0:T(8,128)(2,1)S(1)}, bf16[1,64,1024]{2,1,0:T(8,128)(2,1)S(1)}, u32[]{:S(2)}, u32[]{:S(2)}) collective-permute-start(bf16[1,64,1024]{2,1,0:T(8,128)(2,1)S(1)} %get-tuple-element.75), channel_id=1, source_target_pairs={{0,1},{1,0},{2,3},{3,2},{4,5},{5,4},{6,7},{7,6},{8,9},{9,8},{10,11... | collective-permute-start | bytes 393224 | tf_op jit(solution)/shard_map/ppermute | solution.py:18
  33.8 1.7 %collective-permute-start.8 = (f32[64,17]{1,0:T(8,128)S(1)}, f32[64,17]{1,0:T(8,128)S(1)}, u32[]{:S(2)}, u32[]{:S(2)}) collective-permute-start(f32[64,17]{1,0:T(8,128)S(1)} %add.37), channel_id=1, source_target_pairs={{0,8},{4,12},{8,0},{12,4},{1,9},{5,13},{9,1},{13,5},{2,10},{6,14},... | collective-permute-start | bytes 13064 | tf_op jit(solution)/shard_map/ppermute | solution.py:18
  35.5 2.2 %collective-permute-done.8 = f32[64,17]{1,0:T(8,128)S(1)} collective-permute-done((f32[64,17]{1,0:T(8,128)S(1)}, f32[64,17]{1,0:T(8,128)S(1)}, u32[]{:S(2)}, u32[]{:S(2)}) %collective-permute-start.8) | collective-permute-done | bytes 4384 | tf_op jit(solution)/shard_map/ppermute | solution.py:18
  38.0 2.2 %collective-permute-start.9 = (bf16[1,32,1296]{2,1,0:T(8,128)(2,1)S(1)}, bf16[1,32,1296]{2,1,0:T(8,128)(2,1)S(1)}, u32[]{:S(2)}, u32[]{:S(2)}) collective-permute-start(bf16[1,32,1296]{2,1,0:T(8,128)(2,1)S(1)} %get-tuple-element.79), channel_id=1, source_target_pairs={{0,2},{1,3},{2,0},{3,1},{4,6},{5,7},{6,4},{7,5},{8,10},{9,11},{10,... | collective-permute-start | bytes 248840 | tf_op jit(solution)/shard_map/ppermute | solution.py:18
  41.0 3.5 %load.5.refs_7_.refs_1_ = bf16[512,8192]{1,0:T(8,128)(2,1)S(1)} custom-call(bf16[1,64,1296]{2,1,0:T(8,128)(2,1)S(1)} %add_convert_fusion.after_ref, bf16[1024,8192]{1,0:T(8,128)(2,1)} %refs_0_.5), custom_call_target="tpu_custom_call" | custom-call | bytes 16777216 | tf_op jit(solution)/shard_map/load/pallas_call | solution.py:82
  44.7 3.2 %collective-permute-start.11 = (bf16[1,32,1024]{2,1,0:T(8,128)(2,1)S(1)}, bf16[1,32,1024]{2,1,0:T(8,128)(2,1)S(1)}, u32[]{:S(2)}, u32[]{:S(2)}) collective-permute-start(bf16[1,32,1024]{2,1,0:T(8,128)(2,1)S(1)} %get-tuple-element.81), channel_id=1, source_target_pairs={{0,2},{1,3},{2,0},{3,1},{4,6},{5,7},{6,4},{7,5},{8,10},{9,11},{10,... | collective-permute-start | bytes 196616 | tf_op jit(solution)/shard_map/ppermute | solution.py:18
  48.0 3.4 %collective-permute-done.13 = bf16[1,32,1296]{2,1,0:T(8,128)(2,1)S(1)} collective-permute-done((bf16[1,32,1296]{2,1,0:T(8,128)(2,1)S(1)}, bf16[1,32,1296]{2,1,0:T(8,128)(2,1)S(1)}, u32[]{:S(2)}, u32[]{:S(2)}) %collective-permute-start.13) | collective-permute-done | bytes 82976 | tf_op jit(solution)/shard_map/ppermute | solution.py:18
  51.5 4.8 %recur.1 = (f32[64,1024]{1,0:T(8,128)S(1)}, f32[2,32,1024]{2,1,0:T(8,128)S(1)}, f32[2,32,128]{2,1,0:T(8,128)S(1)}, f32[32,16]{1,0:T(8,128)S(1)}, bf16[32,16,64,128]{3,2,1,0:T(8,128)(2,1)S(1)}) custom-call(s32[1]{0:T(128)} %copy.45.live_ref, bf16[64,1296]{1,0:T(8,128)(2,1)S(1)} %maximum_bitcast_fusion.refs_0_, ...), custom_call_target="tpu_custom_call" | custom-call | flops 268435456 | bytes 10485760 | tf_op jit(solution)/shard_map/recur/pallas_call | solution.py:384
  56.4 1.0 %output_first.1 = (bf16[1,64,2176]{2,1,0:T(8,128)(2,1)S(1)}, bf16[64,1024]{1,0:T(8,128)(2,1)S(1)}, f32[64,1]{1,0:T(8,128)S(1)}) custom-call(bf16[64,1024]{1,0:T(8,128)(2,1)S(1)} %maximum_bitcast_fusion.1.refs_0_, bf16[64,1024]{1,0:T(8,128)(2,1)S(1)} %bitcast.40, bf16[64,1024]{1,0:T(8,128)(2,1)S(1)} %slice_bitcast_fusion.refs_2_, f32[64,17]{1,0:T(8,128)S(1)} %add.38.refs_3_, ...), custom_call_target="tpu_custom_call" | custom-call | flops 268435456 | bytes 4194304 | tf_op jit(solution)/shard_map/output_first/pallas_call | solution.py:558
  57.5 1.6 %output_rest.2.own_ref = bf16[2,64,2048]{2,1,0:T(8,128)(2,1)S(1)} custom-call(bf16[64,1024]{1,0:T(8,128)(2,1)S(1)} %get-tuple-element.61.lhs_ref, bf16[1,64,2176]{2,1,0:T(8,128)(2,1)S(1)} %get-tuple-element.60.after_ref, bf16[512,8192]{1,0:T(8,128)(2,1)S(1)} %load.4.refs_6_.refs_0_, bf16[512,8192]{1,0:T(8,128)(2,1)S(1)} %load.5.refs_7_.refs_1_), custom_call_target="tpu_custom_call" | custom-call | flops 536870912 | bytes 8388608 | tf_op jit(solution)/shard_map/output_rest/pallas_call | solution.py:558
  59.4 2.2 %collective-permute-start.15 = (bf16[1,32,2176]{2,1,0:T(8,128)(2,1)S(1)}, bf16[1,32,2176]{2,1,0:T(8,128)(2,1)S(1)}, u32[]{:S(2)}, u32[]{:S(2)}) collective-permute-start(bf16[1,32,2176]{2,1,0:T(8,128)(2,1)S(1)} %get-tuple-element.73), channel_id=1, source_target_pairs={{0,8},{4,12},{8,0},{12,4},{1,9},{5,13},{9,1},{13,5},{2,10},{6,14},... | collective-permute-start | bytes 417800 | tf_op jit(solution)/shard_map/ppermute | solution.py:18
  63.2 4.9 %state_write.1 = bf16[32,16,64,128]{3,2,1,0:T(8,128)(2,1)} custom-call(f32[2,32,1024]{2,1,0:T(8,128)S(1)} %get-tuple-element.66.feeds_ref, f32[2,32,128]{2,1,0:T(8,128)S(1)} %get-tuple-element.67.b_ref, f32[32,16,128]{2,1,0:T(8,128)S(1)} %broadcast_in_dim.42.decay_ref, bf16[32,16,64,128]{3,2,1,0:T(8,128)(2,1)S(1)} %get-tuple-element.69.state_ref), custom_call_target="tpu_custom_call" | custom-call | flops 134217728 | bytes 16777216 | tf_op jit(solution)/shard_map/state_write/pallas_call | solution.py:446
  69.6 1.0 %copy.39 = bf16[32,2,2048]{2,1,0:T(2,128)(2,1)} copy(bf16[32,2,2048]{2,0,1:T(8,128)(2,1)S(1)} %fusion.3) | data formatting | bytes 524288
  (66 shorter events, 7.5 us)
Async XLA Ops:
  1.8 16.7 %collective-permute-start = (bf16[64,2048]{1,0:T(8,128)(2,1)S(1)}, bf16[64,2048]{1,0:T(8,128)(2,1)S(1)}, u32[]{:S(2)}, u32[]{:S(2)}) collective-permute-start(bf16[64,2048]{1,0:T(8,128)(2,1)S(1)} %bitcast.36), channel_id=1, source_target_pairs={{0,8},{1,12},{2,0},{3,4},{4,9},{5,13},{6,1},{7,5},{8,10},{9,14},{1... | collective-permute-start | bytes 786440 | tf_op jit(solution)/shard_map/ppermute | solution.py:616
  18.5 7.0 %copy-start = (bf16[2048,16]{0,1:T(8,128)(2,1)S(1)}, bf16[2048,16]{0,1:T(8,128)(2,1)}, u32[]{:S(2)}) copy-start(bf16[2048,16]{0,1:T(8,128)(2,1)} %param.20) | copy-start | bytes 196612
  18.5 6.4 %collective-permute-start.2 = (bf16[64,2048]{1,0:T(8,128)(2,1)S(1)}, bf16[64,2048]{1,0:T(8,128)(2,1)S(1)}, u32[]{:S(2)}, u32[]{:S(2)}) collective-permute-start(bf16[64,2048]{1,0:T(8,128)(2,1)S(1)} %collective-permute-done.after_ref.refs_0_), channel_id=1, source_target_pairs={{0,8},{4,12},{8,0},{12,4},{1,9},{5,13},{9,1},{13,5},{2,10},{6,14},... | collective-permute-start | bytes 786440 | tf_op jit(solution)/shard_map/ppermute | solution.py:18
  18.5 7.0 %collective-permute-start.1 = (bf16[64,2048]{1,0:T(8,128)(2,1)S(1)}, bf16[64,2048]{1,0:T(8,128)(2,1)S(1)}, u32[]{:S(2)}, u32[]{:S(2)}) collective-permute-start(bf16[64,2048]{1,0:T(8,128)(2,1)S(1)} %collective-permute-done.after_ref.refs_0_), channel_id=1, source_target_pairs={{0,4},{4,0},{8,12},{12,8},{1,5},{5,1},{9,13},{13,9},{2,6},{6,2},{1... | collective-permute-start | bytes 786440 | tf_op jit(solution)/shard_map/ppermute | solution.py:18
  24.8 3.2 %collective-permute-start.3 = (bf16[64,2048]{1,0:T(8,128)(2,1)S(1)}, bf16[64,2048]{1,0:T(8,128)(2,1)S(1)}, u32[]{:S(2)}, u32[]{:S(2)}) collective-permute-start(bf16[64,2048]{1,0:T(8,128)(2,1)S(1)} %collective-permute-done.2.refs_2_.refs_0_), channel_id=1, source_target_pairs={{0,4},{4,0},{8,12},{12,8},{1,5},{5,1},{9,13},{13,9},{2,6},{6,2},{1... | collective-permute-start | bytes 786440 | tf_op jit(solution)/shard_map/ppermute | solution.py:18
  26.6 11.1 %collective-permute-start.6 = (bf16[1,64,1296]{2,1,0:T(8,128)(2,1)S(1)}, bf16[1,64,1296]{2,1,0:T(8,128)(2,1)S(1)}, u32[]{:S(2)}, u32[]{:S(2)}) collective-permute-start(bf16[1,64,1296]{2,1,0:T(8,128)(2,1)S(1)} %get-tuple-element.43.refs_2_), channel_id=1, source_target_pairs={{0,1},{1,0},{2,3},{3,2},{4,5},{5,4},{6,7},{7,6},{8,9},{9,8},{10,11... | collective-permute-start | bytes 497672 | tf_op jit(solution)/shard_map/ppermute | solution.py:18
  29.1 8.8 %collective-permute-start.5 = (bf16[1,64,1296]{2,1,0:T(8,128)(2,1)S(1)}, bf16[1,64,1296]{2,1,0:T(8,128)(2,1)S(1)}, u32[]{:S(2)}, u32[]{:S(2)}) collective-permute-start(bf16[1,64,1296]{2,1,0:T(8,128)(2,1)S(1)} %get-tuple-element.46.refs_3_), channel_id=1, source_target_pairs={{0,1},{1,0},{2,3},{3,2},{4,5},{5,4},{6,7},{7,6},{8,9},{9,8},{10,11... | collective-permute-start | bytes 497672 | tf_op jit(solution)/shard_map/ppermute | solution.py:18
  31.1 13.4 %collective-permute-start.4 = (bf16[1,64,1024]{2,1,0:T(8,128)(2,1)S(1)}, bf16[1,64,1024]{2,1,0:T(8,128)(2,1)S(1)}, u32[]{:S(2)}, u32[]{:S(2)}) collective-permute-start(bf16[1,64,1024]{2,1,0:T(8,128)(2,1)S(1)} %get-tuple-element.75), channel_id=1, source_target_pairs={{0,1},{1,0},{2,3},{3,2},{4,5},{5,4},{6,7},{7,6},{8,9},{9,8},{10,11... | collective-permute-start | bytes 393224 | tf_op jit(solution)/shard_map/ppermute | solution.py:18
  32.6 1.2 %collective-permute-start.7 = (f32[64,17]{1,0:T(8,128)S(1)}, f32[64,17]{1,0:T(8,128)S(1)}, u32[]{:S(2)}, u32[]{:S(2)}) collective-permute-start(f32[64,17]{1,0:T(8,128)S(1)} %get-tuple-element.51.after_ref), channel_id=1, source_target_pairs={{0,4},{4,0},{8,12},{12,8},{1,5},{5,1},{9,13},{13,9},{2,6},{6,2},{1... | collective-permute-start | bytes 13064 | tf_op jit(solution)/shard_map/ppermute | solution.py:18
  32.6 23.8 %collective-permute-start.12 = (bf16[1,64,1024]{2,1,0:T(8,128)(2,1)S(1)}, bf16[1,64,1024]{2,1,0:T(8,128)(2,1)S(1)}, u32[]{:S(2)}, u32[]{:S(2)}) collective-permute-start(bf16[1,64,1024]{2,1,0:T(8,128)(2,1)S(1)} %get-tuple-element.74), channel_id=1, source_target_pairs={{0,1},{1,0},{2,3},{3,2},{4,5},{5,4},{6,7},{7,6},{8,9},{9,8},{10,11... | collective-permute-start | bytes 393224 | tf_op jit(solution)/shard_map/ppermute | solution.py:18
  33.8 3.9 %collective-permute-start.8 = (f32[64,17]{1,0:T(8,128)S(1)}, f32[64,17]{1,0:T(8,128)S(1)}, u32[]{:S(2)}, u32[]{:S(2)}) collective-permute-start(f32[64,17]{1,0:T(8,128)S(1)} %add.37), channel_id=1, source_target_pairs={{0,8},{4,12},{8,0},{12,4},{1,9},{5,13},{9,1},{13,5},{2,10},{6,14},... | collective-permute-start | bytes 13064 | tf_op jit(solution)/shard_map/ppermute | solution.py:18
  38.0 6.6 %collective-permute-start.9 = (bf16[1,32,1296]{2,1,0:T(8,128)(2,1)S(1)}, bf16[1,32,1296]{2,1,0:T(8,128)(2,1)S(1)}, u32[]{:S(2)}, u32[]{:S(2)}) collective-permute-start(bf16[1,32,1296]{2,1,0:T(8,128)(2,1)S(1)} %get-tuple-element.79), channel_id=1, source_target_pairs={{0,2},{1,3},{2,0},{3,1},{4,6},{5,7},{6,4},{7,5},{8,10},{9,11},{10,... | collective-permute-start | bytes 248840 | tf_op jit(solution)/shard_map/ppermute | solution.py:18
  40.2 11.2 %collective-permute-start.13 = (bf16[1,32,1296]{2,1,0:T(8,128)(2,1)S(1)}, bf16[1,32,1296]{2,1,0:T(8,128)(2,1)S(1)}, u32[]{:S(2)}, u32[]{:S(2)}) collective-permute-start(bf16[1,32,1296]{2,1,0:T(8,128)(2,1)S(1)} %get-tuple-element.78), channel_id=1, source_target_pairs={{0,2},{1,3},{2,0},{3,1},{4,6},{5,7},{6,4},{7,5},{8,10},{9,11},{10,... | collective-permute-start | bytes 248840 | tf_op jit(solution)/shard_map/ppermute | solution.py:18
  41.0 10.5 %copy-start.3 = (f32[16]{0:T(128)S(1)}, f32[16]{0:T(128)}, u32[]{:S(2)}) copy-start(f32[16]{0:T(128)} %param.22) | copy-start | bytes 196
  41.0 10.5 %copy-start.4 = (f32[16]{0:T(128)S(1)}, f32[16]{0:T(128)}, u32[]{:S(2)}) copy-start(f32[16]{0:T(128)} %param.23) | copy-start | bytes 196
  41.0 10.5 %copy-start.5 = (f32[16]{0:T(128)S(1)}, f32[16]{0:T(128)}, u32[]{:S(2)}) copy-start(f32[16]{0:T(128)} %param.24) | copy-start | bytes 196
  44.5 11.9 %copy-start.1 = (f32[1024]{0:T(1024)S(1)}, f32[1024]{0:T(1024)}, u32[]{:S(2)}) copy-start(f32[1024]{0:T(1024)} %param.25) | copy-start | bytes 12292
  44.7 11.7 %collective-permute-start.11 = (bf16[1,32,1024]{2,1,0:T(8,128)(2,1)S(1)}, bf16[1,32,1024]{2,1,0:T(8,128)(2,1)S(1)}, u32[]{:S(2)}, u32[]{:S(2)}) collective-permute-start(bf16[1,32,1024]{2,1,0:T(8,128)(2,1)S(1)} %get-tuple-element.81), channel_id=1, source_target_pairs={{0,2},{1,3},{2,0},{3,1},{4,6},{5,7},{6,4},{7,5},{8,10},{9,11},{10,... | collective-permute-start | bytes 196616 | tf_op jit(solution)/shard_map/ppermute | solution.py:18
  47.9 8.4 %collective-permute-start.10 = (bf16[1,32,1024]{2,1,0:T(8,128)(2,1)S(1)}, bf16[1,32,1024]{2,1,0:T(8,128)(2,1)S(1)}, u32[]{:S(2)}, u32[]{:S(2)}) collective-permute-start(bf16[1,32,1024]{2,1,0:T(8,128)(2,1)S(1)} %get-tuple-element.80), channel_id=1, source_target_pairs={{0,2},{1,3},{2,0},{3,1},{4,6},{5,7},{6,4},{7,5},{8,10},{9,11},{10,... | collective-permute-start | bytes 196616 | tf_op jit(solution)/shard_map/ppermute | solution.py:18
  57.4 1.7 %collective-permute-start.14 = (bf16[1,64,2176]{2,1,0:T(8,128)(2,1)S(1)}, bf16[1,64,2176]{2,1,0:T(8,128)(2,1)S(1)}, u32[]{:S(2)}, u32[]{:S(2)}) collective-permute-start(bf16[1,64,2176]{2,1,0:T(8,128)(2,1)S(1)} %get-tuple-element.60.after_ref), channel_id=1, source_target_pairs={{0,4},{4,0},{8,12},{12,8},{1,5},{5,1},{9,13},{13,9},{2,6},{6,2},{1... | collective-permute-start | bytes 835592 | tf_op jit(solution)/shard_map/ppermute | solution.py:18
  59.4 8.7 %collective-permute-start.15 = (bf16[1,32,2176]{2,1,0:T(8,128)(2,1)S(1)}, bf16[1,32,2176]{2,1,0:T(8,128)(2,1)S(1)}, u32[]{:S(2)}, u32[]{:S(2)}) collective-permute-start(bf16[1,32,2176]{2,1,0:T(8,128)(2,1)S(1)} %get-tuple-element.73), channel_id=1, source_target_pairs={{0,8},{4,12},{8,0},{12,4},{1,9},{5,13},{9,1},{13,5},{2,10},{6,14},... | collective-permute-start | bytes 417800 | tf_op jit(solution)/shard_map/ppermute | solution.py:18
  61.6 7.7 %collective-permute-start.17 = (bf16[1,64,2048]{2,1,0:T(8,128)(2,1)S(1)}, bf16[1,64,2048]{2,1,0:T(8,128)(2,1)S(1)}, u32[]{:S(2)}, u32[]{:S(2)}) collective-permute-start(bf16[1,64,2048]{2,1,0:T(8,128)(2,1)S(1)} %slice.21), channel_id=1, source_target_pairs={{0,4},{4,0},{8,12},{12,8},{1,5},{5,1},{9,13},{13,9},{2,6},{6,2},{1... | collective-permute-start | bytes 786440 | tf_op jit(solution)/shard_map/ppermute | solution.py:18
  61.9 7.0 %collective-permute-start.16 = (bf16[1,32,2176]{2,1,0:T(8,128)(2,1)S(1)}, bf16[1,32,2176]{2,1,0:T(8,128)(2,1)S(1)}, u32[]{:S(2)}, u32[]{:S(2)}) collective-permute-start(bf16[1,32,2176]{2,1,0:T(8,128)(2,1)S(1)} %get-tuple-element.72), channel_id=1, source_target_pairs={{0,8},{4,12},{8,0},{12,4},{1,9},{5,13},{9,1},{13,5},{2,10},{6,14},... | collective-permute-start | bytes 417800 | tf_op jit(solution)/shard_map/ppermute | solution.py:18
  63.2 6.3 %copy-start.6 = (bf16[32,2,2048]{2,1,0:T(2,128)(2,1)S(1)}, bf16[32,2,2048]{2,1,0:T(2,128)(2,1)}, u32[]{:S(2)}) copy-start(bf16[32,2,2048]{2,1,0:T(2,128)(2,1)} %param.16) | copy-start | bytes 786436
  (1 other events, 0.7 us)

commit v13 on v12

--- a/solution.py
+++ b/solution.py
@@ -9,6 +9,7 @@
 
 BF16 = jnp.bfloat16
 EPSILON = 1e-05
+LANES = 128
 F32 = jnp.float32
 VMEM_GRANT = 12 * 1024 * 1024
 
@@ -160,6 +161,10 @@
     )(tenants, scaled, squares, in_hbm(jnp.swapaxes(down, 1, 2)), in_hbm(up))
 
 
+def lead_of(mix, steps):
+    return -(-(mix + steps) // LANES) * LANES
+
+
 def project_signal_body(owners, order, *refs):
     blocks, refs = refs[: len(order)], refs[len(order) :]
     weight_ref, mix_ref, step_ref, send_ref, keep_ref, lhs_ref, semaphores = refs
@@ -187,20 +192,23 @@
                 target.dtype
             )
 
+    mix = mix_ref.shape[1]
+    put(jnp.dot(lhs, mix_ref[...], preferred_element_type=F32), 0)
+    acc = lax.dot_general(lhs, step_ref[...], (((1,), (1,)), ((), ())), preferred_element_type=F32)
+    put(acc, mix)
     columns = weight_ref.shape[1]
+    lead = send_ref.shape[2] - columns
+    put(jnp.zeros((lhs.shape[0], lead - mix - acc.shape[1]), F32), mix + acc.shape[1])
     tile = min(columns, 512)
     for t in range(0, columns, tile):
-        put(jnp.dot(lhs, weight_ref[:, t : t + tile], preferred_element_type=F32), t)
-    put(jnp.dot(lhs, mix_ref[...], preferred_element_type=F32), columns)
-    acc = lax.dot_general(lhs, step_ref[...], (((1,), (1,)), ((), ())), preferred_element_type=F32)
-    put(acc, columns + mix_ref.shape[1])
+        put(jnp.dot(lhs, weight_ref[:, t : t + tile], preferred_element_type=F32), lead + t)
 
 
 def project_signal(blocks, order, owners, weight, mix, step, after):
     pieces = len(blocks)
     depth = blocks[0].shape[1]
     rows = pieces * blocks[0].shape[0]
-    columns = weight.shape[1] + mix.shape[1] + step.shape[0]
+    columns = weight.shape[1] + lead_of(mix.shape[1], step.shape[0])
     half = jax.ShapeDtypeStruct((owners // 2, rows // owners, columns), BF16)
     whole = pl.BlockSpec(memory_space=pltpu.VMEM)
     anywhere = pl.BlockSpec(memory_space=pl.ANY)
@@ -280,19 +288,13 @@
     return lax.rsqrt(sums_ref[:, sums_ref.shape[1] - 1 :] / width + EPSILON)
 
 
-def recur_body(
-    terms,
-    group,
-    model_width,
-    live_ref,
-    *refs,
-):
+def read_body(terms, group, model_width, live_ref, *refs):
     term_refs = refs[:terms]
     sums_ref, up_ref, bias_ref, rate_ref, skip_ref, source_ref, _ = refs[terms : terms + 7]
-    result_ref, feeds_ref, b_ref, both_ref, state_ref, *scratch = refs[terms + 7 :]
-    c_ref, read_ref, spread_ref, signal_ref, semaphores = scratch
+    adapted_ref, read_ref, spread_ref, b_ref, both_ref, state_ref, *scratch = refs[terms + 7 :]
+    c_ref, semaphores = scratch
     heads, head, width = state_ref.shape[1:]
-    streams, inner = feeds_ref.shape[1:]
+    streams, inner = read_ref.shape[1:]
     step = pl.program_id(0)
 
     def fetch(i):
@@ -306,16 +308,9 @@
         rows = sums_ref.shape[0]
         rank = sums_ref.shape[1] - 1
         inverse = inverse_of(sums_ref, model_width)
-        lowrank = (sums_ref[:, :rank] * inverse).astype(BF16)
-        repeat = lax.broadcasted_iota(jnp.int32, (rank, streams * rank), 1) % rank
-        repeat = (repeat == lax.broadcasted_iota(jnp.int32, (rank, streams * rank), 0)).astype(BF16)
-        every = jnp.dot(lowrank, repeat, preferred_element_type=F32)
-        own = jnp.where(own_columns(rows, streams, rank), every, 0.0).astype(BF16)
-        adapted = jnp.dot(own, up_ref[...], preferred_element_type=F32)
-        total = sum(t[...].astype(F32) for t in term_refs) * inverse
-        signal_ref[...] = silu(total[:, :inner] + adapted)
-        gates = silu(total[:, inner : inner + 2 * width])
-        steps_dt = softplus(total[:, inner + 2 * width :] + bias_ref[...])
+        total = sum(t[:, : 2 * width + heads].astype(F32) for t in term_refs) * inverse
+        gates = silu(total[:, : 2 * width])
+        steps_dt = softplus(total[:, 2 * width :] + bias_ref[...])
         b = [gates[p * streams : (p + 1) * streams, :width] for p in range(2)]
         c = [gates[p * streams : (p + 1) * streams, width:] for p in range(2)]
         for p in range(2):
@@ -351,6 +346,12 @@
         spread_ref[...] = jnp.dot(high, ones, preferred_element_type=F32) + jnp.dot(
             low, ones, preferred_element_type=F32
         )
+        lowrank = (sums_ref[:, :rank] * inverse).astype(BF16)
+        repeat = lax.broadcasted_iota(jnp.int32, (rank, streams * rank), 1) % rank
+        repeat = (repeat == lax.broadcasted_iota(jnp.int32, (rank, streams * rank), 0)).astype(BF16)
+        every = jnp.dot(lowrank, repeat, preferred_element_type=F32)
+        own = jnp.where(own_columns(rows, streams, rank), every, 0.0).astype(BF16)
+        adapted_ref[...] = jnp.dot(own, up_ref[...], preferred_element_type=F32)
 
     fetch(step).wait()
     at = pl.multiple_of(step * group, group)
@@ -364,28 +365,19 @@
             low = 2 * group + row
             read_ref[p, pl.ds(at + g, 1), :] = found[row : row + 1] + found[low : low + 1]
 
-    @pl.when(step == pl.num_programs(0) - 1)
-    def _():
-        factor = [spread_ref[i * streams : (i + 1) * streams, :] for i in range(7)]
-        first = signal_ref[:streams, :]
-        second = signal_ref[streams:, :]
-        result_ref[:streams, :] = factor[0] * read_ref[0] + factor[2] * first
-        result_ref[streams:, :] = factor[1] * read_ref[1] + factor[4] * first + factor[3] * second
-        feeds_ref[0] = factor[5] * first
-        feeds_ref[1] = factor[6] * second
-
-
-def recur(model_width, after, live_rows, terms, sums, up_rows, bias, rate, skip, state):
+
+def read_state(model_width, after, live_rows, terms, sums, up_rows, bias, rate, skip, state):
     streams, heads, head, width = state.shape
     group = 8
     inner = heads * head
     rows = 2 * streams
     whole = pl.BlockSpec(memory_space=pltpu.VMEM)
     return pl.pallas_call(
-        functools.partial(recur_body, len(terms), group, model_width),
+        functools.partial(read_body, len(terms), group, model_width),
         out_shape=(
             jax.ShapeDtypeStruct((rows, inner), F32),
             jax.ShapeDtypeStruct((2, streams, inner), F32),
+            jax.ShapeDtypeStruct((7 * streams, inner), F32),
             jax.ShapeDtypeStruct((2, streams, width), F32),
             jax.ShapeDtypeStruct((streams, heads), F32),
             pltpu.VMEM(state.shape, state.dtype),
@@ -394,17 +386,14 @@
         in_specs=[pl.BlockSpec(memory_space=pltpu.SMEM)]
         + [whole] * (len(terms) + 5)
         + [pl.BlockSpec(memory_space=pl.ANY)] * 2,
-        out_specs=(whole,) * 5,
+        out_specs=(whole,) * 6,
         scratch_shapes=[
             pltpu.VMEM((2, streams, width), F32),
-            pltpu.VMEM((2, streams, inner), F32),
-            pltpu.VMEM((7 * streams, inner), F32),
-            pltpu.VMEM((rows, inner), F32),
             pltpu.SemaphoreType.DMA((streams // group,)),
         ],
         compiler_params=params(),
         cost_estimate=cost(64 * state.size, 2 * state.size + 32 * rows * inner),
-        name="recur",
+        name="read_state",
     )(
         live_rows,
         *terms,
@@ -478,9 +467,6 @@
             out_ref[j, :, t : t + tile] = acc.astype(out_ref.dtype)
 
 
-LANES = 128
-
-
 def put_lanes(values, out_ref, j):
     lane = lax.broadcasted_iota(jnp.int32, (values.shape[0], LANES), 1)
     tail = jnp.zeros(lane.shape, F32)
@@ -522,11 +508,31 @@
     return jnp.sum(values.astype(F32), -1, keepdims=True)
 
 
-def output_first_body(distances, terms, model_width, *refs):
-    term_refs = refs[:terms]
-    sums_ref, result_ref, scale_ref, *weight_refs, out_ref, lhs_ref, squares_ref = refs[terms:]
-    total = sum(t[...].astype(F32) for t in term_refs) * inverse_of(sums_ref, model_width)
-    gated = result_ref[...] * silu(total)
+def output_first_body(distances, shapes, model_width, *refs):
+    refs = list(refs)
+    gate_refs = [refs.pop(0) for _ in range(shapes[0])]
+    signal_refs = [[refs.pop(0) for _ in range(count)] for count in shapes[1:]]
+    sums_ref, adapted_ref, read_ref, spread_ref, scale_ref, *weight_refs = refs[:-4]
+    out_ref, lhs_ref, squares_ref, feeds_ref = refs[-4:]
+    streams, inner = read_ref.shape[1:]
+    inverse = inverse_of(sums_ref, model_width)
+    total = 0.0
+    for pieces in signal_refs:
+        pieces = [piece[...] for piece in pieces]
+        width = sum(piece.shape[1] for piece in pieces)
+        pieces[0] = pieces[0][:, width - inner :]
+        total += jnp.concatenate([piece.astype(F32) for piece in pieces], 1)
+    signal = silu(total * inverse + adapted_ref[...])
+    first, second = signal[:streams], signal[streams:]
+    factor = [spread_ref[i * streams : (i + 1) * streams, :] for i in range(7)]
+    feeds_ref[0] = factor[5] * first
+    feeds_ref[1] = factor[6] * second
+    result = [
+        factor[0] * read_ref[0] + factor[2] * first,
+        factor[1] * read_ref[1] + factor[4] * first + factor[3] * second,
+    ]
+    total = sum(t[...].astype(F32) for t in gate_refs) * inverse
+    gated = jnp.concatenate(result, 0) * silu(total)
     squares_ref[...] = jnp.sum(gated * gated, -1, keepdims=True)
     lhs_ref[...] = (gated * scale_ref[...]).astype(lhs_ref.dtype)
     output_tiles(distances, lhs_ref, weight_refs, out_ref)
@@ -534,11 +540,52 @@
         put_lanes(squares_ref[...], out_ref, j)
 
 
+def put_lanes(values, out_ref, j):
+    lane = lax.broadcasted_iota(jnp.int32, (values.shape[0], LANES), 1)
+    tail = jnp.zeros(lane.shape, F32)
+    for i in range(3):
+        term = values.astype(BF16).astype(F32)
+        tail = jnp.where(lane == i, term, tail)
+        values = values - term
+    out_ref[j, :, out_ref.shape[2] - LANES :] = tail.astype(out_ref.dtype)
+
+
+def meet_body(met_ref, own_ref, squares_ref, out_ref, total_ref):
+    count = met_ref.shape[0]
+    width = own_ref.shape[2]
+    total = squares_ref[...] + join_lanes(met_ref[0, :, width:])
+    total_ref[...] = total
+    for j in range(count):
+        both = met_ref[j, :, :width].astype(F32) + own_ref[j].astype(F32)
+        out_ref[j, :, :width] = both.astype(out_ref.dtype)
+        put_lanes(total, out_ref, j)
+
+
+def meet(met, own, squares):
+    whole = pl.BlockSpec(memory_space=pltpu.VMEM)
+    return pl.pallas_call(
+        meet_body,
+        out_shape=(
+            jax.ShapeDtypeStruct(met.shape, met.dtype),
+            jax.ShapeDtypeStruct(squares.shape, squares.dtype),
+        ),
+        in_specs=[whole] * 3,
+        out_specs=(whole, whole),
+        compiler_params=params(),
+        cost_estimate=cost(met.size, 6 * met.size),
+        name="meet",
+    )(met, own, squares)
+
+
+def join_lanes(values):
+    return jnp.sum(values.astype(F32), -1, keepdims=True)
+
+
 def output_rest_body(distances, lhs_ref, after_ref, *refs):
     output_tiles(distances, lhs_ref, refs[:-1], refs[-1])
 
 
-def output_parts(distances, weights, width, operands, model_width=None):
+def output_parts(distances, weights, width, operands, model_width=None, shapes=None):
     first = model_width is not None
     rows, depth = operands[0].shape
     count = len(distances)
@@ -548,10 +595,11 @@
     extra = LANES if first else 0
     out_shape = [jax.ShapeDtypeStruct((count, rows, width + extra), BF16)]
     if first:
-        body = functools.partial(output_first_body, distances, len(operands) - 3, model_width)
+        body = functools.partial(output_first_body, distances, shapes, model_width)
         out_shape += [
             jax.ShapeDtypeStruct((rows, depth), BF16),
             jax.ShapeDtypeStruct((rows, 1), F32),
+            jax.ShapeDtypeStruct((2, rows // 2, depth), F32),
         ]
     else:
         specs[1] = pl.BlockSpec(memory_space=pl.ANY)
@@ -637,10 +685,12 @@
         pick = [(near_keep, far_keep), (near_other, far_other)]
         last_send = sum(jnp.where(own, f, n).astype(F32) for n, f in pick).astype(BF16)
         last_send, sums = lax.optimization_barrier((last_send, sums))
-        last_other = [swap(part, "row", 2) for part in jnp.split(last_send, 2, 1)]
+        lead = last_send.shape[-1] - inner
+        cut = lead + inner * 3 // 8 // LANES * LANES
+        last_other = [swap(part, "row", 2) for part in jnp.split(last_send, [cut], -1)]
         (out_late,) = load(last_send, [], (output_weight, middle, middle))
-        signal_terms = [jnp.where(own, n, f)[0] for n, f in pick]
-        signal_terms = [jnp.concatenate(last_other, 1)[0]] + signal_terms
+        signal_terms = [[part[0] for part in last_other]]
+        signal_terms += [[jnp.where(own, n, f)[0]] for n, f in pick]
         gate_far, _ = lax.optimization_barrier((gate_far, last_other[0]))
         gate_last = (gate_far.astype(F32) + gate_keep[1:].astype(F32)).astype(BF16)
         gate_terms = [swap_halves(gate_last, "row", 2, 1)[0], gate_own[0], gate_keep[0]]
@@ -659,14 +709,15 @@
             gate_send, [keep], (output_weight, 0, middle), (output_weight, middle, middle)
         )
         signal_terms, _ = scatter_rows(received, keep, "row")
+        signal_terms = [[t] for t in signal_terms]
         gate_terms, gate_last = scatter_rows(swap(gate_send, "row", 1), gate_keep, "row")
     out_weights = [out_early, out_late]
 
-    result, feeds, bgate, both, state = recur(
+    adapted, read, spread, bgate, both, state = read_state(
         model_width,
         gate_last,
         live_block_rows,
-        signal_terms,
+        [pieces[0] for pieces in signal_terms],
         sums,
         up_rows,
         step_bias,
@@ -676,12 +727,21 @@
     )
 
     distances = list(range(heads_n))
-    first, out_lhs, gate_squares = output_parts(
+    first, out_lhs, gate_squares, feeds = output_parts(
         distances[3::4],
         out_weights,
         feature_width,
-        [*gate_terms, sums, result, gated_norm_scale[None]],
+        [
+            *gate_terms,
+            *[piece for pieces in signal_terms for piece in pieces],
+            sums,
+            adapted,
+            read,
+            spread,
+            gated_norm_scale[None],
+        ],
         model_width,
+        [len(gate_terms)] + [len(pieces) for pieces in signal_terms],
     )
     (second,) = output_parts(
         distances[2::4] + distances[1::4], out_weights, feature_width, [out_lhs, first]
@@ -706,8 +766,8 @@
     live = jnp.arange(streams) < live_block_rows[0]
     mixed = (wide + jnp.where(live[:, None], mixer, 0.0)).astype(BF16)
 
-    spread = jnp.broadcast_to(both[..., None], both.shape + (bgate.shape[-1],))
-    new_state = state_write(feeds, bgate, spread, state)
+    decays = jnp.broadcast_to(both[..., None], both.shape + (bgate.shape[-1],))
+    new_state = state_write(feeds, bgate, decays, state)
     return (jnp.swapaxes(mixed, 0, 1), new_state)
 
 

time: 70.8 us -> 74.7 us (1.055)
  starting transfers between devices: 18.1 us -> 21.3 us
    ppermute x17, starting transfers between devices: 15.2 us -> 18.4 us  [swap(): return lax.ppermute(values, axis, [(i, i ^ distance) for i in range(size)])]
  transfers between devices with their start and end apart: 18 -> 18, of which waited for: 8 -> 6; matrix products, arithmetic and copies ran while one was open for 1% -> 1% of each run, Pallas kernels for 43% -> 40%
where the time goes in v13:
time: 74.7 us; the launch traced here: 74.5 us
  Pallas kernels  31.5 us (42%)
  starting transfers between devices  21.3 us (29%)
  waiting for transfers between devices  16 us (21%)
  local copies, waits for them, and re-layouts  2.18 us (3%)
  other arithmetic  1.82 us (2%)
  between operations  1.66 us (2%)
    ppermute x17, starting transfers between devices, swap(): return lax.ppermute(values, axis, [(i, i ^ distance) for i in range(size)])  18.4 us
    pallas_call x3, Pallas kernels, load(): pl.pallas_call(functools.partial(load_body, spans), out_shape=tuple((pltp...  10.9 us
    ppermute x17, waiting for transfers between devices, swap(): return lax.ppermute(values, axis, [(i, i ^ distance) for i in range(size)])  10.7 us
    ppermute x1, waiting for transfers between devices, on_device(): turned = lax.ppermute(scaled_flat, ('head', 'row'), turn)  5.32 us
    pallas_call x1, Pallas kernels, state_write(): pl.pallas_call(state_write_body, out_shape=jax.ShapeDtypeStruct(state.sha...  4.88 us
    pallas_call x1, Pallas kernels, read_state(): pl.pallas_call(functools.partial(read_body, len(terms), group, model_widt...  4.76 us
    pallas_call x1, Pallas kernels, adapt(): pl.pallas_call(adapt_body, out_shape=(jax.ShapeDtypeStruct((rows, rank +...  3.74 us
    pallas_call x3, Pallas kernels, output_parts(): pl.pallas_call(body, out_shape=tuple(out_shape), in_specs=specs, out_spec...  3.6 us
  transfers between devices with their start and end apart: 18, of which 6 were waited for; matrix products, arithmetic and copies ran while one was open for 1% of the time, Pallas kernels for 40%

profile of v13, /device:TPU:0, one launch (start us, length us, event | category | flops | bytes accessed | tf_op | source)
XLA Modules:
  0.0 74.5 jit_solution(7530037764211577627)
XLA Ops:
  0.6 1.1 %fusion.1 = (f32[2,32]{1,0:T(2,128)S(1)}, bf16[2,32,2048]{2,1,0:T(8,128)(2,1)S(1)}) fusion(bf16[32,2,2048]{2,1,0:T(2,128)(2,1)} %param.16, f32[2048]{0:T(1024)} %param.17), kind=kLoop, calls=%fused_computation.4 | loop fusion | flops 655296 | bytes 532736 | tf_op jit(solution)/shard_map/reduce_sum | solution.py:652
  1.8 3.0 %collective-permute-start = (bf16[64,2048]{1,0:T(8,128)(2,1)S(1)}, bf16[64,2048]{1,0:T(8,128)(2,1)S(1)}, u32[]{:S(2)}, u32[]{:S(2)}) collective-permute-start(bf16[64,2048]{1,0:T(8,128)(2,1)S(1)} %bitcast.36), channel_id=1, source_target_pairs={{0,8},{1,12},{2,0},{3,4},{4,9},{5,13},{6,1},{7,5},{8,10},{9,14},{1... | collective-permute-start | bytes 786440 | tf_op jit(solution)/shard_map/ppermute | solution.py:664
  5.5 3.7 %adapt.1 = (f32[64,17]{1,0:T(8,128)S(1)}, bf16[512,1024]{1,0:T(8,128)(2,1)S(1)}) custom-call(s32[32]{0:T(128)S(1)} %copy-done.2, bf16[64,2048]{1,0:T(8,128)(2,1)S(1)} %bitcast.37, f32[64,1]{1,0:T(8,128)S(1)} %reshape.29.squares_ref, bf16[128,16,2048]{2,1,0:T(8,128)(2,1)} %bitcast.48, bf16[128,16,1024]{2,1,0:T(8,128)(2,1)} %up_ref.1), custom_call_target="tpu_custom_call" | custom-call | flops 134217728 | bytes 3145728 | tf_op jit(solution)/shard_map/adapt/pallas_call | solution.py:146
  9.2 3.9 %load.3 = (bf16[2048,1024]{1,0:T(8,128)(2,1)S(1)}, bf16[2048,256]{1,0:T(8,128)(2,1)S(1)}, bf16[2048,1024]{1,0:T(8,128)(2,1)S(1)}) custom-call(f32[64,17]{1,0:T(8,128)S(1)} %get-tuple-element.53.after_ref, bf16[2048,1024]{1,0:T(8,128)(2,1)} %refs_0_.3, bf16[2048,256]{1,0:T(8,128)(2,1)} %refs_1_.1, bf16[2048,1024]{1,0:T(8,128)(2,1)} %refs_2_.1), custom_call_target="tpu_custom_call" | custom-call | bytes 18874368 | tf_op jit(solution)/shard_map/load/pallas_call | solution.py:83
  13.1 5.3 %collective-permute-done.after_ref.refs_0_ = bf16[64,2048]{1,0:T(8,128)(2,1)S(1)} collective-permute-done((bf16[64,2048]{1,0:T(8,128)(2,1)S(1)}, bf16[64,2048]{1,0:T(8,128)(2,1)S(1)}, u32[]{:S(2)}, u32[]{:S(2)}) %collective-permute-start) | collective-permute-done | bytes 262176 | tf_op jit(solution)/shard_map/ppermute | solution.py:664
  18.5 3.5 %load.4.refs_12_.refs_0_ = bf16[512,8192]{1,0:T(8,128)(2,1)S(1)} custom-call(bf16[64,2048]{1,0:T(8,128)(2,1)S(1)} %collective-permute-done.after_ref.refs_0_, bf16[1024,8192]{1,0:T(8,128)(2,1)} %refs_0_.5), custom_call_target="tpu_custom_call" | custom-call | bytes 16777216 | tf_op jit(solution)/shard_map/load/pallas_call | solution.py:83
  22.0 2.9 %collective-permute-done.2.refs_2_.refs_0_ = bf16[64,2048]{1,0:T(8,128)(2,1)S(1)} collective-permute-done((bf16[64,2048]{1,0:T(8,128)(2,1)S(1)}, bf16[64,2048]{1,0:T(8,128)(2,1)S(1)}, u32[]{:S(2)}, u32[]{:S(2)}) %collective-permute-start.2) | collective-permute-done | bytes 262176 | tf_op jit(solution)/shard_map/ppermute | solution.py:19
  25.5 1.0 %project_signal.2 = (bf16[1,64,1408]{2,1,0:T(8,128)(2,1)S(1)}, bf16[1,64,1408]{2,1,0:T(8,128)(2,1)S(1)}, bf16[128,2048]{1,0:T(8,128)(2,1)S(1)}) custom-call(bf16[64,2048]{1,0:T(8,128)(2,1)S(1)} %collective-permute-done.after_ref.refs_0_, bf16[64,2048]{1,0:T(8,128)(2,1)S(1)} %collective-permute-done.1.refs_1_, ...), custom_call_target="tpu_custom_call" | custom-call | flops 738197504 | bytes 5767168 | tf_op jit(solution)/shard_map/project_signal/pallas_call | solution.py:219
  26.6 1.4 %collective-permute-start.6 = (bf16[1,64,1408]{2,1,0:T(8,128)(2,1)S(1)}, bf16[1,64,1408]{2,1,0:T(8,128)(2,1)S(1)}, u32[]{:S(2)}, u32[]{:S(2)}) collective-permute-start(bf16[1,64,1408]{2,1,0:T(8,128)(2,1)S(1)} %get-tuple-element.45.refs_2_), channel_id=1, source_target_pairs={{0,1},{1,0},{2,3},{3,2},{4,5},{5,4},{6,7},{7,6},{8,9},{9,8},{10,11... | collective-permute-start | bytes 540680 | tf_op jit(solution)/shard_map/ppermute | solution.py:19
  28.0 1.0 %project_signal.3 = (bf16[1,64,1408]{2,1,0:T(8,128)(2,1)S(1)}, bf16[1,64,1408]{2,1,0:T(8,128)(2,1)S(1)}, bf16[128,2048]{1,0:T(8,128)(2,1)S(1)}) custom-call(bf16[64,2048]{1,0:T(8,128)(2,1)S(1)} %collective-permute-done.2.refs_2_.refs_0_, bf16[64,2048]{1,0:T(8,128)(2,1)S(1)} %collective-permute-done.3.refs_1_, ...), custom_call_target="tpu_custom_call" | custom-call | flops 738197504 | bytes 5767168 | tf_op jit(solution)/shard_map/project_signal/pallas_call | solution.py:219
  29.7 1.3 %project_gate.1 = (bf16[2,64,1024]{2,1,0:T(8,128)(2,1)S(1)}, bf16[2,64,1024]{2,1,0:T(8,128)(2,1)S(1)}) custom-call(bf16[128,2048]{1,0:T(8,128)(2,1)S(1)} %get-tuple-element.44.refs_0_, bf16[128,2048]{1,0:T(8,128)(2,1)S(1)} %get-tuple-element.46.refs_1_, bf16[2048,1024]{1,0:T(8,128)(2,1)S(1)} %get-tuple-element.47.refs_2_, ...), custom_call_target="tpu_custom_call" | custom-call | flops 1073741824 | bytes 4194304 | tf_op jit(solution)/shard_map/project_gate/pallas_call | solution.py:259
  31.1 1.4 %collective-permute-start.4 = (bf16[1,64,1024]{2,1,0:T(8,128)(2,1)S(1)}, bf16[1,64,1024]{2,1,0:T(8,128)(2,1)S(1)}, u32[]{:S(2)}, u32[]{:S(2)}) collective-permute-start(bf16[1,64,1024]{2,1,0:T(8,128)(2,1)S(1)} %get-tuple-element.79), channel_id=1, source_target_pairs={{0,1},{1,0},{2,3},{3,2},{4,5},{5,4},{6,7},{7,6},{8,9},{9,8},{10,11... | collective-permute-start | bytes 393224 | tf_op jit(solution)/shard_map/ppermute | solution.py:19
  33.2 1.4 %collective-permute-start.8 = (f32[64,17]{1,0:T(8,128)S(1)}, f32[64,17]{1,0:T(8,128)S(1)}, u32[]{:S(2)}, u32[]{:S(2)}) collective-permute-start(f32[64,17]{1,0:T(8,128)S(1)} %add.37), channel_id=1, source_target_pairs={{0,8},{4,12},{8,0},{12,4},{1,9},{5,13},{9,1},{13,5},{2,10},{6,14},... | collective-permute-start | bytes 13064 | tf_op jit(solution)/shard_map/ppermute | solution.py:19
  34.6 2.5 %collective-permute-done.8 = f32[64,17]{1,0:T(8,128)S(1)} collective-permute-done((f32[64,17]{1,0:T(8,128)S(1)}, f32[64,17]{1,0:T(8,128)S(1)}, u32[]{:S(2)}, u32[]{:S(2)}) %collective-permute-start.8) | collective-permute-done | bytes 4384 | tf_op jit(solution)/shard_map/ppermute | solution.py:19
  37.9 2.3 %collective-permute-start.9 = (bf16[1,64,768]{2,1,0:T(8,128)(2,1)S(1)}, bf16[1,64,768]{2,1,0:T(8,128)(2,1)S(1)}, u32[]{:S(2)}, u32[]{:S(2)}) collective-permute-start(bf16[1,64,768]{2,1,0:T(8,128)(2,1)S(1)} %split.25), channel_id=1, source_target_pairs={{0,2},{1,3},{2,0},{3,1},{4,6},{5,7},{6,4},{7,5},{8,10},{9,11},{10,... | collective-permute-start | bytes 294920 | tf_op jit(solution)/shard_map/ppermute | solution.py:19
  41.0 3.8 %collective-permute-done.9 = bf16[1,64,768]{2,1,0:T(8,128)(2,1)S(1)} collective-permute-done((bf16[1,64,768]{2,1,0:T(8,128)(2,1)S(1)}, bf16[1,64,768]{2,1,0:T(8,128)(2,1)S(1)}, u32[]{:S(2)}, u32[]{:S(2)}) %collective-permute-start.9) | collective-permute-done | bytes 98336 | tf_op jit(solution)/shard_map/ppermute | solution.py:19
  44.9 3.1 %collective-permute-start.11 = (bf16[1,32,1024]{2,1,0:T(8,128)(2,1)S(1)}, bf16[1,32,1024]{2,1,0:T(8,128)(2,1)S(1)}, u32[]{:S(2)}, u32[]{:S(2)}) collective-permute-start(bf16[1,32,1024]{2,1,0:T(8,128)(2,1)S(1)} %get-tuple-element.83), channel_id=1, source_target_pairs={{0,2},{1,3},{2,0},{3,1},{4,6},{5,7},{6,4},{7,5},{8,10},{9,11},{10,... | collective-permute-start | bytes 196616 | tf_op jit(solution)/shard_map/ppermute | solution.py:19
  48.2 3.5 %load.5.refs_13_.refs_1_ = bf16[512,8192]{1,0:T(8,128)(2,1)S(1)} custom-call(bf16[1,64,1408]{2,1,0:T(8,128)(2,1)S(1)} %add_convert_fusion.after_ref, bf16[1024,8192]{1,0:T(8,128)(2,1)} %refs_0_.5), custom_call_target="tpu_custom_call" | custom-call | bytes 16777216 | tf_op jit(solution)/shard_map/load/pallas_call | solution.py:83
  51.7 4.8 %read_state.1 = (f32[64,1024]{1,0:T(8,128)S(1)}, f32[2,32,1024]{2,1,0:T(8,128)S(1)}, f32[224,1024]{1,0:T(8,128)S(1)}, f32[2,32,128]{2,1,0:T(8,128)S(1)}, f32[32,...) custom-call(s32[1]{0:T(128)} %copy.45.live_ref, bf16[64,768]{1,0:T(8,128)(2,1)S(1)} %bitcast.38, ...), custom_call_target="tpu_custom_call" | custom-call | flops 268435456 | bytes 10485760 | tf_op jit(solution)/shard_map/read_state/pallas_call | solution.py:375
  56.6 1.2 %output_first.1 = (bf16[1,64,2176]{2,1,0:T(8,128)(2,1)S(1)}, bf16[64,1024]{1,0:T(8,128)(2,1)S(1)}, f32[64,1]{1,0:T(8,128)S(1)}, f32[2,32,1024]{2,1,0:T(8,128)S(1)}) custom-call(bf16[64,1024]{1,0:T(8,128)(2,1)S(1)} %maximum_bitcast_fusion.refs_0_, bf16[64,1024]{1,0:T(8,128)(2,1)S(1)} %bitcast.42, bf16[64,1024]{1,0:T(8,128)(2,1)S(1)} %slice_bitcast_fusion.refs_2_, ...), custom_call_target="tpu_custom_call" | custom-call | flops 268435456 | bytes 4194304 | tf_op jit(solution)/shard_map/output_first/pallas_call | solution.py:606
  57.8 1.6 %output_rest.2.own_ref = bf16[2,64,2048]{2,1,0:T(8,128)(2,1)S(1)} custom-call(bf16[64,1024]{1,0:T(8,128)(2,1)S(1)} %get-tuple-element.65.lhs_ref, bf16[1,64,2176]{2,1,0:T(8,128)(2,1)S(1)} %get-tuple-element.64.after_ref, bf16[512,8192]{1,0:T(8,128)(2,1)S(1)} %load.4.refs_12_.refs_0_, bf16[512,8192]{1,0:T(8,128)(2,1)S(1)} %load.5.refs_13_.refs_1_), custom_call_target="tpu_custom_call" | custom-call | flops 536870912 | bytes 8388608 | tf_op jit(solution)/shard_map/output_rest/pallas_call | solution.py:606
  59.7 5.8 %collective-permute-start.15 = (bf16[1,32,2176]{2,1,0:T(8,128)(2,1)S(1)}, bf16[1,32,2176]{2,1,0:T(8,128)(2,1)S(1)}, u32[]{:S(2)}, u32[]{:S(2)}) collective-permute-start(bf16[1,32,2176]{2,1,0:T(8,128)(2,1)S(1)} %get-tuple-element.77), channel_id=1, source_target_pairs={{0,8},{4,12},{8,0},{12,4},{1,9},{5,13},{9,1},{13,5},{2,10},{6,14},... | collective-permute-start | bytes 417800 | tf_op jit(solution)/shard_map/ppermute | solution.py:19
  67.1 4.9 %state_write.1 = bf16[32,16,64,128]{3,2,1,0:T(8,128)(2,1)} custom-call(f32[2,32,1024]{2,1,0:T(8,128)S(1)} %get-tuple-element.70.feeds_ref, f32[2,32,128]{2,1,0:T(8,128)S(1)} %get-tuple-element.71.b_ref, f32[32,16,128]{2,1,0:T(8,128)S(1)} %broadcast_in_dim.42.decay_ref, bf16[32,16,64,128]{3,2,1,0:T(8,128)(2,1)S(1)} %get-tuple-element.73.state_ref), custom_call_target="tpu_custom_call" | custom-call | flops 134217728 | bytes 16777216 | tf_op jit(solution)/shard_map/state_write/pallas_call | solution.py:435
  73.5 1.0 %copy.39 = bf16[32,2,2048]{2,1,0:T(2,128)(2,1)} copy(bf16[32,2,2048]{2,0,1:T(8,128)(2,1)S(1)} %fusion.3) | data formatting | bytes 524288
  (66 shorter events, 7.4 us)
Async XLA Ops:
  1.8 16.7 %collective-permute-start = (bf16[64,2048]{1,0:T(8,128)(2,1)S(1)}, bf16[64,2048]{1,0:T(8,128)(2,1)S(1)}, u32[]{:S(2)}, u32[]{:S(2)}) collective-permute-start(bf16[64,2048]{1,0:T(8,128)(2,1)S(1)} %bitcast.36), channel_id=1, source_target_pairs={{0,8},{1,12},{2,0},{3,4},{4,9},{5,13},{6,1},{7,5},{8,10},{9,14},{1... | collective-permute-start | bytes 786440 | tf_op jit(solution)/shard_map/ppermute | solution.py:664
  18.5 7.0 %copy-start = (bf16[2048,16]{0,1:T(8,128)(2,1)S(1)}, bf16[2048,16]{0,1:T(8,128)(2,1)}, u32[]{:S(2)}) copy-start(bf16[2048,16]{0,1:T(8,128)(2,1)} %param.20) | copy-start | bytes 196612
  18.5 6.4 %collective-permute-start.2 = (bf16[64,2048]{1,0:T(8,128)(2,1)S(1)}, bf16[64,2048]{1,0:T(8,128)(2,1)S(1)}, u32[]{:S(2)}, u32[]{:S(2)}) collective-permute-start(bf16[64,2048]{1,0:T(8,128)(2,1)S(1)} %collective-permute-done.after_ref.refs_0_), channel_id=1, source_target_pairs={{0,8},{4,12},{8,0},{12,4},{1,9},{5,13},{9,1},{13,5},{2,10},{6,14},... | collective-permute-start | bytes 786440 | tf_op jit(solution)/shard_map/ppermute | solution.py:19
  18.5 7.0 %collective-permute-start.1 = (bf16[64,2048]{1,0:T(8,128)(2,1)S(1)}, bf16[64,2048]{1,0:T(8,128)(2,1)S(1)}, u32[]{:S(2)}, u32[]{:S(2)}) collective-permute-start(bf16[64,2048]{1,0:T(8,128)(2,1)S(1)} %collective-permute-done.after_ref.refs_0_), channel_id=1, source_target_pairs={{0,4},{4,0},{8,12},{12,8},{1,5},{5,1},{9,13},{13,9},{2,6},{6,2},{1... | collective-permute-start | bytes 786440 | tf_op jit(solution)/shard_map/ppermute | solution.py:19
  24.8 3.2 %collective-permute-start.3 = (bf16[64,2048]{1,0:T(8,128)(2,1)S(1)}, bf16[64,2048]{1,0:T(8,128)(2,1)S(1)}, u32[]{:S(2)}, u32[]{:S(2)}) collective-permute-start(bf16[64,2048]{1,0:T(8,128)(2,1)S(1)} %collective-permute-done.2.refs_2_.refs_0_), channel_id=1, source_target_pairs={{0,4},{4,0},{8,12},{12,8},{1,5},{5,1},{9,13},{13,9},{2,6},{6,2},{1... | collective-permute-start | bytes 786440 | tf_op jit(solution)/shard_map/ppermute | solution.py:19
  26.6 10.6 %collective-permute-start.6 = (bf16[1,64,1408]{2,1,0:T(8,128)(2,1)S(1)}, bf16[1,64,1408]{2,1,0:T(8,128)(2,1)S(1)}, u32[]{:S(2)}, u32[]{:S(2)}) collective-permute-start(bf16[1,64,1408]{2,1,0:T(8,128)(2,1)S(1)} %get-tuple-element.45.refs_2_), channel_id=1, source_target_pairs={{0,1},{1,0},{2,3},{3,2},{4,5},{5,4},{6,7},{7,6},{8,9},{9,8},{10,11... | collective-permute-start | bytes 540680 | tf_op jit(solution)/shard_map/ppermute | solution.py:19
  29.0 8.8 %collective-permute-start.5 = (bf16[1,64,1408]{2,1,0:T(8,128)(2,1)S(1)}, bf16[1,64,1408]{2,1,0:T(8,128)(2,1)S(1)}, u32[]{:S(2)}, u32[]{:S(2)}) collective-permute-start(bf16[1,64,1408]{2,1,0:T(8,128)(2,1)S(1)} %get-tuple-element.48.refs_3_), channel_id=1, source_target_pairs={{0,1},{1,0},{2,3},{3,2},{4,5},{5,4},{6,7},{7,6},{8,9},{9,8},{10,11... | collective-permute-start | bytes 540680 | tf_op jit(solution)/shard_map/ppermute | solution.py:19
  29.7 3.4 %collective-permute-start.7 = (f32[64,17]{1,0:T(8,128)S(1)}, f32[64,17]{1,0:T(8,128)S(1)}, u32[]{:S(2)}, u32[]{:S(2)}) collective-permute-start(f32[64,17]{1,0:T(8,128)S(1)} %get-tuple-element.53.after_ref), channel_id=1, source_target_pairs={{0,4},{4,0},{8,12},{12,8},{1,5},{5,1},{9,13},{13,9},{2,6},{6,2},{1... | collective-permute-start | bytes 13064 | tf_op jit(solution)/shard_map/ppermute | solution.py:19
  31.1 10.0 %collective-permute-start.4 = (bf16[1,64,1024]{2,1,0:T(8,128)(2,1)S(1)}, bf16[1,64,1024]{2,1,0:T(8,128)(2,1)S(1)}, u32[]{:S(2)}, u32[]{:S(2)}) collective-permute-start(bf16[1,64,1024]{2,1,0:T(8,128)(2,1)S(1)} %get-tuple-element.79), channel_id=1, source_target_pairs={{0,1},{1,0},{2,3},{3,2},{4,5},{5,4},{6,7},{7,6},{8,9},{9,8},{10,11... | collective-permute-start | bytes 393224 | tf_op jit(solution)/shard_map/ppermute | solution.py:19
  32.5 24.1 %collective-permute-start.12 = (bf16[1,64,1024]{2,1,0:T(8,128)(2,1)S(1)}, bf16[1,64,1024]{2,1,0:T(8,128)(2,1)S(1)}, u32[]{:S(2)}, u32[]{:S(2)}) collective-permute-start(bf16[1,64,1024]{2,1,0:T(8,128)(2,1)S(1)} %get-tuple-element.78), channel_id=1, source_target_pairs={{0,1},{1,0},{2,3},{3,2},{4,5},{5,4},{6,7},{7,6},{8,9},{9,8},{10,11... | collective-permute-start | bytes 393224 | tf_op jit(solution)/shard_map/ppermute | solution.py:19
  33.2 4.0 %collective-permute-start.8 = (f32[64,17]{1,0:T(8,128)S(1)}, f32[64,17]{1,0:T(8,128)S(1)}, u32[]{:S(2)}, u32[]{:S(2)}) collective-permute-start(f32[64,17]{1,0:T(8,128)S(1)} %add.37), channel_id=1, source_target_pairs={{0,8},{4,12},{8,0},{12,4},{1,9},{5,13},{9,1},{13,5},{2,10},{6,14},... | collective-permute-start | bytes 13064 | tf_op jit(solution)/shard_map/ppermute | solution.py:19
  37.9 6.9 %collective-permute-start.9 = (bf16[1,64,768]{2,1,0:T(8,128)(2,1)S(1)}, bf16[1,64,768]{2,1,0:T(8,128)(2,1)S(1)}, u32[]{:S(2)}, u32[]{:S(2)}) collective-permute-start(bf16[1,64,768]{2,1,0:T(8,128)(2,1)S(1)} %split.25), channel_id=1, source_target_pairs={{0,2},{1,3},{2,0},{3,1},{4,6},{5,7},{6,4},{7,5},{8,10},{9,11},{10,... | collective-permute-start | bytes 294920 | tf_op jit(solution)/shard_map/ppermute | solution.py:19
  40.3 16.3 %collective-permute-start.13 = (bf16[1,64,640]{2,1,0:T(8,128)(2,1)S(1)}, bf16[1,64,640]{2,1,0:T(8,128)(2,1)S(1)}, u32[]{:S(2)}, u32[]{:S(2)}) collective-permute-start(bf16[1,64,640]{2,1,0:T(8,128)(2,1)S(1)} %split.29), channel_id=1, source_target_pairs={{0,2},{1,3},{2,0},{3,1},{4,6},{5,7},{6,4},{7,5},{8,10},{9,11},{10,... | collective-permute-start | bytes 245768 | tf_op jit(solution)/shard_map/ppermute | solution.py:19
  44.9 11.6 %collective-permute-start.11 = (bf16[1,32,1024]{2,1,0:T(8,128)(2,1)S(1)}, bf16[1,32,1024]{2,1,0:T(8,128)(2,1)S(1)}, u32[]{:S(2)}, u32[]{:S(2)}) collective-permute-start(bf16[1,32,1024]{2,1,0:T(8,128)(2,1)S(1)} %get-tuple-element.83), channel_id=1, source_target_pairs={{0,2},{1,3},{2,0},{3,1},{4,6},{5,7},{6,4},{7,5},{8,10},{9,11},{10,... | collective-permute-start | bytes 196616 | tf_op jit(solution)/shard_map/ppermute | solution.py:19
  48.1 8.5 %collective-permute-start.10 = (bf16[1,32,1024]{2,1,0:T(8,128)(2,1)S(1)}, bf16[1,32,1024]{2,1,0:T(8,128)(2,1)S(1)}, u32[]{:S(2)}, u32[]{:S(2)}) collective-permute-start(bf16[1,32,1024]{2,1,0:T(8,128)(2,1)S(1)} %get-tuple-element.82), channel_id=1, source_target_pairs={{0,2},{1,3},{2,0},{3,1},{4,6},{5,7},{6,4},{7,5},{8,10},{9,11},{10,... | collective-permute-start | bytes 196616 | tf_op jit(solution)/shard_map/ppermute | solution.py:19
  48.2 3.5 %copy-start.3 = (f32[16]{0:T(128)S(1)}, f32[16]{0:T(128)}, u32[]{:S(2)}) copy-start(f32[16]{0:T(128)} %param.22) | copy-start | bytes 196
  48.2 3.5 %copy-start.4 = (f32[16]{0:T(128)S(1)}, f32[16]{0:T(128)}, u32[]{:S(2)}) copy-start(f32[16]{0:T(128)} %param.23) | copy-start | bytes 196
  48.2 3.5 %copy-start.5 = (f32[16]{0:T(128)S(1)}, f32[16]{0:T(128)}, u32[]{:S(2)}) copy-start(f32[16]{0:T(128)} %param.24) | copy-start | bytes 196
  51.7 4.9 %copy-start.1 = (f32[1024]{0:T(1024)S(1)}, f32[1024]{0:T(1024)}, u32[]{:S(2)}) copy-start(f32[1024]{0:T(1024)} %param.25) | copy-start | bytes 12292
  57.7 1.7 %collective-permute-start.14 = (bf16[1,64,2176]{2,1,0:T(8,128)(2,1)S(1)}, bf16[1,64,2176]{2,1,0:T(8,128)(2,1)S(1)}, u32[]{:S(2)}, u32[]{:S(2)}) collective-permute-start(bf16[1,64,2176]{2,1,0:T(8,128)(2,1)S(1)} %get-tuple-element.64.after_ref), channel_id=1, source_target_pairs={{0,4},{4,0},{8,12},{12,8},{1,5},{5,1},{9,13},{13,9},{2,6},{6,2},{1... | collective-permute-start | bytes 835592 | tf_op jit(solution)/shard_map/ppermute | solution.py:19
  59.7 12.2 %collective-permute-start.15 = (bf16[1,32,2176]{2,1,0:T(8,128)(2,1)S(1)}, bf16[1,32,2176]{2,1,0:T(8,128)(2,1)S(1)}, u32[]{:S(2)}, u32[]{:S(2)}) collective-permute-start(bf16[1,32,2176]{2,1,0:T(8,128)(2,1)S(1)} %get-tuple-element.77), channel_id=1, source_target_pairs={{0,8},{4,12},{8,0},{12,4},{1,9},{5,13},{9,1},{13,5},{2,10},{6,14},... | collective-permute-start | bytes 417800 | tf_op jit(solution)/shard_map/ppermute | solution.py:19
  65.5 7.7 %collective-permute-start.17 = (bf16[1,64,2048]{2,1,0:T(8,128)(2,1)S(1)}, bf16[1,64,2048]{2,1,0:T(8,128)(2,1)S(1)}, u32[]{:S(2)}, u32[]{:S(2)}) collective-permute-start(bf16[1,64,2048]{2,1,0:T(8,128)(2,1)S(1)} %slice.21), channel_id=1, source_target_pairs={{0,4},{4,0},{8,12},{12,8},{1,5},{5,1},{9,13},{13,9},{2,6},{6,2},{1... | collective-permute-start | bytes 786440 | tf_op jit(solution)/shard_map/ppermute | solution.py:19
  65.8 7.0 %collective-permute-start.16 = (bf16[1,32,2176]{2,1,0:T(8,128)(2,1)S(1)}, bf16[1,32,2176]{2,1,0:T(8,128)(2,1)S(1)}, u32[]{:S(2)}, u32[]{:S(2)}) collective-permute-start(bf16[1,32,2176]{2,1,0:T(8,128)(2,1)S(1)} %get-tuple-element.76), channel_id=1, source_target_pairs={{0,8},{4,12},{8,0},{12,4},{1,9},{5,13},{9,1},{13,5},{2,10},{6,14},... | collective-permute-start | bytes 417800 | tf_op jit(solution)/shard_map/ppermute | solution.py:19
  67.1 6.3 %copy-start.6 = (bf16[32,2,2048]{2,1,0:T(2,128)(2,1)S(1)}, bf16[32,2,2048]{2,1,0:T(2,128)(2,1)}, u32[]{:S(2)}) copy-start(bf16[32,2,2048]{2,1,0:T(2,128)(2,1)} %param.16) | copy-start | bytes 786436
  (1 other events, 0.7 us)

commit v14 on v13

--- a/solution.py
+++ b/solution.py
@@ -508,20 +508,13 @@
     return jnp.sum(values.astype(F32), -1, keepdims=True)
 
 
-def output_first_body(distances, shapes, model_width, *refs):
-    refs = list(refs)
-    gate_refs = [refs.pop(0) for _ in range(shapes[0])]
-    signal_refs = [[refs.pop(0) for _ in range(count)] for count in shapes[1:]]
+def output_first_body(distances, terms, model_width, *refs):
+    gate_refs, signal_refs, refs = refs[:terms], refs[terms : 2 * terms], refs[2 * terms :]
     sums_ref, adapted_ref, read_ref, spread_ref, scale_ref, *weight_refs = refs[:-4]
     out_ref, lhs_ref, squares_ref, feeds_ref = refs[-4:]
     streams, inner = read_ref.shape[1:]
     inverse = inverse_of(sums_ref, model_width)
-    total = 0.0
-    for pieces in signal_refs:
-        pieces = [piece[...] for piece in pieces]
-        width = sum(piece.shape[1] for piece in pieces)
-        pieces[0] = pieces[0][:, width - inner :]
-        total += jnp.concatenate([piece.astype(F32) for piece in pieces], 1)
+    total = sum(t[:, t.shape[1] - inner :].astype(F32) for t in signal_refs)
     signal = silu(total * inverse + adapted_ref[...])
     first, second = signal[:streams], signal[streams:]
     factor = [spread_ref[i * streams : (i + 1) * streams, :] for i in range(7)]
@@ -585,7 +578,7 @@
     output_tiles(distances, lhs_ref, refs[:-1], refs[-1])
 
 
-def output_parts(distances, weights, width, operands, model_width=None, shapes=None):
+def output_parts(distances, weights, width, operands, model_width=None, terms=None):
     first = model_width is not None
     rows, depth = operands[0].shape
     count = len(distances)
@@ -595,7 +588,7 @@
     extra = LANES if first else 0
     out_shape = [jax.ShapeDtypeStruct((count, rows, width + extra), BF16)]
     if first:
-        body = functools.partial(output_first_body, distances, shapes, model_width)
+        body = functools.partial(output_first_body, distances, terms, model_width)
         out_shape += [
             jax.ShapeDtypeStruct((rows, depth), BF16),
             jax.ShapeDtypeStruct((rows, 1), F32),
@@ -654,9 +647,16 @@
 
     own = group_of_own(2) == 0
     sums, own = lax.optimization_barrier((sums, own))
-    weights = load(sums, [], projection_signal, projection_input_output, projection_gate)
+    middle = output_weight.shape[0] // 2
+    *weights, out_early = load(
+        sums,
+        [],
+        projection_signal,
+        projection_input_output,
+        projection_gate,
+        (output_weight, 0, middle),
+    )
     signal_weights = (*weights[:2], projection_step.T)
-    middle = output_weight.shape[0] // 2
     if heads_n == rows_n and len(bits_of(rows_n)) == 2:
         turn = [
             (h * rows_n + r, (r ^ 2) * rows_n + h) for h in range(heads_n) for r in range(rows_n)
@@ -671,8 +671,8 @@
             ]
 
         near = [turned, swap(turned, "head", 1)]
-        (out_early,) = load(turned, [], (output_weight, 0, middle))
-        crossed, _ = lax.optimization_barrier((crossed, out_early))
+        (out_late,) = load(turned, [], (output_weight, middle, middle))
+        crossed, _ = lax.optimization_barrier((crossed, out_late))
         far = [crossed, swap(crossed, "head", 1)]
         near_send, near_keep, near_lhs = project_signal(near, order(0), 2, *signal_weights, crossed)
         near_other = swap(near_send, "row", 1)
@@ -686,15 +686,13 @@
         last_send = sum(jnp.where(own, f, n).astype(F32) for n, f in pick).astype(BF16)
         last_send, sums = lax.optimization_barrier((last_send, sums))
         lead = last_send.shape[-1] - inner
-        cut = lead + inner * 3 // 8 // LANES * LANES
-        last_other = [swap(part, "row", 2) for part in jnp.split(last_send, [cut], -1)]
-        (out_late,) = load(last_send, [], (output_weight, middle, middle))
-        signal_terms = [[part[0] for part in last_other]]
-        signal_terms += [[jnp.where(own, n, f)[0]] for n, f in pick]
+        last_other = [swap(part, "row", 2) for part in jnp.split(last_send, [lead], -1)]
+        kept = [jnp.where(own, n, f)[0] for n, f in pick]
+        lead_terms = [last_other[0][0]] + kept
+        signal_terms = [last_other[1][0]] + kept
         gate_far, _ = lax.optimization_barrier((gate_far, last_other[0]))
         gate_last = (gate_far.astype(F32) + gate_keep[1:].astype(F32)).astype(BF16)
         gate_terms = [swap_halves(gate_last, "row", 2, 1)[0], gate_own[0], gate_keep[0]]
-        gate_last, out_late = lax.optimization_barrier((gate_last, out_late))
     else:
         features = lax.all_gather(scaled_flat, "head", axis=1, tiled=True)
         blocks = lax.all_to_all(features, "row", split_axis=1, concat_axis=0, tiled=True)
@@ -705,11 +703,9 @@
         received = swap(send, "row", 1)
         gate_send, gate_keep = project_gate(rows, [lhs], weights[2], send)
         sums = sum_over(sums, "head")
-        keep, out_early, out_late = load(
-            gate_send, [keep], (output_weight, 0, middle), (output_weight, middle, middle)
-        )
+        keep, out_late = load(gate_send, [keep], (output_weight, middle, middle))
         signal_terms, _ = scatter_rows(received, keep, "row")
-        signal_terms = [[t] for t in signal_terms]
+        lead_terms = signal_terms
         gate_terms, gate_last = scatter_rows(swap(gate_send, "row", 1), gate_keep, "row")
     out_weights = [out_early, out_late]
 
@@ -717,7 +713,7 @@
         model_width,
         gate_last,
         live_block_rows,
-        [pieces[0] for pieces in signal_terms],
+        lead_terms,
         sums,
         up_rows,
         step_bias,
@@ -733,7 +729,7 @@
         feature_width,
         [
             *gate_terms,
-            *[piece for pieces in signal_terms for piece in pieces],
+            *signal_terms,
             sums,
             adapted,
             read,
@@ -741,7 +737,7 @@
             gated_norm_scale[None],
         ],
         model_width,
-        [len(gate_terms)] + [len(pieces) for pieces in signal_terms],
+        len(gate_terms),
     )
     (second,) = output_parts(
         distances[2::4] + distances[1::4], out_weights, feature_width, [out_lhs, first]

time: 74.7 us -> 71.5 us (0.957)
  starting transfers between devices: 21.3 us -> 20.2 us
  Pallas kernels: 31.5 us -> 30.5 us
  waiting for transfers between devices: 16 us -> 15 us
    ppermute x1, waiting for transfers between devices: 5.32 us -> 2.73 us  [on_device(): turned = lax.ppermute(scaled_flat, ('head', 'row'), turn)]
    ppermute x17, waiting for transfers between devices: 10.7 us -> 12.2 us  [swap(): return lax.ppermute(values, axis, [(i, i ^ distance) for i in range(size)])]
    ppermute x17, starting transfers between devices: 18.4 us -> 17.2 us  [swap(): return lax.ppermute(values, axis, [(i, i ^ distance) for i in range(size)])]
    pallas_call x3 -> x2, Pallas kernels: 10.9 us -> 9.86 us  [load(): pl.pallas_call(functools.partial(load_body, spans), out_shape=tuple((pltp...]
  transfers between devices with their start and end apart: 18 -> 18, of which waited for: 6 -> 8; matrix products, arithmetic and copies ran while one was open for 1% -> 1% of each run, Pallas kernels for 40% -> 41%
where the time goes in v14:
time: 71.5 us; the launch traced here: 71.3 us
  Pallas kernels  30.5 us (43%)
  starting transfers between devices  20.2 us (28%)
  waiting for transfers between devices  15 us (21%)
  local copies, waits for them, and re-layouts  2.18 us (3%)
  other arithmetic  1.83 us (3%)
  between operations  1.63 us (2%)
    ppermute x17, starting transfers between devices, swap(): return lax.ppermute(values, axis, [(i, i ^ distance) for i in range(size)])  17.2 us
    ppermute x17, waiting for transfers between devices, swap(): return lax.ppermute(values, axis, [(i, i ^ distance) for i in range(size)])  12.2 us
    pallas_call x2, Pallas kernels, load(): pl.pallas_call(functools.partial(load_body, spans), out_shape=tuple((pltp...  9.86 us
    pallas_call x1, Pallas kernels, state_write(): pl.pallas_call(state_write_body, out_shape=jax.ShapeDtypeStruct(state.sha...  4.88 us
    pallas_call x1, Pallas kernels, read_state(): pl.pallas_call(functools.partial(read_body, len(terms), group, model_widt...  4.76 us
    pallas_call x1, Pallas kernels, adapt(): pl.pallas_call(adapt_body, out_shape=(jax.ShapeDtypeStruct((rows, rank +...  3.83 us
    pallas_call x3, Pallas kernels, output_parts(): pl.pallas_call(body, out_shape=tuple(out_shape), in_specs=specs, out_spec...  3.6 us
    ppermute x1, starting transfers between devices, on_device(): turned = lax.ppermute(scaled_flat, ('head', 'row'), turn)  2.95 us
  transfers between devices with their start and end apart: 18, of which 8 were waited for; matrix products, arithmetic and copies ran while one was open for 1% of the time, Pallas kernels for 41%

profile of v14, /device:TPU:0, one launch (start us, length us, event | category | flops | bytes accessed | tf_op | source)
XLA Modules:
  0.0 71.3 jit_solution(3946050946274201803)
XLA Ops:
  0.6 1.1 %fusion.1 = (f32[2,32]{1,0:T(2,128)S(1)}, bf16[2,32,2048]{2,1,0:T(8,128)(2,1)S(1)}) fusion(bf16[32,2,2048]{2,1,0:T(2,128)(2,1)} %param.16, f32[2048]{0:T(1024)} %param.17), kind=kLoop, calls=%fused_computation.4 | loop fusion | flops 655296 | bytes 532736 | tf_op jit(solution)/shard_map/reduce_sum | solution.py:645
  1.8 3.0 %collective-permute-start = (bf16[64,2048]{1,0:T(8,128)(2,1)S(1)}, bf16[64,2048]{1,0:T(8,128)(2,1)S(1)}, u32[]{:S(2)}, u32[]{:S(2)}) collective-permute-start(bf16[64,2048]{1,0:T(8,128)(2,1)S(1)} %bitcast.36), channel_id=1, source_target_pairs={{0,8},{1,12},{2,0},{3,4},{4,9},{5,13},{6,1},{7,5},{8,10},{9,14},{1... | collective-permute-start | bytes 786440 | tf_op jit(solution)/shard_map/ppermute | solution.py:664
  5.5 3.8 %adapt.1 = (f32[64,17]{1,0:T(8,128)S(1)}, bf16[512,1024]{1,0:T(8,128)(2,1)S(1)}) custom-call(s32[32]{0:T(128)S(1)} %copy-done.2, bf16[64,2048]{1,0:T(8,128)(2,1)S(1)} %bitcast.37, f32[64,1]{1,0:T(8,128)S(1)} %reshape.29.squares_ref, bf16[128,16,2048]{2,1,0:T(8,128)(2,1)} %bitcast.47, bf16[128,16,1024]{2,1,0:T(8,128)(2,1)} %up_ref.1), custom_call_target="tpu_custom_call" | custom-call | flops 134217728 | bytes 3145728 | tf_op jit(solution)/shard_map/adapt/pallas_call | solution.py:146
  9.3 6.4 %load.2 = (bf16[2048,1024]{1,0:T(8,128)(2,1)S(1)}, bf16[2048,256]{1,0:T(8,128)(2,1)S(1)}, bf16[2048,1024]{1,0:T(8,128)(2,1)S(1)}, bf16[512,8192]{1,0:T(8,128)(2,1)S(1)}) custom-call(f32[64,17]{1,0:T(8,128)S(1)} %get-tuple-element.52.after_ref, bf16[2048,1024]{1,0:T(8,128)(2,1)} %refs_0_.2, bf16[2048,256]{1,0:T(8,128)(2,1)} %refs_1_.1, ...), custom_call_target="tpu_custom_call" | custom-call | bytes 35651584 | tf_op jit(solution)/shard_map/load/pallas_call | solution.py:83
  15.7 2.7 %collective-permute-done.after_ref.refs_0_ = bf16[64,2048]{1,0:T(8,128)(2,1)S(1)} collective-permute-done((bf16[64,2048]{1,0:T(8,128)(2,1)S(1)}, bf16[64,2048]{1,0:T(8,128)(2,1)S(1)}, u32[]{:S(2)}, u32[]{:S(2)}) %collective-permute-start) | collective-permute-done | bytes 262176 | tf_op jit(solution)/shard_map/ppermute | solution.py:664
  19.3 3.5 %load.3.refs_12_.refs_1_ = bf16[512,8192]{1,0:T(8,128)(2,1)S(1)} custom-call(bf16[64,2048]{1,0:T(8,128)(2,1)S(1)} %collective-permute-done.after_ref.refs_0_, bf16[1024,8192]{1,0:T(8,128)(2,1)} %refs_0_.3), custom_call_target="tpu_custom_call" | custom-call | bytes 16777216 | tf_op jit(solution)/shard_map/load/pallas_call | solution.py:83
  22.7 3.3 %collective-permute-done.2.refs_2_.refs_0_ = bf16[64,2048]{1,0:T(8,128)(2,1)S(1)} collective-permute-done((bf16[64,2048]{1,0:T(8,128)(2,1)S(1)}, bf16[64,2048]{1,0:T(8,128)(2,1)S(1)}, u32[]{:S(2)}, u32[]{:S(2)}) %collective-permute-start.2) | collective-permute-done | bytes 262176 | tf_op jit(solution)/shard_map/ppermute | solution.py:19
  26.7 1.0 %project_signal.2 = (bf16[1,64,1408]{2,1,0:T(8,128)(2,1)S(1)}, bf16[1,64,1408]{2,1,0:T(8,128)(2,1)S(1)}, bf16[128,2048]{1,0:T(8,128)(2,1)S(1)}) custom-call(bf16[64,2048]{1,0:T(8,128)(2,1)S(1)} %collective-permute-done.after_ref.refs_0_, bf16[64,2048]{1,0:T(8,128)(2,1)S(1)} %collective-permute-done.1.refs_1_, ...), custom_call_target="tpu_custom_call" | custom-call | flops 738197504 | bytes 5767168 | tf_op jit(solution)/shard_map/project_signal/pallas_call | solution.py:219
  29.1 1.9 %collective-permute-start.5 = (bf16[1,64,1408]{2,1,0:T(8,128)(2,1)S(1)}, bf16[1,64,1408]{2,1,0:T(8,128)(2,1)S(1)}, u32[]{:S(2)}, u32[]{:S(2)}) collective-permute-start(bf16[1,64,1408]{2,1,0:T(8,128)(2,1)S(1)} %get-tuple-element.47.refs_3_), channel_id=1, source_target_pairs={{0,1},{1,0},{2,3},{3,2},{4,5},{5,4},{6,7},{7,6},{8,9},{9,8},{10,11... | collective-permute-start | bytes 540680 | tf_op jit(solution)/shard_map/ppermute | solution.py:19
  30.9 1.3 %project_gate.1 = (bf16[2,64,1024]{2,1,0:T(8,128)(2,1)S(1)}, bf16[2,64,1024]{2,1,0:T(8,128)(2,1)S(1)}) custom-call(bf16[128,2048]{1,0:T(8,128)(2,1)S(1)} %get-tuple-element.43.refs_0_, bf16[128,2048]{1,0:T(8,128)(2,1)S(1)} %get-tuple-element.45.refs_1_, bf16[2048,1024]{1,0:T(8,128)(2,1)S(1)} %get-tuple-element.46.refs_2_, ...), custom_call_target="tpu_custom_call" | custom-call | flops 1073741824 | bytes 4194304 | tf_op jit(solution)/shard_map/project_gate/pallas_call | solution.py:259
  32.6 1.7 %collective-permute-start.12 = (bf16[1,64,1024]{2,1,0:T(8,128)(2,1)S(1)}, bf16[1,64,1024]{2,1,0:T(8,128)(2,1)S(1)}, u32[]{:S(2)}, u32[]{:S(2)}) collective-permute-start(bf16[1,64,1024]{2,1,0:T(8,128)(2,1)S(1)} %get-tuple-element.76), channel_id=1, source_target_pairs={{0,1},{1,0},{2,3},{3,2},{4,5},{5,4},{6,7},{7,6},{8,9},{9,8},{10,11... | collective-permute-start | bytes 393224 | tf_op jit(solution)/shard_map/ppermute | solution.py:19
  34.4 1.8 %collective-permute-start.8 = (f32[64,17]{1,0:T(8,128)S(1)}, f32[64,17]{1,0:T(8,128)S(1)}, u32[]{:S(2)}, u32[]{:S(2)}) collective-permute-start(f32[64,17]{1,0:T(8,128)S(1)} %add.37), channel_id=1, source_target_pairs={{0,8},{4,12},{8,0},{12,4},{1,9},{5,13},{9,1},{13,5},{2,10},{6,14},... | collective-permute-start | bytes 13064 | tf_op jit(solution)/shard_map/ppermute | solution.py:19
  36.1 2.2 %collective-permute-done.8 = f32[64,17]{1,0:T(8,128)S(1)} collective-permute-done((f32[64,17]{1,0:T(8,128)S(1)}, f32[64,17]{1,0:T(8,128)S(1)}, u32[]{:S(2)}, u32[]{:S(2)}) %collective-permute-start.8) | collective-permute-done | bytes 4384 | tf_op jit(solution)/shard_map/ppermute | solution.py:19
  39.2 1.1 %collective-permute-start.9 = (bf16[1,64,384]{2,1,0:T(8,128)(2,1)S(1)}, bf16[1,64,384]{2,1,0:T(8,128)(2,1)S(1)}, u32[]{:S(2)}, u32[]{:S(2)}) collective-permute-start(bf16[1,64,384]{2,1,0:T(8,128)(2,1)S(1)} %split.25), channel_id=1, source_target_pairs={{0,2},{1,3},{2,0},{3,1},{4,6},{5,7},{6,4},{7,5},{8,10},{9,11},{10,... | collective-permute-start | bytes 147464 | tf_op jit(solution)/shard_map/ppermute | solution.py:19
  40.3 1.9 %collective-permute-start.13 = (bf16[1,64,1024]{2,1,0:T(8,128)(2,1)S(1)}, bf16[1,64,1024]{2,1,0:T(8,128)(2,1)S(1)}, u32[]{:S(2)}, u32[]{:S(2)}) collective-permute-start(bf16[1,64,1024]{2,1,0:T(8,128)(2,1)S(1)} %split.29), channel_id=1, source_target_pairs={{0,2},{1,3},{2,0},{3,1},{4,6},{5,7},{6,4},{7,5},{8,10},{9,11},{10,... | collective-permute-start | bytes 393224 | tf_op jit(solution)/shard_map/ppermute | solution.py:19
  42.2 2.8 %collective-permute-done.9 = bf16[1,64,384]{2,1,0:T(8,128)(2,1)S(1)} collective-permute-done((bf16[1,64,384]{2,1,0:T(8,128)(2,1)S(1)}, bf16[1,64,384]{2,1,0:T(8,128)(2,1)S(1)}, u32[]{:S(2)}, u32[]{:S(2)}) %collective-permute-start.9) | collective-permute-done | bytes 49184 | tf_op jit(solution)/shard_map/ppermute | solution.py:19
  45.1 1.9 %collective-permute-start.10 = (bf16[1,32,1024]{2,1,0:T(8,128)(2,1)S(1)}, bf16[1,32,1024]{2,1,0:T(8,128)(2,1)S(1)}, u32[]{:S(2)}, u32[]{:S(2)}) collective-permute-start(bf16[1,32,1024]{2,1,0:T(8,128)(2,1)S(1)} %get-tuple-element.80), channel_id=1, source_target_pairs={{0,2},{1,3},{2,0},{3,1},{4,6},{5,7},{6,4},{7,5},{8,10},{9,11},{10,... | collective-permute-start | bytes 196616 | tf_op jit(solution)/shard_map/ppermute | solution.py:19
  47.0 1.1 %collective-permute-start.11 = (bf16[1,32,1024]{2,1,0:T(8,128)(2,1)S(1)}, bf16[1,32,1024]{2,1,0:T(8,128)(2,1)S(1)}, u32[]{:S(2)}, u32[]{:S(2)}) collective-permute-start(bf16[1,32,1024]{2,1,0:T(8,128)(2,1)S(1)} %get-tuple-element.81), channel_id=1, source_target_pairs={{0,2},{1,3},{2,0},{3,1},{4,6},{5,7},{6,4},{7,5},{8,10},{9,11},{10,... | collective-permute-start | bytes 196616 | tf_op jit(solution)/shard_map/ppermute | solution.py:19
  48.2 4.8 %read_state.1 = (f32[64,1024]{1,0:T(8,128)S(1)}, f32[2,32,1024]{2,1,0:T(8,128)S(1)}, f32[224,1024]{1,0:T(8,128)S(1)}, f32[2,32,128]{2,1,0:T(8,128)S(1)}, f32[32,...) custom-call(s32[1]{0:T(128)} %copy.45.live_ref, bf16[64,384]{1,0:T(8,128)(2,1)S(1)} %bitcast.42, ...), custom_call_target="tpu_custom_call" | custom-call | flops 268435456 | bytes 10485760 | tf_op jit(solution)/shard_map/read_state/pallas_call | solution.py:375
  52.9 1.8 %collective-permute-done.10 = bf16[1,32,1024]{2,1,0:T(8,128)(2,1)S(1)} collective-permute-done((bf16[1,32,1024]{2,1,0:T(8,128)(2,1)S(1)}, bf16[1,32,1024]{2,1,0:T(8,128)(2,1)S(1)}, u32[]{:S(2)}, u32[]{:S(2)}) %collective-permute-start.10) | collective-permute-done | bytes 65568 | tf_op jit(solution)/shard_map/ppermute | solution.py:19
  55.5 1.2 %output_first.1 = (bf16[1,64,2176]{2,1,0:T(8,128)(2,1)S(1)}, bf16[64,1024]{1,0:T(8,128)(2,1)S(1)}, f32[64,1]{1,0:T(8,128)S(1)}, f32[2,32,1024]{2,1,0:T(8,128)S(1)}) custom-call(bf16[64,1024]{1,0:T(8,128)(2,1)S(1)} %maximum_bitcast_fusion.refs_0_, bf16[64,1024]{1,0:T(8,128)(2,1)S(1)} %bitcast.40, bf16[64,1024]{1,0:T(8,128)(2,1)S(1)} %slice_bitcast_fusion.refs_2_, ...), custom_call_target="tpu_custom_call" | custom-call | flops 268435456 | bytes 4194304 | tf_op jit(solution)/shard_map/output_first/pallas_call | solution.py:599
  56.7 1.6 %output_rest.2.own_ref = bf16[2,64,2048]{2,1,0:T(8,128)(2,1)S(1)} custom-call(bf16[64,1024]{1,0:T(8,128)(2,1)S(1)} %get-tuple-element.63.lhs_ref, bf16[1,64,2176]{2,1,0:T(8,128)(2,1)S(1)} %get-tuple-element.62.after_ref, bf16[512,8192]{1,0:T(8,128)(2,1)S(1)} %get-tuple-element.61.refs_11_.refs_0_, bf16[512,8192]{1,0:T(8,128)(2,1)S(1)} %load.3.refs_12_.refs_1_), custom_call_target="tpu_custom_call" | custom-call | flops 536870912 | bytes 8388608 | tf_op jit(solution)/shard_map/output_rest/pallas_call | solution.py:599
  58.6 3.7 %collective-permute-start.15 = (bf16[1,32,2176]{2,1,0:T(8,128)(2,1)S(1)}, bf16[1,32,2176]{2,1,0:T(8,128)(2,1)S(1)}, u32[]{:S(2)}, u32[]{:S(2)}) collective-permute-start(bf16[1,32,2176]{2,1,0:T(8,128)(2,1)S(1)} %get-tuple-element.75), channel_id=1, source_target_pairs={{0,8},{4,12},{8,0},{12,4},{1,9},{5,13},{9,1},{13,5},{2,10},{6,14},... | collective-permute-start | bytes 417800 | tf_op jit(solution)/shard_map/ppermute | solution.py:19
  64.0 4.9 %state_write.1 = bf16[32,16,64,128]{3,2,1,0:T(8,128)(2,1)} custom-call(f32[2,32,1024]{2,1,0:T(8,128)S(1)} %get-tuple-element.68.feeds_ref, f32[2,32,128]{2,1,0:T(8,128)S(1)} %get-tuple-element.69.b_ref, f32[32,16,128]{2,1,0:T(8,128)S(1)} %broadcast_in_dim.42.decay_ref, bf16[32,16,64,128]{3,2,1,0:T(8,128)(2,1)S(1)} %get-tuple-element.71.state_ref), custom_call_target="tpu_custom_call" | custom-call | flops 134217728 | bytes 16777216 | tf_op jit(solution)/shard_map/state_write/pallas_call | solution.py:435
  (65 shorter events, 9.3 us)
Async XLA Ops:
  1.8 16.7 %collective-permute-start = (bf16[64,2048]{1,0:T(8,128)(2,1)S(1)}, bf16[64,2048]{1,0:T(8,128)(2,1)S(1)}, u32[]{:S(2)}, u32[]{:S(2)}) collective-permute-start(bf16[64,2048]{1,0:T(8,128)(2,1)S(1)} %bitcast.36), channel_id=1, source_target_pairs={{0,8},{1,12},{2,0},{3,4},{4,9},{5,13},{6,1},{7,5},{8,10},{9,14},{1... | collective-permute-start | bytes 786440 | tf_op jit(solution)/shard_map/ppermute | solution.py:664
  18.5 8.2 %copy-start = (bf16[2048,16]{0,1:T(8,128)(2,1)S(1)}, bf16[2048,16]{0,1:T(8,128)(2,1)}, u32[]{:S(2)}) copy-start(bf16[2048,16]{0,1:T(8,128)(2,1)} %param.20) | copy-start | bytes 196612
  18.5 7.5 %collective-permute-start.2 = (bf16[64,2048]{1,0:T(8,128)(2,1)S(1)}, bf16[64,2048]{1,0:T(8,128)(2,1)S(1)}, u32[]{:S(2)}, u32[]{:S(2)}) collective-permute-start(bf16[64,2048]{1,0:T(8,128)(2,1)S(1)} %collective-permute-done.after_ref.refs_0_), channel_id=1, source_target_pairs={{0,8},{4,12},{8,0},{12,4},{1,9},{5,13},{9,1},{13,5},{2,10},{6,14},... | collective-permute-start | bytes 786440 | tf_op jit(solution)/shard_map/ppermute | solution.py:19
  18.5 8.2 %collective-permute-start.1 = (bf16[64,2048]{1,0:T(8,128)(2,1)S(1)}, bf16[64,2048]{1,0:T(8,128)(2,1)S(1)}, u32[]{:S(2)}, u32[]{:S(2)}) collective-permute-start(bf16[64,2048]{1,0:T(8,128)(2,1)S(1)} %collective-permute-done.after_ref.refs_0_), channel_id=1, source_target_pairs={{0,4},{4,0},{8,12},{12,8},{1,5},{5,1},{9,13},{13,9},{2,6},{6,2},{1... | collective-permute-start | bytes 786440 | tf_op jit(solution)/shard_map/ppermute | solution.py:19
  26.0 2.0 %collective-permute-start.3 = (bf16[64,2048]{1,0:T(8,128)(2,1)S(1)}, bf16[64,2048]{1,0:T(8,128)(2,1)S(1)}, u32[]{:S(2)}, u32[]{:S(2)}) collective-permute-start(bf16[64,2048]{1,0:T(8,128)(2,1)S(1)} %collective-permute-done.2.refs_2_.refs_0_), channel_id=1, source_target_pairs={{0,4},{4,0},{8,12},{12,8},{1,5},{5,1},{9,13},{13,9},{2,6},{6,2},{1... | collective-permute-start | bytes 786440 | tf_op jit(solution)/shard_map/ppermute | solution.py:19
  27.7 20.4 %copy-start.3 = (f32[16]{0:T(128)S(1)}, f32[16]{0:T(128)}, u32[]{:S(2)}) copy-start(f32[16]{0:T(128)} %param.22) | copy-start | bytes 196
  27.7 20.4 %copy-start.4 = (f32[16]{0:T(128)S(1)}, f32[16]{0:T(128)}, u32[]{:S(2)}) copy-start(f32[16]{0:T(128)} %param.23) | copy-start | bytes 196
  27.8 20.4 %copy-start.5 = (f32[16]{0:T(128)S(1)}, f32[16]{0:T(128)}, u32[]{:S(2)}) copy-start(f32[16]{0:T(128)} %param.24) | copy-start | bytes 196
  27.8 10.6 %collective-permute-start.6 = (bf16[1,64,1408]{2,1,0:T(8,128)(2,1)S(1)}, bf16[1,64,1408]{2,1,0:T(8,128)(2,1)S(1)}, u32[]{:S(2)}, u32[]{:S(2)}) collective-permute-start(bf16[1,64,1408]{2,1,0:T(8,128)(2,1)S(1)} %get-tuple-element.44.refs_2_), channel_id=1, source_target_pairs={{0,1},{1,0},{2,3},{3,2},{4,5},{5,4},{6,7},{7,6},{8,9},{9,8},{10,11... | collective-permute-start | bytes 540680 | tf_op jit(solution)/shard_map/ppermute | solution.py:19
  29.1 10.0 %collective-permute-start.5 = (bf16[1,64,1408]{2,1,0:T(8,128)(2,1)S(1)}, bf16[1,64,1408]{2,1,0:T(8,128)(2,1)S(1)}, u32[]{:S(2)}, u32[]{:S(2)}) collective-permute-start(bf16[1,64,1408]{2,1,0:T(8,128)(2,1)S(1)} %get-tuple-element.47.refs_3_), channel_id=1, source_target_pairs={{0,1},{1,0},{2,3},{3,2},{4,5},{5,4},{6,7},{7,6},{8,9},{9,8},{10,11... | collective-permute-start | bytes 540680 | tf_op jit(solution)/shard_map/ppermute | solution.py:19
  30.9 3.4 %collective-permute-start.7 = (f32[64,17]{1,0:T(8,128)S(1)}, f32[64,17]{1,0:T(8,128)S(1)}, u32[]{:S(2)}, u32[]{:S(2)}) collective-permute-start(f32[64,17]{1,0:T(8,128)S(1)} %get-tuple-element.52.after_ref), channel_id=1, source_target_pairs={{0,4},{4,0},{8,12},{12,8},{1,5},{5,1},{9,13},{13,9},{2,6},{6,2},{1... | collective-permute-start | bytes 13064 | tf_op jit(solution)/shard_map/ppermute | solution.py:19
  32.2 23.3 %copy-start.1 = (f32[1024]{0:T(1024)S(1)}, f32[1024]{0:T(1024)}, u32[]{:S(2)}) copy-start(f32[1024]{0:T(1024)} %param.25) | copy-start | bytes 12292
  32.3 10.0 %collective-permute-start.4 = (bf16[1,64,1024]{2,1,0:T(8,128)(2,1)S(1)}, bf16[1,64,1024]{2,1,0:T(8,128)(2,1)S(1)}, u32[]{:S(2)}, u32[]{:S(2)}) collective-permute-start(bf16[1,64,1024]{2,1,0:T(8,128)(2,1)S(1)} %get-tuple-element.77), channel_id=1, source_target_pairs={{0,1},{1,0},{2,3},{3,2},{4,5},{5,4},{6,7},{7,6},{8,9},{9,8},{10,11... | collective-permute-start | bytes 393224 | tf_op jit(solution)/shard_map/ppermute | solution.py:19
  32.6 22.8 %collective-permute-start.12 = (bf16[1,64,1024]{2,1,0:T(8,128)(2,1)S(1)}, bf16[1,64,1024]{2,1,0:T(8,128)(2,1)S(1)}, u32[]{:S(2)}, u32[]{:S(2)}) collective-permute-start(bf16[1,64,1024]{2,1,0:T(8,128)(2,1)S(1)} %get-tuple-element.76), channel_id=1, source_target_pairs={{0,1},{1,0},{2,3},{3,2},{4,5},{5,4},{6,7},{7,6},{8,9},{9,8},{10,11... | collective-permute-start | bytes 393224 | tf_op jit(solution)/shard_map/ppermute | solution.py:19
  34.4 4.0 %collective-permute-start.8 = (f32[64,17]{1,0:T(8,128)S(1)}, f32[64,17]{1,0:T(8,128)S(1)}, u32[]{:S(2)}, u32[]{:S(2)}) collective-permute-start(f32[64,17]{1,0:T(8,128)S(1)} %add.37), channel_id=1, source_target_pairs={{0,8},{4,12},{8,0},{12,4},{1,9},{5,13},{9,1},{13,5},{2,10},{6,14},... | collective-permute-start | bytes 13064 | tf_op jit(solution)/shard_map/ppermute | solution.py:19
  39.2 5.9 %collective-permute-start.9 = (bf16[1,64,384]{2,1,0:T(8,128)(2,1)S(1)}, bf16[1,64,384]{2,1,0:T(8,128)(2,1)S(1)}, u32[]{:S(2)}, u32[]{:S(2)}) collective-permute-start(bf16[1,64,384]{2,1,0:T(8,128)(2,1)S(1)} %split.25), channel_id=1, source_target_pairs={{0,2},{1,3},{2,0},{3,1},{4,6},{5,7},{6,4},{7,5},{8,10},{9,11},{10,... | collective-permute-start | bytes 147464 | tf_op jit(solution)/shard_map/ppermute | solution.py:19
  40.3 15.2 %collective-permute-start.13 = (bf16[1,64,1024]{2,1,0:T(8,128)(2,1)S(1)}, bf16[1,64,1024]{2,1,0:T(8,128)(2,1)S(1)}, u32[]{:S(2)}, u32[]{:S(2)}) collective-permute-start(bf16[1,64,1024]{2,1,0:T(8,128)(2,1)S(1)} %split.29), channel_id=1, source_target_pairs={{0,2},{1,3},{2,0},{3,1},{4,6},{5,7},{6,4},{7,5},{8,10},{9,11},{10,... | collective-permute-start | bytes 393224 | tf_op jit(solution)/shard_map/ppermute | solution.py:19
  45.1 9.6 %collective-permute-start.10 = (bf16[1,32,1024]{2,1,0:T(8,128)(2,1)S(1)}, bf16[1,32,1024]{2,1,0:T(8,128)(2,1)S(1)}, u32[]{:S(2)}, u32[]{:S(2)}) collective-permute-start(bf16[1,32,1024]{2,1,0:T(8,128)(2,1)S(1)} %get-tuple-element.80), channel_id=1, source_target_pairs={{0,2},{1,3},{2,0},{3,1},{4,6},{5,7},{6,4},{7,5},{8,10},{9,11},{10,... | collective-permute-start | bytes 196616 | tf_op jit(solution)/shard_map/ppermute | solution.py:19
  47.0 8.4 %collective-permute-start.11 = (bf16[1,32,1024]{2,1,0:T(8,128)(2,1)S(1)}, bf16[1,32,1024]{2,1,0:T(8,128)(2,1)S(1)}, u32[]{:S(2)}, u32[]{:S(2)}) collective-permute-start(bf16[1,32,1024]{2,1,0:T(8,128)(2,1)S(1)} %get-tuple-element.81), channel_id=1, source_target_pairs={{0,2},{1,3},{2,0},{3,1},{4,6},{5,7},{6,4},{7,5},{8,10},{9,11},{10,... | collective-permute-start | bytes 196616 | tf_op jit(solution)/shard_map/ppermute | solution.py:19
  56.7 1.7 %collective-permute-start.14 = (bf16[1,64,2176]{2,1,0:T(8,128)(2,1)S(1)}, bf16[1,64,2176]{2,1,0:T(8,128)(2,1)S(1)}, u32[]{:S(2)}, u32[]{:S(2)}) collective-permute-start(bf16[1,64,2176]{2,1,0:T(8,128)(2,1)S(1)} %get-tuple-element.62.after_ref), channel_id=1, source_target_pairs={{0,4},{4,0},{8,12},{12,8},{1,5},{5,1},{9,13},{13,9},{2,6},{6,2},{1... | collective-permute-start | bytes 835592 | tf_op jit(solution)/shard_map/ppermute | solution.py:19
  58.6 10.2 %collective-permute-start.15 = (bf16[1,32,2176]{2,1,0:T(8,128)(2,1)S(1)}, bf16[1,32,2176]{2,1,0:T(8,128)(2,1)S(1)}, u32[]{:S(2)}, u32[]{:S(2)}) collective-permute-start(bf16[1,32,2176]{2,1,0:T(8,128)(2,1)S(1)} %get-tuple-element.75), channel_id=1, source_target_pairs={{0,8},{4,12},{8,0},{12,4},{1,9},{5,13},{9,1},{13,5},{2,10},{6,14},... | collective-permute-start | bytes 417800 | tf_op jit(solution)/shard_map/ppermute | solution.py:19
  62.4 7.7 %collective-permute-start.17 = (bf16[1,64,2048]{2,1,0:T(8,128)(2,1)S(1)}, bf16[1,64,2048]{2,1,0:T(8,128)(2,1)S(1)}, u32[]{:S(2)}, u32[]{:S(2)}) collective-permute-start(bf16[1,64,2048]{2,1,0:T(8,128)(2,1)S(1)} %slice.21), channel_id=1, source_target_pairs={{0,4},{4,0},{8,12},{12,8},{1,5},{5,1},{9,13},{13,9},{2,6},{6,2},{1... | collective-permute-start | bytes 786440 | tf_op jit(solution)/shard_map/ppermute | solution.py:19
  63.5 6.2 %collective-permute-start.16 = (bf16[1,32,2176]{2,1,0:T(8,128)(2,1)S(1)}, bf16[1,32,2176]{2,1,0:T(8,128)(2,1)S(1)}, u32[]{:S(2)}, u32[]{:S(2)}) collective-permute-start(bf16[1,32,2176]{2,1,0:T(8,128)(2,1)S(1)} %get-tuple-element.74), channel_id=1, source_target_pairs={{0,8},{4,12},{8,0},{12,4},{1,9},{5,13},{9,1},{13,5},{2,10},{6,14},... | collective-permute-start | bytes 417800 | tf_op jit(solution)/shard_map/ppermute | solution.py:19
  64.0 6.2 %copy-start.6 = (bf16[32,2,2048]{2,1,0:T(2,128)(2,1)S(1)}, bf16[32,2,2048]{2,1,0:T(2,128)(2,1)}, u32[]{:S(2)}) copy-start(bf16[32,2,2048]{2,1,0:T(2,128)(2,1)} %param.16) | copy-start | bytes 786436
  (1 other events, 0.7 us)

commit v15 on v14

--- a/solution.py
+++ b/solution.py
@@ -681,7 +681,7 @@
         sums, _ = lax.optimization_barrier((sums, far_send))
         sums = sum_over(sums, "head")
         gate_send, gate_keep = project_gate(rows, [near_lhs, far_lhs], weights[2], far_send)
-        gate_own, gate_far = [swap(part, "row", 1) for part in jnp.split(gate_send, 2, 0)]
+        gate_far = swap(gate_send[1:], "row", 1)
         pick = [(near_keep, far_keep), (near_other, far_other)]
         last_send = sum(jnp.where(own, f, n).astype(F32) for n, f in pick).astype(BF16)
         last_send, sums = lax.optimization_barrier((last_send, sums))
@@ -692,7 +692,12 @@
         signal_terms = [last_other[1][0]] + kept
         gate_far, _ = lax.optimization_barrier((gate_far, last_other[0]))
         gate_last = (gate_far.astype(F32) + gate_keep[1:].astype(F32)).astype(BF16)
-        gate_terms = [swap_halves(gate_last, "row", 2, 1)[0], gate_own[0], gate_keep[0]]
+        own_send, _ = lax.optimization_barrier((gate_send[:1], last_other[0]))
+        gate_terms = [
+            swap_halves(gate_last, "row", 2, 1)[0],
+            swap(own_send, "row", 1)[0],
+            gate_keep[0],
+        ]
     else:
         features = lax.all_gather(scaled_flat, "head", axis=1, tiled=True)
         blocks = lax.all_to_all(features, "row", split_axis=1, concat_axis=0, tiled=True)

time: 71.5 us -> 72.1 us (level)
  waiting for transfers between devices: 15 us -> 18.6 us
  starting transfers between devices: 20.2 us -> 17.2 us
    ppermute x17, waiting for transfers between devices: 12.2 us -> 15.8 us  [swap(): return lax.ppermute(values, axis, [(i, i ^ distance) for i in range(size)])]
    ppermute x17, starting transfers between devices: 17.2 us -> 14.3 us  [swap(): return lax.ppermute(values, axis, [(i, i ^ distance) for i in range(size)])]
  transfers between devices with their start and end apart: 18 -> 18, of which waited for: 8 -> 7; matrix products, arithmetic and copies ran while one was open for 1% -> 1% of each run, Pallas kernels for 41% -> 40%
where the time goes in v15:
time: 72.1 us; the launch traced here: 71.9 us
  Pallas kernels  30.4 us (42%)
  waiting for transfers between devices  18.6 us (26%)
  starting transfers between devices  17.2 us (24%)
  local copies, waits for them, and re-layouts  2.18 us (3%)
  other arithmetic  1.83 us (3%)
  between operations  1.65 us (2%)
    ppermute x17, waiting for transfers between devices, swap(): return lax.ppermute(values, axis, [(i, i ^ distance) for i in range(size)])  15.8 us
    ppermute x17, starting transfers between devices, swap(): return lax.ppermute(values, axis, [(i, i ^ distance) for i in range(size)])  14.3 us
    pallas_call x2, Pallas kernels, load(): pl.pallas_call(functools.partial(load_body, spans), out_shape=tuple((pltp...  9.86 us
    pallas_call x1, Pallas kernels, state_write(): pl.pallas_call(state_write_body, out_shape=jax.ShapeDtypeStruct(state.sha...  4.88 us
    pallas_call x1, Pallas kernels, read_state(): pl.pallas_call(functools.partial(read_body, len(terms), group, model_widt...  4.76 us
    pallas_call x1, Pallas kernels, adapt(): pl.pallas_call(adapt_body, out_shape=(jax.ShapeDtypeStruct((rows, rank +...  3.77 us
    pallas_call x3, Pallas kernels, output_parts(): pl.pallas_call(body, out_shape=tuple(out_shape), in_specs=specs, out_spec...  3.59 us
    ppermute x1, starting transfers between devices, on_device(): turned = lax.ppermute(scaled_flat, ('head', 'row'), turn)  2.95 us
  transfers between devices with their start and end apart: 18, of which 7 were waited for; matrix products, arithmetic and copies ran while one was open for 1% of the time, Pallas kernels for 40%

profile of v15, /device:TPU:0, one launch (start us, length us, event | category | flops | bytes accessed | tf_op | source)
XLA Modules:
  0.0 71.9 jit_solution(8190500951832957544)
XLA Ops:
  0.6 1.1 %fusion.1 = (f32[2,32]{1,0:T(2,128)S(1)}, bf16[2,32,2048]{2,1,0:T(8,128)(2,1)S(1)}) fusion(bf16[32,2,2048]{2,1,0:T(2,128)(2,1)} %param.16, f32[2048]{0:T(1024)} %param.17), kind=kLoop, calls=%fused_computation.4 | loop fusion | flops 655296 | bytes 532736 | tf_op jit(solution)/shard_map/reduce_sum | solution.py:645
  1.8 3.0 %collective-permute-start = (bf16[64,2048]{1,0:T(8,128)(2,1)S(1)}, bf16[64,2048]{1,0:T(8,128)(2,1)S(1)}, u32[]{:S(2)}, u32[]{:S(2)}) collective-permute-start(bf16[64,2048]{1,0:T(8,128)(2,1)S(1)} %bitcast.36), channel_id=1, source_target_pairs={{0,8},{1,12},{2,0},{3,4},{4,9},{5,13},{6,1},{7,5},{8,10},{9,14},{1... | collective-permute-start | bytes 786440 | tf_op jit(solution)/shard_map/ppermute | solution.py:664
  5.5 3.8 %adapt.1 = (f32[64,17]{1,0:T(8,128)S(1)}, bf16[512,1024]{1,0:T(8,128)(2,1)S(1)}) custom-call(s32[32]{0:T(128)S(1)} %copy-done.2, bf16[64,2048]{1,0:T(8,128)(2,1)S(1)} %bitcast.37, f32[64,1]{1,0:T(8,128)S(1)} %reshape.29.squares_ref, bf16[128,16,2048]{2,1,0:T(8,128)(2,1)} %bitcast.47, bf16[128,16,1024]{2,1,0:T(8,128)(2,1)} %up_ref.1), custom_call_target="tpu_custom_call" | custom-call | flops 134217728 | bytes 3145728 | tf_op jit(solution)/shard_map/adapt/pallas_call | solution.py:146
  9.3 6.4 %load.2 = (bf16[2048,1024]{1,0:T(8,128)(2,1)S(1)}, bf16[2048,256]{1,0:T(8,128)(2,1)S(1)}, bf16[2048,1024]{1,0:T(8,128)(2,1)S(1)}, bf16[512,8192]{1,0:T(8,128)(2,1)S(1)}) custom-call(f32[64,17]{1,0:T(8,128)S(1)} %get-tuple-element.53.after_ref, bf16[2048,1024]{1,0:T(8,128)(2,1)} %refs_0_.2, bf16[2048,256]{1,0:T(8,128)(2,1)} %refs_1_.1, ...), custom_call_target="tpu_custom_call" | custom-call | bytes 35651584 | tf_op jit(solution)/shard_map/load/pallas_call | solution.py:83
  15.7 2.8 %collective-permute-done.after_ref.refs_0_ = bf16[64,2048]{1,0:T(8,128)(2,1)S(1)} collective-permute-done((bf16[64,2048]{1,0:T(8,128)(2,1)S(1)}, bf16[64,2048]{1,0:T(8,128)(2,1)S(1)}, u32[]{:S(2)}, u32[]{:S(2)}) %collective-permute-start) | collective-permute-done | bytes 262176 | tf_op jit(solution)/shard_map/ppermute | solution.py:664
  19.2 3.5 %load.3.refs_12_.refs_1_ = bf16[512,8192]{1,0:T(8,128)(2,1)S(1)} custom-call(bf16[64,2048]{1,0:T(8,128)(2,1)S(1)} %collective-permute-done.after_ref.refs_0_, bf16[1024,8192]{1,0:T(8,128)(2,1)} %refs_0_.3), custom_call_target="tpu_custom_call" | custom-call | bytes 16777216 | tf_op jit(solution)/shard_map/load/pallas_call | solution.py:83
  22.7 3.3 %collective-permute-done.2.refs_2_.refs_0_ = bf16[64,2048]{1,0:T(8,128)(2,1)S(1)} collective-permute-done((bf16[64,2048]{1,0:T(8,128)(2,1)S(1)}, bf16[64,2048]{1,0:T(8,128)(2,1)S(1)}, u32[]{:S(2)}, u32[]{:S(2)}) %collective-permute-start.2) | collective-permute-done | bytes 262176 | tf_op jit(solution)/shard_map/ppermute | solution.py:19
  26.6 1.0 %project_signal.2 = (bf16[1,64,1408]{2,1,0:T(8,128)(2,1)S(1)}, bf16[1,64,1408]{2,1,0:T(8,128)(2,1)S(1)}, bf16[128,2048]{1,0:T(8,128)(2,1)S(1)}) custom-call(bf16[64,2048]{1,0:T(8,128)(2,1)S(1)} %collective-permute-done.after_ref.refs_0_, bf16[64,2048]{1,0:T(8,128)(2,1)S(1)} %collective-permute-done.1.refs_1_, ...), custom_call_target="tpu_custom_call" | custom-call | flops 738197504 | bytes 5767168 | tf_op jit(solution)/shard_map/project_signal/pallas_call | solution.py:219
  28.0 1.0 %project_signal.3 = (bf16[1,64,1408]{2,1,0:T(8,128)(2,1)S(1)}, bf16[1,64,1408]{2,1,0:T(8,128)(2,1)S(1)}, bf16[128,2048]{1,0:T(8,128)(2,1)S(1)}) custom-call(bf16[64,2048]{1,0:T(8,128)(2,1)S(1)} %collective-permute-done.2.refs_2_.refs_0_, bf16[64,2048]{1,0:T(8,128)(2,1)S(1)} %collective-permute-done.3.refs_1_, ...), custom_call_target="tpu_custom_call" | custom-call | flops 738197504 | bytes 5767168 | tf_op jit(solution)/shard_map/project_signal/pallas_call | solution.py:219
  29.1 1.8 %collective-permute-start.5 = (bf16[1,64,1408]{2,1,0:T(8,128)(2,1)S(1)}, bf16[1,64,1408]{2,1,0:T(8,128)(2,1)S(1)}, u32[]{:S(2)}, u32[]{:S(2)}) collective-permute-start(bf16[1,64,1408]{2,1,0:T(8,128)(2,1)S(1)} %get-tuple-element.48.refs_3_), channel_id=1, source_target_pairs={{0,1},{1,0},{2,3},{3,2},{4,5},{5,4},{6,7},{7,6},{8,9},{9,8},{10,11... | collective-permute-start | bytes 540680 | tf_op jit(solution)/shard_map/ppermute | solution.py:19
  30.9 1.3 %project_gate.1 = (bf16[2,64,1024]{2,1,0:T(8,128)(2,1)S(1)}, bf16[2,64,1024]{2,1,0:T(8,128)(2,1)S(1)}) custom-call(bf16[128,2048]{1,0:T(8,128)(2,1)S(1)} %get-tuple-element.44.refs_0_, bf16[128,2048]{1,0:T(8,128)(2,1)S(1)} %get-tuple-element.46.refs_1_, bf16[2048,1024]{1,0:T(8,128)(2,1)S(1)} %get-tuple-element.47.refs_2_, ...), custom_call_target="tpu_custom_call" | custom-call | flops 1073741824 | bytes 4194304 | tf_op jit(solution)/shard_map/project_gate/pallas_call | solution.py:259
  32.6 1.8 %collective-permute-start.8 = (f32[64,17]{1,0:T(8,128)S(1)}, f32[64,17]{1,0:T(8,128)S(1)}, u32[]{:S(2)}, u32[]{:S(2)}) collective-permute-start(f32[64,17]{1,0:T(8,128)S(1)} %add.37), channel_id=1, source_target_pairs={{0,8},{4,12},{8,0},{12,4},{1,9},{5,13},{9,1},{13,5},{2,10},{6,14},... | collective-permute-start | bytes 13064 | tf_op jit(solution)/shard_map/ppermute | solution.py:19
  34.4 2.2 %collective-permute-done.8 = f32[64,17]{1,0:T(8,128)S(1)} collective-permute-done((f32[64,17]{1,0:T(8,128)S(1)}, f32[64,17]{1,0:T(8,128)S(1)}, u32[]{:S(2)}, u32[]{:S(2)}) %collective-permute-start.8) | collective-permute-done | bytes 4384 | tf_op jit(solution)/shard_map/ppermute | solution.py:19
  36.6 2.4 %collective-permute-done.5 = bf16[1,64,1408]{2,1,0:T(8,128)(2,1)S(1)} collective-permute-done((bf16[1,64,1408]{2,1,0:T(8,128)(2,1)S(1)}, bf16[1,64,1408]{2,1,0:T(8,128)(2,1)S(1)}, u32[]{:S(2)}, u32[]{:S(2)}) %collective-permute-start.5) | collective-permute-done | bytes 180256 | tf_op jit(solution)/shard_map/ppermute | solution.py:19
  39.1 1.2 %collective-permute-start.9 = (bf16[1,64,384]{2,1,0:T(8,128)(2,1)S(1)}, bf16[1,64,384]{2,1,0:T(8,128)(2,1)S(1)}, u32[]{:S(2)}, u32[]{:S(2)}) collective-permute-start(bf16[1,64,384]{2,1,0:T(8,128)(2,1)S(1)} %split.18), channel_id=1, source_target_pairs={{0,2},{1,3},{2,0},{3,1},{4,6},{5,7},{6,4},{7,5},{8,10},{9,11},{10,... | collective-permute-start | bytes 147464 | tf_op jit(solution)/shard_map/ppermute | solution.py:19
  40.3 1.9 %collective-permute-start.13 = (bf16[1,64,1024]{2,1,0:T(8,128)(2,1)S(1)}, bf16[1,64,1024]{2,1,0:T(8,128)(2,1)S(1)}, u32[]{:S(2)}, u32[]{:S(2)}) collective-permute-start(bf16[1,64,1024]{2,1,0:T(8,128)(2,1)S(1)} %split.21), channel_id=1, source_target_pairs={{0,2},{1,3},{2,0},{3,1},{4,6},{5,7},{6,4},{7,5},{8,10},{9,11},{10,... | collective-permute-start | bytes 393224 | tf_op jit(solution)/shard_map/ppermute | solution.py:19
  42.2 6.0 %collective-permute-done.9 = bf16[1,64,384]{2,1,0:T(8,128)(2,1)S(1)} collective-permute-done((bf16[1,64,384]{2,1,0:T(8,128)(2,1)S(1)}, bf16[1,64,384]{2,1,0:T(8,128)(2,1)S(1)}, u32[]{:S(2)}, u32[]{:S(2)}) %collective-permute-start.9) | collective-permute-done | bytes 49184 | tf_op jit(solution)/shard_map/ppermute | solution.py:19
  48.3 2.9 %collective-permute-start.11 = (bf16[1,32,1024]{2,1,0:T(8,128)(2,1)S(1)}, bf16[1,32,1024]{2,1,0:T(8,128)(2,1)S(1)}, u32[]{:S(2)}, u32[]{:S(2)}) collective-permute-start(bf16[1,32,1024]{2,1,0:T(8,128)(2,1)S(1)} %get-tuple-element.83), channel_id=1, source_target_pairs={{0,2},{1,3},{2,0},{3,1},{4,6},{5,7},{6,4},{7,5},{8,10},{9,11},{10,... | collective-permute-start | bytes 196616 | tf_op jit(solution)/shard_map/ppermute | solution.py:19
  51.4 4.8 %read_state.1 = (f32[64,1024]{1,0:T(8,128)S(1)}, f32[2,32,1024]{2,1,0:T(8,128)S(1)}, f32[224,1024]{1,0:T(8,128)S(1)}, f32[2,32,128]{2,1,0:T(8,128)S(1)}, f32[32,...) custom-call(s32[1]{0:T(128)} %copy.45.live_ref, bf16[64,384]{1,0:T(8,128)(2,1)S(1)} %bitcast.42, ...), custom_call_target="tpu_custom_call" | custom-call | flops 268435456 | bytes 10485760 | tf_op jit(solution)/shard_map/read_state/pallas_call | solution.py:375
  56.2 1.2 %collective-permute-done.12 = bf16[1,64,1024]{2,1,0:T(8,128)(2,1)S(1)} collective-permute-done((bf16[1,64,1024]{2,1,0:T(8,128)(2,1)S(1)}, bf16[1,64,1024]{2,1,0:T(8,128)(2,1)S(1)}, u32[]{:S(2)}, u32[]{:S(2)}) %collective-permute-start.12) | collective-permute-done | bytes 131104 | tf_op jit(solution)/shard_map/ppermute | solution.py:19
  57.4 1.2 %output_first.1 = (bf16[1,64,2176]{2,1,0:T(8,128)(2,1)S(1)}, bf16[64,1024]{1,0:T(8,128)(2,1)S(1)}, f32[64,1]{1,0:T(8,128)S(1)}, f32[2,32,1024]{2,1,0:T(8,128)S(1)}) custom-call(bf16[64,1024]{1,0:T(8,128)(2,1)S(1)} %maximum_bitcast_fusion.refs_0_, bf16[64,1024]{1,0:T(8,128)(2,1)S(1)} %bitcast.41, bf16[64,1024]{1,0:T(8,128)(2,1)S(1)} %slice_bitcast_fusion.refs_2_, ...), custom_call_target="tpu_custom_call" | custom-call | flops 268435456 | bytes 4194304 | tf_op jit(solution)/shard_map/output_first/pallas_call | solution.py:599
  58.6 1.6 %output_rest.2.own_ref = bf16[2,64,2048]{2,1,0:T(8,128)(2,1)S(1)} custom-call(bf16[64,1024]{1,0:T(8,128)(2,1)S(1)} %get-tuple-element.65.lhs_ref, bf16[1,64,2176]{2,1,0:T(8,128)(2,1)S(1)} %get-tuple-element.64.after_ref, bf16[512,8192]{1,0:T(8,128)(2,1)S(1)} %get-tuple-element.63.refs_11_.refs_0_, bf16[512,8192]{1,0:T(8,128)(2,1)S(1)} %load.3.refs_12_.refs_1_), custom_call_target="tpu_custom_call" | custom-call | flops 536870912 | bytes 8388608 | tf_op jit(solution)/shard_map/output_rest/pallas_call | solution.py:599
  60.5 2.4 %collective-permute-start.15 = (bf16[1,32,2176]{2,1,0:T(8,128)(2,1)S(1)}, bf16[1,32,2176]{2,1,0:T(8,128)(2,1)S(1)}, u32[]{:S(2)}, u32[]{:S(2)}) collective-permute-start(bf16[1,32,2176]{2,1,0:T(8,128)(2,1)S(1)} %get-tuple-element.77), channel_id=1, source_target_pairs={{0,8},{4,12},{8,0},{12,4},{1,9},{5,13},{9,1},{13,5},{2,10},{6,14},... | collective-permute-start | bytes 417800 | tf_op jit(solution)/shard_map/ppermute | solution.py:19
  64.6 4.9 %state_write.1 = bf16[32,16,64,128]{3,2,1,0:T(8,128)(2,1)} custom-call(f32[2,32,1024]{2,1,0:T(8,128)S(1)} %get-tuple-element.70.feeds_ref, f32[2,32,128]{2,1,0:T(8,128)S(1)} %get-tuple-element.71.b_ref, f32[32,16,128]{2,1,0:T(8,128)S(1)} %broadcast_in_dim.42.decay_ref, bf16[32,16,64,128]{3,2,1,0:T(8,128)(2,1)S(1)} %get-tuple-element.73.state_ref), custom_call_target="tpu_custom_call" | custom-call | flops 134217728 | bytes 16777216 | tf_op jit(solution)/shard_map/state_write/pallas_call | solution.py:435
  (65 shorter events, 7.1 us)
Async XLA Ops:
  1.8 16.7 %collective-permute-start = (bf16[64,2048]{1,0:T(8,128)(2,1)S(1)}, bf16[64,2048]{1,0:T(8,128)(2,1)S(1)}, u32[]{:S(2)}, u32[]{:S(2)}) collective-permute-start(bf16[64,2048]{1,0:T(8,128)(2,1)S(1)} %bitcast.36), channel_id=1, source_target_pairs={{0,8},{1,12},{2,0},{3,4},{4,9},{5,13},{6,1},{7,5},{8,10},{9,14},{1... | collective-permute-start | bytes 786440 | tf_op jit(solution)/shard_map/ppermute | solution.py:664
  18.5 8.1 %copy-start = (bf16[2048,16]{0,1:T(8,128)(2,1)S(1)}, bf16[2048,16]{0,1:T(8,128)(2,1)}, u32[]{:S(2)}) copy-start(bf16[2048,16]{0,1:T(8,128)(2,1)} %param.20) | copy-start | bytes 196612
  18.5 7.5 %collective-permute-start.2 = (bf16[64,2048]{1,0:T(8,128)(2,1)S(1)}, bf16[64,2048]{1,0:T(8,128)(2,1)S(1)}, u32[]{:S(2)}, u32[]{:S(2)}) collective-permute-start(bf16[64,2048]{1,0:T(8,128)(2,1)S(1)} %collective-permute-done.after_ref.refs_0_), channel_id=1, source_target_pairs={{0,8},{4,12},{8,0},{12,4},{1,9},{5,13},{9,1},{13,5},{2,10},{6,14},... | collective-permute-start | bytes 786440 | tf_op jit(solution)/shard_map/ppermute | solution.py:19
  18.5 8.1 %collective-permute-start.1 = (bf16[64,2048]{1,0:T(8,128)(2,1)S(1)}, bf16[64,2048]{1,0:T(8,128)(2,1)S(1)}, u32[]{:S(2)}, u32[]{:S(2)}) collective-permute-start(bf16[64,2048]{1,0:T(8,128)(2,1)S(1)} %collective-permute-done.after_ref.refs_0_), channel_id=1, source_target_pairs={{0,4},{4,0},{8,12},{12,8},{1,5},{5,1},{9,13},{13,9},{2,6},{6,2},{1... | collective-permute-start | bytes 786440 | tf_op jit(solution)/shard_map/ppermute | solution.py:19
  25.9 2.1 %collective-permute-start.3 = (bf16[64,2048]{1,0:T(8,128)(2,1)S(1)}, bf16[64,2048]{1,0:T(8,128)(2,1)S(1)}, u32[]{:S(2)}, u32[]{:S(2)}) collective-permute-start(bf16[64,2048]{1,0:T(8,128)(2,1)S(1)} %collective-permute-done.2.refs_2_.refs_0_), channel_id=1, source_target_pairs={{0,4},{4,0},{8,12},{12,8},{1,5},{5,1},{9,13},{13,9},{2,6},{6,2},{1... | collective-permute-start | bytes 786440 | tf_op jit(solution)/shard_map/ppermute | solution.py:19
  27.7 23.7 %copy-start.3 = (f32[16]{0:T(128)S(1)}, f32[16]{0:T(128)}, u32[]{:S(2)}) copy-start(f32[16]{0:T(128)} %param.22) | copy-start | bytes 196
  27.7 23.7 %copy-start.4 = (f32[16]{0:T(128)S(1)}, f32[16]{0:T(128)}, u32[]{:S(2)}) copy-start(f32[16]{0:T(128)} %param.23) | copy-start | bytes 196
  27.7 23.7 %copy-start.5 = (f32[16]{0:T(128)S(1)}, f32[16]{0:T(128)}, u32[]{:S(2)}) copy-start(f32[16]{0:T(128)} %param.24) | copy-start | bytes 196
  27.7 8.9 %collective-permute-start.6 = (bf16[1,64,1408]{2,1,0:T(8,128)(2,1)S(1)}, bf16[1,64,1408]{2,1,0:T(8,128)(2,1)S(1)}, u32[]{:S(2)}, u32[]{:S(2)}) collective-permute-start(bf16[1,64,1408]{2,1,0:T(8,128)(2,1)S(1)} %get-tuple-element.45.refs_2_), channel_id=1, source_target_pairs={{0,1},{1,0},{2,3},{3,2},{4,5},{5,4},{6,7},{7,6},{8,9},{9,8},{10,11... | collective-permute-start | bytes 540680 | tf_op jit(solution)/shard_map/ppermute | solution.py:19
  29.1 9.9 %collective-permute-start.5 = (bf16[1,64,1408]{2,1,0:T(8,128)(2,1)S(1)}, bf16[1,64,1408]{2,1,0:T(8,128)(2,1)S(1)}, u32[]{:S(2)}, u32[]{:S(2)}) collective-permute-start(bf16[1,64,1408]{2,1,0:T(8,128)(2,1)S(1)} %get-tuple-element.48.refs_3_), channel_id=1, source_target_pairs={{0,1},{1,0},{2,3},{3,2},{4,5},{5,4},{6,7},{7,6},{8,9},{9,8},{10,11... | collective-permute-start | bytes 540680 | tf_op jit(solution)/shard_map/ppermute | solution.py:19
  30.9 1.7 %collective-permute-start.7 = (f32[64,17]{1,0:T(8,128)S(1)}, f32[64,17]{1,0:T(8,128)S(1)}, u32[]{:S(2)}, u32[]{:S(2)}) collective-permute-start(f32[64,17]{1,0:T(8,128)S(1)} %get-tuple-element.53.after_ref), channel_id=1, source_target_pairs={{0,4},{4,0},{8,12},{12,8},{1,5},{5,1},{9,13},{13,9},{2,6},{6,2},{1... | collective-permute-start | bytes 13064 | tf_op jit(solution)/shard_map/ppermute | solution.py:19
  32.1 25.2 %copy-start.1 = (f32[1024]{0:T(1024)S(1)}, f32[1024]{0:T(1024)}, u32[]{:S(2)}) copy-start(f32[1024]{0:T(1024)} %param.25) | copy-start | bytes 12292
  32.2 10.0 %collective-permute-start.4 = (bf16[1,64,1024]{2,1,0:T(8,128)(2,1)S(1)}, bf16[1,64,1024]{2,1,0:T(8,128)(2,1)S(1)}, u32[]{:S(2)}, u32[]{:S(2)}) collective-permute-start(bf16[1,64,1024]{2,1,0:T(8,128)(2,1)S(1)} %get-tuple-element.79), channel_id=1, source_target_pairs={{0,1},{1,0},{2,3},{3,2},{4,5},{5,4},{6,7},{7,6},{8,9},{9,8},{10,11... | collective-permute-start | bytes 393224 | tf_op jit(solution)/shard_map/ppermute | solution.py:19
  32.6 4.0 %collective-permute-start.8 = (f32[64,17]{1,0:T(8,128)S(1)}, f32[64,17]{1,0:T(8,128)S(1)}, u32[]{:S(2)}, u32[]{:S(2)}) collective-permute-start(f32[64,17]{1,0:T(8,128)S(1)} %add.37), channel_id=1, source_target_pairs={{0,8},{4,12},{8,0},{12,4},{1,9},{5,13},{9,1},{13,5},{2,10},{6,14},... | collective-permute-start | bytes 13064 | tf_op jit(solution)/shard_map/ppermute | solution.py:19
  39.1 9.1 %collective-permute-start.9 = (bf16[1,64,384]{2,1,0:T(8,128)(2,1)S(1)}, bf16[1,64,384]{2,1,0:T(8,128)(2,1)S(1)}, u32[]{:S(2)}, u32[]{:S(2)}) collective-permute-start(bf16[1,64,384]{2,1,0:T(8,128)(2,1)S(1)} %split.18), channel_id=1, source_target_pairs={{0,2},{1,3},{2,0},{3,1},{4,6},{5,7},{6,4},{7,5},{8,10},{9,11},{10,... | collective-permute-start | bytes 147464 | tf_op jit(solution)/shard_map/ppermute | solution.py:19
  40.3 15.9 %collective-permute-start.13 = (bf16[1,64,1024]{2,1,0:T(8,128)(2,1)S(1)}, bf16[1,64,1024]{2,1,0:T(8,128)(2,1)S(1)}, u32[]{:S(2)}, u32[]{:S(2)}) collective-permute-start(bf16[1,64,1024]{2,1,0:T(8,128)(2,1)S(1)} %split.21), channel_id=1, source_target_pairs={{0,2},{1,3},{2,0},{3,1},{4,6},{5,7},{6,4},{7,5},{8,10},{9,11},{10,... | collective-permute-start | bytes 393224 | tf_op jit(solution)/shard_map/ppermute | solution.py:19
  48.3 7.9 %collective-permute-start.10 = (bf16[1,32,1024]{2,1,0:T(8,128)(2,1)S(1)}, bf16[1,32,1024]{2,1,0:T(8,128)(2,1)S(1)}, u32[]{:S(2)}, u32[]{:S(2)}) collective-permute-start(bf16[1,32,1024]{2,1,0:T(8,128)(2,1)S(1)} %get-tuple-element.82), channel_id=1, source_target_pairs={{0,2},{1,3},{2,0},{3,1},{4,6},{5,7},{6,4},{7,5},{8,10},{9,11},{10,... | collective-permute-start | bytes 196616 | tf_op jit(solution)/shard_map/ppermute | solution.py:19
  48.3 7.8 %collective-permute-start.11 = (bf16[1,32,1024]{2,1,0:T(8,128)(2,1)S(1)}, bf16[1,32,1024]{2,1,0:T(8,128)(2,1)S(1)}, u32[]{:S(2)}, u32[]{:S(2)}) collective-permute-start(bf16[1,32,1024]{2,1,0:T(8,128)(2,1)S(1)} %get-tuple-element.83), channel_id=1, source_target_pairs={{0,2},{1,3},{2,0},{3,1},{4,6},{5,7},{6,4},{7,5},{8,10},{9,11},{10,... | collective-permute-start | bytes 196616 | tf_op jit(solution)/shard_map/ppermute | solution.py:19
  51.3 6.1 %collective-permute-start.12 = (bf16[1,64,1024]{2,1,0:T(8,128)(2,1)S(1)}, bf16[1,64,1024]{2,1,0:T(8,128)(2,1)S(1)}, u32[]{:S(2)}, u32[]{:S(2)}) collective-permute-start(bf16[1,64,1024]{2,1,0:T(8,128)(2,1)S(1)} %get-tuple-element.57), channel_id=1, source_target_pairs={{0,1},{1,0},{2,3},{3,2},{4,5},{5,4},{6,7},{7,6},{8,9},{9,8},{10,11... | collective-permute-start | bytes 393224 | tf_op jit(solution)/shard_map/ppermute | solution.py:19
  58.5 1.7 %collective-permute-start.14 = (bf16[1,64,2176]{2,1,0:T(8,128)(2,1)S(1)}, bf16[1,64,2176]{2,1,0:T(8,128)(2,1)S(1)}, u32[]{:S(2)}, u32[]{:S(2)}) collective-permute-start(bf16[1,64,2176]{2,1,0:T(8,128)(2,1)S(1)} %get-tuple-element.64.after_ref), channel_id=1, source_target_pairs={{0,4},{4,0},{8,12},{12,8},{1,5},{5,1},{9,13},{13,9},{2,6},{6,2},{1... | collective-permute-start | bytes 835592 | tf_op jit(solution)/shard_map/ppermute | solution.py:19
  60.5 9.0 %collective-permute-start.15 = (bf16[1,32,2176]{2,1,0:T(8,128)(2,1)S(1)}, bf16[1,32,2176]{2,1,0:T(8,128)(2,1)S(1)}, u32[]{:S(2)}, u32[]{:S(2)}) collective-permute-start(bf16[1,32,2176]{2,1,0:T(8,128)(2,1)S(1)} %get-tuple-element.77), channel_id=1, source_target_pairs={{0,8},{4,12},{8,0},{12,4},{1,9},{5,13},{9,1},{13,5},{2,10},{6,14},... | collective-permute-start | bytes 417800 | tf_op jit(solution)/shard_map/ppermute | solution.py:19
  62.9 7.7 %collective-permute-start.17 = (bf16[1,64,2048]{2,1,0:T(8,128)(2,1)S(1)}, bf16[1,64,2048]{2,1,0:T(8,128)(2,1)S(1)}, u32[]{:S(2)}, u32[]{:S(2)}) collective-permute-start(bf16[1,64,2048]{2,1,0:T(8,128)(2,1)S(1)} %slice.29), channel_id=1, source_target_pairs={{0,4},{4,0},{8,12},{12,8},{1,5},{5,1},{9,13},{13,9},{2,6},{6,2},{1... | collective-permute-start | bytes 786440 | tf_op jit(solution)/shard_map/ppermute | solution.py:19
  64.1 6.2 %collective-permute-start.16 = (bf16[1,32,2176]{2,1,0:T(8,128)(2,1)S(1)}, bf16[1,32,2176]{2,1,0:T(8,128)(2,1)S(1)}, u32[]{:S(2)}, u32[]{:S(2)}) collective-permute-start(bf16[1,32,2176]{2,1,0:T(8,128)(2,1)S(1)} %get-tuple-element.76), channel_id=1, source_target_pairs={{0,8},{4,12},{8,0},{12,4},{1,9},{5,13},{9,1},{13,5},{2,10},{6,14},... | collective-permute-start | bytes 417800 | tf_op jit(solution)/shard_map/ppermute | solution.py:19
  64.6 6.2 %copy-start.6 = (bf16[32,2,2048]{2,1,0:T(2,128)(2,1)S(1)}, bf16[32,2,2048]{2,1,0:T(2,128)(2,1)}, u32[]{:S(2)}) copy-start(bf16[32,2,2048]{2,1,0:T(2,128)(2,1)} %param.16) | copy-start | bytes 786436
  (1 other events, 0.7 us)

commit v16 on v12

--- a/solution.py
+++ b/solution.py
@@ -613,20 +613,22 @@
         turn = [
             (h * rows_n + r, (r ^ 2) * rows_n + h) for h in range(heads_n) for r in range(rows_n)
         ]
-        turned = lax.ppermute(scaled_flat, ("head", "row"), turn)
+        turned = [lax.ppermute(scaled[p], ("head", "row"), turn) for p in range(positions)]
         turned, _ = lax.optimization_barrier((turned, weights[0]))
-        crossed = swap(turned, "head", 2)
+        crossed = [swap(part, "head", 2) for part in turned]
 
         def order(distance):
             return [
-                (lambda d=d: lax.axis_index("head") ^ 2 ^ d, 0) for d in (distance, distance ^ 1)
+                (lambda d=d: lax.axis_index("head") ^ 2 ^ d, p)
+                for d in (distance, distance ^ 1)
+                for p in range(positions)
             ]
 
-        near = [turned, swap(turned, "head", 1)]
-        (out_early,) = load(turned, [], (output_weight, 0, middle))
+        near = turned + [swap(part, "head", 1) for part in turned]
+        (out_early,) = load(turned[0], [], (output_weight, 0, middle))
         crossed, _ = lax.optimization_barrier((crossed, out_early))
-        far = [crossed, swap(crossed, "head", 1)]
-        near_send, near_keep, near_lhs = project_signal(near, order(0), 2, *signal_weights, crossed)
+        far = crossed + [swap(part, "head", 1) for part in crossed]
+        near_send, near_keep, near_lhs = project_signal(near, order(0), 2, *signal_weights, crossed[0])
         near_other = swap(near_send, "row", 1)
         far_send, far_keep, far_lhs = project_signal(far, order(2), 2, *signal_weights, near_send)
         far_other = swap(far_send, "row", 1)

time: 70.8 us -> 74.8 us (1.056)
  starting transfers between devices: 18.1 us -> 25.4 us
  waiting for transfers between devices: 15.3 us -> 10.6 us
  Pallas kernels: 31.5 us -> 32.8 us
    ppermute x17 -> x20, starting transfers between devices: 15.2 us -> 19.8 us  [swap(): return lax.ppermute(values, axis, [(i, i ^ distance) for i in range(size)])]
    ppermute x1 -> x2, waiting for transfers between devices: 5.27 us -> 2.58 us  [on_device(): lax.ppermute(scaled[p], ('head', 'row'), turn)]
    ppermute x1 -> x2, starting transfers between devices: 2.95 us -> 5.58 us  [on_device(): lax.ppermute(scaled[p], ('head', 'row'), turn)]
    ppermute x17 -> x20, waiting for transfers between devices: 10 us -> 8.03 us  [swap(): return lax.ppermute(values, axis, [(i, i ^ distance) for i in range(size)])]
    pallas_call x2, Pallas kernels: 2.13 us -> 3.43 us  [project_signal(): pl.pallas_call(body, out_shape=(half, half, jax.ShapeDtypeStruct((rows, d...]
  transfers between devices with their start and end apart: 18 -> 22, of which waited for: 8 -> 7; matrix products, arithmetic and copies ran while one was open for 1% -> 1% of each run, Pallas kernels for 43% -> 42%
where the time goes in v16:
time: 74.8 us; the launch traced here: 74.5 us
  Pallas kernels  32.8 us (44%)
  starting transfers between devices  25.4 us (34%)
  waiting for transfers between devices  10.6 us (14%)
  local copies, waits for them, and re-layouts  2.2 us (3%)
  other arithmetic  1.84 us (2%)
  between operations  1.7 us (2%)
    ppermute x20, starting transfers between devices, swap(): return lax.ppermute(values, axis, [(i, i ^ distance) for i in range(size)])  19.8 us
    pallas_call x3, Pallas kernels, load(): pl.pallas_call(functools.partial(load_body, spans), out_shape=tuple((pltp...  10.8 us
    ppermute x20, waiting for transfers between devices, swap(): return lax.ppermute(values, axis, [(i, i ^ distance) for i in range(size)])  8.03 us
    ppermute x2, starting transfers between devices, on_device(): lax.ppermute(scaled[p], ('head', 'row'), turn)  5.58 us
    pallas_call x1, Pallas kernels, state_write(): pl.pallas_call(state_write_body, out_shape=jax.ShapeDtypeStruct(state.sha...  4.89 us
    pallas_call x1, Pallas kernels, recur(): pl.pallas_call(functools.partial(recur_body, len(terms), group, model_wid...  4.84 us
    pallas_call x1, Pallas kernels, adapt(): pl.pallas_call(adapt_body, out_shape=(jax.ShapeDtypeStruct((rows, rank +...  3.89 us
    pallas_call x2, Pallas kernels, project_signal(): pl.pallas_call(body, out_shape=(half, half, jax.ShapeDtypeStruct((rows, d...  3.43 us
  transfers between devices with their start and end apart: 22, of which 7 were waited for; matrix products, arithmetic and copies ran while one was open for 1% of the time, Pallas kernels for 42%

profile of v16, /device:TPU:0, one launch (start us, length us, event | category | flops | bytes accessed | tf_op | source)
XLA Modules:
  0.0 74.5 jit_solution(17029725134327160087)
XLA Ops:
  0.6 1.1 %fusion.1 = (f32[2,32]{1,0:T(2,128)S(1)}, bf16[2,32,2048]{2,1,0:T(8,128)(2,1)S(1)}) fusion(bf16[32,2,2048]{2,1,0:T(2,128)(2,1)} %param.16, f32[2048]{0:T(1024)} %param.17), kind=kLoop, calls=%fused_computation.4 | loop fusion | flops 655296 | bytes 532736 | tf_op jit(solution)/shard_map/reduce_sum | solution.py:604
  1.8 3.0 %collective-permute-start = (bf16[32,2048]{1,0:T(8,128)(2,1)S(1)}, bf16[32,2048]{1,0:T(8,128)(2,1)S(1)}, u32[]{:S(2)}, u32[]{:S(2)}) collective-permute-start(bf16[32,2048]{1,0:T(8,128)(2,1)S(1)} %get-tuple-element.85), channel_id=1, source_target_pairs={{0,8},{1,12},{2,0},{3,4},{4,9},{5,13},{6,1},{7,5},{8,10},{9,14},{1... | collective-permute-start | bytes 393224 | tf_op jit(solution)/shard_map/ppermute | solution.py:616
  4.8 2.6 %collective-permute-start.1 = (bf16[32,2048]{1,0:T(8,128)(2,1)S(1)}, bf16[32,2048]{1,0:T(8,128)(2,1)S(1)}, u32[]{:S(2)}, u32[]{:S(2)}) collective-permute-start(bf16[32,2048]{1,0:T(8,128)(2,1)S(1)} %get-tuple-element.84), channel_id=1, source_target_pairs={{0,8},{1,12},{2,0},{3,4},{4,9},{5,13},{6,1},{7,5},{8,10},{9,14},{1... | collective-permute-start | bytes 393224 | tf_op jit(solution)/shard_map/ppermute | solution.py:616
  8.1 3.9 %adapt.1 = (f32[64,17]{1,0:T(8,128)S(1)}, bf16[512,1024]{1,0:T(8,128)(2,1)S(1)}) custom-call(s32[32]{0:T(128)S(1)} %copy-done.2, bf16[64,2048]{1,0:T(8,128)(2,1)S(1)} %bitcast.40, f32[64,1]{1,0:T(8,128)S(1)} %reshape.29.squares_ref, bf16[128,16,2048]{2,1,0:T(8,128)(2,1)} %bitcast.48, bf16[128,16,1024]{2,1,0:T(8,128)(2,1)} %up_ref.1), custom_call_target="tpu_custom_call" | custom-call | flops 134217728 | bytes 3145728 | tf_op jit(solution)/shard_map/adapt/pallas_call | solution.py:145
  12.0 3.9 %load.3 = (bf16[2048,1024]{1,0:T(8,128)(2,1)S(1)}, bf16[2048,256]{1,0:T(8,128)(2,1)S(1)}, bf16[2048,1024]{1,0:T(8,128)(2,1)S(1)}) custom-call(f32[64,17]{1,0:T(8,128)S(1)} %get-tuple-element.55.after_ref, bf16[2048,1024]{1,0:T(8,128)(2,1)} %refs_0_.3, bf16[2048,256]{1,0:T(8,128)(2,1)} %refs_1_.1, bf16[2048,1024]{1,0:T(8,128)(2,1)} %refs_2_.1), custom_call_target="tpu_custom_call" | custom-call | bytes 18874368 | tf_op jit(solution)/shard_map/load/pallas_call | solution.py:82
  15.9 2.6 %collective-permute-done.1.refs_1_ = bf16[32,2048]{1,0:T(8,128)(2,1)S(1)} collective-permute-done((bf16[32,2048]{1,0:T(8,128)(2,1)S(1)}, bf16[32,2048]{1,0:T(8,128)(2,1)S(1)}, u32[]{:S(2)}, u32[]{:S(2)}) %collective-permute-start.1) | collective-permute-done | bytes 131104 | tf_op jit(solution)/shard_map/ppermute | solution.py:616
  18.5 2.0 %collective-permute-start.5 = (bf16[32,2048]{1,0:T(8,128)(2,1)S(1)}, bf16[32,2048]{1,0:T(8,128)(2,1)S(1)}, u32[]{:S(2)}, u32[]{:S(2)}) collective-permute-start(bf16[32,2048]{1,0:T(8,128)(2,1)S(1)} %collective-permute-done.1.refs_1_), channel_id=1, source_target_pairs={{0,8},{4,12},{8,0},{12,4},{1,9},{5,13},{9,1},{13,5},{2,10},{6,14},... | collective-permute-start | bytes 393224 | tf_op jit(solution)/shard_map/ppermute | solution.py:18
  21.1 3.5 %load.4.refs_6_.refs_0_ = bf16[512,8192]{1,0:T(8,128)(2,1)S(1)} custom-call(bf16[32,2048]{1,0:T(8,128)(2,1)S(1)} %collective-permute-done.after_ref.refs_0_, bf16[1024,8192]{1,0:T(8,128)(2,1)} %refs_0_.5), custom_call_target="tpu_custom_call" | custom-call | bytes 16777216 | tf_op jit(solution)/shard_map/load/pallas_call | solution.py:82
  26.1 1.7 %project_signal.2 = (bf16[1,64,1296]{2,1,0:T(8,128)(2,1)S(1)}, bf16[1,64,1296]{2,1,0:T(8,128)(2,1)S(1)}, bf16[128,2048]{1,0:T(8,128)(2,1)S(1)}) custom-call(bf16[32,2048]{1,0:T(8,128)(2,1)S(1)} %collective-permute-done.after_ref.refs_0_, bf16[32,2048]{1,0:T(8,128)(2,1)S(1)} %collective-permute-done.1.refs_1_, ...), custom_call_target="tpu_custom_call" | custom-call | flops 679477248 | bytes 5308416 | tf_op jit(solution)/shard_map/project_signal/pallas_call | solution.py:211
  27.8 1.5 %collective-permute-start.10 = (bf16[1,64,1296]{2,1,0:T(8,128)(2,1)S(1)}, bf16[1,64,1296]{2,1,0:T(8,128)(2,1)S(1)}, u32[]{:S(2)}, u32[]{:S(2)}) collective-permute-start(bf16[1,64,1296]{2,1,0:T(8,128)(2,1)S(1)} %get-tuple-element.47.refs_4_), channel_id=1, source_target_pairs={{0,1},{1,0},{2,3},{3,2},{4,5},{5,4},{6,7},{7,6},{8,9},{9,8},{10,11... | collective-permute-start | bytes 497672 | tf_op jit(solution)/shard_map/ppermute | solution.py:18
  29.3 1.7 %project_signal.3 = (bf16[1,64,1296]{2,1,0:T(8,128)(2,1)S(1)}, bf16[1,64,1296]{2,1,0:T(8,128)(2,1)S(1)}, bf16[128,2048]{1,0:T(8,128)(2,1)S(1)}) custom-call(bf16[32,2048]{1,0:T(8,128)(2,1)S(1)} %collective-permute-done.4.refs_4_.refs_0_, bf16[32,2048]{1,0:T(8,128)(2,1)S(1)} %collective-permute-done.5.refs_1_, ...), custom_call_target="tpu_custom_call" | custom-call | flops 679477248 | bytes 5308416 | tf_op jit(solution)/shard_map/project_signal/pallas_call | solution.py:211
  31.7 1.3 %project_gate.1 = (bf16[2,64,1024]{2,1,0:T(8,128)(2,1)S(1)}, bf16[2,64,1024]{2,1,0:T(8,128)(2,1)S(1)}) custom-call(bf16[128,2048]{1,0:T(8,128)(2,1)S(1)} %get-tuple-element.45.refs_0_, bf16[128,2048]{1,0:T(8,128)(2,1)S(1)} %get-tuple-element.48.refs_1_, bf16[2048,1024]{1,0:T(8,128)(2,1)S(1)} %get-tuple-element.49.refs_2_, ...), custom_call_target="tpu_custom_call" | custom-call | flops 1073741824 | bytes 4194304 | tf_op jit(solution)/shard_map/project_gate/pallas_call | solution.py:251
  33.0 1.5 %collective-permute-start.8 = (bf16[1,64,1024]{2,1,0:T(8,128)(2,1)S(1)}, bf16[1,64,1024]{2,1,0:T(8,128)(2,1)S(1)}, u32[]{:S(2)}, u32[]{:S(2)}) collective-permute-start(bf16[1,64,1024]{2,1,0:T(8,128)(2,1)S(1)} %get-tuple-element.81), channel_id=1, source_target_pairs={{0,1},{1,0},{2,3},{3,2},{4,5},{5,4},{6,7},{7,6},{8,9},{9,8},{10,11... | collective-permute-start | bytes 393224 | tf_op jit(solution)/shard_map/ppermute | solution.py:18
  35.7 1.7 %collective-permute-start.12 = (f32[64,17]{1,0:T(8,128)S(1)}, f32[64,17]{1,0:T(8,128)S(1)}, u32[]{:S(2)}, u32[]{:S(2)}) collective-permute-start(f32[64,17]{1,0:T(8,128)S(1)} %add.37), channel_id=1, source_target_pairs={{0,8},{4,12},{8,0},{12,4},{1,9},{5,13},{9,1},{13,5},{2,10},{6,14},... | collective-permute-start | bytes 13064 | tf_op jit(solution)/shard_map/ppermute | solution.py:18
  37.4 2.2 %collective-permute-done.12 = f32[64,17]{1,0:T(8,128)S(1)} collective-permute-done((f32[64,17]{1,0:T(8,128)S(1)}, f32[64,17]{1,0:T(8,128)S(1)}, u32[]{:S(2)}, u32[]{:S(2)}) %collective-permute-start.12) | collective-permute-done | bytes 4384 | tf_op jit(solution)/shard_map/ppermute | solution.py:18
  39.8 1.7 %collective-permute-start.13 = (bf16[1,32,1296]{2,1,0:T(8,128)(2,1)S(1)}, bf16[1,32,1296]{2,1,0:T(8,128)(2,1)S(1)}, u32[]{:S(2)}, u32[]{:S(2)}) collective-permute-start(bf16[1,32,1296]{2,1,0:T(8,128)(2,1)S(1)} %get-tuple-element.87), channel_id=1, source_target_pairs={{0,2},{1,3},{2,0},{3,1},{4,6},{5,7},{6,4},{7,5},{8,10},{9,11},{10,... | collective-permute-start | bytes 248840 | tf_op jit(solution)/shard_map/ppermute | solution.py:18
  41.4 1.3 %collective-permute-start.17 = (bf16[1,32,1296]{2,1,0:T(8,128)(2,1)S(1)}, bf16[1,32,1296]{2,1,0:T(8,128)(2,1)S(1)}, u32[]{:S(2)}, u32[]{:S(2)}) collective-permute-start(bf16[1,32,1296]{2,1,0:T(8,128)(2,1)S(1)} %get-tuple-element.86), channel_id=1, source_target_pairs={{0,2},{1,3},{2,0},{3,1},{4,6},{5,7},{6,4},{7,5},{8,10},{9,11},{10,... | collective-permute-start | bytes 248840 | tf_op jit(solution)/shard_map/ppermute | solution.py:18
  42.8 3.5 %load.5.refs_7_.refs_1_ = bf16[512,8192]{1,0:T(8,128)(2,1)S(1)} custom-call(bf16[1,64,1296]{2,1,0:T(8,128)(2,1)S(1)} %add_convert_fusion.after_ref, bf16[1024,8192]{1,0:T(8,128)(2,1)} %refs_0_.5), custom_call_target="tpu_custom_call" | custom-call | bytes 16777216 | tf_op jit(solution)/shard_map/load/pallas_call | solution.py:82
  46.4 3.8 %collective-permute-done.13 = bf16[1,32,1296]{2,1,0:T(8,128)(2,1)S(1)} collective-permute-done((bf16[1,32,1296]{2,1,0:T(8,128)(2,1)S(1)}, bf16[1,32,1296]{2,1,0:T(8,128)(2,1)S(1)}, u32[]{:S(2)}, u32[]{:S(2)}) %collective-permute-start.13) | collective-permute-done | bytes 82976 | tf_op jit(solution)/shard_map/ppermute | solution.py:18
  50.2 2.9 %collective-permute-start.14 = (bf16[1,32,1024]{2,1,0:T(8,128)(2,1)S(1)}, bf16[1,32,1024]{2,1,0:T(8,128)(2,1)S(1)}, u32[]{:S(2)}, u32[]{:S(2)}) collective-permute-start(bf16[1,32,1024]{2,1,0:T(8,128)(2,1)S(1)} %get-tuple-element.88), channel_id=1, source_target_pairs={{0,2},{1,3},{2,0},{3,1},{4,6},{5,7},{6,4},{7,5},{8,10},{9,11},{10,... | collective-permute-start | bytes 196616 | tf_op jit(solution)/shard_map/ppermute | solution.py:18
  53.5 4.8 %recur.1 = (f32[64,1024]{1,0:T(8,128)S(1)}, f32[2,32,1024]{2,1,0:T(8,128)S(1)}, f32[2,32,128]{2,1,0:T(8,128)S(1)}, f32[32,16]{1,0:T(8,128)S(1)}, bf16[32,16,64,128]{3,2,1,0:T(8,128)(2,1)S(1)}) custom-call(s32[1]{0:T(128)} %copy.30.live_ref, bf16[64,1296]{1,0:T(8,128)(2,1)S(1)} %maximum_bitcast_fusion.refs_0_, ...), custom_call_target="tpu_custom_call" | custom-call | flops 268435456 | bytes 10485760 | tf_op jit(solution)/shard_map/recur/pallas_call | solution.py:384
  59.5 1.6 %output_rest.2.own_ref = bf16[2,64,2048]{2,1,0:T(8,128)(2,1)S(1)} custom-call(bf16[64,1024]{1,0:T(8,128)(2,1)S(1)} %get-tuple-element.65.lhs_ref, bf16[1,64,2176]{2,1,0:T(8,128)(2,1)S(1)} %get-tuple-element.64.after_ref, bf16[512,8192]{1,0:T(8,128)(2,1)S(1)} %load.4.refs_6_.refs_0_, bf16[512,8192]{1,0:T(8,128)(2,1)S(1)} %load.5.refs_7_.refs_1_), custom_call_target="tpu_custom_call" | custom-call | flops 536870912 | bytes 8388608 | tf_op jit(solution)/shard_map/output_rest/pallas_call | solution.py:558
  61.4 4.2 %collective-permute-start.19 = (bf16[1,32,2176]{2,1,0:T(8,128)(2,1)S(1)}, bf16[1,32,2176]{2,1,0:T(8,128)(2,1)S(1)}, u32[]{:S(2)}, u32[]{:S(2)}) collective-permute-start(bf16[1,32,2176]{2,1,0:T(8,128)(2,1)S(1)} %get-tuple-element.79), channel_id=1, source_target_pairs={{0,8},{4,12},{8,0},{12,4},{1,9},{5,13},{9,1},{13,5},{2,10},{6,14},... | collective-permute-start | bytes 417800 | tf_op jit(solution)/shard_map/ppermute | solution.py:18
  67.1 4.9 %state_write.1 = bf16[32,16,64,128]{3,2,1,0:T(8,128)(2,1)} custom-call(f32[2,32,1024]{2,1,0:T(8,128)S(1)} %get-tuple-element.70.feeds_ref, f32[2,32,128]{2,1,0:T(8,128)S(1)} %get-tuple-element.71.b_ref, f32[32,16,128]{2,1,0:T(8,128)S(1)} %broadcast_in_dim.42.decay_ref, bf16[32,16,64,128]{3,2,1,0:T(8,128)(2,1)S(1)} %get-tuple-element.73.state_ref), custom_call_target="tpu_custom_call" | custom-call | flops 134217728 | bytes 16777216 | tf_op jit(solution)/shard_map/state_write/pallas_call | solution.py:446
  (75 shorter events, 10.0 us)
Async XLA Ops:
  1.8 14.2 %collective-permute-start = (bf16[32,2048]{1,0:T(8,128)(2,1)S(1)}, bf16[32,2048]{1,0:T(8,128)(2,1)S(1)}, u32[]{:S(2)}, u32[]{:S(2)}) collective-permute-start(bf16[32,2048]{1,0:T(8,128)(2,1)S(1)} %get-tuple-element.85), channel_id=1, source_target_pairs={{0,8},{1,12},{2,0},{3,4},{4,9},{5,13},{6,1},{7,5},{8,10},{9,14},{1... | collective-permute-start | bytes 393224 | tf_op jit(solution)/shard_map/ppermute | solution.py:616
  4.8 13.7 %collective-permute-start.1 = (bf16[32,2048]{1,0:T(8,128)(2,1)S(1)}, bf16[32,2048]{1,0:T(8,128)(2,1)S(1)}, u32[]{:S(2)}, u32[]{:S(2)}) collective-permute-start(bf16[32,2048]{1,0:T(8,128)(2,1)S(1)} %get-tuple-element.84), channel_id=1, source_target_pairs={{0,8},{1,12},{2,0},{3,4},{4,9},{5,13},{6,1},{7,5},{8,10},{9,14},{1... | collective-permute-start | bytes 393224 | tf_op jit(solution)/shard_map/ppermute | solution.py:616
  18.5 6.0 %collective-permute-start.4 = (bf16[32,2048]{1,0:T(8,128)(2,1)S(1)}, bf16[32,2048]{1,0:T(8,128)(2,1)S(1)}, u32[]{:S(2)}, u32[]{:S(2)}) collective-permute-start(bf16[32,2048]{1,0:T(8,128)(2,1)S(1)} %collective-permute-done.after_ref.refs_0_), channel_id=1, source_target_pairs={{0,8},{4,12},{8,0},{12,4},{1,9},{5,13},{9,1},{13,5},{2,10},{6,14},... | collective-permute-start | bytes 393224 | tf_op jit(solution)/shard_map/ppermute | solution.py:18
  18.5 6.4 %collective-permute-start.5 = (bf16[32,2048]{1,0:T(8,128)(2,1)S(1)}, bf16[32,2048]{1,0:T(8,128)(2,1)S(1)}, u32[]{:S(2)}, u32[]{:S(2)}) collective-permute-start(bf16[32,2048]{1,0:T(8,128)(2,1)S(1)} %collective-permute-done.1.refs_1_), channel_id=1, source_target_pairs={{0,8},{4,12},{8,0},{12,4},{1,9},{5,13},{9,1},{13,5},{2,10},{6,14},... | collective-permute-start | bytes 393224 | tf_op jit(solution)/shard_map/ppermute | solution.py:18
  20.5 5.5 %collective-permute-start.2 = (bf16[32,2048]{1,0:T(8,128)(2,1)S(1)}, bf16[32,2048]{1,0:T(8,128)(2,1)S(1)}, u32[]{:S(2)}, u32[]{:S(2)}) collective-permute-start(bf16[32,2048]{1,0:T(8,128)(2,1)S(1)} %collective-permute-done.after_ref.refs_0_), channel_id=1, source_target_pairs={{0,4},{4,0},{8,12},{12,8},{1,5},{5,1},{9,13},{13,9},{2,6},{6,2},{1... | collective-permute-start | bytes 393224 | tf_op jit(solution)/shard_map/ppermute | solution.py:18
  20.6 5.5 %collective-permute-start.3 = (bf16[32,2048]{1,0:T(8,128)(2,1)S(1)}, bf16[32,2048]{1,0:T(8,128)(2,1)S(1)}, u32[]{:S(2)}, u32[]{:S(2)}) collective-permute-start(bf16[32,2048]{1,0:T(8,128)(2,1)S(1)} %collective-permute-done.1.refs_1_), channel_id=1, source_target_pairs={{0,4},{4,0},{8,12},{12,8},{1,5},{5,1},{9,13},{13,9},{2,6},{6,2},{1... | collective-permute-start | bytes 393224 | tf_op jit(solution)/shard_map/ppermute | solution.py:18
  24.9 4.4 %collective-permute-start.6 = (bf16[32,2048]{1,0:T(8,128)(2,1)S(1)}, bf16[32,2048]{1,0:T(8,128)(2,1)S(1)}, u32[]{:S(2)}, u32[]{:S(2)}) collective-permute-start(bf16[32,2048]{1,0:T(8,128)(2,1)S(1)} %collective-permute-done.4.refs_4_.refs_0_), channel_id=1, source_target_pairs={{0,4},{4,0},{8,12},{12,8},{1,5},{5,1},{9,13},{13,9},{2,6},{6,2},{1... | collective-permute-start | bytes 393224 | tf_op jit(solution)/shard_map/ppermute | solution.py:18
  24.9 4.4 %collective-permute-start.7 = (bf16[32,2048]{1,0:T(8,128)(2,1)S(1)}, bf16[32,2048]{1,0:T(8,128)(2,1)S(1)}, u32[]{:S(2)}, u32[]{:S(2)}) collective-permute-start(bf16[32,2048]{1,0:T(8,128)(2,1)S(1)} %collective-permute-done.5.refs_1_), channel_id=1, source_target_pairs={{0,4},{4,0},{8,12},{12,8},{1,5},{5,1},{9,13},{13,9},{2,6},{6,2},{1... | collective-permute-start | bytes 393224 | tf_op jit(solution)/shard_map/ppermute | solution.py:18
  27.8 11.8 %collective-permute-start.10 = (bf16[1,64,1296]{2,1,0:T(8,128)(2,1)S(1)}, bf16[1,64,1296]{2,1,0:T(8,128)(2,1)S(1)}, u32[]{:S(2)}, u32[]{:S(2)}) collective-permute-start(bf16[1,64,1296]{2,1,0:T(8,128)(2,1)S(1)} %get-tuple-element.47.refs_4_), channel_id=1, source_target_pairs={{0,1},{1,0},{2,3},{3,2},{4,5},{5,4},{6,7},{7,6},{8,9},{9,8},{10,11... | collective-permute-start | bytes 497672 | tf_op jit(solution)/shard_map/ppermute | solution.py:18
  31.0 8.6 %collective-permute-start.9 = (bf16[1,64,1296]{2,1,0:T(8,128)(2,1)S(1)}, bf16[1,64,1296]{2,1,0:T(8,128)(2,1)S(1)}, u32[]{:S(2)}, u32[]{:S(2)}) collective-permute-start(bf16[1,64,1296]{2,1,0:T(8,128)(2,1)S(1)} %get-tuple-element.50.refs_3_), channel_id=1, source_target_pairs={{0,1},{1,0},{2,3},{3,2},{4,5},{5,4},{6,7},{7,6},{8,9},{9,8},{10,11... | collective-permute-start | bytes 497672 | tf_op jit(solution)/shard_map/ppermute | solution.py:18
  33.0 13.3 %collective-permute-start.8 = (bf16[1,64,1024]{2,1,0:T(8,128)(2,1)S(1)}, bf16[1,64,1024]{2,1,0:T(8,128)(2,1)S(1)}, u32[]{:S(2)}, u32[]{:S(2)}) collective-permute-start(bf16[1,64,1024]{2,1,0:T(8,128)(2,1)S(1)} %get-tuple-element.81), channel_id=1, source_target_pairs={{0,1},{1,0},{2,3},{3,2},{4,5},{5,4},{6,7},{7,6},{8,9},{9,8},{10,11... | collective-permute-start | bytes 393224 | tf_op jit(solution)/shard_map/ppermute | solution.py:18
  34.5 1.2 %collective-permute-start.11 = (f32[64,17]{1,0:T(8,128)S(1)}, f32[64,17]{1,0:T(8,128)S(1)}, u32[]{:S(2)}, u32[]{:S(2)}) collective-permute-start(f32[64,17]{1,0:T(8,128)S(1)} %get-tuple-element.55.after_ref), channel_id=1, source_target_pairs={{0,4},{4,0},{8,12},{12,8},{1,5},{5,1},{9,13},{13,9},{2,6},{6,2},{1... | collective-permute-start | bytes 13064 | tf_op jit(solution)/shard_map/ppermute | solution.py:18
  34.5 23.9 %collective-permute-start.16 = (bf16[1,64,1024]{2,1,0:T(8,128)(2,1)S(1)}, bf16[1,64,1024]{2,1,0:T(8,128)(2,1)S(1)}, u32[]{:S(2)}, u32[]{:S(2)}) collective-permute-start(bf16[1,64,1024]{2,1,0:T(8,128)(2,1)S(1)} %get-tuple-element.80), channel_id=1, source_target_pairs={{0,1},{1,0},{2,3},{3,2},{4,5},{5,4},{6,7},{7,6},{8,9},{9,8},{10,11... | collective-permute-start | bytes 393224 | tf_op jit(solution)/shard_map/ppermute | solution.py:18
  35.7 3.9 %collective-permute-start.12 = (f32[64,17]{1,0:T(8,128)S(1)}, f32[64,17]{1,0:T(8,128)S(1)}, u32[]{:S(2)}, u32[]{:S(2)}) collective-permute-start(f32[64,17]{1,0:T(8,128)S(1)} %add.37), channel_id=1, source_target_pairs={{0,8},{4,12},{8,0},{12,4},{1,9},{5,13},{9,1},{13,5},{2,10},{6,14},... | collective-permute-start | bytes 13064 | tf_op jit(solution)/shard_map/ppermute | solution.py:18
  39.8 10.3 %collective-permute-start.13 = (bf16[1,32,1296]{2,1,0:T(8,128)(2,1)S(1)}, bf16[1,32,1296]{2,1,0:T(8,128)(2,1)S(1)}, u32[]{:S(2)}, u32[]{:S(2)}) collective-permute-start(bf16[1,32,1296]{2,1,0:T(8,128)(2,1)S(1)} %get-tuple-element.87), channel_id=1, source_target_pairs={{0,2},{1,3},{2,0},{3,1},{4,6},{5,7},{6,4},{7,5},{8,10},{9,11},{10,... | collective-permute-start | bytes 248840 | tf_op jit(solution)/shard_map/ppermute | solution.py:18
  41.4 12.0 %collective-permute-start.17 = (bf16[1,32,1296]{2,1,0:T(8,128)(2,1)S(1)}, bf16[1,32,1296]{2,1,0:T(8,128)(2,1)S(1)}, u32[]{:S(2)}, u32[]{:S(2)}) collective-permute-start(bf16[1,32,1296]{2,1,0:T(8,128)(2,1)S(1)} %get-tuple-element.86), channel_id=1, source_target_pairs={{0,2},{1,3},{2,0},{3,1},{4,6},{5,7},{6,4},{7,5},{8,10},{9,11},{10,... | collective-permute-start | bytes 248840 | tf_op jit(solution)/shard_map/ppermute | solution.py:18
  42.8 10.7 %copy-start.3 = (f32[16]{0:T(128)S(1)}, f32[16]{0:T(128)}, u32[]{:S(2)}) copy-start(f32[16]{0:T(128)} %param.22) | copy-start | bytes 196
  46.3 12.1 %copy-start.1 = (f32[1024]{0:T(1024)S(1)}, f32[1024]{0:T(1024)}, u32[]{:S(2)}) copy-start(f32[1024]{0:T(1024)} %param.25) | copy-start | bytes 12292
  50.2 8.2 %collective-permute-start.15 = (bf16[1,32,1024]{2,1,0:T(8,128)(2,1)S(1)}, bf16[1,32,1024]{2,1,0:T(8,128)(2,1)S(1)}, u32[]{:S(2)}, u32[]{:S(2)}) collective-permute-start(bf16[1,32,1024]{2,1,0:T(8,128)(2,1)S(1)} %get-tuple-element.89), channel_id=1, source_target_pairs={{0,2},{1,3},{2,0},{3,1},{4,6},{5,7},{6,4},{7,5},{8,10},{9,11},{10,... | collective-permute-start | bytes 196616 | tf_op jit(solution)/shard_map/ppermute | solution.py:18
  50.2 8.1 %collective-permute-start.14 = (bf16[1,32,1024]{2,1,0:T(8,128)(2,1)S(1)}, bf16[1,32,1024]{2,1,0:T(8,128)(2,1)S(1)}, u32[]{:S(2)}, u32[]{:S(2)}) collective-permute-start(bf16[1,32,1024]{2,1,0:T(8,128)(2,1)S(1)} %get-tuple-element.88), channel_id=1, source_target_pairs={{0,2},{1,3},{2,0},{3,1},{4,6},{5,7},{6,4},{7,5},{8,10},{9,11},{10,... | collective-permute-start | bytes 196616 | tf_op jit(solution)/shard_map/ppermute | solution.py:18
  59.4 1.7 %collective-permute-start.18 = (bf16[1,64,2176]{2,1,0:T(8,128)(2,1)S(1)}, bf16[1,64,2176]{2,1,0:T(8,128)(2,1)S(1)}, u32[]{:S(2)}, u32[]{:S(2)}) collective-permute-start(bf16[1,64,2176]{2,1,0:T(8,128)(2,1)S(1)} %get-tuple-element.64.after_ref), channel_id=1, source_target_pairs={{0,4},{4,0},{8,12},{12,8},{1,5},{5,1},{9,13},{13,9},{2,6},{6,2},{1... | collective-permute-start | bytes 835592 | tf_op jit(solution)/shard_map/ppermute | solution.py:18
  61.4 10.7 %collective-permute-start.19 = (bf16[1,32,2176]{2,1,0:T(8,128)(2,1)S(1)}, bf16[1,32,2176]{2,1,0:T(8,128)(2,1)S(1)}, u32[]{:S(2)}, u32[]{:S(2)}) collective-permute-start(bf16[1,32,2176]{2,1,0:T(8,128)(2,1)S(1)} %get-tuple-element.79), channel_id=1, source_target_pairs={{0,8},{4,12},{8,0},{12,4},{1,9},{5,13},{9,1},{13,5},{2,10},{6,14},... | collective-permute-start | bytes 417800 | tf_op jit(solution)/shard_map/ppermute | solution.py:18
  65.6 7.7 %collective-permute-start.21 = (bf16[1,64,2048]{2,1,0:T(8,128)(2,1)S(1)}, bf16[1,64,2048]{2,1,0:T(8,128)(2,1)S(1)}, u32[]{:S(2)}, u32[]{:S(2)}) collective-permute-start(bf16[1,64,2048]{2,1,0:T(8,128)(2,1)S(1)} %slice.31), channel_id=1, source_target_pairs={{0,4},{4,0},{8,12},{12,8},{1,5},{5,1},{9,13},{13,9},{2,6},{6,2},{1... | collective-permute-start | bytes 786440 | tf_op jit(solution)/shard_map/ppermute | solution.py:18
  65.8 7.0 %collective-permute-start.20 = (bf16[1,32,2176]{2,1,0:T(8,128)(2,1)S(1)}, bf16[1,32,2176]{2,1,0:T(8,128)(2,1)S(1)}, u32[]{:S(2)}, u32[]{:S(2)}) collective-permute-start(bf16[1,32,2176]{2,1,0:T(8,128)(2,1)S(1)} %get-tuple-element.78), channel_id=1, source_target_pairs={{0,8},{4,12},{8,0},{12,4},{1,9},{5,13},{9,1},{13,5},{2,10},{6,14},... | collective-permute-start | bytes 417800 | tf_op jit(solution)/shard_map/ppermute | solution.py:18
  (5 other events, 35.8 us)

commit v17 on v12

--- a/solution.py
+++ b/solution.py
@@ -683,14 +683,14 @@
         [*gate_terms, sums, result, gated_norm_scale[None]],
         model_width,
     )
-    (second,) = output_parts(
-        distances[2::4] + distances[1::4], out_weights, feature_width, [out_lhs, first]
+    (second,) = output_parts(distances[2::4], out_weights, feature_width, [out_lhs, first])
+    send, gate_squares = meet(swap(first, "head", 1), second, gate_squares)
+    (rest,) = output_parts(
+        distances[1::4] + distances[0::4], out_weights, feature_width, [out_lhs, send]
     )
-    half = second.shape[0] // 2
-    send, gate_squares = meet(swap(first, "head", 1), second, gate_squares)
-    (rest,) = output_parts(distances[0::4], out_weights, feature_width, [out_lhs, send])
+    half = rest.shape[0] // 2
     feeds, _ = lax.optimization_barrier((feeds, rest))
-    kept = [swap(second[half:], "head", 1), rest]
+    kept = [swap(rest[:half], "head", 1), rest[half:]]
     if len(bits_of(heads_n)) == 2:
         received = swap_halves(send, "head", 2, 1)
         mixer = sum(t[0].astype(F32) for t in [received[..., :feature_width]] + kept)

time: 70.8 us -> 71.2 us (level)
  waiting for transfers between devices: 15.3 us -> 16.1 us
    ppermute x17, waiting for transfers between devices: 10 us -> 10.8 us  [swap(): return lax.ppermute(values, axis, [(i, i ^ distance) for i in range(size)])]
  transfers between devices with their start and end apart: 18 -> 18, of which waited for: 8 -> 9; matrix products, arithmetic and copies ran while one was open for 1% -> 1% of each run, Pallas kernels for 43% -> 43%
where the time goes in v17:
time: 71.2 us; the launch traced here: 71 us
  Pallas kernels  31.4 us (44%)
  starting transfers between devices  17.8 us (25%)
  waiting for transfers between devices  16.1 us (23%)
  local copies, waits for them, and re-layouts  2.18 us (3%)
  other arithmetic  1.84 us (3%)
  between operations  1.66 us (2%)
    ppermute x17, starting transfers between devices, swap(): return lax.ppermute(values, axis, [(i, i ^ distance) for i in range(size)])  14.8 us
    pallas_call x3, Pallas kernels, load(): pl.pallas_call(functools.partial(load_body, spans), out_shape=tuple((pltp...  10.9 us
    ppermute x17, waiting for transfers between devices, swap(): return lax.ppermute(values, axis, [(i, i ^ distance) for i in range(size)])  10.8 us
    ppermute x1, waiting for transfers between devices, on_device(): turned = lax.ppermute(scaled_flat, ('head', 'row'), turn)  5.3 us
    pallas_call x1, Pallas kernels, state_write(): pl.pallas_call(state_write_body, out_shape=jax.ShapeDtypeStruct(state.sha...  4.89 us
    pallas_call x1, Pallas kernels, recur(): pl.pallas_call(functools.partial(recur_body, len(terms), group, model_wid...  4.84 us
    pallas_call x1, Pallas kernels, adapt(): pl.pallas_call(adapt_body, out_shape=(jax.ShapeDtypeStruct((rows, rank +...  3.77 us
    pallas_call x3, Pallas kernels, output_parts(): pl.pallas_call(body, out_shape=tuple(out_shape), in_specs=specs, out_spec...  3.41 us
  transfers between devices with their start and end apart: 18, of which 9 were waited for; matrix products, arithmetic and copies ran while one was open for 1% of the time, Pallas kernels for 43%

profile of v17, /device:TPU:0, one launch (start us, length us, event | category | flops | bytes accessed | tf_op | source)
XLA Modules:
  0.0 71.0 jit_solution(11344106962598191362)
XLA Ops:
  0.6 1.1 %fusion.1 = (f32[2,32]{1,0:T(2,128)S(1)}, bf16[2,32,2048]{2,1,0:T(8,128)(2,1)S(1)}) fusion(bf16[32,2,2048]{2,1,0:T(2,128)(2,1)} %param.16, f32[2048]{0:T(1024)} %param.17), kind=kLoop, calls=%fused_computation.4 | loop fusion | flops 655296 | bytes 532736 | tf_op jit(solution)/shard_map/reduce_sum | solution.py:604
  1.8 3.0 %collective-permute-start = (bf16[64,2048]{1,0:T(8,128)(2,1)S(1)}, bf16[64,2048]{1,0:T(8,128)(2,1)S(1)}, u32[]{:S(2)}, u32[]{:S(2)}) collective-permute-start(bf16[64,2048]{1,0:T(8,128)(2,1)S(1)} %bitcast.36), channel_id=1, source_target_pairs={{0,8},{1,12},{2,0},{3,4},{4,9},{5,13},{6,1},{7,5},{8,10},{9,14},{1... | collective-permute-start | bytes 786440 | tf_op jit(solution)/shard_map/ppermute | solution.py:616
  5.5 3.8 %adapt.1 = (f32[64,17]{1,0:T(8,128)S(1)}, bf16[512,1024]{1,0:T(8,128)(2,1)S(1)}) custom-call(s32[32]{0:T(128)S(1)} %copy-done.2, bf16[64,2048]{1,0:T(8,128)(2,1)S(1)} %bitcast.37, f32[64,1]{1,0:T(8,128)S(1)} %reshape.29.squares_ref, bf16[128,16,2048]{2,1,0:T(8,128)(2,1)} %bitcast.45, bf16[128,16,1024]{2,1,0:T(8,128)(2,1)} %up_ref.1), custom_call_target="tpu_custom_call" | custom-call | flops 134217728 | bytes 3145728 | tf_op jit(solution)/shard_map/adapt/pallas_call | solution.py:145
  9.3 3.9 %load.3 = (bf16[2048,1024]{1,0:T(8,128)(2,1)S(1)}, bf16[2048,256]{1,0:T(8,128)(2,1)S(1)}, bf16[2048,1024]{1,0:T(8,128)(2,1)S(1)}) custom-call(f32[64,17]{1,0:T(8,128)S(1)} %get-tuple-element.51.after_ref, bf16[2048,1024]{1,0:T(8,128)(2,1)} %refs_0_.3, bf16[2048,256]{1,0:T(8,128)(2,1)} %refs_1_.1, bf16[2048,1024]{1,0:T(8,128)(2,1)} %refs_2_.1), custom_call_target="tpu_custom_call" | custom-call | bytes 18874368 | tf_op jit(solution)/shard_map/load/pallas_call | solution.py:82
  13.2 5.3 %collective-permute-done.after_ref.refs_0_ = bf16[64,2048]{1,0:T(8,128)(2,1)S(1)} collective-permute-done((bf16[64,2048]{1,0:T(8,128)(2,1)S(1)}, bf16[64,2048]{1,0:T(8,128)(2,1)S(1)}, u32[]{:S(2)}, u32[]{:S(2)}) %collective-permute-start) | collective-permute-done | bytes 262176 | tf_op jit(solution)/shard_map/ppermute | solution.py:616
  18.5 3.5 %load.4.refs_6_.refs_0_ = bf16[512,8192]{1,0:T(8,128)(2,1)S(1)} custom-call(bf16[64,2048]{1,0:T(8,128)(2,1)S(1)} %collective-permute-done.after_ref.refs_0_, bf16[1024,8192]{1,0:T(8,128)(2,1)} %refs_0_.5), custom_call_target="tpu_custom_call" | custom-call | bytes 16777216 | tf_op jit(solution)/shard_map/load/pallas_call | solution.py:82
  22.0 2.9 %collective-permute-done.2.refs_2_.refs_0_ = bf16[64,2048]{1,0:T(8,128)(2,1)S(1)} collective-permute-done((bf16[64,2048]{1,0:T(8,128)(2,1)S(1)}, bf16[64,2048]{1,0:T(8,128)(2,1)S(1)}, u32[]{:S(2)}, u32[]{:S(2)}) %collective-permute-start.2) | collective-permute-done | bytes 262176 | tf_op jit(solution)/shard_map/ppermute | solution.py:18
  25.5 1.1 %project_signal.2 = (bf16[1,64,1296]{2,1,0:T(8,128)(2,1)S(1)}, bf16[1,64,1296]{2,1,0:T(8,128)(2,1)S(1)}, bf16[128,2048]{1,0:T(8,128)(2,1)S(1)}) custom-call(bf16[64,2048]{1,0:T(8,128)(2,1)S(1)} %collective-permute-done.after_ref.refs_0_, bf16[64,2048]{1,0:T(8,128)(2,1)S(1)} %collective-permute-done.1.refs_1_, ...), custom_call_target="tpu_custom_call" | custom-call | flops 679477248 | bytes 5308416 | tf_op jit(solution)/shard_map/project_signal/pallas_call | solution.py:211
  26.6 1.4 %collective-permute-start.6 = (bf16[1,64,1296]{2,1,0:T(8,128)(2,1)S(1)}, bf16[1,64,1296]{2,1,0:T(8,128)(2,1)S(1)}, u32[]{:S(2)}, u32[]{:S(2)}) collective-permute-start(bf16[1,64,1296]{2,1,0:T(8,128)(2,1)S(1)} %get-tuple-element.43.refs_2_), channel_id=1, source_target_pairs={{0,1},{1,0},{2,3},{3,2},{4,5},{5,4},{6,7},{7,6},{8,9},{9,8},{10,11... | collective-permute-start | bytes 497672 | tf_op jit(solution)/shard_map/ppermute | solution.py:18
  28.0 1.1 %project_signal.3 = (bf16[1,64,1296]{2,1,0:T(8,128)(2,1)S(1)}, bf16[1,64,1296]{2,1,0:T(8,128)(2,1)S(1)}, bf16[128,2048]{1,0:T(8,128)(2,1)S(1)}) custom-call(bf16[64,2048]{1,0:T(8,128)(2,1)S(1)} %collective-permute-done.2.refs_2_.refs_0_, bf16[64,2048]{1,0:T(8,128)(2,1)S(1)} %collective-permute-done.3.refs_1_, ...), custom_call_target="tpu_custom_call" | custom-call | flops 679477248 | bytes 5308416 | tf_op jit(solution)/shard_map/project_signal/pallas_call | solution.py:211
  29.8 1.3 %project_gate.1 = (bf16[2,64,1024]{2,1,0:T(8,128)(2,1)S(1)}, bf16[2,64,1024]{2,1,0:T(8,128)(2,1)S(1)}) custom-call(bf16[128,2048]{1,0:T(8,128)(2,1)S(1)} %get-tuple-element.42.refs_0_, bf16[128,2048]{1,0:T(8,128)(2,1)S(1)} %get-tuple-element.44.refs_1_, bf16[2048,1024]{1,0:T(8,128)(2,1)S(1)} %get-tuple-element.45.refs_2_, ...), custom_call_target="tpu_custom_call" | custom-call | flops 1073741824 | bytes 4194304 | tf_op jit(solution)/shard_map/project_gate/pallas_call | solution.py:251
  31.1 1.4 %collective-permute-start.4 = (bf16[1,64,1024]{2,1,0:T(8,128)(2,1)S(1)}, bf16[1,64,1024]{2,1,0:T(8,128)(2,1)S(1)}, u32[]{:S(2)}, u32[]{:S(2)}) collective-permute-start(bf16[1,64,1024]{2,1,0:T(8,128)(2,1)S(1)} %get-tuple-element.75), channel_id=1, source_target_pairs={{0,1},{1,0},{2,3},{3,2},{4,5},{5,4},{6,7},{7,6},{8,9},{9,8},{10,11... | collective-permute-start | bytes 393224 | tf_op jit(solution)/shard_map/ppermute | solution.py:18
  33.8 1.7 %collective-permute-start.8 = (f32[64,17]{1,0:T(8,128)S(1)}, f32[64,17]{1,0:T(8,128)S(1)}, u32[]{:S(2)}, u32[]{:S(2)}) collective-permute-start(f32[64,17]{1,0:T(8,128)S(1)} %add.37), channel_id=1, source_target_pairs={{0,8},{4,12},{8,0},{12,4},{1,9},{5,13},{9,1},{13,5},{2,10},{6,14},... | collective-permute-start | bytes 13064 | tf_op jit(solution)/shard_map/ppermute | solution.py:18
  35.5 2.2 %collective-permute-done.8 = f32[64,17]{1,0:T(8,128)S(1)} collective-permute-done((f32[64,17]{1,0:T(8,128)S(1)}, f32[64,17]{1,0:T(8,128)S(1)}, u32[]{:S(2)}, u32[]{:S(2)}) %collective-permute-start.8) | collective-permute-done | bytes 4384 | tf_op jit(solution)/shard_map/ppermute | solution.py:18
  38.0 2.2 %collective-permute-start.9 = (bf16[1,32,1296]{2,1,0:T(8,128)(2,1)S(1)}, bf16[1,32,1296]{2,1,0:T(8,128)(2,1)S(1)}, u32[]{:S(2)}, u32[]{:S(2)}) collective-permute-start(bf16[1,32,1296]{2,1,0:T(8,128)(2,1)S(1)} %get-tuple-element.79), channel_id=1, source_target_pairs={{0,2},{1,3},{2,0},{3,1},{4,6},{5,7},{6,4},{7,5},{8,10},{9,11},{10,... | collective-permute-start | bytes 248840 | tf_op jit(solution)/shard_map/ppermute | solution.py:18
  41.0 3.5 %load.5.refs_7_.refs_1_ = bf16[512,8192]{1,0:T(8,128)(2,1)S(1)} custom-call(bf16[1,64,1296]{2,1,0:T(8,128)(2,1)S(1)} %add_convert_fusion.after_ref, bf16[1024,8192]{1,0:T(8,128)(2,1)} %refs_0_.5), custom_call_target="tpu_custom_call" | custom-call | bytes 16777216 | tf_op jit(solution)/shard_map/load/pallas_call | solution.py:82
  44.7 3.2 %collective-permute-start.11 = (bf16[1,32,1024]{2,1,0:T(8,128)(2,1)S(1)}, bf16[1,32,1024]{2,1,0:T(8,128)(2,1)S(1)}, u32[]{:S(2)}, u32[]{:S(2)}) collective-permute-start(bf16[1,32,1024]{2,1,0:T(8,128)(2,1)S(1)} %get-tuple-element.81), channel_id=1, source_target_pairs={{0,2},{1,3},{2,0},{3,1},{4,6},{5,7},{6,4},{7,5},{8,10},{9,11},{10,... | collective-permute-start | bytes 196616 | tf_op jit(solution)/shard_map/ppermute | solution.py:18
  48.0 3.4 %collective-permute-done.13 = bf16[1,32,1296]{2,1,0:T(8,128)(2,1)S(1)} collective-permute-done((bf16[1,32,1296]{2,1,0:T(8,128)(2,1)S(1)}, bf16[1,32,1296]{2,1,0:T(8,128)(2,1)S(1)}, u32[]{:S(2)}, u32[]{:S(2)}) %collective-permute-start.13) | collective-permute-done | bytes 82976 | tf_op jit(solution)/shard_map/ppermute | solution.py:18
  51.5 4.8 %recur.1 = (f32[64,1024]{1,0:T(8,128)S(1)}, f32[2,32,1024]{2,1,0:T(8,128)S(1)}, f32[2,32,128]{2,1,0:T(8,128)S(1)}, f32[32,16]{1,0:T(8,128)S(1)}, bf16[32,16,64,128]{3,2,1,0:T(8,128)(2,1)S(1)}) custom-call(s32[1]{0:T(128)} %copy.45.live_ref, bf16[64,1296]{1,0:T(8,128)(2,1)S(1)} %maximum_bitcast_fusion.refs_0_, ...), custom_call_target="tpu_custom_call" | custom-call | flops 268435456 | bytes 10485760 | tf_op jit(solution)/shard_map/recur/pallas_call | solution.py:384
  56.4 1.0 %output_first.1 = (bf16[1,64,2176]{2,1,0:T(8,128)(2,1)S(1)}, bf16[64,1024]{1,0:T(8,128)(2,1)S(1)}, f32[64,1]{1,0:T(8,128)S(1)}) custom-call(bf16[64,1024]{1,0:T(8,128)(2,1)S(1)} %maximum_bitcast_fusion.1.refs_0_, bf16[64,1024]{1,0:T(8,128)(2,1)S(1)} %bitcast.40, bf16[64,1024]{1,0:T(8,128)(2,1)S(1)} %slice_bitcast_fusion.refs_2_, f32[64,17]{1,0:T(8,128)S(1)} %add.38.refs_3_, ...), custom_call_target="tpu_custom_call" | custom-call | flops 268435456 | bytes 4194304 | tf_op jit(solution)/shard_map/output_first/pallas_call | solution.py:558
  59.3 2.2 %collective-permute-start.15 = (bf16[1,32,2176]{2,1,0:T(8,128)(2,1)S(1)}, bf16[1,32,2176]{2,1,0:T(8,128)(2,1)S(1)}, u32[]{:S(2)}, u32[]{:S(2)}) collective-permute-start(bf16[1,32,2176]{2,1,0:T(8,128)(2,1)S(1)} %get-tuple-element.73), channel_id=1, source_target_pairs={{0,8},{4,12},{8,0},{12,4},{1,9},{5,13},{9,1},{13,5},{2,10},{6,14},... | collective-permute-start | bytes 417800 | tf_op jit(solution)/shard_map/ppermute | solution.py:18
  61.5 1.6 %output_rest.3 = bf16[2,64,2048]{2,1,0:T(8,128)(2,1)S(1)} custom-call(bf16[64,1024]{1,0:T(8,128)(2,1)S(1)} %get-tuple-element.61.lhs_ref, bf16[1,64,2176]{2,1,0:T(8,128)(2,1)S(1)} %get-tuple-element.63.after_ref, bf16[512,8192]{1,0:T(8,128)(2,1)S(1)} %load.4.refs_6_.refs_0_, bf16[512,8192]{1,0:T(8,128)(2,1)S(1)} %load.5.refs_7_.refs_1_), custom_call_target="tpu_custom_call" | custom-call | flops 536870912 | bytes 8388608 | tf_op jit(solution)/shard_map/output_rest/pallas_call | solution.py:558
  63.5 4.9 %state_write.1 = bf16[32,16,64,128]{3,2,1,0:T(8,128)(2,1)} custom-call(f32[2,32,1024]{2,1,0:T(8,128)S(1)} %get-tuple-element.66.feeds_ref, f32[2,32,128]{2,1,0:T(8,128)S(1)} %get-tuple-element.67.b_ref, f32[32,16,128]{2,1,0:T(8,128)S(1)} %broadcast_in_dim.42.decay_ref, bf16[32,16,64,128]{3,2,1,0:T(8,128)(2,1)S(1)} %get-tuple-element.69.state_ref), custom_call_target="tpu_custom_call" | custom-call | flops 134217728 | bytes 16777216 | tf_op jit(solution)/shard_map/state_write/pallas_call | solution.py:446
  70.0 1.0 %copy.39 = bf16[32,2,2048]{2,1,0:T(2,128)(2,1)} copy(bf16[32,2,2048]{2,0,1:T(8,128)(2,1)S(1)} %fusion.3) | data formatting | bytes 524288
  (66 shorter events, 7.9 us)
Async XLA Ops:
  1.8 16.7 %collective-permute-start = (bf16[64,2048]{1,0:T(8,128)(2,1)S(1)}, bf16[64,2048]{1,0:T(8,128)(2,1)S(1)}, u32[]{:S(2)}, u32[]{:S(2)}) collective-permute-start(bf16[64,2048]{1,0:T(8,128)(2,1)S(1)} %bitcast.36), channel_id=1, source_target_pairs={{0,8},{1,12},{2,0},{3,4},{4,9},{5,13},{6,1},{7,5},{8,10},{9,14},{1... | collective-permute-start | bytes 786440 | tf_op jit(solution)/shard_map/ppermute | solution.py:616
  18.5 7.0 %copy-start = (bf16[2048,16]{0,1:T(8,128)(2,1)S(1)}, bf16[2048,16]{0,1:T(8,128)(2,1)}, u32[]{:S(2)}) copy-start(bf16[2048,16]{0,1:T(8,128)(2,1)} %param.20) | copy-start | bytes 196612
  18.5 6.4 %collective-permute-start.2 = (bf16[64,2048]{1,0:T(8,128)(2,1)S(1)}, bf16[64,2048]{1,0:T(8,128)(2,1)S(1)}, u32[]{:S(2)}, u32[]{:S(2)}) collective-permute-start(bf16[64,2048]{1,0:T(8,128)(2,1)S(1)} %collective-permute-done.after_ref.refs_0_), channel_id=1, source_target_pairs={{0,8},{4,12},{8,0},{12,4},{1,9},{5,13},{9,1},{13,5},{2,10},{6,14},... | collective-permute-start | bytes 786440 | tf_op jit(solution)/shard_map/ppermute | solution.py:18
  18.5 7.0 %collective-permute-start.1 = (bf16[64,2048]{1,0:T(8,128)(2,1)S(1)}, bf16[64,2048]{1,0:T(8,128)(2,1)S(1)}, u32[]{:S(2)}, u32[]{:S(2)}) collective-permute-start(bf16[64,2048]{1,0:T(8,128)(2,1)S(1)} %collective-permute-done.after_ref.refs_0_), channel_id=1, source_target_pairs={{0,4},{4,0},{8,12},{12,8},{1,5},{5,1},{9,13},{13,9},{2,6},{6,2},{1... | collective-permute-start | bytes 786440 | tf_op jit(solution)/shard_map/ppermute | solution.py:18
  24.8 3.2 %collective-permute-start.3 = (bf16[64,2048]{1,0:T(8,128)(2,1)S(1)}, bf16[64,2048]{1,0:T(8,128)(2,1)S(1)}, u32[]{:S(2)}, u32[]{:S(2)}) collective-permute-start(bf16[64,2048]{1,0:T(8,128)(2,1)S(1)} %collective-permute-done.2.refs_2_.refs_0_), channel_id=1, source_target_pairs={{0,4},{4,0},{8,12},{12,8},{1,5},{5,1},{9,13},{13,9},{2,6},{6,2},{1... | collective-permute-start | bytes 786440 | tf_op jit(solution)/shard_map/ppermute | solution.py:18
  26.6 11.1 %collective-permute-start.6 = (bf16[1,64,1296]{2,1,0:T(8,128)(2,1)S(1)}, bf16[1,64,1296]{2,1,0:T(8,128)(2,1)S(1)}, u32[]{:S(2)}, u32[]{:S(2)}) collective-permute-start(bf16[1,64,1296]{2,1,0:T(8,128)(2,1)S(1)} %get-tuple-element.43.refs_2_), channel_id=1, source_target_pairs={{0,1},{1,0},{2,3},{3,2},{4,5},{5,4},{6,7},{7,6},{8,9},{9,8},{10,11... | collective-permute-start | bytes 497672 | tf_op jit(solution)/shard_map/ppermute | solution.py:18
  29.1 8.8 %collective-permute-start.5 = (bf16[1,64,1296]{2,1,0:T(8,128)(2,1)S(1)}, bf16[1,64,1296]{2,1,0:T(8,128)(2,1)S(1)}, u32[]{:S(2)}, u32[]{:S(2)}) collective-permute-start(bf16[1,64,1296]{2,1,0:T(8,128)(2,1)S(1)} %get-tuple-element.46.refs_3_), channel_id=1, source_target_pairs={{0,1},{1,0},{2,3},{3,2},{4,5},{5,4},{6,7},{7,6},{8,9},{9,8},{10,11... | collective-permute-start | bytes 497672 | tf_op jit(solution)/shard_map/ppermute | solution.py:18
  31.1 13.4 %collective-permute-start.4 = (bf16[1,64,1024]{2,1,0:T(8,128)(2,1)S(1)}, bf16[1,64,1024]{2,1,0:T(8,128)(2,1)S(1)}, u32[]{:S(2)}, u32[]{:S(2)}) collective-permute-start(bf16[1,64,1024]{2,1,0:T(8,128)(2,1)S(1)} %get-tuple-element.75), channel_id=1, source_target_pairs={{0,1},{1,0},{2,3},{3,2},{4,5},{5,4},{6,7},{7,6},{8,9},{9,8},{10,11... | collective-permute-start | bytes 393224 | tf_op jit(solution)/shard_map/ppermute | solution.py:18
  32.6 1.2 %collective-permute-start.7 = (f32[64,17]{1,0:T(8,128)S(1)}, f32[64,17]{1,0:T(8,128)S(1)}, u32[]{:S(2)}, u32[]{:S(2)}) collective-permute-start(f32[64,17]{1,0:T(8,128)S(1)} %get-tuple-element.51.after_ref), channel_id=1, source_target_pairs={{0,4},{4,0},{8,12},{12,8},{1,5},{5,1},{9,13},{13,9},{2,6},{6,2},{1... | collective-permute-start | bytes 13064 | tf_op jit(solution)/shard_map/ppermute | solution.py:18
  32.6 23.8 %collective-permute-start.12 = (bf16[1,64,1024]{2,1,0:T(8,128)(2,1)S(1)}, bf16[1,64,1024]{2,1,0:T(8,128)(2,1)S(1)}, u32[]{:S(2)}, u32[]{:S(2)}) collective-permute-start(bf16[1,64,1024]{2,1,0:T(8,128)(2,1)S(1)} %get-tuple-element.74), channel_id=1, source_target_pairs={{0,1},{1,0},{2,3},{3,2},{4,5},{5,4},{6,7},{7,6},{8,9},{9,8},{10,11... | collective-permute-start | bytes 393224 | tf_op jit(solution)/shard_map/ppermute | solution.py:18
  33.8 3.9 %collective-permute-start.8 = (f32[64,17]{1,0:T(8,128)S(1)}, f32[64,17]{1,0:T(8,128)S(1)}, u32[]{:S(2)}, u32[]{:S(2)}) collective-permute-start(f32[64,17]{1,0:T(8,128)S(1)} %add.37), channel_id=1, source_target_pairs={{0,8},{4,12},{8,0},{12,4},{1,9},{5,13},{9,1},{13,5},{2,10},{6,14},... | collective-permute-start | bytes 13064 | tf_op jit(solution)/shard_map/ppermute | solution.py:18
  38.0 6.6 %collective-permute-start.9 = (bf16[1,32,1296]{2,1,0:T(8,128)(2,1)S(1)}, bf16[1,32,1296]{2,1,0:T(8,128)(2,1)S(1)}, u32[]{:S(2)}, u32[]{:S(2)}) collective-permute-start(bf16[1,32,1296]{2,1,0:T(8,128)(2,1)S(1)} %get-tuple-element.79), channel_id=1, source_target_pairs={{0,2},{1,3},{2,0},{3,1},{4,6},{5,7},{6,4},{7,5},{8,10},{9,11},{10,... | collective-permute-start | bytes 248840 | tf_op jit(solution)/shard_map/ppermute | solution.py:18
  40.2 11.2 %collective-permute-start.13 = (bf16[1,32,1296]{2,1,0:T(8,128)(2,1)S(1)}, bf16[1,32,1296]{2,1,0:T(8,128)(2,1)S(1)}, u32[]{:S(2)}, u32[]{:S(2)}) collective-permute-start(bf16[1,32,1296]{2,1,0:T(8,128)(2,1)S(1)} %get-tuple-element.78), channel_id=1, source_target_pairs={{0,2},{1,3},{2,0},{3,1},{4,6},{5,7},{6,4},{7,5},{8,10},{9,11},{10,... | collective-permute-start | bytes 248840 | tf_op jit(solution)/shard_map/ppermute | solution.py:18
  41.0 10.5 %copy-start.3 = (f32[16]{0:T(128)S(1)}, f32[16]{0:T(128)}, u32[]{:S(2)}) copy-start(f32[16]{0:T(128)} %param.22) | copy-start | bytes 196
  41.0 10.5 %copy-start.4 = (f32[16]{0:T(128)S(1)}, f32[16]{0:T(128)}, u32[]{:S(2)}) copy-start(f32[16]{0:T(128)} %param.23) | copy-start | bytes 196
  41.0 10.5 %copy-start.5 = (f32[16]{0:T(128)S(1)}, f32[16]{0:T(128)}, u32[]{:S(2)}) copy-start(f32[16]{0:T(128)} %param.24) | copy-start | bytes 196
  44.5 11.9 %copy-start.1 = (f32[1024]{0:T(1024)S(1)}, f32[1024]{0:T(1024)}, u32[]{:S(2)}) copy-start(f32[1024]{0:T(1024)} %param.25) | copy-start | bytes 12292
  44.7 11.7 %collective-permute-start.11 = (bf16[1,32,1024]{2,1,0:T(8,128)(2,1)S(1)}, bf16[1,32,1024]{2,1,0:T(8,128)(2,1)S(1)}, u32[]{:S(2)}, u32[]{:S(2)}) collective-permute-start(bf16[1,32,1024]{2,1,0:T(8,128)(2,1)S(1)} %get-tuple-element.81), channel_id=1, source_target_pairs={{0,2},{1,3},{2,0},{3,1},{4,6},{5,7},{6,4},{7,5},{8,10},{9,11},{10,... | collective-permute-start | bytes 196616 | tf_op jit(solution)/shard_map/ppermute | solution.py:18
  47.9 8.4 %collective-permute-start.10 = (bf16[1,32,1024]{2,1,0:T(8,128)(2,1)S(1)}, bf16[1,32,1024]{2,1,0:T(8,128)(2,1)S(1)}, u32[]{:S(2)}, u32[]{:S(2)}) collective-permute-start(bf16[1,32,1024]{2,1,0:T(8,128)(2,1)S(1)} %get-tuple-element.80), channel_id=1, source_target_pairs={{0,2},{1,3},{2,0},{3,1},{4,6},{5,7},{6,4},{7,5},{8,10},{9,11},{10,... | collective-permute-start | bytes 196616 | tf_op jit(solution)/shard_map/ppermute | solution.py:18
  57.4 1.6 %collective-permute-start.14 = (bf16[1,64,2176]{2,1,0:T(8,128)(2,1)S(1)}, bf16[1,64,2176]{2,1,0:T(8,128)(2,1)S(1)}, u32[]{:S(2)}, u32[]{:S(2)}) collective-permute-start(bf16[1,64,2176]{2,1,0:T(8,128)(2,1)S(1)} %get-tuple-element.60.after_ref), channel_id=1, source_target_pairs={{0,4},{4,0},{8,12},{12,8},{1,5},{5,1},{9,13},{13,9},{2,6},{6,2},{1... | collective-permute-start | bytes 835592 | tf_op jit(solution)/shard_map/ppermute | solution.py:18
  59.3 9.1 %collective-permute-start.15 = (bf16[1,32,2176]{2,1,0:T(8,128)(2,1)S(1)}, bf16[1,32,2176]{2,1,0:T(8,128)(2,1)S(1)}, u32[]{:S(2)}, u32[]{:S(2)}) collective-permute-start(bf16[1,32,2176]{2,1,0:T(8,128)(2,1)S(1)} %get-tuple-element.73), channel_id=1, source_target_pairs={{0,8},{4,12},{8,0},{12,4},{1,9},{5,13},{9,1},{13,5},{2,10},{6,14},... | collective-permute-start | bytes 417800 | tf_op jit(solution)/shard_map/ppermute | solution.py:18
  63.1 6.6 %collective-permute-start.17 = (bf16[1,64,2048]{2,1,0:T(8,128)(2,1)S(1)}, bf16[1,64,2048]{2,1,0:T(8,128)(2,1)S(1)}, u32[]{:S(2)}, u32[]{:S(2)}) collective-permute-start(bf16[1,64,2048]{2,1,0:T(8,128)(2,1)S(1)} %slice.25), channel_id=1, source_target_pairs={{0,4},{4,0},{8,12},{12,8},{1,5},{5,1},{9,13},{13,9},{2,6},{6,2},{1... | collective-permute-start | bytes 786440 | tf_op jit(solution)/shard_map/ppermute | solution.py:18
  63.2 6.1 %collective-permute-start.16 = (bf16[1,32,2176]{2,1,0:T(8,128)(2,1)S(1)}, bf16[1,32,2176]{2,1,0:T(8,128)(2,1)S(1)}, u32[]{:S(2)}, u32[]{:S(2)}) collective-permute-start(bf16[1,32,2176]{2,1,0:T(8,128)(2,1)S(1)} %get-tuple-element.72), channel_id=1, source_target_pairs={{0,8},{4,12},{8,0},{12,4},{1,9},{5,13},{9,1},{13,5},{2,10},{6,14},... | collective-permute-start | bytes 417800 | tf_op jit(solution)/shard_map/ppermute | solution.py:18
  63.5 6.3 %copy-start.6 = (bf16[32,2,2048]{2,1,0:T(2,128)(2,1)S(1)}, bf16[32,2,2048]{2,1,0:T(2,128)(2,1)}, u32[]{:S(2)}) copy-start(bf16[32,2,2048]{2,1,0:T(2,128)(2,1)} %param.16) | copy-start | bytes 786436
  (1 other events, 0.7 us)

commit v18 on v12

--- a/solution.py
+++ b/solution.py
@@ -601,7 +601,9 @@
     scaled = (wide * input_norm_scale).astype(BF16)
     scaled_flat = scaled.reshape(rows, feature_width)
 
-    squares = jnp.sum(wide * wide, -1).reshape(rows, 1)
+    later, _ = lax.optimization_barrier((hidden, scaled_flat))
+    later = jnp.swapaxes(later, 0, 1).astype(F32)
+    squares = jnp.sum(later * later, -1).reshape(rows, 1)
     sums, up_rows = adapt(stream_tenant_index, scaled_flat, squares, adapter_down_weight, adapter_up_weight)
 
     own = group_of_own(2) == 0

time: 70.8 us -> 71 us (level)
  other arithmetic: 1.84 us -> 3.06 us
  waiting for transfers between devices: 15.3 us -> 14.1 us
    ppermute x1, waiting for transfers between devices: 5.27 us -> 3.87 us  [on_device(): turned = lax.ppermute(scaled_flat, ('head', 'row'), turn)]
    convert_element_type x0 -> x1, other arithmetic: none -> 1.06 us  [on_device(): scaled = (wide * input_norm_scale).astype(BF16)]
  transfers between devices with their start and end apart: 18 -> 18, of which waited for: 8 -> 8; matrix products, arithmetic and copies ran while one was open for 1% -> 3% of each run, Pallas kernels for 43% -> 43%
where the time goes in v18:
time: 71 us; the launch traced here: 70.8 us
  Pallas kernels  31.5 us (44%)
  starting transfers between devices  18.2 us (26%)
  waiting for transfers between devices  14.1 us (20%)
  other arithmetic  3.06 us (4%)
  local copies, waits for them, and re-layouts  2.27 us (3%)
  between operations  1.66 us (2%)
    ppermute x17, starting transfers between devices, swap(): return lax.ppermute(values, axis, [(i, i ^ distance) for i in range(size)])  15.2 us
    pallas_call x3, Pallas kernels, load(): pl.pallas_call(functools.partial(load_body, spans), out_shape=tuple((pltp...  10.9 us
    ppermute x17, waiting for transfers between devices, swap(): return lax.ppermute(values, axis, [(i, i ^ distance) for i in range(size)])  10.3 us
    pallas_call x1, Pallas kernels, state_write(): pl.pallas_call(state_write_body, out_shape=jax.ShapeDtypeStruct(state.sha...  4.89 us
    pallas_call x1, Pallas kernels, recur(): pl.pallas_call(functools.partial(recur_body, len(terms), group, model_wid...  4.84 us
    ppermute x1, waiting for transfers between devices, on_device(): turned = lax.ppermute(scaled_flat, ('head', 'row'), turn)  3.87 us
    pallas_call x1, Pallas kernels, adapt(): pl.pallas_call(adapt_body, out_shape=(jax.ShapeDtypeStruct((rows, rank +...  3.81 us
    pallas_call x3, Pallas kernels, output_parts(): pl.pallas_call(body, out_shape=tuple(out_shape), in_specs=specs, out_spec...  3.42 us
  transfers between devices with their start and end apart: 18, of which 8 were waited for; matrix products, arithmetic and copies ran while one was open for 3% of the time, Pallas kernels for 43%

profile of v18, /device:TPU:0, one launch (start us, length us, event | category | flops | bytes accessed | tf_op | source)
XLA Modules:
  0.0 70.8 jit_solution(10948534228171684109)
XLA Ops:
  0.6 1.1 %fusion = bf16[2,32,2048]{2,1,0:T(8,128)(2,1)S(1)} fusion(f32[2048]{0:T(1024)} %param.17, bf16[32,2,2048]{2,1,0:T(2,128)(2,1)} %param.16), kind=kLoop, calls=%fused_computation.2 | loop fusion | flops 393216 | bytes 532480 | tf_op jit(solution)/shard_map/convert_element_type | solution.py:601
  1.7 3.0 %collective-permute-start = (bf16[64,2048]{1,0:T(8,128)(2,1)S(1)}, bf16[64,2048]{1,0:T(8,128)(2,1)S(1)}, u32[]{:S(2)}, u32[]{:S(2)}) collective-permute-start(bf16[64,2048]{1,0:T(8,128)(2,1)S(1)} %bitcast.34), channel_id=1, source_target_pairs={{0,8},{1,12},{2,0},{3,4},{4,9},{5,13},{6,1},{7,5},{8,10},{9,14},{1... | collective-permute-start | bytes 786440 | tf_op jit(solution)/shard_map/ppermute | solution.py:618
  4.7 1.3 %multiply_reduce_fusion = f32[32,2]{1,0:T(8,128)S(1)} fusion(bf16[32,2,2048]{2,1,0:T(2,128)(2,1)} %param.16), kind=kLoop, calls=%fused_computation.5 | loop fusion | flops 393152 | bytes 262400 | tf_op jit(solution)/shard_map/reduce_sum | solution.py:606
  6.8 3.8 %adapt.1 = (f32[64,17]{1,0:T(8,128)S(1)}, bf16[512,1024]{1,0:T(8,128)(2,1)S(1)}) custom-call(s32[32]{0:T(128)S(1)} %copy-done.2, bf16[64,2048]{1,0:T(8,128)(2,1)S(1)} %bitcast.35, f32[64,1]{1,0:T(8,128)S(1)} %reshape.29.squares_ref, bf16[128,16,2048]{2,1,0:T(8,128)(2,1)} %bitcast.43, bf16[128,16,1024]{2,1,0:T(8,128)(2,1)} %up_ref.1), custom_call_target="tpu_custom_call" | custom-call | flops 134217728 | bytes 3145728 | tf_op jit(solution)/shard_map/adapt/pallas_call | solution.py:145
  10.7 3.9 %load.3 = (bf16[2048,1024]{1,0:T(8,128)(2,1)S(1)}, bf16[2048,256]{1,0:T(8,128)(2,1)S(1)}, bf16[2048,1024]{1,0:T(8,128)(2,1)S(1)}) custom-call(f32[64,17]{1,0:T(8,128)S(1)} %get-tuple-element.53.after_ref, bf16[2048,1024]{1,0:T(8,128)(2,1)} %refs_0_.3, bf16[2048,256]{1,0:T(8,128)(2,1)} %refs_1_.1, bf16[2048,1024]{1,0:T(8,128)(2,1)} %refs_2_.1), custom_call_target="tpu_custom_call" | custom-call | bytes 18874368 | tf_op jit(solution)/shard_map/load/pallas_call | solution.py:82
  14.6 3.9 %collective-permute-done.after_ref.refs_0_ = bf16[64,2048]{1,0:T(8,128)(2,1)S(1)} collective-permute-done((bf16[64,2048]{1,0:T(8,128)(2,1)S(1)}, bf16[64,2048]{1,0:T(8,128)(2,1)S(1)}, u32[]{:S(2)}, u32[]{:S(2)}) %collective-permute-start) | collective-permute-done | bytes 262176 | tf_op jit(solution)/shard_map/ppermute | solution.py:618
  18.4 3.5 %load.4.refs_6_.refs_0_ = bf16[512,8192]{1,0:T(8,128)(2,1)S(1)} custom-call(bf16[64,2048]{1,0:T(8,128)(2,1)S(1)} %collective-permute-done.after_ref.refs_0_, bf16[1024,8192]{1,0:T(8,128)(2,1)} %refs_0_.5), custom_call_target="tpu_custom_call" | custom-call | bytes 16777216 | tf_op jit(solution)/shard_map/load/pallas_call | solution.py:82
  21.9 2.9 %collective-permute-done.2.refs_2_.refs_0_ = bf16[64,2048]{1,0:T(8,128)(2,1)S(1)} collective-permute-done((bf16[64,2048]{1,0:T(8,128)(2,1)S(1)}, bf16[64,2048]{1,0:T(8,128)(2,1)S(1)}, u32[]{:S(2)}, u32[]{:S(2)}) %collective-permute-start.2) | collective-permute-done | bytes 262176 | tf_op jit(solution)/shard_map/ppermute | solution.py:18
  25.5 1.1 %project_signal.2 = (bf16[1,64,1296]{2,1,0:T(8,128)(2,1)S(1)}, bf16[1,64,1296]{2,1,0:T(8,128)(2,1)S(1)}, bf16[128,2048]{1,0:T(8,128)(2,1)S(1)}) custom-call(bf16[64,2048]{1,0:T(8,128)(2,1)S(1)} %collective-permute-done.after_ref.refs_0_, bf16[64,2048]{1,0:T(8,128)(2,1)S(1)} %collective-permute-done.1.refs_1_, ...), custom_call_target="tpu_custom_call" | custom-call | flops 679477248 | bytes 5308416 | tf_op jit(solution)/shard_map/project_signal/pallas_call | solution.py:211
  26.6 1.4 %collective-permute-start.6 = (bf16[1,64,1296]{2,1,0:T(8,128)(2,1)S(1)}, bf16[1,64,1296]{2,1,0:T(8,128)(2,1)S(1)}, u32[]{:S(2)}, u32[]{:S(2)}) collective-permute-start(bf16[1,64,1296]{2,1,0:T(8,128)(2,1)S(1)} %get-tuple-element.45.refs_2_), channel_id=1, source_target_pairs={{0,1},{1,0},{2,3},{3,2},{4,5},{5,4},{6,7},{7,6},{8,9},{9,8},{10,11... | collective-permute-start | bytes 497672 | tf_op jit(solution)/shard_map/ppermute | solution.py:18
  28.0 1.1 %project_signal.3 = (bf16[1,64,1296]{2,1,0:T(8,128)(2,1)S(1)}, bf16[1,64,1296]{2,1,0:T(8,128)(2,1)S(1)}, bf16[128,2048]{1,0:T(8,128)(2,1)S(1)}) custom-call(bf16[64,2048]{1,0:T(8,128)(2,1)S(1)} %collective-permute-done.2.refs_2_.refs_0_, bf16[64,2048]{1,0:T(8,128)(2,1)S(1)} %collective-permute-done.3.refs_1_, ...), custom_call_target="tpu_custom_call" | custom-call | flops 679477248 | bytes 5308416 | tf_op jit(solution)/shard_map/project_signal/pallas_call | solution.py:211
  29.8 1.3 %project_gate.1 = (bf16[2,64,1024]{2,1,0:T(8,128)(2,1)S(1)}, bf16[2,64,1024]{2,1,0:T(8,128)(2,1)S(1)}) custom-call(bf16[128,2048]{1,0:T(8,128)(2,1)S(1)} %get-tuple-element.44.refs_0_, bf16[128,2048]{1,0:T(8,128)(2,1)S(1)} %get-tuple-element.46.refs_1_, bf16[2048,1024]{1,0:T(8,128)(2,1)S(1)} %get-tuple-element.47.refs_2_, ...), custom_call_target="tpu_custom_call" | custom-call | flops 1073741824 | bytes 4194304 | tf_op jit(solution)/shard_map/project_gate/pallas_call | solution.py:251
  31.1 1.4 %collective-permute-start.4 = (bf16[1,64,1024]{2,1,0:T(8,128)(2,1)S(1)}, bf16[1,64,1024]{2,1,0:T(8,128)(2,1)S(1)}, u32[]{:S(2)}, u32[]{:S(2)}) collective-permute-start(bf16[1,64,1024]{2,1,0:T(8,128)(2,1)S(1)} %get-tuple-element.77), channel_id=1, source_target_pairs={{0,1},{1,0},{2,3},{3,2},{4,5},{5,4},{6,7},{7,6},{8,9},{9,8},{10,11... | collective-permute-start | bytes 393224 | tf_op jit(solution)/shard_map/ppermute | solution.py:18
  33.7 1.7 %collective-permute-start.8 = (f32[64,17]{1,0:T(8,128)S(1)}, f32[64,17]{1,0:T(8,128)S(1)}, u32[]{:S(2)}, u32[]{:S(2)}) collective-permute-start(f32[64,17]{1,0:T(8,128)S(1)} %add.37), channel_id=1, source_target_pairs={{0,8},{4,12},{8,0},{12,4},{1,9},{5,13},{9,1},{13,5},{2,10},{6,14},... | collective-permute-start | bytes 13064 | tf_op jit(solution)/shard_map/ppermute | solution.py:18
  35.5 2.2 %collective-permute-done.8 = f32[64,17]{1,0:T(8,128)S(1)} collective-permute-done((f32[64,17]{1,0:T(8,128)S(1)}, f32[64,17]{1,0:T(8,128)S(1)}, u32[]{:S(2)}, u32[]{:S(2)}) %collective-permute-start.8) | collective-permute-done | bytes 4384 | tf_op jit(solution)/shard_map/ppermute | solution.py:18
  38.0 2.3 %collective-permute-start.9 = (bf16[1,32,1296]{2,1,0:T(8,128)(2,1)S(1)}, bf16[1,32,1296]{2,1,0:T(8,128)(2,1)S(1)}, u32[]{:S(2)}, u32[]{:S(2)}) collective-permute-start(bf16[1,32,1296]{2,1,0:T(8,128)(2,1)S(1)} %get-tuple-element.79), channel_id=1, source_target_pairs={{0,2},{1,3},{2,0},{3,1},{4,6},{5,7},{6,4},{7,5},{8,10},{9,11},{10,... | collective-permute-start | bytes 248840 | tf_op jit(solution)/shard_map/ppermute | solution.py:18
  41.0 3.5 %load.5.refs_7_.refs_1_ = bf16[512,8192]{1,0:T(8,128)(2,1)S(1)} custom-call(bf16[1,64,1296]{2,1,0:T(8,128)(2,1)S(1)} %add_convert_fusion.after_ref, bf16[1024,8192]{1,0:T(8,128)(2,1)} %refs_0_.5), custom_call_target="tpu_custom_call" | custom-call | bytes 16777216 | tf_op jit(solution)/shard_map/load/pallas_call | solution.py:82
  44.9 3.0 %collective-permute-start.11 = (bf16[1,32,1024]{2,1,0:T(8,128)(2,1)S(1)}, bf16[1,32,1024]{2,1,0:T(8,128)(2,1)S(1)}, u32[]{:S(2)}, u32[]{:S(2)}) collective-permute-start(bf16[1,32,1024]{2,1,0:T(8,128)(2,1)S(1)} %get-tuple-element.81), channel_id=1, source_target_pairs={{0,2},{1,3},{2,0},{3,1},{4,6},{5,7},{6,4},{7,5},{8,10},{9,11},{10,... | collective-permute-start | bytes 196616 | tf_op jit(solution)/shard_map/ppermute | solution.py:18
  48.0 3.4 %collective-permute-done.13 = bf16[1,32,1296]{2,1,0:T(8,128)(2,1)S(1)} collective-permute-done((bf16[1,32,1296]{2,1,0:T(8,128)(2,1)S(1)}, bf16[1,32,1296]{2,1,0:T(8,128)(2,1)S(1)}, u32[]{:S(2)}, u32[]{:S(2)}) %collective-permute-start.13) | collective-permute-done | bytes 82976 | tf_op jit(solution)/shard_map/ppermute | solution.py:18
  51.4 4.8 %recur.1 = (f32[64,1024]{1,0:T(8,128)S(1)}, f32[2,32,1024]{2,1,0:T(8,128)S(1)}, f32[2,32,128]{2,1,0:T(8,128)S(1)}, f32[32,16]{1,0:T(8,128)S(1)}, bf16[32,16,64,128]{3,2,1,0:T(8,128)(2,1)S(1)}) custom-call(s32[1]{0:T(128)} %copy.42.live_ref, bf16[64,1296]{1,0:T(8,128)(2,1)S(1)} %maximum_bitcast_fusion.refs_0_, ...), custom_call_target="tpu_custom_call" | custom-call | flops 268435456 | bytes 10485760 | tf_op jit(solution)/shard_map/recur/pallas_call | solution.py:384
  56.3 1.0 %output_first.1 = (bf16[1,64,2176]{2,1,0:T(8,128)(2,1)S(1)}, bf16[64,1024]{1,0:T(8,128)(2,1)S(1)}, f32[64,1]{1,0:T(8,128)S(1)}) custom-call(bf16[64,1024]{1,0:T(8,128)(2,1)S(1)} %maximum_bitcast_fusion.1.refs_0_, bf16[64,1024]{1,0:T(8,128)(2,1)S(1)} %bitcast.38, bf16[64,1024]{1,0:T(8,128)(2,1)S(1)} %slice_bitcast_fusion.refs_2_, f32[64,17]{1,0:T(8,128)S(1)} %add.38.refs_3_, ...), custom_call_target="tpu_custom_call" | custom-call | flops 268435456 | bytes 4194304 | tf_op jit(solution)/shard_map/output_first/pallas_call | solution.py:558
  57.4 1.6 %output_rest.2.own_ref = bf16[2,64,2048]{2,1,0:T(8,128)(2,1)S(1)} custom-call(bf16[64,1024]{1,0:T(8,128)(2,1)S(1)} %get-tuple-element.63.lhs_ref, bf16[1,64,2176]{2,1,0:T(8,128)(2,1)S(1)} %get-tuple-element.62.after_ref, bf16[512,8192]{1,0:T(8,128)(2,1)S(1)} %load.4.refs_6_.refs_0_, bf16[512,8192]{1,0:T(8,128)(2,1)S(1)} %load.5.refs_7_.refs_1_), custom_call_target="tpu_custom_call" | custom-call | flops 536870912 | bytes 8388608 | tf_op jit(solution)/shard_map/output_rest/pallas_call | solution.py:558
  59.3 2.6 %collective-permute-start.15 = (bf16[1,32,2176]{2,1,0:T(8,128)(2,1)S(1)}, bf16[1,32,2176]{2,1,0:T(8,128)(2,1)S(1)}, u32[]{:S(2)}, u32[]{:S(2)}) collective-permute-start(bf16[1,32,2176]{2,1,0:T(8,128)(2,1)S(1)} %get-tuple-element.75), channel_id=1, source_target_pairs={{0,8},{4,12},{8,0},{12,4},{1,9},{5,13},{9,1},{13,5},{2,10},{6,14},... | collective-permute-start | bytes 417800 | tf_op jit(solution)/shard_map/ppermute | solution.py:18
  63.4 4.9 %state_write.1 = bf16[32,16,64,128]{3,2,1,0:T(8,128)(2,1)} custom-call(f32[2,32,1024]{2,1,0:T(8,128)S(1)} %get-tuple-element.68.feeds_ref, f32[2,32,128]{2,1,0:T(8,128)S(1)} %get-tuple-element.69.b_ref, f32[32,16,128]{2,1,0:T(8,128)S(1)} %broadcast_in_dim.42.decay_ref, bf16[32,16,64,128]{3,2,1,0:T(8,128)(2,1)S(1)} %get-tuple-element.71.state_ref), custom_call_target="tpu_custom_call" | custom-call | flops 134217728 | bytes 16777216 | tf_op jit(solution)/shard_map/state_write/pallas_call | solution.py:446
  (68 shorter events, 8.8 us)
Async XLA Ops:
  1.7 16.7 %collective-permute-start = (bf16[64,2048]{1,0:T(8,128)(2,1)S(1)}, bf16[64,2048]{1,0:T(8,128)(2,1)S(1)}, u32[]{:S(2)}, u32[]{:S(2)}) collective-permute-start(bf16[64,2048]{1,0:T(8,128)(2,1)S(1)} %bitcast.34), channel_id=1, source_target_pairs={{0,8},{1,12},{2,0},{3,4},{4,9},{5,13},{6,1},{7,5},{8,10},{9,14},{1... | collective-permute-start | bytes 786440 | tf_op jit(solution)/shard_map/ppermute | solution.py:618
  18.4 7.1 %copy-start = (bf16[2048,16]{0,1:T(8,128)(2,1)S(1)}, bf16[2048,16]{0,1:T(8,128)(2,1)}, u32[]{:S(2)}) copy-start(bf16[2048,16]{0,1:T(8,128)(2,1)} %param.20) | copy-start | bytes 196612
  18.4 6.4 %collective-permute-start.2 = (bf16[64,2048]{1,0:T(8,128)(2,1)S(1)}, bf16[64,2048]{1,0:T(8,128)(2,1)S(1)}, u32[]{:S(2)}, u32[]{:S(2)}) collective-permute-start(bf16[64,2048]{1,0:T(8,128)(2,1)S(1)} %collective-permute-done.after_ref.refs_0_), channel_id=1, source_target_pairs={{0,8},{4,12},{8,0},{12,4},{1,9},{5,13},{9,1},{13,5},{2,10},{6,14},... | collective-permute-start | bytes 786440 | tf_op jit(solution)/shard_map/ppermute | solution.py:18
  18.4 7.1 %collective-permute-start.1 = (bf16[64,2048]{1,0:T(8,128)(2,1)S(1)}, bf16[64,2048]{1,0:T(8,128)(2,1)S(1)}, u32[]{:S(2)}, u32[]{:S(2)}) collective-permute-start(bf16[64,2048]{1,0:T(8,128)(2,1)S(1)} %collective-permute-done.after_ref.refs_0_), channel_id=1, source_target_pairs={{0,4},{4,0},{8,12},{12,8},{1,5},{5,1},{9,13},{13,9},{2,6},{6,2},{1... | collective-permute-start | bytes 786440 | tf_op jit(solution)/shard_map/ppermute | solution.py:18
  24.8 3.2 %collective-permute-start.3 = (bf16[64,2048]{1,0:T(8,128)(2,1)S(1)}, bf16[64,2048]{1,0:T(8,128)(2,1)S(1)}, u32[]{:S(2)}, u32[]{:S(2)}) collective-permute-start(bf16[64,2048]{1,0:T(8,128)(2,1)S(1)} %collective-permute-done.2.refs_2_.refs_0_), channel_id=1, source_target_pairs={{0,4},{4,0},{8,12},{12,8},{1,5},{5,1},{9,13},{13,9},{2,6},{6,2},{1... | collective-permute-start | bytes 786440 | tf_op jit(solution)/shard_map/ppermute | solution.py:18
  26.6 11.1 %collective-permute-start.6 = (bf16[1,64,1296]{2,1,0:T(8,128)(2,1)S(1)}, bf16[1,64,1296]{2,1,0:T(8,128)(2,1)S(1)}, u32[]{:S(2)}, u32[]{:S(2)}) collective-permute-start(bf16[1,64,1296]{2,1,0:T(8,128)(2,1)S(1)} %get-tuple-element.45.refs_2_), channel_id=1, source_target_pairs={{0,1},{1,0},{2,3},{3,2},{4,5},{5,4},{6,7},{7,6},{8,9},{9,8},{10,11... | collective-permute-start | bytes 497672 | tf_op jit(solution)/shard_map/ppermute | solution.py:18
  29.1 8.8 %collective-permute-start.5 = (bf16[1,64,1296]{2,1,0:T(8,128)(2,1)S(1)}, bf16[1,64,1296]{2,1,0:T(8,128)(2,1)S(1)}, u32[]{:S(2)}, u32[]{:S(2)}) collective-permute-start(bf16[1,64,1296]{2,1,0:T(8,128)(2,1)S(1)} %get-tuple-element.48.refs_3_), channel_id=1, source_target_pairs={{0,1},{1,0},{2,3},{3,2},{4,5},{5,4},{6,7},{7,6},{8,9},{9,8},{10,11... | collective-permute-start | bytes 497672 | tf_op jit(solution)/shard_map/ppermute | solution.py:18
  31.1 13.4 %collective-permute-start.4 = (bf16[1,64,1024]{2,1,0:T(8,128)(2,1)S(1)}, bf16[1,64,1024]{2,1,0:T(8,128)(2,1)S(1)}, u32[]{:S(2)}, u32[]{:S(2)}) collective-permute-start(bf16[1,64,1024]{2,1,0:T(8,128)(2,1)S(1)} %get-tuple-element.77), channel_id=1, source_target_pairs={{0,1},{1,0},{2,3},{3,2},{4,5},{5,4},{6,7},{7,6},{8,9},{9,8},{10,11... | collective-permute-start | bytes 393224 | tf_op jit(solution)/shard_map/ppermute | solution.py:18
  32.5 1.2 %collective-permute-start.7 = (f32[64,17]{1,0:T(8,128)S(1)}, f32[64,17]{1,0:T(8,128)S(1)}, u32[]{:S(2)}, u32[]{:S(2)}) collective-permute-start(f32[64,17]{1,0:T(8,128)S(1)} %get-tuple-element.53.after_ref), channel_id=1, source_target_pairs={{0,4},{4,0},{8,12},{12,8},{1,5},{5,1},{9,13},{13,9},{2,6},{6,2},{1... | collective-permute-start | bytes 13064 | tf_op jit(solution)/shard_map/ppermute | solution.py:18
  32.5 23.8 %collective-permute-start.12 = (bf16[1,64,1024]{2,1,0:T(8,128)(2,1)S(1)}, bf16[1,64,1024]{2,1,0:T(8,128)(2,1)S(1)}, u32[]{:S(2)}, u32[]{:S(2)}) collective-permute-start(bf16[1,64,1024]{2,1,0:T(8,128)(2,1)S(1)} %get-tuple-element.76), channel_id=1, source_target_pairs={{0,1},{1,0},{2,3},{3,2},{4,5},{5,4},{6,7},{7,6},{8,9},{9,8},{10,11... | collective-permute-start | bytes 393224 | tf_op jit(solution)/shard_map/ppermute | solution.py:18
  33.7 3.9 %collective-permute-start.8 = (f32[64,17]{1,0:T(8,128)S(1)}, f32[64,17]{1,0:T(8,128)S(1)}, u32[]{:S(2)}, u32[]{:S(2)}) collective-permute-start(f32[64,17]{1,0:T(8,128)S(1)} %add.37), channel_id=1, source_target_pairs={{0,8},{4,12},{8,0},{12,4},{1,9},{5,13},{9,1},{13,5},{2,10},{6,14},... | collective-permute-start | bytes 13064 | tf_op jit(solution)/shard_map/ppermute | solution.py:18
  38.0 6.9 %collective-permute-start.9 = (bf16[1,32,1296]{2,1,0:T(8,128)(2,1)S(1)}, bf16[1,32,1296]{2,1,0:T(8,128)(2,1)S(1)}, u32[]{:S(2)}, u32[]{:S(2)}) collective-permute-start(bf16[1,32,1296]{2,1,0:T(8,128)(2,1)S(1)} %get-tuple-element.79), channel_id=1, source_target_pairs={{0,2},{1,3},{2,0},{3,1},{4,6},{5,7},{6,4},{7,5},{8,10},{9,11},{10,... | collective-permute-start | bytes 248840 | tf_op jit(solution)/shard_map/ppermute | solution.py:18
  40.2 11.1 %collective-permute-start.13 = (bf16[1,32,1296]{2,1,0:T(8,128)(2,1)S(1)}, bf16[1,32,1296]{2,1,0:T(8,128)(2,1)S(1)}, u32[]{:S(2)}, u32[]{:S(2)}) collective-permute-start(bf16[1,32,1296]{2,1,0:T(8,128)(2,1)S(1)} %get-tuple-element.78), channel_id=1, source_target_pairs={{0,2},{1,3},{2,0},{3,1},{4,6},{5,7},{6,4},{7,5},{8,10},{9,11},{10,... | collective-permute-start | bytes 248840 | tf_op jit(solution)/shard_map/ppermute | solution.py:18
  41.0 10.4 %copy-start.3 = (f32[16]{0:T(128)S(1)}, f32[16]{0:T(128)}, u32[]{:S(2)}) copy-start(f32[16]{0:T(128)} %param.22) | copy-start | bytes 196
  41.0 10.4 %copy-start.4 = (f32[16]{0:T(128)S(1)}, f32[16]{0:T(128)}, u32[]{:S(2)}) copy-start(f32[16]{0:T(128)} %param.23) | copy-start | bytes 196
  41.0 10.4 %copy-start.5 = (f32[16]{0:T(128)S(1)}, f32[16]{0:T(128)}, u32[]{:S(2)}) copy-start(f32[16]{0:T(128)} %param.24) | copy-start | bytes 196
  44.5 11.8 %copy-start.1 = (f32[1024]{0:T(1024)S(1)}, f32[1024]{0:T(1024)}, u32[]{:S(2)}) copy-start(f32[1024]{0:T(1024)} %param.25) | copy-start | bytes 12292
  44.9 11.3 %collective-permute-start.11 = (bf16[1,32,1024]{2,1,0:T(8,128)(2,1)S(1)}, bf16[1,32,1024]{2,1,0:T(8,128)(2,1)S(1)}, u32[]{:S(2)}, u32[]{:S(2)}) collective-permute-start(bf16[1,32,1024]{2,1,0:T(8,128)(2,1)S(1)} %get-tuple-element.81), channel_id=1, source_target_pairs={{0,2},{1,3},{2,0},{3,1},{4,6},{5,7},{6,4},{7,5},{8,10},{9,11},{10,... | collective-permute-start | bytes 196616 | tf_op jit(solution)/shard_map/ppermute | solution.py:18
  47.9 8.4 %collective-permute-start.10 = (bf16[1,32,1024]{2,1,0:T(8,128)(2,1)S(1)}, bf16[1,32,1024]{2,1,0:T(8,128)(2,1)S(1)}, u32[]{:S(2)}, u32[]{:S(2)}) collective-permute-start(bf16[1,32,1024]{2,1,0:T(8,128)(2,1)S(1)} %get-tuple-element.80), channel_id=1, source_target_pairs={{0,2},{1,3},{2,0},{3,1},{4,6},{5,7},{6,4},{7,5},{8,10},{9,11},{10,... | collective-permute-start | bytes 196616 | tf_op jit(solution)/shard_map/ppermute | solution.py:18
  57.3 1.7 %collective-permute-start.14 = (bf16[1,64,2176]{2,1,0:T(8,128)(2,1)S(1)}, bf16[1,64,2176]{2,1,0:T(8,128)(2,1)S(1)}, u32[]{:S(2)}, u32[]{:S(2)}) collective-permute-start(bf16[1,64,2176]{2,1,0:T(8,128)(2,1)S(1)} %get-tuple-element.62.after_ref), channel_id=1, source_target_pairs={{0,4},{4,0},{8,12},{12,8},{1,5},{5,1},{9,13},{13,9},{2,6},{6,2},{1... | collective-permute-start | bytes 835592 | tf_op jit(solution)/shard_map/ppermute | solution.py:18
  59.3 9.0 %collective-permute-start.15 = (bf16[1,32,2176]{2,1,0:T(8,128)(2,1)S(1)}, bf16[1,32,2176]{2,1,0:T(8,128)(2,1)S(1)}, u32[]{:S(2)}, u32[]{:S(2)}) collective-permute-start(bf16[1,32,2176]{2,1,0:T(8,128)(2,1)S(1)} %get-tuple-element.75), channel_id=1, source_target_pairs={{0,8},{4,12},{8,0},{12,4},{1,9},{5,13},{9,1},{13,5},{2,10},{6,14},... | collective-permute-start | bytes 417800 | tf_op jit(solution)/shard_map/ppermute | solution.py:18
  61.9 7.7 %collective-permute-start.17 = (bf16[1,64,2048]{2,1,0:T(8,128)(2,1)S(1)}, bf16[1,64,2048]{2,1,0:T(8,128)(2,1)S(1)}, u32[]{:S(2)}, u32[]{:S(2)}) collective-permute-start(bf16[1,64,2048]{2,1,0:T(8,128)(2,1)S(1)} %slice.21), channel_id=1, source_target_pairs={{0,4},{4,0},{8,12},{12,8},{1,5},{5,1},{9,13},{13,9},{2,6},{6,2},{1... | collective-permute-start | bytes 786440 | tf_op jit(solution)/shard_map/ppermute | solution.py:18
  62.1 7.0 %collective-permute-start.16 = (bf16[1,32,2176]{2,1,0:T(8,128)(2,1)S(1)}, bf16[1,32,2176]{2,1,0:T(8,128)(2,1)S(1)}, u32[]{:S(2)}, u32[]{:S(2)}) collective-permute-start(bf16[1,32,2176]{2,1,0:T(8,128)(2,1)S(1)} %get-tuple-element.74), channel_id=1, source_target_pairs={{0,8},{4,12},{8,0},{12,4},{1,9},{5,13},{9,1},{13,5},{2,10},{6,14},... | collective-permute-start | bytes 417800 | tf_op jit(solution)/shard_map/ppermute | solution.py:18
  63.4 6.3 %copy-start.6 = (bf16[32,2,2048]{2,1,0:T(2,128)(2,1)S(1)}, bf16[32,2,2048]{2,1,0:T(2,128)(2,1)}, u32[]{:S(2)}) copy-start(bf16[32,2,2048]{2,1,0:T(2,128)(2,1)} %param.16) | copy-start | bytes 786436
  (1 other events, 0.7 us)
